TPU v7x, 32 devices: a whole 2x2x4 slice. The times are simulated.
32 devices in a mesh: groups: 2 (over y), dp: 4 (over z), sub: 2 (over x), pair: 2 (over core).
Axes of the slice: x: 2, y: 2, z: 4, core: 2. Of those that a mesh axis runs over, the one named last changes fastest.
Arguments:
- inputs: bfloat16 [16384, 2048], P(('groups', 'dp', 'sub', 'pair')), parts along dimension 0, may hold values from -6 to 6
- cotangent: bfloat16 [16384, 256], P(('groups', 'dp', 'sub', 'pair')), parts along dimension 0, may hold values from -0.25 to 0.25
- error_prev: bfloat16 [32, 2048, 256], P(('groups', 'dp', 'sub', 'pair')), parts along dimension 0, may hold values from -16 to 16
- seed_q: float32 [32, 256], replicated, may hold values from -6 to 6
Outputs:
- error_next: bfloat16 [32, 2048, 256], P(('groups', 'dp', 'sub', 'pair')), parts along dimension 0
- basis: float32 [64, 2048], P('groups'), parts along dimension 0
- second: float32 [64, 256], P('groups'), parts along dimension 0
There are 2 independent parts, one for each index of `groups`. A program takes and returns all parts, laid end to end along the dimension named above; an argument that names none is the same for every part. Nothing has to cross between parts.
All inputs are finite; a program needn't handle non-finite values.
Results may differ from a plain program's by a relative error of at most 0.001.
Values sent between devices are 32-bit elements; how exact they have to be, the bound alone decides.
No kernel may reach another device: no remote copies, remote signals or barrier semaphores. Data moves between devices by JAX's collectives and lax.ppermute only.
A program may use at most 64 MiB of HBM per device.

v0:
```python
import jax
import jax.numpy as jnp
from jax import lax
from jax.sharding import PartitionSpec as P


def orthonormal_rows(rows, gram_of):
    for sweep in range(2):
        gram = gram_of(jnp.dot(rows, rows.T, precision=lax.Precision.HIGHEST))
        lower = jnp.linalg.cholesky(gram)
        rows = jax.scipy.linalg.solve_triangular(lower, rows, lower=True)
    return rows


def keep_local(gram):
    return gram


def local(inputs, cotangent, error_prev, seed_q):
    merged = lax.dot_general(
        inputs, cotangent, (((0,), (0,)), ((), ())), preferred_element_type=jnp.float32
    )
    merged = merged + error_prev[0].astype(jnp.float32)
    first_local = lax.dot_general(
        seed_q, merged, (((1,), (1,)), ((), ())), precision=lax.Precision.HIGHEST
    )
    first = lax.psum(first_local, ("dp", "sub", "pair"))
    basis = orthonormal_rows(first, keep_local)
    workers = lax.axis_size(("dp", "sub", "pair"))
    second_local = jnp.dot(basis, merged, precision=lax.Precision.HIGHEST)
    second = lax.psum(second_local, ("dp", "sub", "pair")) / workers
    approx = lax.dot_general(
        basis, second, (((0,), (0,)), ((), ())), precision=lax.Precision.HIGHEST
    )
    error_next = (merged - approx).astype(jnp.bfloat16)[None]
    return (error_next, basis, second)


def solution(mesh):
    placed = (
        P(("groups", "dp", "sub", "pair"), None),
        P(("groups", "dp", "sub", "pair"), None),
        P(("groups", "dp", "sub", "pair"), None, None),
        P(),
    )
    return jax.shard_map(
        local,
        mesh=mesh,
        in_specs=placed,
        out_specs=(
            P(("groups", "dp", "sub", "pair"), None, None),
            P("groups", None),
            P("groups", None),
        ),
        check_vma=False,
    )
```

profile of v0, /device:TPU:0, one launch (start us, length us, event | category | flops | bytes accessed | tf_op | source)
XLA Modules:
  0.0 197.8 jit_solution(9901037770016582590)
XLA Ops:
  7.2 0.0 copy-start
  7.2 0.0 copy-start.4
  7.2 0.0 all-reduce.2.cloned.1.call-start
  7.2 1.5 copy-done
  8.8 2.1 %convolution_add_fusion = f32[2048,256]{1,0:T(8,128)S(1)} fusion(bf16[512,2048]{1,0:T(8,128)(2,1)S(1)} %copy-done, bf16[512,256]{1,0:T(8,128)(2,1)} %param.8, bf16[1,2048,256]{2,1,0:T(8,128)(2,1)} %param.9), kind=kOutput, calls=%fused_computation.1 | convolution fusion | flops 537919488 | bytes 5505024 | tf_op jit(solution)/shard_map/dot_general | solution.py:20
  10.8 0.0 copy-start.1
  10.8 1.3 copy-done.1
  12.2 0.0 copy-done.4
  12.2 2.7 %convolution_bitcast_fusion = f32[32,2048]{1,0:T(8,128)} fusion(f32[2048,256]{1,0:T(8,128)S(1)} %convolution_add_fusion, f32[32,256]{1,0:T(8,128)S(1)} %copy-done.4), kind=kOutput, calls=%fused_computation.4 | convolution fusion | flops 201326592 | bytes 2392064 | tf_op jit(solution)/shard_map/dot_general | solution.py:24
  14.9 0.0 all-reduce.2.cloned.1.call-update
  14.9 91.6 %all-reduce.2.cloned.1.call-done = f32[32,2048]{1,0:T(8,128)} async-done(((f32[32,2048]{1,0:T(8,128)}), f32[32,2048]{1,0:T(8,128)}) %all-reduce.2.cloned.1.call-update) | async-done | bytes 262160 | tf_op jit(solution)/shard_map/psum | solution.py:27
  106.5 1.4 fusion.12
  107.9 0.1 copy.7
  108.0 2.9 %cholesky.44 = f32[32,32]{1,0:T(8,128)S(1)} custom-call(f32[32,32]{1,0:T(8,128)S(1)} %fusion.9), custom_call_target="Cholesky" | custom-call | tf_op jit(solution)/shard_map/jit(cholesky)/cholesky | solution.py:10
  111.0 0.6 compare_reduce_fusion.1
  111.6 0.7 fusion.2
  112.3 2.4 %custom-call.6 = f32[1,32,32]{1,2,0:T(8,128)S(1)} custom-call(f32[1,32,32]{2,1,0:T(8,128)S(1)} %fusion.2), custom_call_target="InvertDiagBlocksLowerTriangular" | custom-call | tf_op jit(solution)/shard_map/jit(_solve_triangular)/triangular_solve | solution.py:11
  114.7 1.4 fusion.7
  116.1 0.3 fusion.13
  116.4 0.1 copy.8
  116.5 2.9 %cholesky.55 = f32[32,32]{1,0:T(8,128)S(1)} custom-call(f32[32,32]{1,0:T(8,128)S(1)} %fusion.6), custom_call_target="Cholesky" | custom-call | tf_op jit(solution)/shard_map/jit(cholesky)/cholesky | solution.py:10
  119.5 0.6 compare_reduce_fusion
  120.1 0.7 fusion.3
  120.8 2.4 %custom-call.7 = f32[1,32,32]{1,2,0:T(8,128)S(1)} custom-call(f32[1,32,32]{2,1,0:T(8,128)S(1)} %fusion.3), custom_call_target="InvertDiagBlocksLowerTriangular" | custom-call | tf_op jit(solution)/shard_map/jit(_solve_triangular)/triangular_solve | solution.py:11
  123.2 0.4 fusion.4
  123.7 0.0 copy-start.2
  123.7 2.8 %fusion.14 = f32[32,256]{1,0:T(8,128)S(1)} fusion(f32[32,2048]{1,0:T(8,128)S(1)} %fusion.4, f32[2048,256]{1,0:T(8,128)} %copy-done.1), kind=kOutput, calls=%fused_computation.27 | convolution fusion | flops 201326592 | bytes 2392064 | tf_op jit(solution)/shard_map/dot_general | solution.py:30
  126.5 60.0 %psum.15 = f32[32,256]{1,0:T(8,128)S(1)} all-reduce(f32[32,256]{1,0:T(8,128)S(1)} %fusion.14), channel_id=1, replica_groups=mesh['groups'=2,'dp'=4,'sub'=2,'pair'=2] {'dp','sub','pair'}, use_global_device_ids=true, to_apply=%region_3.6 | all-reduce | flops 8192 | bytes 65536 | tf_op jit(solution)/shard_map/psum | solution.py:31
  186.5 0.0 copy-start.3
  186.5 4.4 %fusion.1 = bf16[1,2048,256]{2,1,0:T(8,128)(2,1)} fusion(f32[2048,256]{1,0:T(8,128)} %copy-done.1, f32[32,2048]{1,0:T(8,128)S(1)} %fusion.4, f32[32,256]{1,0:T(8,128)S(1)} %broadcast_multiply_fusion), kind=kOutput, calls=%fused_computation.3 | convolution fusion | flops 202375168 | bytes 3440640 | tf_op jit(solution)/shard_map/dot_general | solution.py:32
  190.9 0.0 copy-done.2
  190.9 0.0 copy-done.3
  (5 shorter events, 0.1 us)
Async XLA Ops:
  7.2 1.6 copy-start
  7.2 5.0 %copy-start.4 = (f32[32,256]{1,0:T(8,128)S(1)}, f32[32,256]{1,0:T(8,128)}, u32[]{:S(2)}) copy-start(f32[32,256]{1,0:T(8,128)} %param.10) | copy-start | bytes 98308
  7.2 99.3 %all-reduce.2.cloned.1.call-start = ((), (), s32[]{:S(2)}) async-start(), calls=%async_computation | async-start | bytes 524288 | tf_op jit(solution)/shard_map/psum | solution.py:27
  10.8 1.4 copy-start.1
  123.7 67.2 %copy-start.2 = (f32[32,2048]{1,0:T(8,128)}, f32[32,2048]{1,0:T(8,128)S(1)}, u32[]{:S(2)}) copy-start(f32[32,2048]{1,0:T(8,128)S(1)} %fusion.4) | copy-start | bytes 786436
  186.5 4.4 %copy-start.3 = (f32[32,256]{1,0:T(8,128)}, f32[32,256]{1,0:T(8,128)S(1)}, u32[]{:S(2)}) copy-start(f32[32,256]{1,0:T(8,128)S(1)} %broadcast_multiply_fusion) | copy-start | bytes 98308
Sparse Core Ops, SparseCore 0:
  15.0 91.4 all-reduce.1
where the time goes:
time: 198 us
  waiting for transfers between devices  91.6 us (46%)
  blocking collectives  60 us (30%)
  matrix products  15.5 us (8%)
  between operations  14.1 us (7%)
  other arithmetic  13.4 us (7%)
  local copies, waits for them, and re-layouts  3.04 us (2%)
    psum x1, waiting for transfers between devices, local(): first = lax.psum(first_local, ('dp', 'sub', 'pair'))  91.6 us
    psum x1, blocking collectives, local(): second = lax.psum(second_local, ('dp', 'sub', 'pair')) / workers  60 us
    another operation x6, other arithmetic, orthonormal_rows(): lower = jnp.linalg.cholesky(gram)  7.19 us
    another operation x4, other arithmetic, orthonormal_rows(): rows = jax.scipy.linalg.solve_triangular(lower, rows, lower=True)  6.17 us
    dot_general x1, matrix products, local(): lax.dot_general(basis, second, (((0,), (0,)), ((), ())), precision=lax.Pr...  4.41 us
  transfers between devices with their start and end apart: 1, of which 1 were waited for; matrix products, arithmetic and copies ran while one was open for 0% of the time, Pallas kernels for 0%

commit v1 on v0

v1 whole, which is shorter than its diff:
```python
import jax
import jax.numpy as jnp
from jax import lax
from jax.sharding import PartitionSpec as P

AXES = ("dp", "sub", "pair")
HIGHEST = lax.Precision.HIGHEST


def split_axes(mesh):
    direct, count = (), 1
    for axis in AXES:
        if count * mesh.shape[axis] <= 16:
            direct, count = direct + (axis,), count * mesh.shape[axis]
    rest = tuple(axis for axis in AXES if axis not in direct)
    return direct, rest, count


def exchange(block, shift, direct, count):
    return lax.ppermute(block, direct, [(i, (i + shift) % count) for i in range(count)])


def local(direct, rest, count, workers, inputs, cotangent, error_prev, seed_q):
    merged = lax.dot_general(
        inputs, cotangent, (((0,), (0,)), ((), ())), preferred_element_type=jnp.float32
    )
    merged = merged + error_prev[0].astype(jnp.float32)
    term = lax.dot_general(seed_q, merged, (((1,), (1,)), ((), ())), precision=HIGHEST)
    if rest:
        term = lax.psum(term, rest)
    me = lax.axis_index(direct)
    rank, width = term.shape
    piece = width // count
    pieces = term.reshape(rank, count, piece).transpose(1, 0, 2)
    pieces = jnp.roll(pieces, -me, axis=0)
    chunk = pieces[0]
    for shift in range(1, count):
        chunk = chunk + exchange(pieces[shift], shift, direct, count)
    chunks = [chunk] + [exchange(chunk, shift, direct, count) for shift in range(1, count)]
    first = jnp.roll(jnp.stack(chunks[::-1]), me + 1, axis=0)
    first = first.transpose(1, 0, 2).reshape(rank, width)

    product = jnp.dot(first, merged, precision=HIGHEST)
    if rest:
        product = lax.psum(product, rest)
    slim = product.shape[0] // count
    rows = product.reshape(count, slim, product.shape[1])
    rows = jnp.roll(rows, -me, axis=0)
    own = rows[0]
    for shift in range(1, count):
        own = own + exchange(rows[shift], shift, direct, count)
    owns = [own] + [exchange(own, shift, direct, count) for shift in range(1, count)]
    product = jnp.roll(jnp.stack(owns[::-1]), me + 1, axis=0).reshape(product.shape)

    basis = first
    for sweep in range(2):
        gram = jnp.dot(basis, basis.T, precision=HIGHEST)
        lower = jnp.linalg.cholesky(gram)
        basis = jax.scipy.linalg.solve_triangular(lower, basis, lower=True)
        product = jax.scipy.linalg.solve_triangular(lower, product, lower=True)
    second = product / workers
    approx = lax.dot_general(basis, second, (((0,), (0,)), ((), ())), precision=HIGHEST)
    error_next = (merged - approx).astype(jnp.bfloat16)[None]
    return (error_next, basis, second)


def solution(mesh):
    direct, rest, count = split_axes(mesh)
    workers = 1
    for axis in AXES:
        workers *= mesh.shape[axis]
    everyone = ("groups",) + AXES

    def run(*args):
        return local(direct, rest, count, workers, *args)

    return jax.shard_map(
        run,
        mesh=mesh,
        in_specs=(P(everyone, None), P(everyone, None), P(everyone, None, None), P()),
        out_specs=(P(everyone, None, None), P("groups", None), P("groups", None)),
        check_vma=False,
    )
```

time: 198 us -> 188 us (0.949)
  starting transfers between devices: 0.04 us -> 119 us
  blocking collectives: 60 us -> 0 us
  waiting for transfers between devices: 91.6 us -> 36.7 us
  between operations: 14.1 us -> 1.19 us
  matrix products: 15.5 us -> 13.2 us
    ppermute x0 -> x60, starting transfers between devices: none -> 119 us  [exchange(): lax.ppermute(block, direct, [(i, (i + shift) % count) for i in range(coun...]
    psum x1 -> x0, waiting for transfers between devices: 91.6 us -> none  [local(): first = lax.psum(first_local, ('dp', 'sub', 'pair'))]
    psum x1 -> x0, blocking collectives: 60 us -> none  [local(): second = lax.psum(second_local, ('dp', 'sub', 'pair')) / workers]
    ppermute x0 -> x60, waiting for transfers between devices: none -> 36.7 us  [exchange(): lax.ppermute(block, direct, [(i, (i + shift) % count) for i in range(coun...]
  transfers between devices with their start and end apart: 1 -> 60, of which waited for: 1 -> 23; matrix products, arithmetic and copies ran while one was open for 0% -> 8% of each run, Pallas kernels for 0% -> 0%
where the time goes in v1:
time: 188 us
  starting transfers between devices  119 us (63%)
  waiting for transfers between devices  36.7 us (20%)
  other arithmetic  13.6 us (7%)
  matrix products  13.2 us (7%)
  local copies, waits for them, and re-layouts  3.64 us (2%)
    ppermute x60, starting transfers between devices, exchange(): lax.ppermute(block, direct, [(i, (i + shift) % count) for i in range(coun...  119 us
    ppermute x60, waiting for transfers between devices, exchange(): lax.ppermute(block, direct, [(i, (i + shift) % count) for i in range(coun...  36.7 us
    another operation x6, other arithmetic, local(): lower = jnp.linalg.cholesky(gram)  7.18 us
    another operation x4, other arithmetic, local(): basis = jax.scipy.linalg.solve_triangular(lower, basis, lower=True)  6.17 us
    dot_general x1, matrix products, local(): lax.dot_general(basis, second, (((0,), (0,)), ((), ())), precision=HIGHEST)  4.42 us
  transfers between devices with their start and end apart: 60, of which 23 were waited for; matrix products, arithmetic and copies ran while one was open for 8% of the time, Pallas kernels for 0%

profile of v1, /device:TPU:0, one launch (start us, length us, event | category | flops | bytes accessed | tf_op | source)
XLA Modules:
  0.0 187.8 jit_solution(1319218965617642665)
XLA Ops:
  0.7 1.6 copy-done
  2.2 2.1 %convolution_add_fusion = f32[2048,256]{1,0:T(8,128)S(1)} fusion(bf16[512,2048]{1,0:T(8,128)(2,1)S(1)} %copy-done, bf16[512,256]{1,0:T(8,128)(2,1)} %param.14, bf16[1,2048,256]{2,1,0:T(8,128)(2,1)} %param.15), kind=kOutput, calls=%fused_computation.1 | convolution fusion | flops 537919488 | bytes 5505024 | tf_op jit(solution)/shard_map/dot_general | solution.py:24
  4.3 1.3 copy-done.1
  5.7 2.0 %convolution_bitcast_fusion = f32[4,16,8,128]{3,2,1,0:T(8,128)S(1)} fusion(f32[2048,256]{1,0:T(8,128)S(1)} %convolution_add_fusion, f32[32,256]{1,0:T(8,128)S(1)} %copy-done.4), kind=kOutput, calls=%fused_computation.6 | convolution fusion | flops 201326592 | bytes 2392064 | tf_op jit(solution)/shard_map/dot_general | solution.py:28
  8.3 5.6 %collective-permute-start.13 = (f32[32,128]{1,0:T(8,128)S(1)}, f32[32,128]{1,0:T(8,128)S(1)}, u32[]{:S(2)}, u32[]{:S(2)}) collective-permute-start(f32[32,128]{1,0:T(8,128)S(1)} %get-tuple-element.11), channel_id=1, source_target_pairs={{0,14},{1,15},{2,0},{3,1},{4,2},{5,3},{6,4},{7,5},{8,6},{9,7},{10,... | collective-permute-start | bytes 49160 | tf_op jit(solution)/shard_map/ppermute | solution.py:20
  13.9 1.4 collective-permute-start.12
  15.7 2.5 %collective-permute-start.9 = (f32[32,128]{1,0:T(8,128)S(1)}, f32[32,128]{1,0:T(8,128)S(1)}, u32[]{:S(2)}, u32[]{:S(2)}) collective-permute-start(f32[32,128]{1,0:T(8,128)S(1)} %get-tuple-element.15), channel_id=1, source_target_pairs={{0,10},{1,11},{2,12},{3,13},{4,14},{5,15},{6,0},{7,1},{8,2},{9,3},... | collective-permute-start | bytes 49160 | tf_op jit(solution)/shard_map/ppermute | solution.py:20
  18.6 2.6 %collective-permute-start.7 = (f32[32,128]{1,0:T(8,128)S(1)}, f32[32,128]{1,0:T(8,128)S(1)}, u32[]{:S(2)}, u32[]{:S(2)}) collective-permute-start(f32[32,128]{1,0:T(8,128)S(1)} %get-tuple-element.17), channel_id=1, source_target_pairs={{0,8},{1,9},{2,10},{3,11},{4,12},{5,13},{6,14},{7,15},{8,0},{9,1},... | collective-permute-start | bytes 49160 | tf_op jit(solution)/shard_map/ppermute | solution.py:20
  21.7 2.7 %collective-permute-start.5 = (f32[32,128]{1,0:T(8,128)S(1)}, f32[32,128]{1,0:T(8,128)S(1)}, u32[]{:S(2)}, u32[]{:S(2)}) collective-permute-start(f32[32,128]{1,0:T(8,128)S(1)} %get-tuple-element.19), channel_id=1, source_target_pairs={{0,6},{1,7},{2,8},{3,9},{4,10},{5,11},{6,12},{7,13},{8,14},{9,15},... | collective-permute-start | bytes 49160 | tf_op jit(solution)/shard_map/ppermute | solution.py:20
  24.4 2.5 %collective-permute-start.3 = (f32[32,128]{1,0:T(8,128)S(1)}, f32[32,128]{1,0:T(8,128)S(1)}, u32[]{:S(2)}, u32[]{:S(2)}) collective-permute-start(f32[32,128]{1,0:T(8,128)S(1)} %get-tuple-element.21), channel_id=1, source_target_pairs={{0,4},{1,5},{2,6},{3,7},{4,8},{5,9},{6,10},{7,11},{8,12},{9,13},{1... | collective-permute-start | bytes 49160 | tf_op jit(solution)/shard_map/ppermute | solution.py:20
  26.9 2.1 %collective-permute-start.2 = (f32[32,128]{1,0:T(8,128)S(1)}, f32[32,128]{1,0:T(8,128)S(1)}, u32[]{:S(2)}, u32[]{:S(2)}) collective-permute-start(f32[32,128]{1,0:T(8,128)S(1)} %get-tuple-element.22), channel_id=1, source_target_pairs={{0,3},{1,4},{2,5},{3,6},{4,7},{5,8},{6,9},{7,10},{8,11},{9,12},{10... | collective-permute-start | bytes 49160 | tf_op jit(solution)/shard_map/ppermute | solution.py:20
  29.5 2.4 %collective-permute-start.14 = (f32[32,128]{1,0:T(8,128)S(1)}, f32[32,128]{1,0:T(8,128)S(1)}, u32[]{:S(2)}, u32[]{:S(2)}) collective-permute-start(f32[32,128]{1,0:T(8,128)S(1)} %get-tuple-element.24), channel_id=1, source_target_pairs={{0,15},{1,0},{2,1},{3,2},{4,3},{5,4},{6,5},{7,6},{8,7},{9,8},{10,9... | collective-permute-start | bytes 49160 | tf_op jit(solution)/shard_map/ppermute | solution.py:20
  31.9 3.6 %collective-permute-done.1 = f32[32,128]{1,0:T(8,128)S(1)} collective-permute-done((f32[32,128]{1,0:T(8,128)S(1)}, f32[32,128]{1,0:T(8,128)S(1)}, u32[]{:S(2)}, u32[]{:S(2)}) %collective-permute-start.1) | collective-permute-done | bytes 16416 | tf_op jit(solution)/shard_map/ppermute | solution.py:20
  35.5 2.3 %collective-permute-start.15 = (f32[32,128]{1,0:T(8,128)S(1)}, f32[32,128]{1,0:T(8,128)S(1)}, u32[]{:S(2)}, u32[]{:S(2)}) collective-permute-start(f32[32,128]{1,0:T(8,128)S(1)} %fusion.30), channel_id=1, source_target_pairs={{0,15},{1,0},{2,1},{3,2},{4,3},{5,4},{6,5},{7,6},{8,7},{9,8},{10,9... | collective-permute-start | bytes 49160 | tf_op jit(solution)/shard_map/ppermute | solution.py:20
  37.9 1.4 collective-permute-done.15
  39.3 3.4 %collective-permute-start.16 = (f32[32,128]{1,0:T(8,128)S(1)}, f32[32,128]{1,0:T(8,128)S(1)}, u32[]{:S(2)}, u32[]{:S(2)}) collective-permute-start(f32[32,128]{1,0:T(8,128)S(1)} %fusion.30), channel_id=1, source_target_pairs={{0,14},{1,15},{2,0},{3,1},{4,2},{5,3},{6,4},{7,5},{8,6},{9,7},{10,... | collective-permute-start | bytes 49160 | tf_op jit(solution)/shard_map/ppermute | solution.py:20
  42.6 1.4 collective-permute-done.16
  45.2 2.0 %collective-permute-done.17 = f32[32,128]{1,0:T(8,128)S(1)} collective-permute-done((f32[32,128]{1,0:T(8,128)S(1)}, f32[32,128]{1,0:T(8,128)S(1)}, u32[]{:S(2)}, u32[]{:S(2)}) %collective-permute-start.17) | collective-permute-done | bytes 16416 | tf_op jit(solution)/shard_map/ppermute | solution.py:20
  47.3 3.7 %collective-permute-start.18 = (f32[32,128]{1,0:T(8,128)S(1)}, f32[32,128]{1,0:T(8,128)S(1)}, u32[]{:S(2)}, u32[]{:S(2)}) collective-permute-start(f32[32,128]{1,0:T(8,128)S(1)} %fusion.30), channel_id=1, source_target_pairs={{0,12},{1,13},{2,14},{3,15},{4,0},{5,1},{6,2},{7,3},{8,4},{9,5},{1... | collective-permute-start | bytes 49160 | tf_op jit(solution)/shard_map/ppermute | solution.py:20
  51.0 1.4 collective-permute-done.18
  52.4 3.2 %collective-permute-start.19 = (f32[32,128]{1,0:T(8,128)S(1)}, f32[32,128]{1,0:T(8,128)S(1)}, u32[]{:S(2)}, u32[]{:S(2)}) collective-permute-start(f32[32,128]{1,0:T(8,128)S(1)} %fusion.30), channel_id=1, source_target_pairs={{0,11},{1,12},{2,13},{3,14},{4,15},{5,0},{6,1},{7,2},{8,3},{9,4},{... | collective-permute-start | bytes 49160 | tf_op jit(solution)/shard_map/ppermute | solution.py:20
  55.7 1.4 collective-permute-done.19
  57.1 3.5 %collective-permute-start.20 = (f32[32,128]{1,0:T(8,128)S(1)}, f32[32,128]{1,0:T(8,128)S(1)}, u32[]{:S(2)}, u32[]{:S(2)}) collective-permute-start(f32[32,128]{1,0:T(8,128)S(1)} %fusion.30), channel_id=1, source_target_pairs={{0,10},{1,11},{2,12},{3,13},{4,14},{5,15},{6,0},{7,1},{8,2},{9,3},... | collective-permute-start | bytes 49160 | tf_op jit(solution)/shard_map/ppermute | solution.py:20
  60.6 1.4 collective-permute-done.20
  62.1 3.6 %collective-permute-start.21 = (f32[32,128]{1,0:T(8,128)S(1)}, f32[32,128]{1,0:T(8,128)S(1)}, u32[]{:S(2)}, u32[]{:S(2)}) collective-permute-start(f32[32,128]{1,0:T(8,128)S(1)} %fusion.30), channel_id=1, source_target_pairs={{0,9},{1,10},{2,11},{3,12},{4,13},{5,14},{6,15},{7,0},{8,1},{9,2},... | collective-permute-start | bytes 49160 | tf_op jit(solution)/shard_map/ppermute | solution.py:20
  65.7 1.4 collective-permute-done.21
  67.1 4.7 %collective-permute-start.22 = (f32[32,128]{1,0:T(8,128)S(1)}, f32[32,128]{1,0:T(8,128)S(1)}, u32[]{:S(2)}, u32[]{:S(2)}) collective-permute-start(f32[32,128]{1,0:T(8,128)S(1)} %fusion.30), channel_id=1, source_target_pairs={{0,8},{1,9},{2,10},{3,11},{4,12},{5,13},{6,14},{7,15},{8,0},{9,1},... | collective-permute-start | bytes 49160 | tf_op jit(solution)/shard_map/ppermute | solution.py:20
  71.8 1.7 collective-permute-done.22
  73.5 2.7 %collective-permute-start.23 = (f32[32,128]{1,0:T(8,128)S(1)}, f32[32,128]{1,0:T(8,128)S(1)}, u32[]{:S(2)}, u32[]{:S(2)}) collective-permute-start(f32[32,128]{1,0:T(8,128)S(1)} %fusion.30), channel_id=1, source_target_pairs={{0,7},{1,8},{2,9},{3,10},{4,11},{5,12},{6,13},{7,14},{8,15},{9,0},... | collective-permute-start | bytes 49160 | tf_op jit(solution)/shard_map/ppermute | solution.py:20
  76.2 1.4 collective-permute-done.23
  77.6 4.7 %collective-permute-start.24 = (f32[32,128]{1,0:T(8,128)S(1)}, f32[32,128]{1,0:T(8,128)S(1)}, u32[]{:S(2)}, u32[]{:S(2)}) collective-permute-start(f32[32,128]{1,0:T(8,128)S(1)} %fusion.30), channel_id=1, source_target_pairs={{0,6},{1,7},{2,8},{3,9},{4,10},{5,11},{6,12},{7,13},{8,14},{9,15},... | collective-permute-start | bytes 49160 | tf_op jit(solution)/shard_map/ppermute | solution.py:20
  82.3 1.4 collective-permute-done.24
  83.7 2.9 %collective-permute-start.25 = (f32[32,128]{1,0:T(8,128)S(1)}, f32[32,128]{1,0:T(8,128)S(1)}, u32[]{:S(2)}, u32[]{:S(2)}) collective-permute-start(f32[32,128]{1,0:T(8,128)S(1)} %fusion.30), channel_id=1, source_target_pairs={{0,5},{1,6},{2,7},{3,8},{4,9},{5,10},{6,11},{7,12},{8,13},{9,14},{... | collective-permute-start | bytes 49160 | tf_op jit(solution)/shard_map/ppermute | solution.py:20
  86.7 2.0 %collective-permute-done.25 = f32[32,128]{1,0:T(8,128)S(1)} collective-permute-done((f32[32,128]{1,0:T(8,128)S(1)}, f32[32,128]{1,0:T(8,128)S(1)}, u32[]{:S(2)}, u32[]{:S(2)}) %collective-permute-start.25) | collective-permute-done | bytes 16416 | tf_op jit(solution)/shard_map/ppermute | solution.py:20
  89.5 2.7 %fusion.2 = f32[16,2,256]{2,0,1:T(8,128)S(1)} fusion(f32[2048,256]{1,0:T(8,128)} %copy-done.1, f32[16,2,2048]{2,1,0:T(2,128)S(1)} %dot_general.27), kind=kOutput, calls=%fused_computation.4 | convolution fusion | flops 201326592 | bytes 2392064 | tf_op jit(solution)/shard_map/dot_general | solution.py:43
  93.3 3.8 %collective-permute-start.43 = (f32[2,256]{1,0:T(2,128)S(1)}, f32[2,256]{1,0:T(2,128)S(1)}, u32[]{:S(2)}, u32[]{:S(2)}) collective-permute-start(f32[2,256]{1,0:T(2,128)S(1)} %bitcast.260), channel_id=1, source_target_pairs={{0,14},{1,15},{2,0},{3,1},{4,2},{5,3},{6,4},{7,5},{8,6},{9,7},{10,... | collective-permute-start | bytes 6152 | tf_op jit(solution)/shard_map/ppermute | solution.py:20
  98.0 1.7 collective-permute-start.31
  99.8 2.9 %cholesky.44 = f32[32,32]{1,0:T(8,128)S(1)} custom-call(f32[32,32]{1,0:T(8,128)S(1)} %fusion.38), custom_call_target="Cholesky" | custom-call | tf_op jit(solution)/shard_map/jit(cholesky)/cholesky | solution.py:58
  104.0 2.4 %custom-call.10 = f32[1,32,32]{1,2,0:T(8,128)S(1)} custom-call(f32[1,32,32]{2,1,0:T(8,128)S(1)} %fusion.14), custom_call_target="InvertDiagBlocksLowerTriangular" | custom-call | tf_op jit(solution)/shard_map/jit(_solve_triangular)/triangular_solve | solution.py:59
  107.3 2.9 %cholesky.55 = f32[32,32]{1,0:T(8,128)S(1)} custom-call(f32[32,32]{1,0:T(8,128)S(1)} %fusion.34), custom_call_target="Cholesky" | custom-call | tf_op jit(solution)/shard_map/jit(cholesky)/cholesky | solution.py:58
  110.4 1.6 collective-permute-start.32
  112.4 3.7 %collective-permute-start.35 = (f32[2,256]{1,0:T(2,128)S(1)}, f32[2,256]{1,0:T(2,128)S(1)}, u32[]{:S(2)}, u32[]{:S(2)}) collective-permute-start(f32[2,256]{1,0:T(2,128)S(1)} %bitcast.256), channel_id=1, source_target_pairs={{0,6},{1,7},{2,8},{3,9},{4,10},{5,11},{6,12},{7,13},{8,14},{9,15},... | collective-permute-start | bytes 6152 | tf_op jit(solution)/shard_map/ppermute | solution.py:20
  117.8 3.7 %collective-permute-start.37 = (f32[2,256]{1,0:T(2,128)S(1)}, f32[2,256]{1,0:T(2,128)S(1)}, u32[]{:S(2)}, u32[]{:S(2)}) collective-permute-start(f32[2,256]{1,0:T(2,128)S(1)} %bitcast.267), channel_id=1, source_target_pairs={{0,8},{1,9},{2,10},{3,11},{4,12},{5,13},{6,14},{7,15},{8,0},{9,1},... | collective-permute-start | bytes 6152 | tf_op jit(solution)/shard_map/ppermute | solution.py:20
  122.8 4.0 %collective-permute-start.40 = (f32[2,256]{1,0:T(2,128)S(1)}, f32[2,256]{1,0:T(2,128)S(1)}, u32[]{:S(2)}, u32[]{:S(2)}) collective-permute-start(f32[2,256]{1,0:T(2,128)S(1)} %bitcast.261), channel_id=1, source_target_pairs={{0,11},{1,12},{2,13},{3,14},{4,15},{5,0},{6,1},{7,2},{8,3},{9,4},{... | collective-permute-start | bytes 6152 | tf_op jit(solution)/shard_map/ppermute | solution.py:20
  127.4 2.4 %custom-call.11 = f32[1,32,32]{1,2,0:T(8,128)S(1)} custom-call(f32[1,32,32]{2,1,0:T(8,128)S(1)} %fusion.15), custom_call_target="InvertDiagBlocksLowerTriangular" | custom-call | tf_op jit(solution)/shard_map/jit(_solve_triangular)/triangular_solve | solution.py:59
  132.8 1.6 collective-permute-start.57
  134.4 3.8 %collective-permute-start.46 = (f32[2,256]{1,0:T(2,128)S(1)}, f32[2,256]{1,0:T(2,128)S(1)}, u32[]{:S(2)}, u32[]{:S(2)}) collective-permute-start(f32[2,256]{1,0:T(2,128)S(1)} %add_add_fusion), channel_id=1, source_target_pairs={{0,14},{1,15},{2,0},{3,1},{4,2},{5,3},{6,4},{7,5},{8,6},{9,7},{10,... | collective-permute-start | bytes 6152 | tf_op jit(solution)/shard_map/ppermute | solution.py:20
  138.2 1.3 collective-permute-done.46
  139.7 2.8 %collective-permute-done.47 = f32[2,256]{1,0:T(2,128)S(1)} collective-permute-done((f32[2,256]{1,0:T(2,128)S(1)}, f32[2,256]{1,0:T(2,128)S(1)}, u32[]{:S(2)}, u32[]{:S(2)}) %collective-permute-start.47) | collective-permute-done | bytes 2080 | tf_op jit(solution)/shard_map/ppermute | solution.py:20
  142.5 2.3 %collective-permute-start.48 = (f32[2,256]{1,0:T(2,128)S(1)}, f32[2,256]{1,0:T(2,128)S(1)}, u32[]{:S(2)}, u32[]{:S(2)}) collective-permute-start(f32[2,256]{1,0:T(2,128)S(1)} %add_add_fusion), channel_id=1, source_target_pairs={{0,12},{1,13},{2,14},{3,15},{4,0},{5,1},{6,2},{7,3},{8,4},{9,5},{1... | collective-permute-start | bytes 6152 | tf_op jit(solution)/shard_map/ppermute | solution.py:20
  144.8 1.3 collective-permute-done.48
  146.1 2.6 %collective-permute-start.49 = (f32[2,256]{1,0:T(2,128)S(1)}, f32[2,256]{1,0:T(2,128)S(1)}, u32[]{:S(2)}, u32[]{:S(2)}) collective-permute-start(f32[2,256]{1,0:T(2,128)S(1)} %add_add_fusion), channel_id=1, source_target_pairs={{0,11},{1,12},{2,13},{3,14},{4,15},{5,0},{6,1},{7,2},{8,3},{9,4},{... | collective-permute-start | bytes 6152 | tf_op jit(solution)/shard_map/ppermute | solution.py:20
  148.7 1.3 collective-permute-done.49
  150.0 5.3 %collective-permute-start.50 = (f32[2,256]{1,0:T(2,128)S(1)}, f32[2,256]{1,0:T(2,128)S(1)}, u32[]{:S(2)}, u32[]{:S(2)}) collective-permute-start(f32[2,256]{1,0:T(2,128)S(1)} %add_add_fusion), channel_id=1, source_target_pairs={{0,10},{1,11},{2,12},{3,13},{4,14},{5,15},{6,0},{7,1},{8,2},{9,3},... | collective-permute-start | bytes 6152 | tf_op jit(solution)/shard_map/ppermute | solution.py:20
  155.3 1.3 collective-permute-done.50
  156.6 3.8 %collective-permute-start.51 = (f32[2,256]{1,0:T(2,128)S(1)}, f32[2,256]{1,0:T(2,128)S(1)}, u32[]{:S(2)}, u32[]{:S(2)}) collective-permute-start(f32[2,256]{1,0:T(2,128)S(1)} %add_add_fusion), channel_id=1, source_target_pairs={{0,9},{1,10},{2,11},{3,12},{4,13},{5,14},{6,15},{7,0},{8,1},{9,2},... | collective-permute-start | bytes 6152 | tf_op jit(solution)/shard_map/ppermute | solution.py:20
  160.4 1.3 collective-permute-done.51
  161.7 4.6 %collective-permute-start.52 = (f32[2,256]{1,0:T(2,128)S(1)}, f32[2,256]{1,0:T(2,128)S(1)}, u32[]{:S(2)}, u32[]{:S(2)}) collective-permute-start(f32[2,256]{1,0:T(2,128)S(1)} %add_add_fusion), channel_id=1, source_target_pairs={{0,8},{1,9},{2,10},{3,11},{4,12},{5,13},{6,14},{7,15},{8,0},{9,1},... | collective-permute-start | bytes 6152 | tf_op jit(solution)/shard_map/ppermute | solution.py:20
  166.4 1.6 collective-permute-done.52
  168.0 2.7 %collective-permute-start.53 = (f32[2,256]{1,0:T(2,128)S(1)}, f32[2,256]{1,0:T(2,128)S(1)}, u32[]{:S(2)}, u32[]{:S(2)}) collective-permute-start(f32[2,256]{1,0:T(2,128)S(1)} %add_add_fusion), channel_id=1, source_target_pairs={{0,7},{1,8},{2,9},{3,10},{4,11},{5,12},{6,13},{7,14},{8,15},{9,0},... | collective-permute-start | bytes 6152 | tf_op jit(solution)/shard_map/ppermute | solution.py:20
  171.9 4.6 %collective-permute-start.54 = (f32[2,256]{1,0:T(2,128)S(1)}, f32[2,256]{1,0:T(2,128)S(1)}, u32[]{:S(2)}, u32[]{:S(2)}) collective-permute-start(f32[2,256]{1,0:T(2,128)S(1)} %add_add_fusion), channel_id=1, source_target_pairs={{0,6},{1,7},{2,8},{3,9},{4,10},{5,11},{6,12},{7,13},{8,14},{9,15},... | collective-permute-start | bytes 6152 | tf_op jit(solution)/shard_map/ppermute | solution.py:20
  177.9 2.9 %collective-permute-start.55 = (f32[2,256]{1,0:T(2,128)S(1)}, f32[2,256]{1,0:T(2,128)S(1)}, u32[]{:S(2)}, u32[]{:S(2)}) collective-permute-start(f32[2,256]{1,0:T(2,128)S(1)} %add_add_fusion), channel_id=1, source_target_pairs={{0,5},{1,6},{2,7},{3,8},{4,9},{5,10},{6,11},{7,12},{8,13},{9,14},{... | collective-permute-start | bytes 6152 | tf_op jit(solution)/shard_map/ppermute | solution.py:20
  180.8 1.9 collective-permute-done.55
  183.4 4.4 %fusion.1 = bf16[1,2048,256]{2,1,0:T(8,128)(2,1)} fusion(f32[2048,256]{1,0:T(8,128)} %copy-done.1, f32[32,2048]{1,0:T(8,128)S(1)} %fusion.32, f32[32,256]{1,0:T(8,128)S(1)} %convolution_multiply_fusion), kind=kOutput, calls=%fused_computation.3 | convolution fusion | flops 202375168 | bytes 3440640 | tf_op jit(solution)/shard_map/dot_general | solution.py:62
  (149 shorter events, 19.0 us)
Async XLA Ops:
  0.6 1.6 copy-start
  2.2 3.4 %copy-start.4 = (f32[32,256]{1,0:T(8,128)S(1)}, f32[32,256]{1,0:T(8,128)}, u32[]{:S(2)}) copy-start(f32[32,256]{1,0:T(8,128)} %param.16) | copy-start | bytes 98308
  7.8 7.9 %collective-permute-start = (f32[32,128]{1,0:T(8,128)S(1)}, f32[32,128]{1,0:T(8,128)S(1)}, u32[]{:S(2)}, u32[]{:S(2)}) collective-permute-start(f32[32,128]{1,0:T(8,128)S(1)} %get-tuple-element.10), channel_id=1, source_target_pairs={{0,1},{1,2},{2,3},{3,4},{4,5},{5,6},{6,7},{7,8},{8,9},{9,10},{10,1... | collective-permute-start | bytes 49160 | tf_op jit(solution)/shard_map/ppermute | solution.py:20
  8.3 10.0 %collective-permute-start.13 = (f32[32,128]{1,0:T(8,128)S(1)}, f32[32,128]{1,0:T(8,128)S(1)}, u32[]{:S(2)}, u32[]{:S(2)}) collective-permute-start(f32[32,128]{1,0:T(8,128)S(1)} %get-tuple-element.11), channel_id=1, source_target_pairs={{0,14},{1,15},{2,0},{3,1},{4,2},{5,3},{6,4},{7,5},{8,6},{9,7},{10,... | collective-permute-start | bytes 49160 | tf_op jit(solution)/shard_map/ppermute | solution.py:20
  13.9 4.7 %collective-permute-start.12 = (f32[32,128]{1,0:T(8,128)S(1)}, f32[32,128]{1,0:T(8,128)S(1)}, u32[]{:S(2)}, u32[]{:S(2)}) collective-permute-start(f32[32,128]{1,0:T(8,128)S(1)} %get-tuple-element.12), channel_id=1, source_target_pairs={{0,13},{1,14},{2,15},{3,0},{4,1},{5,2},{6,3},{7,4},{8,5},{9,6},{10... | collective-permute-start | bytes 49160 | tf_op jit(solution)/shard_map/ppermute | solution.py:20
  15.3 5.9 %collective-permute-start.11 = (f32[32,128]{1,0:T(8,128)S(1)}, f32[32,128]{1,0:T(8,128)S(1)}, u32[]{:S(2)}, u32[]{:S(2)}) collective-permute-start(f32[32,128]{1,0:T(8,128)S(1)} %get-tuple-element.13), channel_id=1, source_target_pairs={{0,12},{1,13},{2,14},{3,15},{4,0},{5,1},{6,2},{7,3},{8,4},{9,5},{1... | collective-permute-start | bytes 49160 | tf_op jit(solution)/shard_map/ppermute | solution.py:20
  15.7 6.0 %collective-permute-start.10 = (f32[32,128]{1,0:T(8,128)S(1)}, f32[32,128]{1,0:T(8,128)S(1)}, u32[]{:S(2)}, u32[]{:S(2)}) collective-permute-start(f32[32,128]{1,0:T(8,128)S(1)} %get-tuple-element.14), channel_id=1, source_target_pairs={{0,11},{1,12},{2,13},{3,14},{4,15},{5,0},{6,1},{7,2},{8,3},{9,4},{... | collective-permute-start | bytes 49160 | tf_op jit(solution)/shard_map/ppermute | solution.py:20
  15.7 8.7 %collective-permute-start.9 = (f32[32,128]{1,0:T(8,128)S(1)}, f32[32,128]{1,0:T(8,128)S(1)}, u32[]{:S(2)}, u32[]{:S(2)}) collective-permute-start(f32[32,128]{1,0:T(8,128)S(1)} %get-tuple-element.15), channel_id=1, source_target_pairs={{0,10},{1,11},{2,12},{3,13},{4,14},{5,15},{6,0},{7,1},{8,2},{9,3},... | collective-permute-start | bytes 49160 | tf_op jit(solution)/shard_map/ppermute | solution.py:20
  18.3 6.1 %collective-permute-start.8 = (f32[32,128]{1,0:T(8,128)S(1)}, f32[32,128]{1,0:T(8,128)S(1)}, u32[]{:S(2)}, u32[]{:S(2)}) collective-permute-start(f32[32,128]{1,0:T(8,128)S(1)} %get-tuple-element.16), channel_id=1, source_target_pairs={{0,9},{1,10},{2,11},{3,12},{4,13},{5,14},{6,15},{7,0},{8,1},{9,2},... | collective-permute-start | bytes 49160 | tf_op jit(solution)/shard_map/ppermute | solution.py:20
  18.6 8.4 %collective-permute-start.7 = (f32[32,128]{1,0:T(8,128)S(1)}, f32[32,128]{1,0:T(8,128)S(1)}, u32[]{:S(2)}, u32[]{:S(2)}) collective-permute-start(f32[32,128]{1,0:T(8,128)S(1)} %get-tuple-element.17), channel_id=1, source_target_pairs={{0,8},{1,9},{2,10},{3,11},{4,12},{5,13},{6,14},{7,15},{8,0},{9,1},... | collective-permute-start | bytes 49160 | tf_op jit(solution)/shard_map/ppermute | solution.py:20
  21.2 7.8 %collective-permute-start.6 = (f32[32,128]{1,0:T(8,128)S(1)}, f32[32,128]{1,0:T(8,128)S(1)}, u32[]{:S(2)}, u32[]{:S(2)}) collective-permute-start(f32[32,128]{1,0:T(8,128)S(1)} %get-tuple-element.18), channel_id=1, source_target_pairs={{0,7},{1,8},{2,9},{3,10},{4,11},{5,12},{6,13},{7,14},{8,15},{9,0},... | collective-permute-start | bytes 49160 | tf_op jit(solution)/shard_map/ppermute | solution.py:20
  21.7 7.8 %collective-permute-start.5 = (f32[32,128]{1,0:T(8,128)S(1)}, f32[32,128]{1,0:T(8,128)S(1)}, u32[]{:S(2)}, u32[]{:S(2)}) collective-permute-start(f32[32,128]{1,0:T(8,128)S(1)} %get-tuple-element.19), channel_id=1, source_target_pairs={{0,6},{1,7},{2,8},{3,9},{4,10},{5,11},{6,12},{7,13},{8,14},{9,15},... | collective-permute-start | bytes 49160 | tf_op jit(solution)/shard_map/ppermute | solution.py:20
  24.4 7.5 %collective-permute-start.4 = (f32[32,128]{1,0:T(8,128)S(1)}, f32[32,128]{1,0:T(8,128)S(1)}, u32[]{:S(2)}, u32[]{:S(2)}) collective-permute-start(f32[32,128]{1,0:T(8,128)S(1)} %get-tuple-element.20), channel_id=1, source_target_pairs={{0,5},{1,6},{2,7},{3,8},{4,9},{5,10},{6,11},{7,12},{8,13},{9,14},{... | collective-permute-start | bytes 49160 | tf_op jit(solution)/shard_map/ppermute | solution.py:20
  24.4 7.5 %collective-permute-start.3 = (f32[32,128]{1,0:T(8,128)S(1)}, f32[32,128]{1,0:T(8,128)S(1)}, u32[]{:S(2)}, u32[]{:S(2)}) collective-permute-start(f32[32,128]{1,0:T(8,128)S(1)} %get-tuple-element.21), channel_id=1, source_target_pairs={{0,4},{1,5},{2,6},{3,7},{4,8},{5,9},{6,10},{7,11},{8,12},{9,13},{1... | collective-permute-start | bytes 49160 | tf_op jit(solution)/shard_map/ppermute | solution.py:20
  26.9 5.0 %collective-permute-start.2 = (f32[32,128]{1,0:T(8,128)S(1)}, f32[32,128]{1,0:T(8,128)S(1)}, u32[]{:S(2)}, u32[]{:S(2)}) collective-permute-start(f32[32,128]{1,0:T(8,128)S(1)} %get-tuple-element.22), channel_id=1, source_target_pairs={{0,3},{1,4},{2,5},{3,6},{4,7},{5,8},{6,9},{7,10},{8,11},{9,12},{10... | collective-permute-start | bytes 49160 | tf_op jit(solution)/shard_map/ppermute | solution.py:20
  29.0 6.4 %collective-permute-start.1 = (f32[32,128]{1,0:T(8,128)S(1)}, f32[32,128]{1,0:T(8,128)S(1)}, u32[]{:S(2)}, u32[]{:S(2)}) collective-permute-start(f32[32,128]{1,0:T(8,128)S(1)} %get-tuple-element.23), channel_id=1, source_target_pairs={{0,2},{1,3},{2,4},{3,5},{4,6},{5,7},{6,8},{7,9},{8,10},{9,11},{10,... | collective-permute-start | bytes 49160 | tf_op jit(solution)/shard_map/ppermute | solution.py:20
  29.5 6.0 %collective-permute-start.14 = (f32[32,128]{1,0:T(8,128)S(1)}, f32[32,128]{1,0:T(8,128)S(1)}, u32[]{:S(2)}, u32[]{:S(2)}) collective-permute-start(f32[32,128]{1,0:T(8,128)S(1)} %get-tuple-element.24), channel_id=1, source_target_pairs={{0,15},{1,0},{2,1},{3,2},{4,3},{5,4},{6,5},{7,6},{8,7},{9,8},{10,9... | collective-permute-start | bytes 49160 | tf_op jit(solution)/shard_map/ppermute | solution.py:20
  35.5 3.8 %collective-permute-start.15 = (f32[32,128]{1,0:T(8,128)S(1)}, f32[32,128]{1,0:T(8,128)S(1)}, u32[]{:S(2)}, u32[]{:S(2)}) collective-permute-start(f32[32,128]{1,0:T(8,128)S(1)} %fusion.30), channel_id=1, source_target_pairs={{0,15},{1,0},{2,1},{3,2},{4,3},{5,4},{6,5},{7,6},{8,7},{9,8},{10,9... | collective-permute-start | bytes 49160 | tf_op jit(solution)/shard_map/ppermute | solution.py:20
  37.8 50.9 %collective-permute-start.29 = (f32[32,128]{1,0:T(8,128)S(1)}, f32[32,128]{1,0:T(8,128)S(1)}, u32[]{:S(2)}, u32[]{:S(2)}) collective-permute-start(f32[32,128]{1,0:T(8,128)S(1)} %fusion.30), channel_id=1, source_target_pairs={{0,1},{1,2},{2,3},{3,4},{4,5},{5,6},{6,7},{7,8},{8,9},{9,10},{10,1... | collective-permute-start | bytes 49160 | tf_op jit(solution)/shard_map/ppermute | solution.py:20
  37.8 50.9 %collective-permute-start.28 = (f32[32,128]{1,0:T(8,128)S(1)}, f32[32,128]{1,0:T(8,128)S(1)}, u32[]{:S(2)}, u32[]{:S(2)}) collective-permute-start(f32[32,128]{1,0:T(8,128)S(1)} %fusion.30), channel_id=1, source_target_pairs={{0,2},{1,3},{2,4},{3,5},{4,6},{5,7},{6,8},{7,9},{8,10},{9,11},{10,... | collective-permute-start | bytes 49160 | tf_op jit(solution)/shard_map/ppermute | solution.py:20
  37.8 50.9 %collective-permute-start.27 = (f32[32,128]{1,0:T(8,128)S(1)}, f32[32,128]{1,0:T(8,128)S(1)}, u32[]{:S(2)}, u32[]{:S(2)}) collective-permute-start(f32[32,128]{1,0:T(8,128)S(1)} %fusion.30), channel_id=1, source_target_pairs={{0,3},{1,4},{2,5},{3,6},{4,7},{5,8},{6,9},{7,10},{8,11},{9,12},{10... | collective-permute-start | bytes 49160 | tf_op jit(solution)/shard_map/ppermute | solution.py:20
  37.8 50.9 %collective-permute-start.26 = (f32[32,128]{1,0:T(8,128)S(1)}, f32[32,128]{1,0:T(8,128)S(1)}, u32[]{:S(2)}, u32[]{:S(2)}) collective-permute-start(f32[32,128]{1,0:T(8,128)S(1)} %fusion.30), channel_id=1, source_target_pairs={{0,4},{1,5},{2,6},{3,7},{4,8},{5,9},{6,10},{7,11},{8,12},{9,13},{1... | collective-permute-start | bytes 49160 | tf_op jit(solution)/shard_map/ppermute | solution.py:20
  39.3 4.8 %collective-permute-start.16 = (f32[32,128]{1,0:T(8,128)S(1)}, f32[32,128]{1,0:T(8,128)S(1)}, u32[]{:S(2)}, u32[]{:S(2)}) collective-permute-start(f32[32,128]{1,0:T(8,128)S(1)} %fusion.30), channel_id=1, source_target_pairs={{0,14},{1,15},{2,0},{3,1},{4,2},{5,3},{6,4},{7,5},{8,6},{9,7},{10,... | collective-permute-start | bytes 49160 | tf_op jit(solution)/shard_map/ppermute | solution.py:20
  44.1 3.2 %collective-permute-start.17 = (f32[32,128]{1,0:T(8,128)S(1)}, f32[32,128]{1,0:T(8,128)S(1)}, u32[]{:S(2)}, u32[]{:S(2)}) collective-permute-start(f32[32,128]{1,0:T(8,128)S(1)} %fusion.30), channel_id=1, source_target_pairs={{0,13},{1,14},{2,15},{3,0},{4,1},{5,2},{6,3},{7,4},{8,5},{9,6},{10... | collective-permute-start | bytes 49160 | tf_op jit(solution)/shard_map/ppermute | solution.py:20
  47.3 5.2 %collective-permute-start.18 = (f32[32,128]{1,0:T(8,128)S(1)}, f32[32,128]{1,0:T(8,128)S(1)}, u32[]{:S(2)}, u32[]{:S(2)}) collective-permute-start(f32[32,128]{1,0:T(8,128)S(1)} %fusion.30), channel_id=1, source_target_pairs={{0,12},{1,13},{2,14},{3,15},{4,0},{5,1},{6,2},{7,3},{8,4},{9,5},{1... | collective-permute-start | bytes 49160 | tf_op jit(solution)/shard_map/ppermute | solution.py:20
  52.4 4.7 %collective-permute-start.19 = (f32[32,128]{1,0:T(8,128)S(1)}, f32[32,128]{1,0:T(8,128)S(1)}, u32[]{:S(2)}, u32[]{:S(2)}) collective-permute-start(f32[32,128]{1,0:T(8,128)S(1)} %fusion.30), channel_id=1, source_target_pairs={{0,11},{1,12},{2,13},{3,14},{4,15},{5,0},{6,1},{7,2},{8,3},{9,4},{... | collective-permute-start | bytes 49160 | tf_op jit(solution)/shard_map/ppermute | solution.py:20
  57.1 5.0 %collective-permute-start.20 = (f32[32,128]{1,0:T(8,128)S(1)}, f32[32,128]{1,0:T(8,128)S(1)}, u32[]{:S(2)}, u32[]{:S(2)}) collective-permute-start(f32[32,128]{1,0:T(8,128)S(1)} %fusion.30), channel_id=1, source_target_pairs={{0,10},{1,11},{2,12},{3,13},{4,14},{5,15},{6,0},{7,1},{8,2},{9,3},... | collective-permute-start | bytes 49160 | tf_op jit(solution)/shard_map/ppermute | solution.py:20
  62.1 5.0 %collective-permute-start.21 = (f32[32,128]{1,0:T(8,128)S(1)}, f32[32,128]{1,0:T(8,128)S(1)}, u32[]{:S(2)}, u32[]{:S(2)}) collective-permute-start(f32[32,128]{1,0:T(8,128)S(1)} %fusion.30), channel_id=1, source_target_pairs={{0,9},{1,10},{2,11},{3,12},{4,13},{5,14},{6,15},{7,0},{8,1},{9,2},... | collective-permute-start | bytes 49160 | tf_op jit(solution)/shard_map/ppermute | solution.py:20
  67.1 6.4 %collective-permute-start.22 = (f32[32,128]{1,0:T(8,128)S(1)}, f32[32,128]{1,0:T(8,128)S(1)}, u32[]{:S(2)}, u32[]{:S(2)}) collective-permute-start(f32[32,128]{1,0:T(8,128)S(1)} %fusion.30), channel_id=1, source_target_pairs={{0,8},{1,9},{2,10},{3,11},{4,12},{5,13},{6,14},{7,15},{8,0},{9,1},... | collective-permute-start | bytes 49160 | tf_op jit(solution)/shard_map/ppermute | solution.py:20
  73.5 4.1 %collective-permute-start.23 = (f32[32,128]{1,0:T(8,128)S(1)}, f32[32,128]{1,0:T(8,128)S(1)}, u32[]{:S(2)}, u32[]{:S(2)}) collective-permute-start(f32[32,128]{1,0:T(8,128)S(1)} %fusion.30), channel_id=1, source_target_pairs={{0,7},{1,8},{2,9},{3,10},{4,11},{5,12},{6,13},{7,14},{8,15},{9,0},... | collective-permute-start | bytes 49160 | tf_op jit(solution)/shard_map/ppermute | solution.py:20
  77.6 6.1 %collective-permute-start.24 = (f32[32,128]{1,0:T(8,128)S(1)}, f32[32,128]{1,0:T(8,128)S(1)}, u32[]{:S(2)}, u32[]{:S(2)}) collective-permute-start(f32[32,128]{1,0:T(8,128)S(1)} %fusion.30), channel_id=1, source_target_pairs={{0,6},{1,7},{2,8},{3,9},{4,10},{5,11},{6,12},{7,13},{8,14},{9,15},... | collective-permute-start | bytes 49160 | tf_op jit(solution)/shard_map/ppermute | solution.py:20
  83.7 5.0 %collective-permute-start.25 = (f32[32,128]{1,0:T(8,128)S(1)}, f32[32,128]{1,0:T(8,128)S(1)}, u32[]{:S(2)}, u32[]{:S(2)}) collective-permute-start(f32[32,128]{1,0:T(8,128)S(1)} %fusion.30), channel_id=1, source_target_pairs={{0,5},{1,6},{2,7},{3,8},{4,9},{5,10},{6,11},{7,12},{8,13},{9,14},{... | collective-permute-start | bytes 49160 | tf_op jit(solution)/shard_map/ppermute | solution.py:20
  92.4 18.0 %collective-permute-start.42 = (f32[2,256]{1,0:T(2,128)S(1)}, f32[2,256]{1,0:T(2,128)S(1)}, u32[]{:S(2)}, u32[]{:S(2)}) collective-permute-start(f32[2,256]{1,0:T(2,128)S(1)} %bitcast.264), channel_id=1, source_target_pairs={{0,13},{1,14},{2,15},{3,0},{4,1},{5,2},{6,3},{7,4},{8,5},{9,6},{10... | collective-permute-start | bytes 6152 | tf_op jit(solution)/shard_map/ppermute | solution.py:20
  93.3 18.6 %collective-permute-start.43 = (f32[2,256]{1,0:T(2,128)S(1)}, f32[2,256]{1,0:T(2,128)S(1)}, u32[]{:S(2)}, u32[]{:S(2)}) collective-permute-start(f32[2,256]{1,0:T(2,128)S(1)} %bitcast.260), channel_id=1, source_target_pairs={{0,14},{1,15},{2,0},{3,1},{4,2},{5,3},{6,4},{7,5},{8,6},{9,7},{10,... | collective-permute-start | bytes 6152 | tf_op jit(solution)/shard_map/ppermute | solution.py:20
  97.1 15.2 %collective-permute-start.44 = (f32[2,256]{1,0:T(2,128)S(1)}, f32[2,256]{1,0:T(2,128)S(1)}, u32[]{:S(2)}, u32[]{:S(2)}) collective-permute-start(f32[2,256]{1,0:T(2,128)S(1)} %bitcast.257), channel_id=1, source_target_pairs={{0,15},{1,0},{2,1},{3,2},{4,3},{5,4},{6,5},{7,6},{8,7},{9,8},{10,9... | collective-permute-start | bytes 6152 | tf_op jit(solution)/shard_map/ppermute | solution.py:20
  97.9 14.4 %collective-permute-start.30 = (f32[2,256]{1,0:T(2,128)S(1)}, f32[2,256]{1,0:T(2,128)S(1)}, u32[]{:S(2)}, u32[]{:S(2)}) collective-permute-start(f32[2,256]{1,0:T(2,128)S(1)} %bitcast.255), channel_id=1, source_target_pairs={{0,1},{1,2},{2,3},{3,4},{4,5},{5,6},{6,7},{7,8},{8,9},{9,10},{10,1... | collective-permute-start | bytes 6152 | tf_op jit(solution)/shard_map/ppermute | solution.py:20
  98.0 18.1 %collective-permute-start.31 = (f32[2,256]{1,0:T(2,128)S(1)}, f32[2,256]{1,0:T(2,128)S(1)}, u32[]{:S(2)}, u32[]{:S(2)}) collective-permute-start(f32[2,256]{1,0:T(2,128)S(1)} %bitcast.253), channel_id=1, source_target_pairs={{0,2},{1,3},{2,4},{3,5},{4,6},{5,7},{6,8},{7,9},{8,10},{9,11},{10,... | collective-permute-start | bytes 6152 | tf_op jit(solution)/shard_map/ppermute | solution.py:20
  110.4 7.4 %collective-permute-start.32 = (f32[2,256]{1,0:T(2,128)S(1)}, f32[2,256]{1,0:T(2,128)S(1)}, u32[]{:S(2)}, u32[]{:S(2)}) collective-permute-start(f32[2,256]{1,0:T(2,128)S(1)} %bitcast.265), channel_id=1, source_target_pairs={{0,3},{1,4},{2,5},{3,6},{4,7},{5,8},{6,9},{7,10},{8,11},{9,12},{10... | collective-permute-start | bytes 6152 | tf_op jit(solution)/shard_map/ppermute | solution.py:20
  111.9 9.6 %collective-permute-start.33 = (f32[2,256]{1,0:T(2,128)S(1)}, f32[2,256]{1,0:T(2,128)S(1)}, u32[]{:S(2)}, u32[]{:S(2)}) collective-permute-start(f32[2,256]{1,0:T(2,128)S(1)} %bitcast.262), channel_id=1, source_target_pairs={{0,4},{1,5},{2,6},{3,7},{4,8},{5,9},{6,10},{7,11},{8,12},{9,13},{1... | collective-permute-start | bytes 6152 | tf_op jit(solution)/shard_map/ppermute | solution.py:20
  112.4 9.1 %collective-permute-start.34 = (f32[2,256]{1,0:T(2,128)S(1)}, f32[2,256]{1,0:T(2,128)S(1)}, u32[]{:S(2)}, u32[]{:S(2)}) collective-permute-start(f32[2,256]{1,0:T(2,128)S(1)} %bitcast.258), channel_id=1, source_target_pairs={{0,5},{1,6},{2,7},{3,8},{4,9},{5,10},{6,11},{7,12},{8,13},{9,14},{... | collective-permute-start | bytes 6152 | tf_op jit(solution)/shard_map/ppermute | solution.py:20
  112.4 10.4 %collective-permute-start.35 = (f32[2,256]{1,0:T(2,128)S(1)}, f32[2,256]{1,0:T(2,128)S(1)}, u32[]{:S(2)}, u32[]{:S(2)}) collective-permute-start(f32[2,256]{1,0:T(2,128)S(1)} %bitcast.256), channel_id=1, source_target_pairs={{0,6},{1,7},{2,8},{3,9},{4,10},{5,11},{6,12},{7,13},{8,14},{9,15},... | collective-permute-start | bytes 6152 | tf_op jit(solution)/shard_map/ppermute | solution.py:20
  116.1 10.7 %collective-permute-start.36 = (f32[2,256]{1,0:T(2,128)S(1)}, f32[2,256]{1,0:T(2,128)S(1)}, u32[]{:S(2)}, u32[]{:S(2)}) collective-permute-start(f32[2,256]{1,0:T(2,128)S(1)} %bitcast.254), channel_id=1, source_target_pairs={{0,7},{1,8},{2,9},{3,10},{4,11},{5,12},{6,13},{7,14},{8,15},{9,0},... | collective-permute-start | bytes 6152 | tf_op jit(solution)/shard_map/ppermute | solution.py:20
  117.8 12.1 %collective-permute-start.37 = (f32[2,256]{1,0:T(2,128)S(1)}, f32[2,256]{1,0:T(2,128)S(1)}, u32[]{:S(2)}, u32[]{:S(2)}) collective-permute-start(f32[2,256]{1,0:T(2,128)S(1)} %bitcast.267), channel_id=1, source_target_pairs={{0,8},{1,9},{2,10},{3,11},{4,12},{5,13},{6,14},{7,15},{8,0},{9,1},... | collective-permute-start | bytes 6152 | tf_op jit(solution)/shard_map/ppermute | solution.py:20
  121.5 8.4 %collective-permute-start.38 = (f32[2,256]{1,0:T(2,128)S(1)}, f32[2,256]{1,0:T(2,128)S(1)}, u32[]{:S(2)}, u32[]{:S(2)}) collective-permute-start(f32[2,256]{1,0:T(2,128)S(1)} %bitcast.266), channel_id=1, source_target_pairs={{0,9},{1,10},{2,11},{3,12},{4,13},{5,14},{6,15},{7,0},{8,1},{9,2},... | collective-permute-start | bytes 6152 | tf_op jit(solution)/shard_map/ppermute | solution.py:20
  121.5 8.4 %collective-permute-start.39 = (f32[2,256]{1,0:T(2,128)S(1)}, f32[2,256]{1,0:T(2,128)S(1)}, u32[]{:S(2)}, u32[]{:S(2)}) collective-permute-start(f32[2,256]{1,0:T(2,128)S(1)} %bitcast.263), channel_id=1, source_target_pairs={{0,10},{1,11},{2,12},{3,13},{4,14},{5,15},{6,0},{7,1},{8,2},{9,3},... | collective-permute-start | bytes 6152 | tf_op jit(solution)/shard_map/ppermute | solution.py:20
  122.8 7.2 %collective-permute-start.40 = (f32[2,256]{1,0:T(2,128)S(1)}, f32[2,256]{1,0:T(2,128)S(1)}, u32[]{:S(2)}, u32[]{:S(2)}) collective-permute-start(f32[2,256]{1,0:T(2,128)S(1)} %bitcast.261), channel_id=1, source_target_pairs={{0,11},{1,12},{2,13},{3,14},{4,15},{5,0},{6,1},{7,2},{8,3},{9,4},{... | collective-permute-start | bytes 6152 | tf_op jit(solution)/shard_map/ppermute | solution.py:20
  126.8 3.6 %collective-permute-start.41 = (f32[2,256]{1,0:T(2,128)S(1)}, f32[2,256]{1,0:T(2,128)S(1)}, u32[]{:S(2)}, u32[]{:S(2)}) collective-permute-start(f32[2,256]{1,0:T(2,128)S(1)} %bitcast.259), channel_id=1, source_target_pairs={{0,12},{1,13},{2,14},{3,15},{4,0},{5,1},{6,2},{7,3},{8,4},{9,5},{1... | collective-permute-start | bytes 6152 | tf_op jit(solution)/shard_map/ppermute | solution.py:20
  130.4 4.0 %collective-permute-start.45 = (f32[2,256]{1,0:T(2,128)S(1)}, f32[2,256]{1,0:T(2,128)S(1)}, u32[]{:S(2)}, u32[]{:S(2)}) collective-permute-start(f32[2,256]{1,0:T(2,128)S(1)} %add_add_fusion), channel_id=1, source_target_pairs={{0,15},{1,0},{2,1},{3,2},{4,3},{5,4},{6,5},{7,6},{8,7},{9,8},{10,9... | collective-permute-start | bytes 6152 | tf_op jit(solution)/shard_map/ppermute | solution.py:20
  131.7 56.1 %copy-start.2 = (f32[32,2048]{1,0:T(8,128)}, f32[32,2048]{1,0:T(8,128)S(1)}, u32[]{:S(2)}) copy-start(f32[32,2048]{1,0:T(8,128)S(1)} %fusion.32) | copy-start | bytes 786436
  131.7 51.1 %collective-permute-start.59 = (f32[2,256]{1,0:T(2,128)S(1)}, f32[2,256]{1,0:T(2,128)S(1)}, u32[]{:S(2)}, u32[]{:S(2)}) collective-permute-start(f32[2,256]{1,0:T(2,128)S(1)} %add_add_fusion), channel_id=1, source_target_pairs={{0,1},{1,2},{2,3},{3,4},{4,5},{5,6},{6,7},{7,8},{8,9},{9,10},{10,1... | collective-permute-start | bytes 6152 | tf_op jit(solution)/shard_map/ppermute | solution.py:20
  131.8 51.0 %collective-permute-start.58 = (f32[2,256]{1,0:T(2,128)S(1)}, f32[2,256]{1,0:T(2,128)S(1)}, u32[]{:S(2)}, u32[]{:S(2)}) collective-permute-start(f32[2,256]{1,0:T(2,128)S(1)} %add_add_fusion), channel_id=1, source_target_pairs={{0,2},{1,3},{2,4},{3,5},{4,6},{5,7},{6,8},{7,9},{8,10},{9,11},{10,... | collective-permute-start | bytes 6152 | tf_op jit(solution)/shard_map/ppermute | solution.py:20
  132.8 49.9 %collective-permute-start.57 = (f32[2,256]{1,0:T(2,128)S(1)}, f32[2,256]{1,0:T(2,128)S(1)}, u32[]{:S(2)}, u32[]{:S(2)}) collective-permute-start(f32[2,256]{1,0:T(2,128)S(1)} %add_add_fusion), channel_id=1, source_target_pairs={{0,3},{1,4},{2,5},{3,6},{4,7},{5,8},{6,9},{7,10},{8,11},{9,12},{10... | collective-permute-start | bytes 6152 | tf_op jit(solution)/shard_map/ppermute | solution.py:20
  134.4 48.4 %collective-permute-start.56 = (f32[2,256]{1,0:T(2,128)S(1)}, f32[2,256]{1,0:T(2,128)S(1)}, u32[]{:S(2)}, u32[]{:S(2)}) collective-permute-start(f32[2,256]{1,0:T(2,128)S(1)} %add_add_fusion), channel_id=1, source_target_pairs={{0,4},{1,5},{2,6},{3,7},{4,8},{5,9},{6,10},{7,11},{8,12},{9,13},{1... | collective-permute-start | bytes 6152 | tf_op jit(solution)/shard_map/ppermute | solution.py:20
  134.4 5.1 %collective-permute-start.46 = (f32[2,256]{1,0:T(2,128)S(1)}, f32[2,256]{1,0:T(2,128)S(1)}, u32[]{:S(2)}, u32[]{:S(2)}) collective-permute-start(f32[2,256]{1,0:T(2,128)S(1)} %add_add_fusion), channel_id=1, source_target_pairs={{0,14},{1,15},{2,0},{3,1},{4,2},{5,3},{6,4},{7,5},{8,6},{9,7},{10,... | collective-permute-start | bytes 6152 | tf_op jit(solution)/shard_map/ppermute | solution.py:20
  139.5 3.0 %collective-permute-start.47 = (f32[2,256]{1,0:T(2,128)S(1)}, f32[2,256]{1,0:T(2,128)S(1)}, u32[]{:S(2)}, u32[]{:S(2)}) collective-permute-start(f32[2,256]{1,0:T(2,128)S(1)} %add_add_fusion), channel_id=1, source_target_pairs={{0,13},{1,14},{2,15},{3,0},{4,1},{5,2},{6,3},{7,4},{8,5},{9,6},{10... | collective-permute-start | bytes 6152 | tf_op jit(solution)/shard_map/ppermute | solution.py:20
  142.5 3.6 %collective-permute-start.48 = (f32[2,256]{1,0:T(2,128)S(1)}, f32[2,256]{1,0:T(2,128)S(1)}, u32[]{:S(2)}, u32[]{:S(2)}) collective-permute-start(f32[2,256]{1,0:T(2,128)S(1)} %add_add_fusion), channel_id=1, source_target_pairs={{0,12},{1,13},{2,14},{3,15},{4,0},{5,1},{6,2},{7,3},{8,4},{9,5},{1... | collective-permute-start | bytes 6152 | tf_op jit(solution)/shard_map/ppermute | solution.py:20
  146.1 3.9 %collective-permute-start.49 = (f32[2,256]{1,0:T(2,128)S(1)}, f32[2,256]{1,0:T(2,128)S(1)}, u32[]{:S(2)}, u32[]{:S(2)}) collective-permute-start(f32[2,256]{1,0:T(2,128)S(1)} %add_add_fusion), channel_id=1, source_target_pairs={{0,11},{1,12},{2,13},{3,14},{4,15},{5,0},{6,1},{7,2},{8,3},{9,4},{... | collective-permute-start | bytes 6152 | tf_op jit(solution)/shard_map/ppermute | solution.py:20
  150.0 6.6 %collective-permute-start.50 = (f32[2,256]{1,0:T(2,128)S(1)}, f32[2,256]{1,0:T(2,128)S(1)}, u32[]{:S(2)}, u32[]{:S(2)}) collective-permute-start(f32[2,256]{1,0:T(2,128)S(1)} %add_add_fusion), channel_id=1, source_target_pairs={{0,10},{1,11},{2,12},{3,13},{4,14},{5,15},{6,0},{7,1},{8,2},{9,3},... | collective-permute-start | bytes 6152 | tf_op jit(solution)/shard_map/ppermute | solution.py:20
  156.6 5.1 %collective-permute-start.51 = (f32[2,256]{1,0:T(2,128)S(1)}, f32[2,256]{1,0:T(2,128)S(1)}, u32[]{:S(2)}, u32[]{:S(2)}) collective-permute-start(f32[2,256]{1,0:T(2,128)S(1)} %add_add_fusion), channel_id=1, source_target_pairs={{0,9},{1,10},{2,11},{3,12},{4,13},{5,14},{6,15},{7,0},{8,1},{9,2},... | collective-permute-start | bytes 6152 | tf_op jit(solution)/shard_map/ppermute | solution.py:20
  161.7 6.2 %collective-permute-start.52 = (f32[2,256]{1,0:T(2,128)S(1)}, f32[2,256]{1,0:T(2,128)S(1)}, u32[]{:S(2)}, u32[]{:S(2)}) collective-permute-start(f32[2,256]{1,0:T(2,128)S(1)} %add_add_fusion), channel_id=1, source_target_pairs={{0,8},{1,9},{2,10},{3,11},{4,12},{5,13},{6,14},{7,15},{8,0},{9,1},... | collective-permute-start | bytes 6152 | tf_op jit(solution)/shard_map/ppermute | solution.py:20
  168.0 4.0 %collective-permute-start.53 = (f32[2,256]{1,0:T(2,128)S(1)}, f32[2,256]{1,0:T(2,128)S(1)}, u32[]{:S(2)}, u32[]{:S(2)}) collective-permute-start(f32[2,256]{1,0:T(2,128)S(1)} %add_add_fusion), channel_id=1, source_target_pairs={{0,7},{1,8},{2,9},{3,10},{4,11},{5,12},{6,13},{7,14},{8,15},{9,0},... | collective-permute-start | bytes 6152 | tf_op jit(solution)/shard_map/ppermute | solution.py:20
  171.9 6.0 %collective-permute-start.54 = (f32[2,256]{1,0:T(2,128)S(1)}, f32[2,256]{1,0:T(2,128)S(1)}, u32[]{:S(2)}, u32[]{:S(2)}) collective-permute-start(f32[2,256]{1,0:T(2,128)S(1)} %add_add_fusion), channel_id=1, source_target_pairs={{0,6},{1,7},{2,8},{3,9},{4,10},{5,11},{6,12},{7,13},{8,14},{9,15},... | collective-permute-start | bytes 6152 | tf_op jit(solution)/shard_map/ppermute | solution.py:20
  177.9 4.8 %collective-permute-start.55 = (f32[2,256]{1,0:T(2,128)S(1)}, f32[2,256]{1,0:T(2,128)S(1)}, u32[]{:S(2)}, u32[]{:S(2)}) collective-permute-start(f32[2,256]{1,0:T(2,128)S(1)} %add_add_fusion), channel_id=1, source_target_pairs={{0,5},{1,6},{2,7},{3,8},{4,9},{5,10},{6,11},{7,12},{8,13},{9,14},{... | collective-permute-start | bytes 6152 | tf_op jit(solution)/shard_map/ppermute | solution.py:20
  183.4 4.4 %copy-start.3 = (f32[32,256]{1,0:T(8,128)}, f32[32,256]{1,0:T(8,128)S(1)}, u32[]{:S(2)}) copy-start(f32[32,256]{1,0:T(8,128)S(1)} %convolution_multiply_fusion) | copy-start | bytes 98308
  (1 other events, 1.4 us)

commit v2 on v1

--- a/solution.py
+++ b/solution.py
@@ -16,8 +16,13 @@
     return direct, rest, count
 
 
-def exchange(block, shift, direct, count):
-    return lax.ppermute(block, direct, [(i, (i + shift) % count) for i in range(count)])
+def swap(pieces, direct):
+    return lax.all_to_all(pieces, direct, 0, 0, tiled=True)
+
+
+def total_of(pieces, direct):
+    own = jnp.sum(swap(pieces, direct), axis=0)
+    return swap(jnp.broadcast_to(own[None], pieces.shape), direct)
 
 
 def local(direct, rest, count, workers, inputs, cotangent, error_prev, seed_q):
@@ -28,29 +33,15 @@
     term = lax.dot_general(seed_q, merged, (((1,), (1,)), ((), ())), precision=HIGHEST)
     if rest:
         term = lax.psum(term, rest)
-    me = lax.axis_index(direct)
     rank, width = term.shape
-    piece = width // count
-    pieces = term.reshape(rank, count, piece).transpose(1, 0, 2)
-    pieces = jnp.roll(pieces, -me, axis=0)
-    chunk = pieces[0]
-    for shift in range(1, count):
-        chunk = chunk + exchange(pieces[shift], shift, direct, count)
-    chunks = [chunk] + [exchange(chunk, shift, direct, count) for shift in range(1, count)]
-    first = jnp.roll(jnp.stack(chunks[::-1]), me + 1, axis=0)
-    first = first.transpose(1, 0, 2).reshape(rank, width)
+    pieces = term.reshape(rank, count, width // count).transpose(1, 0, 2)
+    first = total_of(pieces, direct).transpose(1, 0, 2).reshape(rank, width)
 
     product = jnp.dot(first, merged, precision=HIGHEST)
     if rest:
         product = lax.psum(product, rest)
-    slim = product.shape[0] // count
-    rows = product.reshape(count, slim, product.shape[1])
-    rows = jnp.roll(rows, -me, axis=0)
-    own = rows[0]
-    for shift in range(1, count):
-        own = own + exchange(rows[shift], shift, direct, count)
-    owns = [own] + [exchange(own, shift, direct, count) for shift in range(1, count)]
-    product = jnp.roll(jnp.stack(owns[::-1]), me + 1, axis=0).reshape(product.shape)
+    rows = product.reshape(count, -1, product.shape[1])
+    product = total_of(rows, direct).reshape(product.shape)
 
     basis = first
     for sweep in range(2):

time: 188 us -> 79.3 us (0.42)
  starting transfers between devices: 119 us -> 6.99 us
  blocking collectives: 0 us -> 30 us
  waiting for transfers between devices: 36.7 us -> 9.66 us
    ppermute x60 -> x0, starting transfers between devices: 119 us -> none  [exchange(): lax.ppermute(block, direct, [(i, (i + shift) % count) for i in range(coun...]
    ppermute x60 -> x0, waiting for transfers between devices: 36.7 us -> none  [exchange(): lax.ppermute(block, direct, [(i, (i + shift) % count) for i in range(coun...]
    all_to_all x0 -> x2, blocking collectives: none -> 30 us  [swap(): return lax.all_to_all(pieces, direct, 0, 0, tiled=True)]
    all_to_all x0 -> x2, waiting for transfers between devices: none -> 9.66 us  [swap(): return lax.all_to_all(pieces, direct, 0, 0, tiled=True)]
    all_to_all x0 -> x2, starting transfers between devices: none -> 6.99 us  [swap(): return lax.all_to_all(pieces, direct, 0, 0, tiled=True)]
  transfers between devices with their start and end apart: 60 -> 2, of which waited for: 23 -> 2; matrix products, arithmetic and copies ran while one was open for 8% -> 4% of each run, Pallas kernels for 0% -> 0%
where the time goes in v2:
time: 79.3 us; the launch traced here: 78.8 us
  blocking collectives  30 us (38%)
  other arithmetic  13.4 us (17%)
  matrix products  13.2 us (17%)
  waiting for transfers between devices  9.66 us (12%)
  starting transfers between devices  6.99 us (9%)
  local copies, waits for them, and re-layouts  4.72 us (6%)
  between operations  0.81 us (1%)
    all_to_all x2, blocking collectives, swap(): return lax.all_to_all(pieces, direct, 0, 0, tiled=True)  30 us
    all_to_all x2, waiting for transfers between devices, swap(): return lax.all_to_all(pieces, direct, 0, 0, tiled=True)  9.66 us
    another operation x6, other arithmetic, local(): lower = jnp.linalg.cholesky(gram)  7.19 us
    all_to_all x2, starting transfers between devices, swap(): return lax.all_to_all(pieces, direct, 0, 0, tiled=True)  6.99 us
    another operation x4, other arithmetic, local(): basis = jax.scipy.linalg.solve_triangular(lower, basis, lower=True)  6.17 us
    dot_general x1, matrix products, local(): lax.dot_general(basis, second, (((0,), (0,)), ((), ())), precision=HIGHEST)  4.41 us
    unnamed x10, local copies, waits for them, and re-layouts  2.95 us
    dot_general x1, matrix products, local(): product = jnp.dot(first, merged, precision=HIGHEST)  2.71 us
  transfers between devices with their start and end apart: 2, of which 2 were waited for; matrix products, arithmetic and copies ran while one was open for 4% of the time, Pallas kernels for 0%

profile of v2, /device:TPU:0, one launch (start us, length us, event | category | flops | bytes accessed | tf_op | source)
XLA Modules:
  0.0 78.8 jit_solution(3845815333979833355)
XLA Ops:
  0.6 0.0 copy-start
  0.6 1.6 %copy-done = bf16[512,2048]{1,0:T(8,128)(2,1)S(1)} copy-done((bf16[512,2048]{1,0:T(8,128)(2,1)S(1)}, bf16[512,2048]{1,0:T(8,128)(2,1)}, u32[]{:S(2)}) %copy-start) | copy-done | bytes 2097176
  2.2 0.0 copy-start.4
  2.2 2.1 %convolution_add_fusion = f32[2048,256]{1,0:T(8,128)S(1)} fusion(bf16[512,2048]{1,0:T(8,128)(2,1)S(1)} %copy-done, bf16[512,256]{1,0:T(8,128)(2,1)} %param.10, bf16[1,2048,256]{2,1,0:T(8,128)(2,1)} %param.11), kind=kOutput, calls=%fused_computation.1 | convolution fusion | flops 537919488 | bytes 5505024 | tf_op jit(solution)/shard_map/dot_general | solution.py:29
  4.3 0.0 copy-start.1
  4.3 1.3 %copy-done.1 = f32[2048,256]{1,0:T(8,128)} copy-done((f32[2048,256]{1,0:T(8,128)}, f32[2048,256]{1,0:T(8,128)S(1)}, u32[]{:S(2)}) %copy-start.1) | copy-done | bytes 2097176
  5.7 0.0 copy-done.4
  5.7 2.0 %convolution_bitcast_fusion = f32[4,16,8,128]{3,2,1,0:T(8,128)S(1)} fusion(f32[2048,256]{1,0:T(8,128)S(1)} %convolution_add_fusion, f32[32,256]{1,0:T(8,128)S(1)} %copy-done.4), kind=kOutput, calls=%fused_computation.6 | convolution fusion | flops 201326592 | bytes 2392064 | tf_op jit(solution)/shard_map/dot_general | solution.py:33
  7.7 17.2 %all_to_all.20 = f32[16,32,128]{2,1,0:T(8,128)S(1)} all-to-all(f32[16,32,128]{2,1,0:T(8,128)S(1)} %bitcast.67), channel_id=1, replica_groups=mesh['groups'=2,'dp'=4,'sub'=2,'pair'=2] {'dp','sub','pair'}, dimensions={0} | all-to-all | bytes 524288 | tf_op jit(solution)/shard_map/all_to_all | solution.py:20
  25.0 12.8 %all_to_all.21 = f32[16,32,128]{2,1,0:T(8,128)S(1)} all-to-all(f32[16,32,128]{2,1,0:T(8,128)S(1)} %broadcast_in_dim.6), channel_id=1, replica_groups=mesh['groups'=2,'dp'=4,'sub'=2,'pair'=2] {'dp','sub','pair'}, dimensions={0} | all-to-all | bytes 524288 | tf_op jit(solution)/shard_map/all_to_all | solution.py:20
  37.8 0.4 convolution_bitcast_fusion.1
  38.1 0.1 copy.15
  38.2 2.9 %cholesky.44 = f32[32,32]{1,0:T(8,128)S(1)} custom-call(f32[32,32]{1,0:T(8,128)S(1)} %fusion.17), custom_call_target="Cholesky" | custom-call | tf_op jit(solution)/shard_map/jit(cholesky)/cholesky | solution.py:49
  41.2 0.6 compare_reduce_fusion.1
  41.8 0.7 fusion.8
  42.5 2.4 %custom-call.10 = f32[1,32,32]{1,2,0:T(8,128)S(1)} custom-call(f32[1,32,32]{2,1,0:T(8,128)S(1)} %fusion.8), custom_call_target="InvertDiagBlocksLowerTriangular" | custom-call | tf_op jit(solution)/shard_map/jit(_solve_triangular)/triangular_solve | solution.py:50
  44.9 0.4 fusion.4
  45.4 0.4 fusion.21
  45.7 0.1 copy.17
  45.8 2.9 %cholesky.55 = f32[32,32]{1,0:T(8,128)S(1)} custom-call(f32[32,32]{1,0:T(8,128)S(1)} %fusion.13), custom_call_target="Cholesky" | custom-call | tf_op jit(solution)/shard_map/jit(cholesky)/cholesky | solution.py:49
  48.8 0.6 compare_reduce_fusion
  49.4 0.2 copy.16
  49.6 0.1 dot_general.27
  49.7 2.7 %fusion.2 = f32[16,2,256]{2,0,1:T(8,128)S(1)} fusion(f32[2048,256]{1,0:T(8,128)} %copy-done.1, f32[16,2,2048]{2,1,0:T(2,128)S(1)} %dot_general.27), kind=kOutput, calls=%fused_computation.4 | convolution fusion | flops 201326592 | bytes 2392064 | tf_op jit(solution)/shard_map/dot_general | solution.py:40
  52.4 0.6 copy.20
  53.1 3.5 %all-to-all-start.2 = ((f32[16,2,256]{2,1,0:T(2,128)}), f32[16,2,256]{2,1,0:T(2,128)S(1)}, u32[]{:S(2)}, u32[]{:S(2)}) async-start(f32[16,2,256]{2,1,0:T(2,128)} %copy.20), calls=%async_computation.2 | async-start | bytes 65536 | tf_op jit(solution)/shard_map/all_to_all | solution.py:20
  56.6 0.7 fusion.9
  57.2 2.4 %custom-call.11 = f32[1,32,32]{1,2,0:T(8,128)S(1)} custom-call(f32[1,32,32]{2,1,0:T(8,128)S(1)} %fusion.9), custom_call_target="InvertDiagBlocksLowerTriangular" | custom-call | tf_op jit(solution)/shard_map/jit(_solve_triangular)/triangular_solve | solution.py:50
  59.7 3.5 %all-to-all-done.2 = f32[16,2,256]{2,1,0:T(2,128)S(1)} async-done(((f32[16,2,256]{2,1,0:T(2,128)}), f32[16,2,256]{2,1,0:T(2,128)S(1)}, u32[]{:S(2)}, u32[]{:S(2)}) %all-to-all-start.2) | async-done | bytes 32800 | tf_op jit(solution)/shard_map/all_to_all | solution.py:20
  63.2 0.6 broadcast_in_dim.7
  63.8 3.5 %all-to-all-start.3 = ((f32[16,2,256]{2,1,0:T(2,128)}), f32[16,2,256]{2,1,0:T(2,128)S(1)}, u32[]{:S(2)}, u32[]{:S(2)}) async-start(f32[16,2,256]{2,1,0:T(2,128)} %broadcast_in_dim.7), calls=%async_computation.3 | async-start | bytes 65536 | tf_op jit(solution)/shard_map/all_to_all | solution.py:20
  67.3 0.4 fusion.11
  67.8 0.0 copy-start.2
  67.8 6.2 %all-to-all-done.3 = f32[16,2,256]{2,1,0:T(2,128)S(1)} async-done(((f32[16,2,256]{2,1,0:T(2,128)}), f32[16,2,256]{2,1,0:T(2,128)S(1)}, u32[]{:S(2)}, u32[]{:S(2)}) %all-to-all-start.3) | async-done | bytes 32800 | tf_op jit(solution)/shard_map/all_to_all | solution.py:20
  74.0 0.2 fusion.14
  74.2 0.2 convolution_multiply_fusion
  74.4 0.0 copy-start.3
  74.4 4.4 %fusion.1 = bf16[1,2048,256]{2,1,0:T(8,128)(2,1)} fusion(f32[2048,256]{1,0:T(8,128)} %copy-done.1, f32[32,2048]{1,0:T(8,128)S(1)} %fusion.11, f32[32,256]{1,0:T(8,128)S(1)} %convolution_multiply_fusion), kind=kOutput, calls=%fused_computation.3 | convolution fusion | flops 202375168 | bytes 3440640 | tf_op jit(solution)/shard_map/dot_general | solution.py:53
  78.8 0.0 copy-done.2
  78.8 0.0 copy-done.3
  (9 shorter events, 0.2 us)
Async XLA Ops:
  0.6 1.6 %copy-start = (bf16[512,2048]{1,0:T(8,128)(2,1)S(1)}, bf16[512,2048]{1,0:T(8,128)(2,1)}, u32[]{:S(2)}) copy-start(bf16[512,2048]{1,0:T(8,128)(2,1)} %param.9) | copy-start | bytes 6291460
  2.2 3.4 %copy-start.4 = (f32[32,256]{1,0:T(8,128)S(1)}, f32[32,256]{1,0:T(8,128)}, u32[]{:S(2)}) copy-start(f32[32,256]{1,0:T(8,128)} %param.12) | copy-start | bytes 98308
  4.3 1.4 %copy-start.1 = (f32[2048,256]{1,0:T(8,128)}, f32[2048,256]{1,0:T(8,128)S(1)}, u32[]{:S(2)}) copy-start(f32[2048,256]{1,0:T(8,128)S(1)} %convolution_add_fusion) | copy-start | bytes 6291460
  53.1 10.1 %all-to-all-start.2 = ((f32[16,2,256]{2,1,0:T(2,128)}), f32[16,2,256]{2,1,0:T(2,128)S(1)}, u32[]{:S(2)}, u32[]{:S(2)}) async-start(f32[16,2,256]{2,1,0:T(2,128)} %copy.20), calls=%async_computation.2 | async-start | bytes 65536 | tf_op jit(solution)/shard_map/all_to_all | solution.py:20
  63.8 10.1 %all-to-all-start.3 = ((f32[16,2,256]{2,1,0:T(2,128)}), f32[16,2,256]{2,1,0:T(2,128)S(1)}, u32[]{:S(2)}, u32[]{:S(2)}) async-start(f32[16,2,256]{2,1,0:T(2,128)} %broadcast_in_dim.7), calls=%async_computation.3 | async-start | bytes 65536 | tf_op jit(solution)/shard_map/all_to_all | solution.py:20
  67.8 11.1 %copy-start.2 = (f32[32,2048]{1,0:T(8,128)}, f32[32,2048]{1,0:T(8,128)S(1)}, u32[]{:S(2)}) copy-start(f32[32,2048]{1,0:T(8,128)S(1)} %fusion.11) | copy-start | bytes 786436
  74.4 4.4 %copy-start.3 = (f32[32,256]{1,0:T(8,128)}, f32[32,256]{1,0:T(8,128)S(1)}, u32[]{:S(2)}) copy-start(f32[32,256]{1,0:T(8,128)S(1)} %convolution_multiply_fusion) | copy-start | bytes 98308

commit v3 on v2

v3 whole, which is shorter than its diff:
```python
import jax
import jax.numpy as jnp
from jax import lax
from jax.sharding import PartitionSpec as P

NEAR = ("sub", "pair")
FAR = ("dp",)
EVERYONE = ("groups",) + FAR + NEAR
HIGHEST = lax.Precision.HIGHEST


def swap(pieces, axes):
    return lax.all_to_all(pieces, axes, 0, 0, tiled=True)


def copies(block, axes, count):
    return swap(jnp.broadcast_to(block[None], (count,) + block.shape), axes)


def local(near, far, inputs, cotangent, error_prev, seed_q):
    merged = lax.dot_general(
        inputs, cotangent, (((0,), (0,)), ((), ())), preferred_element_type=jnp.float32
    )
    merged = merged + error_prev[0].astype(jnp.float32)
    term = lax.dot_general(seed_q, merged, (((1,), (1,)), ((), ())), precision=HIGHEST)
    rank, width = term.shape
    pieces = term.reshape(rank, near, width // near).transpose(1, 0, 2)
    part = jnp.sum(swap(pieces, NEAR), axis=0)
    chunk = jnp.sum(copies(part, FAR, far), axis=0)
    first = copies(chunk, NEAR, near).transpose(1, 0, 2).reshape(rank, width)

    product = jnp.dot(first, merged, precision=HIGHEST)
    product = jnp.sum(copies(product, NEAR, near), axis=0)
    product = jnp.sum(copies(product, FAR, far), axis=0)

    basis = first
    for sweep in range(2):
        gram = jnp.dot(basis, basis.T, precision=HIGHEST)
        lower = jnp.linalg.cholesky(gram)
        basis = jax.scipy.linalg.solve_triangular(lower, basis, lower=True)
        product = jax.scipy.linalg.solve_triangular(lower, product, lower=True)
    second = product / (near * far)
    approx = lax.dot_general(basis, second, (((0,), (0,)), ((), ())), precision=HIGHEST)
    error_next = (merged - approx).astype(jnp.bfloat16)[None]
    return (error_next, basis, second)


def solution(mesh):
    near = mesh.shape["sub"] * mesh.shape["pair"]
    far = mesh.shape["dp"]

    def run(*args):
        return local(near, far, *args)

    return jax.shard_map(
        run,
        mesh=mesh,
        in_specs=(P(EVERYONE, None), P(EVERYONE, None), P(EVERYONE, None, None), P()),
        out_specs=(P(EVERYONE, None, None), P("groups", None), P("groups", None)),
        check_vma=False,
    )
```

time: 79.3 us -> 77.9 us (0.982)
  waiting for transfers between devices: 9.66 us -> 7.1 us
  blocking collectives: 30 us -> 31.6 us
    all_to_all x2, waiting for transfers between devices: 9.66 us -> 7.1 us  [swap(): return lax.all_to_all(pieces, axes, 0, 0, tiled=True)]
    all_to_all x2 -> x3, blocking collectives: 30 us -> 31.6 us  [swap(): return lax.all_to_all(pieces, axes, 0, 0, tiled=True)]
  transfers between devices with their start and end apart: 2 -> 2, of which waited for: 2 -> 2; matrix products, arithmetic and copies ran while one was open for 4% -> 5% of each run, Pallas kernels for 0% -> 0%
where the time goes in v3:
time: 77.9 us; the launch traced here: 77.3 us
  blocking collectives  31.6 us (41%)
  other arithmetic  13.4 us (17%)
  matrix products  13.1 us (17%)
  waiting for transfers between devices  7.1 us (9%)
  starting transfers between devices  6.65 us (9%)
  local copies, waits for them, and re-layouts  4.52 us (6%)
  between operations  0.82 us (1%)
    all_to_all x3, blocking collectives, swap(): return lax.all_to_all(pieces, axes, 0, 0, tiled=True)  31.6 us
    another operation x6, other arithmetic, local(): lower = jnp.linalg.cholesky(gram)  7.19 us
    all_to_all x2, waiting for transfers between devices, swap(): return lax.all_to_all(pieces, axes, 0, 0, tiled=True)  7.1 us
    all_to_all x2, starting transfers between devices, swap(): return lax.all_to_all(pieces, axes, 0, 0, tiled=True)  6.65 us
    another operation x4, other arithmetic, local(): basis = jax.scipy.linalg.solve_triangular(lower, basis, lower=True)  6.17 us
    dot_general x1, matrix products, local(): lax.dot_general(basis, second, (((0,), (0,)), ((), ())), precision=HIGHEST)  4.41 us
    unnamed x10, local copies, waits for them, and re-layouts  2.95 us
    dot_general x1, matrix products, local(): product = jnp.dot(first, merged, precision=HIGHEST)  2.69 us
  transfers between devices with their start and end apart: 2, of which 2 were waited for; matrix products, arithmetic and copies ran while one was open for 5% of the time, Pallas kernels for 0%

profile of v3, /device:TPU:0, one launch (start us, length us, event | category | flops | bytes accessed | tf_op | source)
XLA Modules:
  0.0 77.3 jit_solution(7413095156047277889)
XLA Ops:
  0.6 0.0 copy-start
  0.6 1.6 %copy-done = bf16[512,2048]{1,0:T(8,128)(2,1)S(1)} copy-done((bf16[512,2048]{1,0:T(8,128)(2,1)S(1)}, bf16[512,2048]{1,0:T(8,128)(2,1)}, u32[]{:S(2)}) %copy-start) | copy-done | bytes 2097176
  2.2 0.0 copy-start.4
  2.2 2.1 %convolution_add_fusion = f32[2048,256]{1,0:T(8,128)S(1)} fusion(bf16[512,2048]{1,0:T(8,128)(2,1)S(1)} %copy-done, bf16[512,256]{1,0:T(8,128)(2,1)} %param.10, bf16[1,2048,256]{2,1,0:T(8,128)(2,1)} %param.11), kind=kOutput, calls=%fused_computation.1 | convolution fusion | flops 537919488 | bytes 5505024 | tf_op jit(solution)/shard_map/dot_general | solution.py:21
  4.3 0.0 copy-start.1
  4.3 1.3 %copy-done.1 = f32[2048,256]{1,0:T(8,128)} copy-done((f32[2048,256]{1,0:T(8,128)}, f32[2048,256]{1,0:T(8,128)S(1)}, u32[]{:S(2)}) %copy-start.1) | copy-done | bytes 2097176
  5.7 0.0 copy-done.4
  5.7 2.0 %fusion.16 = f32[2048,32]{0,1:T(8,128)S(1)} fusion(f32[2048,256]{1,0:T(8,128)S(1)} %convolution_add_fusion, f32[32,256]{1,0:T(8,128)S(1)} %copy-done.4), kind=kOutput, calls=%fused_computation.30 | convolution fusion | flops 201326592 | bytes 2392064 | tf_op jit(solution)/shard_map/dot_general | solution.py:25
  7.7 10.0 %all_to_all.25 = f32[4,32,512]{2,1,0:T(8,128)S(1)} all-to-all(f32[4,32,512]{2,1,0:T(8,128)S(1)} %bitcast.64), channel_id=1, replica_groups=mesh['groups'=2,'dp'=4,'sub'=2,'pair'=2] {'sub','pair'}, dimensions={0} | all-to-all | bytes 524288 | tf_op jit(solution)/shard_map/all_to_all | solution.py:13
  17.8 13.2 %all_to_all.26 = f32[4,32,512]{2,1,0:T(8,128)S(1)} all-to-all(f32[4,32,512]{2,1,0:T(8,128)S(1)} %broadcast_in_dim.10), channel_id=1, replica_groups=mesh['groups'=2,'dp'=4,'sub'=2,'pair'=2] {'dp'}, dimensions={0} | all-to-all | bytes 524288 | tf_op jit(solution)/shard_map/all_to_all | solution.py:13
  31.0 8.4 %all_to_all.27 = f32[4,32,512]{2,1,0:T(8,128)S(1)} all-to-all(f32[4,32,512]{2,1,0:T(8,128)S(1)} %broadcast_in_dim.11), channel_id=1, replica_groups=mesh['groups'=2,'dp'=4,'sub'=2,'pair'=2] {'sub','pair'}, dimensions={0} | all-to-all | bytes 524288 | tf_op jit(solution)/shard_map/all_to_all | solution.py:13
  39.5 0.3 convolution_bitcast_fusion
  39.8 0.1 copy.17
  39.9 2.9 %cholesky.44 = f32[32,32]{1,0:T(8,128)S(1)} custom-call(f32[32,32]{1,0:T(8,128)S(1)} %fusion.13), custom_call_target="Cholesky" | custom-call | tf_op jit(solution)/shard_map/jit(cholesky)/cholesky | solution.py:39
  42.8 0.6 compare_reduce_fusion.1
  43.5 0.7 fusion.3
  44.1 2.4 %custom-call.10 = f32[1,32,32]{1,2,0:T(8,128)S(1)} custom-call(f32[1,32,32]{2,1,0:T(8,128)S(1)} %fusion.3), custom_call_target="InvertDiagBlocksLowerTriangular" | custom-call | tf_op jit(solution)/shard_map/jit(_solve_triangular)/triangular_solve | solution.py:40
  46.6 2.7 %fusion.18 = f32[32,256]{1,0:T(8,128)S(1)} fusion(f32[32,2048]{1,0:T(8,128)S(1)} %bitcast.60, f32[2048,256]{1,0:T(8,128)} %copy-done.1), kind=kOutput, calls=%fused_computation.32 | convolution fusion | flops 201326592 | bytes 2392064 | tf_op jit(solution)/shard_map/dot_general | solution.py:32
  49.3 0.4 fusion.11
  49.7 0.3 fusion.17
  50.1 0.1 copy.19
  50.2 2.9 %cholesky.55 = f32[32,32]{1,0:T(8,128)S(1)} custom-call(f32[32,32]{1,0:T(8,128)S(1)} %fusion.8), custom_call_target="Cholesky" | custom-call | tf_op jit(solution)/shard_map/jit(cholesky)/cholesky | solution.py:39
  53.1 0.6 compare_reduce_fusion
  53.8 0.7 broadcast_in_dim.12
  54.4 3.3 %all-to-all-start.3 = ((f32[4,32,256]{2,1,0:T(8,128)}), f32[4,32,256]{2,1,0:T(8,128)S(1)}, u32[]{:S(2)}, u32[]{:S(2)}) async-start(f32[4,32,256]{2,1,0:T(8,128)} %broadcast_in_dim.12), calls=%async_computation.3 | async-start | bytes 262144 | tf_op jit(solution)/shard_map/all_to_all | solution.py:13
  57.8 0.7 fusion.4
  58.4 2.4 %custom-call.11 = f32[1,32,32]{1,2,0:T(8,128)S(1)} custom-call(f32[1,32,32]{2,1,0:T(8,128)S(1)} %fusion.4), custom_call_target="InvertDiagBlocksLowerTriangular" | custom-call | tf_op jit(solution)/shard_map/jit(_solve_triangular)/triangular_solve | solution.py:40
  60.9 1.5 %all-to-all-done.3 = f32[4,32,256]{2,1,0:T(8,128)S(1)} async-done(((f32[4,32,256]{2,1,0:T(8,128)}), f32[4,32,256]{2,1,0:T(8,128)S(1)}, u32[]{:S(2)}, u32[]{:S(2)}) %all-to-all-start.3) | async-done | bytes 131104 | tf_op jit(solution)/shard_map/all_to_all | solution.py:13
  62.4 0.7 broadcast_in_dim.13
  63.1 3.3 %all-to-all-start.4 = ((f32[4,32,256]{2,1,0:T(8,128)}), f32[4,32,256]{2,1,0:T(8,128)S(1)}, u32[]{:S(2)}, u32[]{:S(2)}) async-start(f32[4,32,256]{2,1,0:T(8,128)} %broadcast_in_dim.13), calls=%async_computation.4 | async-start | bytes 262144 | tf_op jit(solution)/shard_map/all_to_all | solution.py:13
  66.4 0.4 fusion.6
  66.8 0.0 copy-start.2
  66.8 5.6 %all-to-all-done.4 = f32[4,32,256]{2,1,0:T(8,128)S(1)} async-done(((f32[4,32,256]{2,1,0:T(8,128)}), f32[4,32,256]{2,1,0:T(8,128)S(1)}, u32[]{:S(2)}, u32[]{:S(2)}) %all-to-all-start.4) | async-done | bytes 131104 | tf_op jit(solution)/shard_map/all_to_all | solution.py:13
  72.4 0.2 fusion.9
  72.7 0.2 convolution_multiply_fusion
  72.9 0.0 copy-start.3
  72.9 4.4 %fusion.1 = bf16[1,2048,256]{2,1,0:T(8,128)(2,1)} fusion(f32[2048,256]{1,0:T(8,128)} %copy-done.1, f32[32,2048]{1,0:T(8,128)S(1)} %fusion.6, f32[32,256]{1,0:T(8,128)S(1)} %convolution_multiply_fusion), kind=kOutput, calls=%fused_computation.3 | convolution fusion | flops 202375168 | bytes 3440640 | tf_op jit(solution)/shard_map/dot_general | solution.py:43
  77.3 0.0 copy-done.2
  77.3 0.0 copy-done.3
  (12 shorter events, 0.2 us)
Async XLA Ops:
  0.6 1.6 %copy-start = (bf16[512,2048]{1,0:T(8,128)(2,1)S(1)}, bf16[512,2048]{1,0:T(8,128)(2,1)}, u32[]{:S(2)}) copy-start(bf16[512,2048]{1,0:T(8,128)(2,1)} %param.9) | copy-start | bytes 6291460
  2.2 3.4 %copy-start.4 = (f32[32,256]{1,0:T(8,128)S(1)}, f32[32,256]{1,0:T(8,128)}, u32[]{:S(2)}) copy-start(f32[32,256]{1,0:T(8,128)} %param.12) | copy-start | bytes 98308
  4.3 1.4 %copy-start.1 = (f32[2048,256]{1,0:T(8,128)}, f32[2048,256]{1,0:T(8,128)S(1)}, u32[]{:S(2)}) copy-start(f32[2048,256]{1,0:T(8,128)S(1)} %convolution_add_fusion) | copy-start | bytes 6291460
  54.4 7.9 %all-to-all-start.3 = ((f32[4,32,256]{2,1,0:T(8,128)}), f32[4,32,256]{2,1,0:T(8,128)S(1)}, u32[]{:S(2)}, u32[]{:S(2)}) async-start(f32[4,32,256]{2,1,0:T(8,128)} %broadcast_in_dim.12), calls=%async_computation.3 | async-start | bytes 262144 | tf_op jit(solution)/shard_map/all_to_all | solution.py:13
  63.1 9.4 %all-to-all-start.4 = ((f32[4,32,256]{2,1,0:T(8,128)}), f32[4,32,256]{2,1,0:T(8,128)S(1)}, u32[]{:S(2)}, u32[]{:S(2)}) async-start(f32[4,32,256]{2,1,0:T(8,128)} %broadcast_in_dim.13), calls=%async_computation.4 | async-start | bytes 262144 | tf_op jit(solution)/shard_map/all_to_all | solution.py:13
  66.8 10.5 %copy-start.2 = (f32[32,2048]{1,0:T(8,128)}, f32[32,2048]{1,0:T(8,128)S(1)}, u32[]{:S(2)}) copy-start(f32[32,2048]{1,0:T(8,128)S(1)} %fusion.6) | copy-start | bytes 786436
  72.9 4.4 %copy-start.3 = (f32[32,256]{1,0:T(8,128)}, f32[32,256]{1,0:T(8,128)S(1)}, u32[]{:S(2)}) copy-start(f32[32,256]{1,0:T(8,128)S(1)} %convolution_multiply_fusion) | copy-start | bytes 98308

commit v4 on v2

v4 whole, which is shorter than its diff:
```python
import functools

import jax
import jax.numpy as jnp
from jax import lax
from jax.experimental import pallas as pl
from jax.experimental.pallas import tpu as pltpu
from jax.sharding import PartitionSpec as P

AXES = ("dp", "sub", "pair")
EVERYONE = ("groups",) + AXES
VMEM_BYTES = 24 * 1024 * 1024
BF16, F32 = jnp.bfloat16, jnp.float32


def split_axes(mesh):
    direct, count = (), 1
    for axis in AXES:
        if count * mesh.shape[axis] <= 16:
            direct, count = direct + (axis,), count * mesh.shape[axis]
    rest = tuple(axis for axis in AXES if axis not in direct)
    return direct, rest, count


def swap(pieces, direct):
    return lax.all_to_all(pieces, direct, 0, 0, tiled=True)


def parts_of(value, count):
    parts = []
    for _ in range(count):
        part = value.astype(BF16)
        parts.append(part)
        value = value - part.astype(F32)
    return parts


def dot(a, b, dims):
    return lax.dot_general(a, b, (dims, ((), ())), preferred_element_type=F32)


def params(semantics=None):
    return pltpu.CompilerParams(dimension_semantics=semantics, vmem_limit_bytes=VMEM_BYTES)


def cost(flops, nbytes):
    return pl.CostEstimate(flops=flops, bytes_accessed=nbytes, transcendentals=0)


def merge_kernel(x_ref, c_ref, e_ref, seed_ref, merged_ref, pieces_ref):
    merged = dot(x_ref[...], c_ref[...], ((0,), (0,))) + e_ref[0].astype(F32)
    merged_ref[...] = merged
    rank = seed_ref.shape[0]
    m_high, m_low = parts_of(merged, 2)
    s_high, s_low = parts_of(seed_ref[...], 2)
    both = dot(jnp.concatenate([s_high, s_low], axis=0), m_high, ((1,), (1,)))
    term = both[:rank] + both[rank:] + dot(s_high, m_low, ((1,), (1,)))
    piece = pieces_ref.shape[2]
    for i in range(pieces_ref.shape[0]):
        pieces_ref[i] = term[:, i * piece:(i + 1) * piece]


def merge(inputs, cotangent, error_prev, seed_q, count):
    tokens, width = inputs.shape
    out = cotangent.shape[1]
    rank = seed_q.shape[0]
    piece = width // count
    block = max(piece, 512)
    per = block // piece
    return pl.pallas_call(
        merge_kernel,
        grid=(width // block,),
        in_specs=[
            pl.BlockSpec((tokens, block), lambda i: (0, i)),
            pl.BlockSpec((tokens, out), lambda i: (0, 0)),
            pl.BlockSpec((1, block, out), lambda i: (0, i, 0)),
            pl.BlockSpec((rank, out), lambda i: (0, 0)),
        ],
        out_specs=[
            pl.BlockSpec((block, out), lambda i: (i, 0)),
            pl.BlockSpec((per, rank, piece), lambda i: (i, 0, 0)),
        ],
        out_shape=[
            jax.ShapeDtypeStruct((width, out), F32),
            jax.ShapeDtypeStruct((count, rank, piece), F32),
        ],
        compiler_params=params(("arbitrary",)),
        cost_estimate=cost(2 * tokens * width * out, 6 * width * out + 2 * tokens * width),
        name="merge",
    )(inputs, cotangent, error_prev, seed_q)


def rows_of(pieces_ref):
    return jnp.concatenate([pieces_ref[i] for i in range(pieces_ref.shape[0])], axis=1)


def product_kernel(pieces_ref, merged_ref, copies_ref):
    first = rows_of(pieces_ref)
    rank = first.shape[0]
    f_high, f_low = parts_of(first, 2)
    m_high, m_low = parts_of(merged_ref[...], 2)
    both = dot(jnp.concatenate([f_high, f_low], axis=0), m_high, ((1,), (0,)))
    product = both[:rank] + both[rank:] + dot(f_high, m_low, ((1,), (0,)))
    for i in range(copies_ref.shape[0]):
        copies_ref[i] = product


def product_copies(pieces, merged, copies):
    count, rank, piece = pieces.shape
    width, out = merged.shape
    return pl.pallas_call(
        product_kernel,
        out_shape=jax.ShapeDtypeStruct((copies, rank, out), F32),
        compiler_params=params(),
        cost_estimate=cost(2 * rank * width * out, 4 * width * out),
        name="product",
    )(pieces, merged)


def gram_of(rows):
    rank = rows.shape[0]
    stack = jnp.concatenate(parts_of(rows, 3), axis=0)
    full = dot(stack, stack, ((1,), (1,)))
    gram = None
    for i, j in ((2, 0), (0, 2), (1, 1), (1, 0), (0, 1), (0, 0)):
        term = full[i * rank:(i + 1) * rank, j * rank:(j + 1) * rank]
        gram = term if gram is None else gram + term
    return gram


def inverse_factor(gram):
    rank = gram.shape[0]
    row = lax.broadcasted_iota(jnp.int32, (rank, rank), 0)
    lane = lax.broadcasted_iota(jnp.int32, (rank, rank), 1)
    eye = jnp.where(row == lane, 1.0, 0.0).astype(F32)
    wide = jnp.concatenate([gram, eye], axis=1)
    index = lax.broadcasted_iota(jnp.int32, (rank, 1), 0)
    for k in range(rank - 1):
        pivot = wide[k:k + 1, :]
        scale = 1.0 / wide[k:k + 1, k:k + 1]
        factor = jnp.where(index > k, wide[:, k:k + 1] * scale, 0.0)
        wide = wide - factor * pivot
    diagonal = jnp.sum(jnp.where(row == lane, wide[:, :rank], 0.0), axis=1, keepdims=True)
    return wide[:, rank:] * lax.rsqrt(diagonal)


def short_dot(left, right):
    a, b, c = parts_of(left, 3)
    d, e, f = parts_of(right, 3)
    lefts = jnp.concatenate([c, a, b, b, a, a], axis=1)
    rights = jnp.concatenate([d, f, e, d, e, d], axis=0)
    return dot(lefts, rights, ((1,), (0,)))


def sweep_kernel(pieces_ref, basis_ref, inverse_ref):
    rows = rows_of(pieces_ref)
    inverse = None
    for sweep in range(2):
        step = inverse_factor(gram_of(rows))
        rows = short_dot(step, rows)
        inverse = step if inverse is None else short_dot(step, inverse)
    basis_ref[...] = rows
    inverse_ref[...] = inverse


def sweeps(pieces):
    count, rank, piece = pieces.shape
    width = count * piece
    return pl.pallas_call(
        sweep_kernel,
        out_shape=[
            jax.ShapeDtypeStruct((rank, width), F32),
            jax.ShapeDtypeStruct((rank, rank), F32),
        ],
        compiler_params=params(),
        cost_estimate=cost(10 ** 10, 10 ** 7),
        name="sweeps",
    )(pieces)


def error_kernel(workers, merged_ref, basis_ref, inverse_ref, products_ref, error_ref, second_ref, right_ref):
    rank = second_ref.shape[0]

    @pl.when(pl.program_id(0) == 0)
    def _():
        product = products_ref[0]
        for i in range(1, products_ref.shape[0]):
            product = product + products_ref[i]
        second = short_dot(inverse_ref[...], product) * (1.0 / workers)
        second_ref[...] = second
        high, low = parts_of(second, 2)
        right_ref[...] = jnp.concatenate([high, low, high], axis=0)

    b_high, b_low = parts_of(basis_ref[...], 2)
    lefts = jnp.concatenate([b_high, b_high, b_low], axis=0)
    approx = dot(lefts, right_ref[...], ((0,), (0,)))
    error_ref[0] = (merged_ref[...] - approx).astype(error_ref.dtype)


def error_of(merged, basis, inverse, products, workers):
    width, out = merged.shape
    rank = basis.shape[0]
    block = min(width, 512)
    return pl.pallas_call(
        functools.partial(error_kernel, workers),
        grid=(width // block,),
        in_specs=[
            pl.BlockSpec((block, out), lambda i: (i, 0)),
            pl.BlockSpec((rank, block), lambda i: (0, i)),
            pl.BlockSpec((rank, rank), lambda i: (0, 0)),
            pl.BlockSpec(products.shape, lambda i: (0, 0, 0)),
        ],
        out_specs=[
            pl.BlockSpec((1, block, out), lambda i: (0, i, 0)),
            pl.BlockSpec((rank, out), lambda i: (0, 0)),
        ],
        out_shape=[
            jax.ShapeDtypeStruct((1, width, out), BF16),
            jax.ShapeDtypeStruct((rank, out), F32),
        ],
        scratch_shapes=[pltpu.VMEM((3 * rank, out), BF16)],
        compiler_params=params(("arbitrary",)),
        cost_estimate=cost(2 * rank * width * out, 6 * width * out),
        name="error_next",
    )(merged, basis, inverse, products)


def local(direct, rest, count, workers, inputs, cotangent, error_prev, seed_q):
    merged, pieces = merge(inputs, cotangent, error_prev, seed_q, count)
    if rest:
        pieces = lax.psum(pieces, rest)
    chunk = jnp.sum(swap(pieces, direct), axis=0)
    pieces = swap(jnp.broadcast_to(chunk[None], pieces.shape), direct)
    copies = product_copies(pieces, merged, count)
    if rest:
        copies = lax.psum(copies, rest)
    products = swap(copies, direct)
    basis, inverse = sweeps(pieces)
    error_next, second = error_of(merged, basis, inverse, products, workers)
    return (error_next, basis, second)


def solution(mesh):
    direct, rest, count = split_axes(mesh)
    workers = 1
    for axis in AXES:
        workers *= mesh.shape[axis]

    def run(*args):
        return local(direct, rest, count, workers, *args)

    return jax.shard_map(
        run,
        mesh=mesh,
        in_specs=(P(EVERYONE, None), P(EVERYONE, None), P(EVERYONE, None, None), P()),
        out_specs=(P(EVERYONE, None, None), P("groups", None), P("groups", None)),
        check_vma=False,
    )
```

time: 79.3 us -> 61.4 us (0.77)
  Pallas kernels: 0 us -> 13.9 us
  other arithmetic: 13.4 us -> 0.02 us
  matrix products: 13.2 us -> 0 us
  starting transfers between devices: 6.99 us -> 3.57 us
  waiting for transfers between devices: 9.66 us -> 7.13 us
    pallas_call x0 -> x4, Pallas kernels: none -> 13.9 us  [the longest x1 7.3 us: sweeps(): pl.pallas_call(sweep_kernel, out_shape=[jax.ShapeDtypeStruct((rank, width...]
    another operation x10 -> x0, other arithmetic: 13.4 us -> none  [the longest x6 7.19 us: local(): lower = jnp.linalg.cholesky(gram)]
    dot_general x6 -> x0, matrix products: 11.9 us -> none  [the longest x1 4.41 us: local(): lax.dot_general(basis, second, (((0,), (0,)), ((), ())), precision=HIGHEST)]
    all_to_all x2 -> x1, starting transfers between devices: 6.99 us -> 3.57 us  [swap(): return lax.all_to_all(pieces, direct, 0, 0, tiled=True)]
    all_to_all x2 -> x1, waiting for transfers between devices: 9.66 us -> 7.13 us  [swap(): return lax.all_to_all(pieces, direct, 0, 0, tiled=True)]
    unnamed x10, local copies, waits for them, and re-layouts: 2.95 us -> 5.47 us
    another operation x4 -> x0, matrix products: 1.3 us -> none  [the longest x2 0.86 us: local(): basis = jax.scipy.linalg.solve_triangular(lower, basis, lower=True)]
    dot_general x4 -> x0, local copies, waits for them, and re-layouts: 0.92 us -> none  [the longest x2 0.78 us: local(): product = jnp.dot(first, merged, precision=HIGHEST)]
  transfers between devices with their start and end apart: 2 -> 1, of which waited for: 2 -> 1; matrix products, arithmetic and copies ran while one was open for 4% -> 0% of each run, Pallas kernels for 0% -> 12%
where the time goes in v4:
time: 61.4 us; the launch traced here: 60.9 us
  blocking collectives  30.1 us (49%)
  Pallas kernels  13.9 us (23%)
  waiting for transfers between devices  7.13 us (12%)
  local copies, waits for them, and re-layouts  5.48 us (9%)
  starting transfers between devices  3.57 us (6%)
  between operations  0.67 us (1%)
    all_to_all x2, blocking collectives, swap(): return lax.all_to_all(pieces, direct, 0, 0, tiled=True)  30.1 us
    pallas_call x1, Pallas kernels, sweeps(): pl.pallas_call(sweep_kernel, out_shape=[jax.ShapeDtypeStruct((rank, width...  7.3 us
    all_to_all x1, waiting for transfers between devices, swap(): return lax.all_to_all(pieces, direct, 0, 0, tiled=True)  7.13 us
    unnamed x10, local copies, waits for them, and re-layouts  5.47 us
    all_to_all x1, starting transfers between devices, swap(): return lax.all_to_all(pieces, direct, 0, 0, tiled=True)  3.57 us
    pallas_call x1, Pallas kernels, merge(): pl.pallas_call(merge_kernel, grid=(width // block,), in_specs=[pl.BlockSp...  2.96 us
    pallas_call x1, Pallas kernels, error_of(): pl.pallas_call(functools.partial(error_kernel, workers), grid=(width // b...  2.39 us
    pallas_call x1, Pallas kernels, product_copies(): pl.pallas_call(product_kernel, out_shape=jax.ShapeDtypeStruct((copies, ra...  1.28 us
  transfers between devices with their start and end apart: 1, of which 1 were waited for; matrix products, arithmetic and copies ran while one was open for 0% of the time, Pallas kernels for 12%

profile of v4, /device:TPU:0, one launch (start us, length us, event | category | flops | bytes accessed | tf_op | source)
XLA Modules:
  0.0 60.9 jit_solution(13523070754229913394)
XLA Ops:
  0.6 0.0 copy-start
  0.6 1.6 %copy-done = bf16[512,2048]{1,0:T(8,128)(2,1)S(1)} copy-done((bf16[512,2048]{1,0:T(8,128)(2,1)S(1)}, bf16[512,2048]{1,0:T(8,128)(2,1)}, u32[]{:S(2)}) %copy-start) | copy-done | bytes 2097176
  2.2 0.0 copy-start.1
  2.2 1.2 %copy-done.1 = bf16[1,2048,256]{2,1,0:T(8,128)(2,1)S(1)} copy-done((bf16[1,2048,256]{2,1,0:T(8,128)(2,1)S(1)}, bf16[1,2048,256]{2,1,0:T(8,128)(2,1)}, u32[]{:S(2)}) %copy-start.1) | copy-done | bytes 1048600
  3.4 0.0 copy-start.2
  3.5 0.9 %copy-done.2 = bf16[512,256]{1,0:T(8,128)(2,1)S(1)} copy-done((bf16[512,256]{1,0:T(8,128)(2,1)S(1)}, bf16[512,256]{1,0:T(8,128)(2,1)}, u32[]{:S(2)}) %copy-start.2) | copy-done | bytes 262168
  4.4 0.0 copy-start.4
  4.4 0.8 %copy-done.4 = f32[32,256]{1,0:T(8,128)S(1)} copy-done((f32[32,256]{1,0:T(8,128)S(1)}, f32[32,256]{1,0:T(8,128)}, u32[]{:S(2)}) %copy-start.4) | copy-done | bytes 32792
  5.2 3.0 %merge.1 = (f32[2048,256]{1,0:T(8,128)S(1)}, f32[16,32,128]{2,1,0:T(8,128)S(1)}) custom-call(bf16[512,2048]{1,0:T(8,128)(2,1)S(1)} %copy-done, bf16[512,256]{1,0:T(8,128)(2,1)S(1)} %copy-done.2, bf16[1,2048,256]{2,1,0:T(8,128)(2,1)S(1)} %copy-done.1, f32[32,256]{1,0:T(8,128)S(1)} %copy-done.4), custom_call_target="tpu_custom_call" | custom-call | flops 536870912 | bytes 5242880 | tf_op jit(solution)/shard_map/merge/pallas_call | solution.py:70
  8.1 17.2 %all_to_all.15 = f32[16,32,128]{2,1,0:T(8,128)S(1)} all-to-all(f32[16,32,128]{2,1,0:T(8,128)S(1)} %get-tuple-element.10), channel_id=1, replica_groups=mesh['groups'=2,'dp'=4,'sub'=2,'pair'=2] {'dp','sub','pair'}, dimensions={0} | all-to-all | bytes 524288 | tf_op jit(solution)/shard_map/all_to_all | solution.py:26
  25.4 12.8 %all_to_all.16.pieces_ref = f32[16,32,128]{2,1,0:T(8,128)S(1)} all-to-all(f32[16,32,128]{2,1,0:T(8,128)S(1)} %broadcast_in_dim.2), channel_id=1, replica_groups=mesh['groups'=2,'dp'=4,'sub'=2,'pair'=2] {'dp','sub','pair'}, dimensions={0} | all-to-all | bytes 524288 | tf_op jit(solution)/shard_map/all_to_all | solution.py:26
  38.2 1.3 %product.1 = f32[16,32,256]{2,1,0:T(8,128)} custom-call(f32[16,32,128]{2,1,0:T(8,128)S(1)} %all_to_all.16.pieces_ref, f32[2048,256]{1,0:T(8,128)S(1)} %get-tuple-element.9.merged_ref), custom_call_target="tpu_custom_call" | custom-call | flops 33554432 | bytes 2097152 | tf_op jit(solution)/shard_map/product/pallas_call | solution.py:111
  39.5 3.6 %all-to-all-start.2 = ((f32[16,32,256]{2,1,0:T(8,128)}), f32[16,32,256]{2,1,0:T(8,128)S(1)}, u32[]{:S(2)}, u32[]{:S(2)}) async-start(f32[16,32,256]{2,1,0:T(8,128)} %product.1), calls=%async_computation.2 | async-start | bytes 1048576 | tf_op jit(solution)/shard_map/all_to_all | solution.py:26
  43.1 7.3 %sweeps.1 = (f32[32,2048]{1,0:T(8,128)}, f32[32,32]{1,0:T(8,128)S(1)}) custom-call(f32[16,32,128]{2,1,0:T(8,128)S(1)} %all_to_all.16.pieces_ref), custom_call_target="tpu_custom_call" | custom-call | flops 10000000000 | bytes 10000000 | tf_op jit(solution)/shard_map/sweeps/pallas_call | solution.py:169
  50.4 7.1 %all-to-all-done.2.products_ref = f32[16,32,256]{2,1,0:T(8,128)S(1)} async-done(((f32[16,32,256]{2,1,0:T(8,128)}), f32[16,32,256]{2,1,0:T(8,128)S(1)}, u32[]{:S(2)}, u32[]{:S(2)}) %all-to-all-start.2) | async-done | bytes 524320 | tf_op jit(solution)/shard_map/all_to_all | solution.py:26
  57.5 0.0 copy-start.3
  57.5 0.9 %copy-done.3 = f32[32,2048]{1,0:T(8,128)S(1)} copy-done((f32[32,2048]{1,0:T(8,128)S(1)}, f32[32,2048]{1,0:T(8,128)}, u32[]{:S(2)}) %copy-start.3) | copy-done | bytes 262168
  58.5 2.4 %error_next.1 = (bf16[1,2048,256]{2,1,0:T(8,128)(2,1)}, f32[32,256]{1,0:T(8,128)}) custom-call(f32[2048,256]{1,0:T(8,128)S(1)} %get-tuple-element.9.merged_ref, f32[32,2048]{1,0:T(8,128)S(1)} %copy-done.3, f32[32,32]{1,0:T(8,128)S(1)} %get-tuple-element.12.inverse_ref, f32[16,32,256]{2,1,0:T(8,128)S(1)} %all-to-all-done.2.products_ref), custom_call_target="tpu_custom_call" | custom-call | flops 33554432 | bytes 3145728 | tf_op jit(solution)/shard_map/error_next/pallas_call | solution.py:204
  (2 shorter events, 0.0 us)
Async XLA Ops:
  0.6 1.6 %copy-start = (bf16[512,2048]{1,0:T(8,128)(2,1)S(1)}, bf16[512,2048]{1,0:T(8,128)(2,1)}, u32[]{:S(2)}) copy-start(bf16[512,2048]{1,0:T(8,128)(2,1)} %x_ref.1) | copy-start | bytes 6291460
  2.2 1.2 %copy-start.1 = (bf16[1,2048,256]{2,1,0:T(8,128)(2,1)S(1)}, bf16[1,2048,256]{2,1,0:T(8,128)(2,1)}, u32[]{:S(2)}) copy-start(bf16[1,2048,256]{2,1,0:T(8,128)(2,1)} %e_ref.1) | copy-start | bytes 3145732
  3.4 0.9 %copy-start.2 = (bf16[512,256]{1,0:T(8,128)(2,1)S(1)}, bf16[512,256]{1,0:T(8,128)(2,1)}, u32[]{:S(2)}) copy-start(bf16[512,256]{1,0:T(8,128)(2,1)} %c_ref.1) | copy-start | bytes 786436
  4.4 0.8 %copy-start.4 = (f32[32,256]{1,0:T(8,128)S(1)}, f32[32,256]{1,0:T(8,128)}, u32[]{:S(2)}) copy-start(f32[32,256]{1,0:T(8,128)} %seed_ref.1) | copy-start | bytes 98308
  39.5 18.0 %all-to-all-start.2 = ((f32[16,32,256]{2,1,0:T(8,128)}), f32[16,32,256]{2,1,0:T(8,128)S(1)}, u32[]{:S(2)}, u32[]{:S(2)}) async-start(f32[16,32,256]{2,1,0:T(8,128)} %product.1), calls=%async_computation.2 | async-start | bytes 1048576 | tf_op jit(solution)/shard_map/all_to_all | solution.py:26
  57.5 1.0 %copy-start.3 = (f32[32,2048]{1,0:T(8,128)S(1)}, f32[32,2048]{1,0:T(8,128)}, u32[]{:S(2)}) copy-start(f32[32,2048]{1,0:T(8,128)} %get-tuple-element.7.basis_ref) | copy-start | bytes 786436

commit v5 on v4

v5 whole, which is shorter than its diff:
```python
import functools

import jax
import jax.numpy as jnp
from jax import lax
from jax.experimental import pallas as pl
from jax.experimental.pallas import tpu as pltpu
from jax.sharding import PartitionSpec as P

AXES = ("dp", "sub", "pair")
EVERYONE = ("groups",) + AXES
VMEM_BYTES = 24 * 1024 * 1024
BF16, F32 = jnp.bfloat16, jnp.float32
HBM = pl.BlockSpec(memory_space=pltpu.HBM)
VMEM = pl.BlockSpec(memory_space=pltpu.VMEM)


def split_axes(mesh):
    count, chips = mesh.shape["pair"], []
    for axis in ("dp", "sub"):
        if count * mesh.shape[axis] <= 16:
            chips.append(axis)
            count *= mesh.shape[axis]
    chips = tuple(chips)
    rest = tuple(axis for axis in AXES if axis not in chips + ("pair",))
    return chips, rest, count // mesh.shape["pair"]


def swap(pieces, axes):
    return lax.all_to_all(pieces, axes, 0, 0, tiled=True)


def across(value):
    return lax.ppermute(value, "pair", [(0, 1), (1, 0)])


def parts_of(value, count):
    parts = []
    for _ in range(count):
        part = value.astype(BF16)
        parts.append(part)
        value = value - part.astype(F32)
    return parts


def dot(a, b, dims):
    return lax.dot_general(a, b, (dims, ((), ())), preferred_element_type=F32)


def params():
    return pltpu.CompilerParams(vmem_limit_bytes=VMEM_BYTES)


def cost(flops, nbytes):
    return pl.CostEstimate(flops=flops, bytes_accessed=nbytes, transcendentals=0)


def merge_kernel(steps, x_hbm, c_hbm, e_hbm, seed_hbm, merged_ref, pieces_ref,
                 x_ref, c_ref, e_ref, seed_ref, x_sem, e_sem, small_sem):
    width, out = merged_ref.shape
    block = width // steps
    copies = [
        pltpu.make_async_copy(c_hbm, c_ref, small_sem.at[0]),
        pltpu.make_async_copy(seed_hbm, seed_ref, small_sem.at[1]),
    ]
    for i in range(steps):
        part = pl.ds(i * block, block)
        copies.append(pltpu.make_async_copy(x_hbm.at[:, part], x_ref.at[:, part], x_sem.at[i]))
        copies.append(pltpu.make_async_copy(e_hbm.at[0, part, :], e_ref.at[part, :], e_sem.at[i]))
    for copy in copies:
        copy.start()
    copies[0].wait()
    copies[1].wait()
    rank = seed_ref.shape[0]
    half, piece = pieces_ref.shape[1:]
    s_high, s_low = parts_of(seed_ref[...], 2)
    s_both = jnp.concatenate([s_high, s_low], axis=0)
    for i in range(steps):
        copies[2 + 2 * i].wait()
        copies[3 + 2 * i].wait()
        part = pl.ds(i * block, block)
        merged = dot(x_ref[:, part], c_ref[...], ((0,), (0,))) + e_ref[part, :].astype(F32)
        merged_ref[part, :] = merged
        m_high, m_low = parts_of(merged, 2)
        both = dot(s_both, m_high, ((1,), (1,)))
        term = both[:rank] + both[rank:] + dot(s_high, m_low, ((1,), (1,)))
        for j in range(block // piece):
            for k in range(rank // half):
                pieces_ref[(i * (block // piece) + j) * (rank // half) + k] = (
                    term[k * half:(k + 1) * half, j * piece:(j + 1) * piece])


def merge(inputs, cotangent, error_prev, seed_q, chips):
    tokens, width = inputs.shape
    out = cotangent.shape[1]
    rank = seed_q.shape[0]
    steps = 4
    return pl.pallas_call(
        functools.partial(merge_kernel, steps),
        in_specs=[HBM, HBM, HBM, HBM],
        out_specs=[VMEM, VMEM],
        out_shape=[
            jax.ShapeDtypeStruct((width, out), F32),
            jax.ShapeDtypeStruct((2 * chips, rank // 2, width // chips), F32),
        ],
        scratch_shapes=[
            pltpu.VMEM((tokens, width), BF16),
            pltpu.VMEM((tokens, out), BF16),
            pltpu.VMEM((width, out), BF16),
            pltpu.VMEM((rank, out), F32),
            pltpu.SemaphoreType.DMA((steps,)),
            pltpu.SemaphoreType.DMA((steps,)),
            pltpu.SemaphoreType.DMA((2,)),
        ],
        compiler_params=params(),
        cost_estimate=cost(2 * tokens * width * out, 6 * width * out + 2 * tokens * width),
        name="merge",
    )(inputs, cotangent, error_prev, seed_q)


def rows_of(pieces_ref):
    return jnp.concatenate([pieces_ref[i] for i in range(pieces_ref.shape[0])], axis=1)


def product_kernel(pieces_ref, mine_ref, other_ref, copies_ref):
    rows = rows_of(pieces_ref)
    half = rows.shape[0]
    f_high, f_low = parts_of(rows, 2)
    m_high, m_low = parts_of(mine_ref[...] + other_ref[...], 2)
    both = dot(jnp.concatenate([f_high, f_low], axis=0), m_high, ((1,), (0,)))
    product = both[:half] + both[half:] + dot(f_high, m_low, ((1,), (0,)))
    for i in range(copies_ref.shape[0]):
        copies_ref[i] = product


def product_copies(pieces, mine, other):
    chips, half, piece = pieces.shape
    width, out = mine.shape
    return pl.pallas_call(
        product_kernel,
        out_shape=jax.ShapeDtypeStruct((chips, half, out), F32),
        compiler_params=params(),
        cost_estimate=cost(2 * half * width * out, 8 * width * out),
        name="product",
    )(pieces, mine, other)


def both_halves(mine, other):
    low = lax.axis_index("pair") == 0
    return jnp.concatenate([jnp.where(low, mine, other), jnp.where(low, other, mine)], axis=0)


def gram_of(rows):
    rank = rows.shape[0]
    stack = jnp.concatenate(parts_of(rows, 3), axis=0)
    full = dot(stack, stack, ((1,), (1,)))
    gram = None
    for i, j in ((2, 0), (0, 2), (1, 1), (1, 0), (0, 1), (0, 0)):
        term = full[i * rank:(i + 1) * rank, j * rank:(j + 1) * rank]
        gram = term if gram is None else gram + term
    return gram


def inverse_factor(gram):
    rank = gram.shape[0]
    row = lax.broadcasted_iota(jnp.int32, (rank, rank), 0)
    lane = lax.broadcasted_iota(jnp.int32, (rank, rank), 1)
    eye = jnp.where(row == lane, 1.0, 0.0).astype(F32)
    wide = jnp.concatenate([gram, eye], axis=1)
    index = lax.broadcasted_iota(jnp.int32, (rank, 1), 0)
    for k in range(rank - 1):
        pivot = wide[k:k + 1, :]
        scale = 1.0 / wide[k:k + 1, k:k + 1]
        factor = jnp.where(index > k, wide[:, k:k + 1] * scale, 0.0)
        wide = wide - factor * pivot
    diagonal = jnp.sum(jnp.where(row == lane, wide[:, :rank], 0.0), axis=1, keepdims=True)
    return wide[:, rank:] * lax.rsqrt(diagonal)


def short_dot(left, right):
    a, b, c = parts_of(left, 3)
    d, e, f = parts_of(right, 3)
    lefts = jnp.concatenate([c, a, b, b, a, a], axis=1)
    rights = jnp.concatenate([d, f, e, d, e, d], axis=0)
    return dot(lefts, rights, ((1,), (0,)))


def sweep_kernel(mine_ref, other_ref, basis_ref, inverse_ref):
    rows = both_halves(rows_of(mine_ref), rows_of(other_ref))
    inverse = None
    for sweep in range(2):
        step = inverse_factor(gram_of(rows))
        rows = short_dot(step, rows)
        inverse = step if inverse is None else short_dot(step, inverse)
    basis_ref[...] = rows
    inverse_ref[...] = inverse


def sweeps(mine, other):
    chips, half, piece = mine.shape
    rank, width = 2 * half, chips * piece
    return pl.pallas_call(
        sweep_kernel,
        out_shape=[
            jax.ShapeDtypeStruct((rank, width), F32),
            jax.ShapeDtypeStruct((rank, rank), F32),
        ],
        compiler_params=params(),
        cost_estimate=cost(10 ** 10, 10 ** 7),
        name="sweeps",
    )(mine, other)


def error_kernel(workers, steps, merged_ref, basis_ref, inverse_ref, mine_ref, other_ref,
                 error_hbm, basis_hbm, second_ref, error_ref, error_sem, basis_sem):
    width = merged_ref.shape[0]
    block = width // steps
    keep = pltpu.make_async_copy(basis_ref, basis_hbm, basis_sem)
    keep.start()
    product = both_halves(mine_ref[...], other_ref[...])
    second = short_dot(inverse_ref[...], product) * (1.0 / workers)
    second_ref[...] = second
    s_high, s_low = parts_of(second, 2)
    rights = jnp.concatenate([s_high, s_low, s_high], axis=0)
    copies = []
    for i in range(steps):
        part = pl.ds(i * block, block)
        b_high, b_low = parts_of(basis_ref[:, part], 2)
        lefts = jnp.concatenate([b_high, b_high, b_low], axis=0)
        approx = dot(lefts, rights, ((0,), (0,)))
        error_ref[part, :] = (merged_ref[part, :] - approx).astype(BF16)
        copies.append(pltpu.make_async_copy(
            error_ref.at[part, :], error_hbm.at[0, part, :], error_sem.at[i]))
        copies[i].start()
    for copy in copies + [keep]:
        copy.wait()


def error_of(merged, basis, inverse, mine, other, workers):
    width, out = merged.shape
    rank = basis.shape[0]
    steps = 4
    return pl.pallas_call(
        functools.partial(error_kernel, workers, steps),
        in_specs=[VMEM] * 5,
        out_specs=[HBM, HBM, VMEM],
        out_shape=[
            jax.ShapeDtypeStruct((1, width, out), BF16),
            jax.ShapeDtypeStruct((rank, width), F32),
            jax.ShapeDtypeStruct((rank, out), F32),
        ],
        scratch_shapes=[
            pltpu.VMEM((width, out), BF16),
            pltpu.SemaphoreType.DMA((steps,)),
            pltpu.SemaphoreType.DMA,
        ],
        compiler_params=params(),
        cost_estimate=cost(2 * rank * width * out, 6 * width * out),
        name="error_next",
    )(merged, basis, inverse, mine, other)


def local(chips, rest, count, workers, inputs, cotangent, error_prev, seed_q):
    inputs, cotangent, error_prev, seed_q = (
        pltpu.with_memory_space_constraint(value, pltpu.HBM)
        for value in (inputs, cotangent, error_prev, seed_q))
    merged, pieces = merge(inputs, cotangent, error_prev, seed_q, count)
    merged_other = across(merged)
    if rest:
        pieces = lax.psum(pieces, rest)
    chunk = jnp.sum(swap(pieces, chips + ("pair",)), axis=0)
    half = swap(jnp.broadcast_to(chunk[None], (count,) + chunk.shape), chips)
    half_other = across(half)
    copies = product_copies(half, merged, merged_other)
    if rest:
        copies = lax.psum(copies, rest)
    product = jnp.sum(swap(copies, chips), axis=0)
    product_other = across(product)
    basis, inverse = sweeps(half, half_other)
    error_next, basis, second = error_of(merged, basis, inverse, product, product_other, workers)
    return (error_next, basis, second)


def solution(mesh):
    chips, rest, count = split_axes(mesh)
    workers = 1
    for axis in AXES:
        workers *= mesh.shape[axis]

    def run(*args):
        return local(chips, rest, count, workers, *args)

    return jax.shard_map(
        run,
        mesh=mesh,
        in_specs=(P(EVERYONE, None), P(EVERYONE, None), P(EVERYONE, None, None), P()),
        out_specs=(P(EVERYONE, None, None), P("groups", None), P("groups", None)),
        check_vma=False,
    )
```

time: 61.4 us -> 55.1 us (0.90)
  local copies, waits for them, and re-layouts: 5.48 us -> 0.01 us
  blocking collectives: 30.1 us -> 26.9 us
  Pallas kernels: 13.9 us -> 15.9 us
    unnamed x10 -> x0, local copies, waits for them, and re-layouts: 5.47 us -> none
    all_to_all x2, blocking collectives: 30.1 us -> 26.9 us  [swap(): return lax.all_to_all(pieces, axes, 0, 0, tiled=True)]
    pallas_call x3, Pallas kernels: 6.64 us -> 9.29 us  [the longest x1 4.5 us: merge(): pl.pallas_call(functools.partial(merge_kernel, steps), in_specs=[HBM, HBM...]
    pallas_call x1, Pallas kernels: 7.3 us -> 6.61 us  [sweeps(): pl.pallas_call(sweep_kernel, out_shape=[jax.ShapeDtypeStruct((rank, width...]
    ppermute x0 -> x3, starting transfers between devices: none -> 0.66 us  [across(): return lax.ppermute(value, 'pair', [(0, 1), (1, 0)])]
  transfers between devices with their start and end apart: 1 -> 4, of which waited for: 1 -> 1; matrix products, arithmetic and copies ran while one was open for 0% -> 0% of each run, Pallas kernels for 12% -> 12%
where the time goes in v5:
time: 55.1 us; the launch traced here: 54.7 us
  blocking collectives  26.9 us (49%)
  Pallas kernels  15.9 us (29%)
  waiting for transfers between devices  7.21 us (13%)
  starting transfers between devices  4.03 us (7%)
  between operations  0.69 us (1%)
    all_to_all x2, blocking collectives, swap(): return lax.all_to_all(pieces, axes, 0, 0, tiled=True)  26.9 us
    all_to_all x1, waiting for transfers between devices, swap(): return lax.all_to_all(pieces, axes, 0, 0, tiled=True)  7.2 us
    pallas_call x1, Pallas kernels, sweeps(): pl.pallas_call(sweep_kernel, out_shape=[jax.ShapeDtypeStruct((rank, width...  6.61 us
    pallas_call x1, Pallas kernels, merge(): pl.pallas_call(functools.partial(merge_kernel, steps), in_specs=[HBM, HBM...  4.5 us
    all_to_all x1, starting transfers between devices, swap(): return lax.all_to_all(pieces, axes, 0, 0, tiled=True)  3.37 us
    pallas_call x1, Pallas kernels, product_copies(): pl.pallas_call(product_kernel, out_shape=jax.ShapeDtypeStruct((chips, hal...  2.68 us
    pallas_call x1, Pallas kernels, error_of(): pl.pallas_call(functools.partial(error_kernel, workers, steps), in_specs=...  2.11 us
  transfers between devices with their start and end apart: 4, of which 1 were waited for; matrix products, arithmetic and copies ran while one was open for 0% of the time, Pallas kernels for 12%

profile of v5, /device:TPU:0, one launch (start us, length us, event | category | flops | bytes accessed | tf_op | source)
XLA Modules:
  0.0 54.7 jit_solution(2747711651600551329)
XLA Ops:
  0.6 4.5 %merge.1 = (f32[2048,256]{1,0:T(8,128)S(1)}, f32[16,16,256]{2,1,0:T(8,128)S(1)}) custom-call(bf16[512,2048]{1,0:T(8,128)(2,1)} %x_hbm.1, bf16[512,256]{1,0:T(8,128)(2,1)} %c_hbm.1, bf16[1,2048,256]{2,1,0:T(8,128)(2,1)} %e_hbm.1, f32[32,256]{1,0:T(8,128)} %seed_hbm.1), custom_call_target="tpu_custom_call" | custom-call | flops 536870912 | bytes 5242880 | tf_op jit(solution)/shard_map/merge/pallas_call | solution.py:98
  5.1 0.5 collective-permute-start.1
  5.7 16.9 %all_to_all.15 = f32[16,16,256]{2,1,0:T(8,128)S(1)} all-to-all(f32[16,16,256]{2,1,0:T(8,128)S(1)} %get-tuple-element.8), channel_id=1, replica_groups=mesh['groups'=2,'dp'=4,'sub'=2,'pair'=2] {'dp','sub','pair'}, dimensions={0} | all-to-all | bytes 524288 | tf_op jit(solution)/shard_map/all_to_all | solution.py:30
  22.6 10.0 %all_to_all.16.mine_ref.pieces_ref = f32[8,16,256]{2,1,0:T(8,128)S(1)} all-to-all(f32[8,16,256]{2,1,0:T(8,128)S(1)} %broadcast_in_dim.2), channel_id=1, replica_groups=mesh['groups'=2,'dp'=4,'sub'=2,'pair'=2] {'dp','sub'}, dimensions={0} | all-to-all | bytes 262144 | tf_op jit(solution)/shard_map/all_to_all | solution.py:30
  32.6 0.0 collective-permute-done.1.other_ref
  32.6 2.7 %product.1 = f32[8,16,256]{2,1,0:T(8,128)} custom-call(f32[8,16,256]{2,1,0:T(8,128)S(1)} %all_to_all.16.mine_ref.pieces_ref, f32[2048,256]{1,0:T(8,128)S(1)} %get-tuple-element.7.mine_ref.merged_ref, f32[2048,256]{1,0:T(8,128)} %collective-permute-done.1.other_ref), custom_call_target="tpu_custom_call" | custom-call | flops 16777216 | bytes 4194304 | tf_op jit(solution)/shard_map/product/pallas_call | solution.py:139
  35.3 3.4 %all-to-all-start.2 = ((f32[8,16,256]{2,1,0:T(8,128)}), f32[8,16,256]{2,1,0:T(8,128)S(1)}, u32[]{:S(2)}, u32[]{:S(2)}) async-start(f32[8,16,256]{2,1,0:T(8,128)} %product.1), calls=%async_computation.2 | async-start | bytes 262144 | tf_op jit(solution)/shard_map/all_to_all | solution.py:30
  38.6 0.1 collective-permute-start
  38.7 7.2 %all-to-all-done.2 = f32[8,16,256]{2,1,0:T(8,128)S(1)} async-done(((f32[8,16,256]{2,1,0:T(8,128)}), f32[8,16,256]{2,1,0:T(8,128)S(1)}, u32[]{:S(2)}, u32[]{:S(2)}) %all-to-all-start.2) | async-done | bytes 131104 | tf_op jit(solution)/shard_map/all_to_all | solution.py:30
  45.9 0.1 collective-permute-start.2
  46.0 0.0 collective-permute-done.other_ref
  46.0 6.6 %sweeps.1 = (f32[32,2048]{1,0:T(8,128)S(1)}, f32[32,32]{1,0:T(8,128)S(1)}) custom-call(f32[8,16,256]{2,1,0:T(8,128)S(1)} %all_to_all.16.mine_ref.pieces_ref, f32[8,16,256]{2,1,0:T(8,128)S(1)} %collective-permute-done.other_ref), custom_call_target="tpu_custom_call" | custom-call | flops 10000000000 | bytes 10000000 | tf_op jit(solution)/shard_map/sweeps/pallas_call | solution.py:202
  52.6 0.0 collective-permute-done.2.other_ref
  52.6 2.1 %error_next.1 = (bf16[1,2048,256]{2,1,0:T(8,128)(2,1)}, f32[32,2048]{1,0:T(8,128)}, f32[32,256]{1,0:T(8,128)}) custom-call(f32[2048,256]{1,0:T(8,128)S(1)} %get-tuple-element.7.mine_ref.merged_ref, f32[32,2048]{1,0:T(8,128)S(1)} %get-tuple-element.9.basis_ref, f32[32,32]{1,0:T(8,128)S(1)} %get-tuple-element.10.inverse_ref, ...), custom_call_target="tpu_custom_call" | custom-call | flops 33554432 | bytes 3145728 | tf_op jit(solution)/shard_map/error_next/pallas_call | solution.py:243
  (3 shorter events, 0.0 us)
Async XLA Ops:
  5.1 27.4 %collective-permute-start.1 = (f32[2048,256]{1,0:T(8,128)S(1)}, f32[2048,256]{1,0:T(8,128)}, u32[]{:S(2)}, u32[]{:S(2)}) collective-permute-start(f32[2048,256]{1,0:T(8,128)S(1)} %get-tuple-element.7.mine_ref.merged_ref), channel_id=1, source_target_pairs={{0,1},{1,0},{2,3},{3,2},{4,5},{5,4},{6,7},{7,6},{8,9},{9,8},{10,11... | collective-permute-start | bytes 6291464 | tf_op jit(solution)/shard_map/ppermute | solution.py:34
  35.3 10.7 %all-to-all-start.2 = ((f32[8,16,256]{2,1,0:T(8,128)}), f32[8,16,256]{2,1,0:T(8,128)S(1)}, u32[]{:S(2)}, u32[]{:S(2)}) async-start(f32[8,16,256]{2,1,0:T(8,128)} %product.1), calls=%async_computation.2 | async-start | bytes 262144 | tf_op jit(solution)/shard_map/all_to_all | solution.py:30
  38.6 7.4 %collective-permute-start = (f32[8,16,256]{2,1,0:T(8,128)S(1)}, f32[8,16,256]{2,1,0:T(8,128)S(1)}, u32[]{:S(2)}, u32[]{:S(2)}) collective-permute-start(f32[8,16,256]{2,1,0:T(8,128)S(1)} %all_to_all.16.mine_ref.pieces_ref), channel_id=1, source_target_pairs={{0,1},{1,0},{2,3},{3,2},{4,5},{5,4},{6,7},{7,6},{8,9},{9,8},{10,11... | collective-permute-start | bytes 393224 | tf_op jit(solution)/shard_map/ppermute | solution.py:34
  45.9 6.7 %collective-permute-start.2 = (f32[16,256]{1,0:T(8,128)S(1)}, f32[16,256]{1,0:T(8,128)S(1)}, u32[]{:S(2)}, u32[]{:S(2)}) collective-permute-start(f32[16,256]{1,0:T(8,128)S(1)} %reduce_sum.19.mine_ref), channel_id=1, source_target_pairs={{0,1},{1,0},{2,3},{3,2},{4,5},{5,4},{6,7},{7,6},{8,9},{9,8},{10,11... | collective-permute-start | bytes 49160 | tf_op jit(solution)/shard_map/ppermute | solution.py:34

commit v6 on v5

--- a/solution.py
+++ b/solution.py
@@ -10,6 +10,8 @@
 AXES = ("dp", "sub", "pair")
 EVERYONE = ("groups",) + AXES
 VMEM_BYTES = 24 * 1024 * 1024
+CHUNK = 256
+GROUP = 4
 BF16, F32 = jnp.bfloat16, jnp.float32
 HBM = pl.BlockSpec(memory_space=pltpu.HBM)
 VMEM = pl.BlockSpec(memory_space=pltpu.VMEM)
@@ -55,81 +57,124 @@
     return pl.CostEstimate(flops=flops, bytes_accessed=nbytes, transcendentals=0)
 
 
-def merge_kernel(steps, x_hbm, c_hbm, e_hbm, seed_hbm, merged_ref, pieces_ref,
-                 x_ref, c_ref, e_ref, seed_ref, x_sem, e_sem, small_sem):
-    width, out = merged_ref.shape
-    block = width // steps
-    copies = [
-        pltpu.make_async_copy(c_hbm, c_ref, small_sem.at[0]),
-        pltpu.make_async_copy(seed_hbm, seed_ref, small_sem.at[1]),
+def split_copies(x_hbm, e_hbm, x_ref, e_ref, x_sem, e_sem, block):
+    copies = []
+    for i in range(x_hbm.shape[1] // block):
+        part = pl.ds(i * block, block)
+        copies.append((
+            pltpu.make_async_copy(x_hbm.at[:, part], x_ref.at[:, part], x_sem.at[i]),
+            pltpu.make_async_copy(e_hbm.at[0, part, :], e_ref.at[part, :], e_sem.at[i]),
+        ))
+    return copies
+
+
+def term_kernel(block, x_hbm, c_hbm, e_hbm, seed_hbm, pieces_ref,
+                x_ref, c_ref, e_ref, seed_ref, x_sem, e_sem, small_sem):
+    small = [
+        pltpu.make_async_copy(seed_hbm, seed_ref, small_sem.at[0]),
+        pltpu.make_async_copy(c_hbm, c_ref, small_sem.at[1]),
     ]
-    for i in range(steps):
-        part = pl.ds(i * block, block)
-        copies.append(pltpu.make_async_copy(x_hbm.at[:, part], x_ref.at[:, part], x_sem.at[i]))
-        copies.append(pltpu.make_async_copy(e_hbm.at[0, part, :], e_ref.at[part, :], e_sem.at[i]))
-    for copy in copies:
+    copies = split_copies(x_hbm, e_hbm, x_ref, e_ref, x_sem, e_sem, block)
+    for copy in small + [copy for pair in copies for copy in pair]:
         copy.start()
-    copies[0].wait()
-    copies[1].wait()
+    small[0].wait()
+    small[1].wait()
     rank = seed_ref.shape[0]
     half, piece = pieces_ref.shape[1:]
-    s_high, s_low = parts_of(seed_ref[...], 2)
-    s_both = jnp.concatenate([s_high, s_low], axis=0)
-    for i in range(steps):
-        copies[2 + 2 * i].wait()
-        copies[3 + 2 * i].wait()
+    seed = jnp.concatenate(parts_of(seed_ref[...], 3), axis=0)
+    mixed = added(dot(seed, c_ref[...], ((1,), (1,))), rank)
+    mixed = jnp.concatenate(parts_of(mixed, 3), axis=0)
+    for i, pair in enumerate(copies):
         part = pl.ds(i * block, block)
-        merged = dot(x_ref[:, part], c_ref[...], ((0,), (0,))) + e_ref[part, :].astype(F32)
-        merged_ref[part, :] = merged
-        m_high, m_low = parts_of(merged, 2)
-        both = dot(s_both, m_high, ((1,), (1,)))
-        term = both[:rank] + both[rank:] + dot(s_high, m_low, ((1,), (1,)))
+        pair[0].wait()
+        pair[1].wait()
+        term = added(dot(mixed, x_ref[:, part], ((1,), (0,)))
+                     + dot(seed, e_ref[part, :], ((1,), (1,))), rank)
         for j in range(block // piece):
             for k in range(rank // half):
                 pieces_ref[(i * (block // piece) + j) * (rank // half) + k] = (
                     term[k * half:(k + 1) * half, j * piece:(j + 1) * piece])
 
 
-def merge(inputs, cotangent, error_prev, seed_q, chips):
+def added(stack, rank):
+    total = stack[stack.shape[0] - rank:]
+    for i in range(stack.shape[0] // rank - 2, -1, -1):
+        total = total + stack[i * rank:(i + 1) * rank]
+    return total
+
+
+def term_pieces(inputs, cotangent, error_prev, seed_q, chips):
     tokens, width = inputs.shape
     out = cotangent.shape[1]
     rank = seed_q.shape[0]
-    steps = 4
-    return pl.pallas_call(
-        functools.partial(merge_kernel, steps),
-        in_specs=[HBM, HBM, HBM, HBM],
-        out_specs=[VMEM, VMEM],
-        out_shape=[
-            jax.ShapeDtypeStruct((width, out), F32),
-            jax.ShapeDtypeStruct((2 * chips, rank // 2, width // chips), F32),
-        ],
+    block = max(CHUNK, width // chips)
+    return pl.pallas_call(
+        functools.partial(term_kernel, block),
+        in_specs=[HBM] * 4,
+        out_specs=VMEM,
+        out_shape=jax.ShapeDtypeStruct((2 * chips, rank // 2, width // chips), F32),
         scratch_shapes=[
             pltpu.VMEM((tokens, width), BF16),
             pltpu.VMEM((tokens, out), BF16),
             pltpu.VMEM((width, out), BF16),
             pltpu.VMEM((rank, out), F32),
-            pltpu.SemaphoreType.DMA((steps,)),
-            pltpu.SemaphoreType.DMA((steps,)),
+            pltpu.SemaphoreType.DMA((width // block,)),
+            pltpu.SemaphoreType.DMA((width // block,)),
             pltpu.SemaphoreType.DMA((2,)),
         ],
         compiler_params=params(),
-        cost_estimate=cost(2 * tokens * width * out, 6 * width * out + 2 * tokens * width),
+        cost_estimate=cost(6 * tokens * rank * width, 2 * tokens * width + 2 * width * out),
+        name="term",
+    )(inputs, cotangent, error_prev, seed_q)
+
+
+def merge_kernel(x_hbm, c_hbm, e_hbm, merged_ref, x_ref, c_ref, e_ref, x_sem, e_sem, c_sem):
+    small = pltpu.make_async_copy(c_hbm, c_ref, c_sem)
+    copies = split_copies(x_hbm, e_hbm, x_ref, e_ref, x_sem, e_sem, CHUNK)
+    for copy in [small] + [copy for pair in copies for copy in pair]:
+        copy.start()
+    small.wait()
+    for i, pair in enumerate(copies):
+        part = pl.ds(i * CHUNK, CHUNK)
+        pair[0].wait()
+        pair[1].wait()
+        merged_ref[part, :] = (
+            dot(x_ref[:, part], c_ref[...], ((0,), (0,))) + e_ref[part, :].astype(F32))
+
+
+def merge(inputs, cotangent, error_prev):
+    tokens, width = inputs.shape
+    out = cotangent.shape[1]
+    return pl.pallas_call(
+        merge_kernel,
+        in_specs=[HBM] * 3,
+        out_specs=VMEM,
+        out_shape=jax.ShapeDtypeStruct((width, out), F32),
+        scratch_shapes=[
+            pltpu.VMEM((tokens, width), BF16),
+            pltpu.VMEM((tokens, out), BF16),
+            pltpu.VMEM((width, out), BF16),
+            pltpu.SemaphoreType.DMA((width // CHUNK,)),
+            pltpu.SemaphoreType.DMA((width // CHUNK,)),
+            pltpu.SemaphoreType.DMA,
+        ],
+        compiler_params=params(),
+        cost_estimate=cost(10 ** 9, 10 ** 7),
         name="merge",
-    )(inputs, cotangent, error_prev, seed_q)
-
-
-def rows_of(pieces_ref):
-    return jnp.concatenate([pieces_ref[i] for i in range(pieces_ref.shape[0])], axis=1)
+    )(inputs, cotangent, error_prev)
 
 
 def product_kernel(pieces_ref, mine_ref, other_ref, copies_ref):
-    rows = rows_of(pieces_ref)
-    half = rows.shape[0]
-    f_high, f_low = parts_of(rows, 2)
-    m_high, m_low = parts_of(mine_ref[...] + other_ref[...], 2)
-    both = dot(jnp.concatenate([f_high, f_low], axis=0), m_high, ((1,), (0,)))
-    product = both[:half] + both[half:] + dot(f_high, m_low, ((1,), (0,)))
-    for i in range(copies_ref.shape[0]):
+    chips, half, piece = pieces_ref.shape
+    product = None
+    for i in range(chips):
+        part = pl.ds(i * piece, piece)
+        m_high, m_low = parts_of(mine_ref[part, :] + other_ref[part, :], 2)
+        f_high, f_low = parts_of(pieces_ref[i], 2)
+        both = jnp.concatenate([f_high, f_low], axis=0)
+        term = added(dot(both, m_high, ((1,), (0,))), half) + dot(f_high, m_low, ((1,), (0,)))
+        product = term if product is None else product + term
+    for i in range(chips):
         copies_ref[i] = product
 
 
@@ -150,13 +195,15 @@
     return jnp.concatenate([jnp.where(low, mine, other), jnp.where(low, other, mine)], axis=0)
 
 
-def gram_of(rows):
-    rank = rows.shape[0]
+def gram_blocks(rows):
     stack = jnp.concatenate(parts_of(rows, 3), axis=0)
-    full = dot(stack, stack, ((1,), (1,)))
+    return dot(stack, stack, ((1,), (1,)))
+
+
+def gram_of(blocks, rank):
     gram = None
     for i, j in ((2, 0), (0, 2), (1, 1), (1, 0), (0, 1), (0, 0)):
-        term = full[i * rank:(i + 1) * rank, j * rank:(j + 1) * rank]
+        term = blocks[i * rank:(i + 1) * rank, j * rank:(j + 1) * rank]
         gram = term if gram is None else gram + term
     return gram
 
@@ -167,14 +214,21 @@
     lane = lax.broadcasted_iota(jnp.int32, (rank, rank), 1)
     eye = jnp.where(row == lane, 1.0, 0.0).astype(F32)
     wide = jnp.concatenate([gram, eye], axis=1)
-    index = lax.broadcasted_iota(jnp.int32, (rank, 1), 0)
-    for k in range(rank - 1):
-        pivot = wide[k:k + 1, :]
-        scale = 1.0 / wide[k:k + 1, k:k + 1]
-        factor = jnp.where(index > k, wide[:, k:k + 1] * scale, 0.0)
-        wide = wide - factor * pivot
-    diagonal = jnp.sum(jnp.where(row == lane, wide[:, :rank], 0.0), axis=1, keepdims=True)
-    return wide[:, rank:] * lax.rsqrt(diagonal)
+    index = lax.broadcasted_iota(jnp.int32, wide.shape, 0)
+    scale = jnp.ones_like(wide)
+    for base in range(0, rank, GROUP):
+        columns = [
+            jnp.broadcast_to(wide[:, k:k + 1], wide.shape) for k in range(base, base + GROUP)
+        ]
+        for j in range(GROUP):
+            k = base + j
+            pivot = columns[j][k:k + 1, :]
+            factor = jnp.where(index > k, columns[j] * (1.0 / pivot), 0.0)
+            for i in range(j + 1, GROUP):
+                columns[i] = columns[i] - factor * columns[i][k:k + 1, :]
+            wide = wide - factor * wide[k:k + 1, :]
+            scale = jnp.where(index == k, lax.rsqrt(pivot), scale)
+    return (wide * scale)[:, rank:]
 
 
 def short_dot(left, right):
@@ -186,14 +240,26 @@
 
 
 def sweep_kernel(mine_ref, other_ref, basis_ref, inverse_ref):
-    rows = both_halves(rows_of(mine_ref), rows_of(other_ref))
-    inverse = None
-    for sweep in range(2):
-        step = inverse_factor(gram_of(rows))
-        rows = short_dot(step, rows)
-        inverse = step if inverse is None else short_dot(step, inverse)
-    basis_ref[...] = rows
-    inverse_ref[...] = inverse
+    chips, half, piece = mine_ref.shape
+    rank = 2 * half
+    blocks = None
+    for i in range(chips):
+        rows = both_halves(mine_ref[i], other_ref[i])
+        basis_ref[:, i * piece:(i + 1) * piece] = rows
+        term = gram_blocks(rows)
+        blocks = term if blocks is None else blocks + term
+    step = inverse_factor(gram_of(blocks, rank))
+    blocks = None
+    for i in range(chips):
+        rows = short_dot(step, basis_ref[:, i * piece:(i + 1) * piece])
+        basis_ref[:, i * piece:(i + 1) * piece] = rows
+        term = gram_blocks(rows)
+        blocks = term if blocks is None else blocks + term
+    last = inverse_factor(gram_of(blocks, rank))
+    for i in range(chips):
+        part = slice(i * piece, (i + 1) * piece)
+        basis_ref[:, part] = short_dot(last, basis_ref[:, part])
+    inverse_ref[...] = short_dot(last, step)
 
 
 def sweeps(mine, other):
@@ -239,7 +305,7 @@
 def error_of(merged, basis, inverse, mine, other, workers):
     width, out = merged.shape
     rank = basis.shape[0]
-    steps = 4
+    steps = width // CHUNK
     return pl.pallas_call(
         functools.partial(error_kernel, workers, steps),
         in_specs=[VMEM] * 5,
@@ -260,11 +326,11 @@
     )(merged, basis, inverse, mine, other)
 
 
-def local(chips, rest, count, workers, inputs, cotangent, error_prev, seed_q):
+def local(chips, rest, count, workers, *arguments):
     inputs, cotangent, error_prev, seed_q = (
-        pltpu.with_memory_space_constraint(value, pltpu.HBM)
-        for value in (inputs, cotangent, error_prev, seed_q))
-    merged, pieces = merge(inputs, cotangent, error_prev, seed_q, count)
+        pltpu.with_memory_space_constraint(value, pltpu.HBM) for value in arguments)
+    pieces = term_pieces(inputs, cotangent, error_prev, seed_q, count)
+    merged = merge(inputs, cotangent, error_prev)
     merged_other = across(merged)
     if rest:
         pieces = lax.psum(pieces, rest)
@@ -274,9 +340,10 @@
     copies = product_copies(half, merged, merged_other)
     if rest:
         copies = lax.psum(copies, rest)
+    basis, inverse = sweeps(half, half_other)
     product = jnp.sum(swap(copies, chips), axis=0)
+    product, basis, inverse = lax.optimization_barrier((product, basis, inverse))
     product_other = across(product)
-    basis, inverse = sweeps(half, half_other)
     error_next, basis, second = error_of(merged, basis, inverse, product, product_other, workers)
     return (error_next, basis, second)
 

time: 55.1 us -> 54.7 us (level)
  waiting for transfers between devices: 7.21 us -> 4.9 us
  Pallas kernels: 15.9 us -> 17.9 us
    pallas_call x1 -> x2, Pallas kernels: 4.5 us -> 8.96 us  [the longest x1 4.48 us: merge(): pl.pallas_call(merge_kernel, in_specs=[HBM] * 3, out_specs=VMEM, out_shap...]
    all_to_all x1, waiting for transfers between devices: 7.2 us -> 3.73 us  [swap(): return lax.all_to_all(pieces, axes, 0, 0, tiled=True)]
    pallas_call x1, Pallas kernels: 6.61 us -> 4.13 us  [sweeps(): pl.pallas_call(sweep_kernel, out_shape=[jax.ShapeDtypeStruct((rank, width...]
    ppermute x3, waiting for transfers between devices: 0.01 us -> 1.18 us  [across(): return lax.ppermute(value, 'pair', [(0, 1), (1, 0)])]
  transfers between devices with their start and end apart: 4 -> 4, of which waited for: 1 -> 2; matrix products, arithmetic and copies ran while one was open for 0% -> 0% of each run, Pallas kernels for 12% -> 21%
where the time goes in v6:
time: 54.7 us; the launch traced here: 54.4 us
  blocking collectives  26.9 us (49%)
  Pallas kernels  17.9 us (33%)
  waiting for transfers between devices  4.9 us (9%)
  starting transfers between devices  3.96 us (7%)
  between operations  0.69 us (1%)
    all_to_all x2, blocking collectives, swap(): return lax.all_to_all(pieces, axes, 0, 0, tiled=True)  26.9 us
    pallas_call x1, Pallas kernels, merge(): pl.pallas_call(merge_kernel, in_specs=[HBM] * 3, out_specs=VMEM, out_shap...  4.48 us
    pallas_call x1, Pallas kernels, term_pieces(): pl.pallas_call(functools.partial(term_kernel, block), in_specs=[HBM] * 4,...  4.48 us
    pallas_call x1, Pallas kernels, sweeps(): pl.pallas_call(sweep_kernel, out_shape=[jax.ShapeDtypeStruct((rank, width...  4.13 us
    all_to_all x1, waiting for transfers between devices, swap(): return lax.all_to_all(pieces, axes, 0, 0, tiled=True)  3.73 us
    all_to_all x1, starting transfers between devices, swap(): return lax.all_to_all(pieces, axes, 0, 0, tiled=True)  3.37 us
    pallas_call x1, Pallas kernels, product_copies(): pl.pallas_call(product_kernel, out_shape=jax.ShapeDtypeStruct((chips, hal...  2.76 us
    pallas_call x1, Pallas kernels, error_of(): pl.pallas_call(functools.partial(error_kernel, workers, steps), in_specs=...  2.05 us
  transfers between devices with their start and end apart: 4, of which 2 were waited for; matrix products, arithmetic and copies ran while one was open for 0% of the time, Pallas kernels for 21%

profile of v6, /device:TPU:0, one launch (start us, length us, event | category | flops | bytes accessed | tf_op | source)
XLA Modules:
  0.0 54.4 jit_solution(10513507829336881508)
XLA Ops:
  0.6 4.5 %merge.1.mine_ref.merged_ref = f32[2048,256]{1,0:T(8,128)S(1)} custom-call(bf16[512,2048]{1,0:T(8,128)(2,1)} %x_hbm.3, bf16[512,256]{1,0:T(8,128)(2,1)} %c_hbm.3, bf16[1,2048,256]{2,1,0:T(8,128)(2,1)} %e_hbm.3), custom_call_target="tpu_custom_call" | custom-call | flops 1000000000 | bytes 10000000 | tf_op jit(solution)/shard_map/merge/pallas_call | solution.py:148
  5.1 0.5 collective-permute-start
  5.6 4.5 %term.1 = f32[16,16,256]{2,1,0:T(8,128)S(1)} custom-call(bf16[512,2048]{1,0:T(8,128)(2,1)} %x_hbm.3, bf16[512,256]{1,0:T(8,128)(2,1)} %c_hbm.3, bf16[1,2048,256]{2,1,0:T(8,128)(2,1)} %e_hbm.3, f32[32,256]{1,0:T(8,128)} %seed_hbm.1), custom_call_target="tpu_custom_call" | custom-call | flops 201326592 | bytes 3145728 | tf_op jit(solution)/shard_map/term/pallas_call | solution.py:111
  10.1 16.9 %all_to_all.15 = f32[16,16,256]{2,1,0:T(8,128)S(1)} all-to-all(f32[16,16,256]{2,1,0:T(8,128)S(1)} %term.1), channel_id=1, replica_groups=mesh['groups'=2,'dp'=4,'sub'=2,'pair'=2] {'dp','sub','pair'}, dimensions={0} | all-to-all | bytes 524288 | tf_op jit(solution)/shard_map/all_to_all | solution.py:32
  27.0 10.0 %all_to_all.16.pieces_ref.mine_ref = f32[8,16,256]{2,1,0:T(8,128)S(1)} all-to-all(f32[8,16,256]{2,1,0:T(8,128)S(1)} %broadcast_in_dim.2), channel_id=1, replica_groups=mesh['groups'=2,'dp'=4,'sub'=2,'pair'=2] {'dp','sub'}, dimensions={0} | all-to-all | bytes 262144 | tf_op jit(solution)/shard_map/all_to_all | solution.py:32
  37.0 0.0 collective-permute-start.1
  37.0 0.0 collective-permute-done.other_ref
  37.1 2.8 %product.1 = f32[8,16,256]{2,1,0:T(8,128)} custom-call(f32[8,16,256]{2,1,0:T(8,128)S(1)} %all_to_all.16.pieces_ref.mine_ref, f32[2048,256]{1,0:T(8,128)S(1)} %merge.1.mine_ref.merged_ref, f32[2048,256]{1,0:T(8,128)} %collective-permute-done.other_ref), custom_call_target="tpu_custom_call" | custom-call | flops 16777216 | bytes 4194304 | tf_op jit(solution)/shard_map/product/pallas_call | solution.py:184
  39.8 3.4 %all-to-all-start.2 = ((f32[8,16,256]{2,1,0:T(8,128)}), f32[8,16,256]{2,1,0:T(8,128)S(1)}, u32[]{:S(2)}, u32[]{:S(2)}) async-start(f32[8,16,256]{2,1,0:T(8,128)} %product.1), calls=%async_computation.2 | async-start | bytes 262144 | tf_op jit(solution)/shard_map/all_to_all | solution.py:32
  43.2 0.0 collective-permute-done.1.other_ref
  43.2 4.1 %sweeps.1 = (f32[32,2048]{1,0:T(8,128)S(1)}, f32[32,32]{1,0:T(8,128)S(1)}) custom-call(f32[8,16,256]{2,1,0:T(8,128)S(1)} %all_to_all.16.pieces_ref.mine_ref, f32[8,16,256]{2,1,0:T(8,128)S(1)} %collective-permute-done.1.other_ref), custom_call_target="tpu_custom_call" | custom-call | flops 10000000000 | bytes 10000000 | tf_op jit(solution)/shard_map/sweeps/pallas_call | solution.py:268
  47.3 3.7 %all-to-all-done.2 = f32[8,16,256]{2,1,0:T(8,128)S(1)} async-done(((f32[8,16,256]{2,1,0:T(8,128)}), f32[8,16,256]{2,1,0:T(8,128)S(1)}, u32[]{:S(2)}, u32[]{:S(2)}) %all-to-all-start.2) | async-done | bytes 131104 | tf_op jit(solution)/shard_map/all_to_all | solution.py:32
  51.1 0.1 collective-permute-start.2
  51.2 1.2 %collective-permute-done.2.other_ref = f32[16,256]{1,0:T(8,128)S(1)} collective-permute-done((f32[16,256]{1,0:T(8,128)S(1)}, f32[16,256]{1,0:T(8,128)S(1)}, u32[]{:S(2)}, u32[]{:S(2)}) %collective-permute-start.2) | collective-permute-done | bytes 16416 | tf_op jit(solution)/shard_map/ppermute | solution.py:36
  52.3 2.0 %error_next.1 = (bf16[1,2048,256]{2,1,0:T(8,128)(2,1)}, f32[32,2048]{1,0:T(8,128)}, f32[32,256]{1,0:T(8,128)}) custom-call(f32[2048,256]{1,0:T(8,128)S(1)} %merge.1.mine_ref.merged_ref, f32[32,2048]{1,0:T(8,128)S(1)} %get-tuple-element.10.basis_ref, f32[32,32]{1,0:T(8,128)S(1)} %get-tuple-element.11.inverse_ref, f32[16,256]{1,0:T(8,128)S(1)} %reduce_sum.19.mine_ref, ...), custom_call_target="tpu_custom_call" | custom-call | flops 33554432 | bytes 3145728 | tf_op jit(solution)/shard_map/error_next/pallas_call | solution.py:309
  (3 shorter events, 0.0 us)
Async XLA Ops:
  5.1 31.9 %collective-permute-start = (f32[2048,256]{1,0:T(8,128)S(1)}, f32[2048,256]{1,0:T(8,128)}, u32[]{:S(2)}, u32[]{:S(2)}) collective-permute-start(f32[2048,256]{1,0:T(8,128)S(1)} %merge.1.mine_ref.merged_ref), channel_id=1, source_target_pairs={{0,1},{1,0},{2,3},{3,2},{4,5},{5,4},{6,7},{7,6},{8,9},{9,8},{10,11... | collective-permute-start | bytes 6291464 | tf_op jit(solution)/shard_map/ppermute | solution.py:36
  37.0 6.2 %collective-permute-start.1 = (f32[8,16,256]{2,1,0:T(8,128)S(1)}, f32[8,16,256]{2,1,0:T(8,128)S(1)}, u32[]{:S(2)}, u32[]{:S(2)}) collective-permute-start(f32[8,16,256]{2,1,0:T(8,128)S(1)} %all_to_all.16.pieces_ref.mine_ref), channel_id=1, source_target_pairs={{0,1},{1,0},{2,3},{3,2},{4,5},{5,4},{6,7},{7,6},{8,9},{9,8},{10,11... | collective-permute-start | bytes 393224 | tf_op jit(solution)/shard_map/ppermute | solution.py:36
  39.8 11.2 %all-to-all-start.2 = ((f32[8,16,256]{2,1,0:T(8,128)}), f32[8,16,256]{2,1,0:T(8,128)S(1)}, u32[]{:S(2)}, u32[]{:S(2)}) async-start(f32[8,16,256]{2,1,0:T(8,128)} %product.1), calls=%async_computation.2 | async-start | bytes 262144 | tf_op jit(solution)/shard_map/all_to_all | solution.py:32
  51.1 1.2 %collective-permute-start.2 = (f32[16,256]{1,0:T(8,128)S(1)}, f32[16,256]{1,0:T(8,128)S(1)}, u32[]{:S(2)}, u32[]{:S(2)}) collective-permute-start(f32[16,256]{1,0:T(8,128)S(1)} %reduce_sum.19.mine_ref), channel_id=1, source_target_pairs={{0,1},{1,0},{2,3},{3,2},{4,5},{5,4},{6,7},{7,6},{8,9},{9,8},{10,11... | collective-permute-start | bytes 49160 | tf_op jit(solution)/shard_map/ppermute | solution.py:36

commit v7 on v6

--- a/solution.py
+++ b/solution.py
@@ -14,6 +14,7 @@
 GROUP = 4
 BF16, F32 = jnp.bfloat16, jnp.float32
 HBM = pl.BlockSpec(memory_space=pltpu.HBM)
+ANY = pl.BlockSpec(memory_space=pl.ANY)
 VMEM = pl.BlockSpec(memory_space=pltpu.VMEM)
 
 
@@ -25,7 +26,7 @@
             count *= mesh.shape[axis]
     chips = tuple(chips)
     rest = tuple(axis for axis in AXES if axis not in chips + ("pair",))
-    return chips, rest, count // mesh.shape["pair"]
+    return chips, rest, tuple(mesh.shape[axis] for axis in chips)
 
 
 def swap(pieces, axes):
@@ -57,43 +58,48 @@
     return pl.CostEstimate(flops=flops, bytes_accessed=nbytes, transcendentals=0)
 
 
-def split_copies(x_hbm, e_hbm, x_ref, e_ref, x_sem, e_sem, block):
-    copies = []
-    for i in range(x_hbm.shape[1] // block):
-        part = pl.ds(i * block, block)
-        copies.append((
-            pltpu.make_async_copy(x_hbm.at[:, part], x_ref.at[:, part], x_sem.at[i]),
-            pltpu.make_async_copy(e_hbm.at[0, part, :], e_ref.at[part, :], e_sem.at[i]),
-        ))
-    return copies
-
-
-def term_kernel(block, x_hbm, c_hbm, e_hbm, seed_hbm, pieces_ref,
-                x_ref, c_ref, e_ref, seed_ref, x_sem, e_sem, small_sem):
-    small = [
-        pltpu.make_async_copy(seed_hbm, seed_ref, small_sem.at[0]),
-        pltpu.make_async_copy(c_hbm, c_ref, small_sem.at[1]),
-    ]
-    copies = split_copies(x_hbm, e_hbm, x_ref, e_ref, x_sem, e_sem, block)
-    for copy in small + [copy for pair in copies for copy in pair]:
+def whole_copies(pairs, sems):
+    return [pltpu.make_async_copy(pair[0], pair[1], sems.at[i]) for i, pair in enumerate(pairs)]
+
+
+def row_parts(source, target, parts):
+    block = target.shape[0] // parts
+    rows = [pl.ds(i * block, block) for i in range(parts)]
+    return [(source.at[part, :], target.at[part, :]) for part in rows]
+
+
+def term_kernel(x_hbm, c_hbm, e_hbm, seed_hbm, pieces_ref,
+                x_ref, c_ref, e_ref, seed_ref, term_ref, sems):
+    copies = whole_copies(
+        [(seed_hbm, seed_ref), (c_hbm, c_ref)] + row_parts(e_hbm.at[0], e_ref, 2)
+        + row_parts(x_hbm, x_ref, 2), sems)
+    for copy in copies:
         copy.start()
-    small[0].wait()
-    small[1].wait()
     rank = seed_ref.shape[0]
+    tokens, width = x_ref.shape
     half, piece = pieces_ref.shape[1:]
+    copies[0].wait()
+    copies[1].wait()
     seed = jnp.concatenate(parts_of(seed_ref[...], 3), axis=0)
     mixed = added(dot(seed, c_ref[...], ((1,), (1,))), rank)
     mixed = jnp.concatenate(parts_of(mixed, 3), axis=0)
-    for i, pair in enumerate(copies):
-        part = pl.ds(i * block, block)
-        pair[0].wait()
-        pair[1].wait()
-        term = added(dot(mixed, x_ref[:, part], ((1,), (0,)))
-                     + dot(seed, e_ref[part, :], ((1,), (1,))), rank)
-        for j in range(block // piece):
-            for k in range(rank // half):
-                pieces_ref[(i * (block // piece) + j) * (rank // half) + k] = (
-                    term[k * half:(k + 1) * half, j * piece:(j + 1) * piece])
+    blocks = width // CHUNK
+    for i in range(blocks):
+        if i % (blocks // 2) == 0:
+            copies[2 + i // (blocks // 2)].wait()
+        part = pl.ds(i * CHUNK, CHUNK)
+        term_ref[:, part] = added(dot(seed, e_ref[part, :], ((1,), (1,))), rank)
+    for t in range(2):
+        copies[4 + t].wait()
+        own = mixed[:, t * (tokens // 2):(t + 1) * (tokens // 2)]
+        rows = pl.ds(t * (tokens // 2), tokens // 2)
+        for i in range(blocks):
+            part = pl.ds(i * CHUNK, CHUNK)
+            term_ref[:, part] += added(dot(own, x_ref[rows, part], ((1,), (0,))), rank)
+    for j in range(width // piece):
+        for k in range(rank // half):
+            pieces_ref[j * (rank // half) + k] = (
+                term_ref[k * half:(k + 1) * half, j * piece:(j + 1) * piece])
 
 
 def added(stack, rank):
@@ -107,9 +113,8 @@
     tokens, width = inputs.shape
     out = cotangent.shape[1]
     rank = seed_q.shape[0]
-    block = max(CHUNK, width // chips)
     return pl.pallas_call(
-        functools.partial(term_kernel, block),
+        term_kernel,
         in_specs=[HBM] * 4,
         out_specs=VMEM,
         out_shape=jax.ShapeDtypeStruct((2 * chips, rank // 2, width // chips), F32),
@@ -118,9 +123,8 @@
             pltpu.VMEM((tokens, out), BF16),
             pltpu.VMEM((width, out), BF16),
             pltpu.VMEM((rank, out), F32),
-            pltpu.SemaphoreType.DMA((width // block,)),
-            pltpu.SemaphoreType.DMA((width // block,)),
-            pltpu.SemaphoreType.DMA((2,)),
+            pltpu.VMEM((rank, width), F32),
+            pltpu.SemaphoreType.DMA((6,)),
         ],
         compiler_params=params(),
         cost_estimate=cost(6 * tokens * rank * width, 2 * tokens * width + 2 * width * out),
@@ -128,62 +132,92 @@
     )(inputs, cotangent, error_prev, seed_q)
 
 
-def merge_kernel(x_hbm, c_hbm, e_hbm, merged_ref, x_ref, c_ref, e_ref, x_sem, e_sem, c_sem):
-    small = pltpu.make_async_copy(c_hbm, c_ref, c_sem)
-    copies = split_copies(x_hbm, e_hbm, x_ref, e_ref, x_sem, e_sem, CHUNK)
-    for copy in [small] + [copy for pair in copies for copy in pair]:
+def merge_kernel(x_hbm, c_hbm, e_hbm, after_hbm, merged_ref, x_ref, c_ref, e_ref, sems):
+    copies = whole_copies([(c_hbm, c_ref), (x_hbm, x_ref), (e_hbm.at[0], e_ref)], sems)
+    for copy in copies:
         copy.start()
-    small.wait()
-    for i, pair in enumerate(copies):
+    for copy in copies:
+        copy.wait()
+    for i in range(merged_ref.shape[0] // CHUNK):
         part = pl.ds(i * CHUNK, CHUNK)
-        pair[0].wait()
-        pair[1].wait()
         merged_ref[part, :] = (
             dot(x_ref[:, part], c_ref[...], ((0,), (0,))) + e_ref[part, :].astype(F32))
 
 
-def merge(inputs, cotangent, error_prev):
+def merge(inputs, cotangent, error_prev, after):
     tokens, width = inputs.shape
     out = cotangent.shape[1]
     return pl.pallas_call(
         merge_kernel,
-        in_specs=[HBM] * 3,
+        in_specs=[HBM] * 3 + [ANY],
         out_specs=VMEM,
         out_shape=jax.ShapeDtypeStruct((width, out), F32),
         scratch_shapes=[
             pltpu.VMEM((tokens, width), BF16),
             pltpu.VMEM((tokens, out), BF16),
             pltpu.VMEM((width, out), BF16),
-            pltpu.SemaphoreType.DMA((width // CHUNK,)),
-            pltpu.SemaphoreType.DMA((width // CHUNK,)),
-            pltpu.SemaphoreType.DMA,
+            pltpu.SemaphoreType.DMA((3,)),
         ],
         compiler_params=params(),
         cost_estimate=cost(10 ** 9, 10 ** 7),
         name="merge",
-    )(inputs, cotangent, error_prev)
-
-
-def product_kernel(pieces_ref, mine_ref, other_ref, copies_ref):
-    chips, half, piece = pieces_ref.shape
+    )(inputs, cotangent, error_prev, after)
+
+
+def gathered(block, rounds):
+    blocks = block[None]
+    for axis, size, bit, mask in rounds:
+        other = lax.ppermute(blocks, axis, [(i, i ^ bit) for i in range(size)])
+        blocks = jnp.concatenate([blocks, other], axis=0)
+    return blocks
+
+
+def masks_of(rounds):
+    masks = [0]
+    for axis, size, bit, mask in rounds:
+        masks = masks + [old ^ mask for old in masks]
+    return masks
+
+
+def chip_index(chips, sizes):
+    index = 0
+    for axis, size in zip(chips, sizes):
+        index = index * size + lax.axis_index(axis)
+    return index
+
+
+def place(chip, mask, piece):
+    return pl.ds(pl.multiple_of((chip ^ mask) * piece, piece), piece)
+
+
+def product_kernel(layout, pieces_ref, mine_ref, other_hbm, copies_ref, other_ref, sems):
+    chips, sizes, masks = layout
+    count, half, piece = pieces_ref.shape
+    chip = chip_index(chips, sizes)
+    parts = [place(chip, mask, piece) for mask in masks]
+    copies = whole_copies([(other_hbm.at[part, :], other_ref.at[part, :]) for part in parts], sems)
+    for copy in copies:
+        copy.start()
     product = None
-    for i in range(chips):
-        part = pl.ds(i * piece, piece)
-        m_high, m_low = parts_of(mine_ref[part, :] + other_ref[part, :], 2)
+    for i, part in enumerate(parts):
         f_high, f_low = parts_of(pieces_ref[i], 2)
         both = jnp.concatenate([f_high, f_low], axis=0)
+        copies[i].wait()
+        m_high, m_low = parts_of(mine_ref[part, :] + other_ref[part, :], 2)
         term = added(dot(both, m_high, ((1,), (0,))), half) + dot(f_high, m_low, ((1,), (0,)))
         product = term if product is None else product + term
-    for i in range(chips):
+    for i in range(count):
         copies_ref[i] = product
 
 
-def product_copies(pieces, mine, other):
-    chips, half, piece = pieces.shape
+def product_copies(layout, pieces, mine, other):
+    count, half, piece = pieces.shape
     width, out = mine.shape
     return pl.pallas_call(
-        product_kernel,
-        out_shape=jax.ShapeDtypeStruct((chips, half, out), F32),
+        functools.partial(product_kernel, layout),
+        in_specs=[VMEM, VMEM, ANY],
+        out_shape=jax.ShapeDtypeStruct((count, half, out), F32),
+        scratch_shapes=[pltpu.VMEM((width, out), F32), pltpu.SemaphoreType.DMA((count,))],
         compiler_params=params(),
         cost_estimate=cost(2 * half * width * out, 8 * width * out),
         name="product",
@@ -239,34 +273,37 @@
     return dot(lefts, rights, ((1,), (0,)))
 
 
-def sweep_kernel(mine_ref, other_ref, basis_ref, inverse_ref):
-    chips, half, piece = mine_ref.shape
+def sweep_kernel(layout, mine_ref, other_ref, basis_ref, inverse_ref):
+    chips, sizes, masks = layout
+    count, half, piece = mine_ref.shape
     rank = 2 * half
+    chip = chip_index(chips, sizes)
     blocks = None
-    for i in range(chips):
+    for i, mask in enumerate(masks):
         rows = both_halves(mine_ref[i], other_ref[i])
-        basis_ref[:, i * piece:(i + 1) * piece] = rows
+        basis_ref[:, place(chip, mask, piece)] = rows
         term = gram_blocks(rows)
         blocks = term if blocks is None else blocks + term
     step = inverse_factor(gram_of(blocks, rank))
     blocks = None
-    for i in range(chips):
-        rows = short_dot(step, basis_ref[:, i * piece:(i + 1) * piece])
-        basis_ref[:, i * piece:(i + 1) * piece] = rows
+    for i in range(count):
+        part = slice(i * piece, (i + 1) * piece)
+        rows = short_dot(step, basis_ref[:, part])
+        basis_ref[:, part] = rows
         term = gram_blocks(rows)
         blocks = term if blocks is None else blocks + term
     last = inverse_factor(gram_of(blocks, rank))
-    for i in range(chips):
+    for i in range(count):
         part = slice(i * piece, (i + 1) * piece)
         basis_ref[:, part] = short_dot(last, basis_ref[:, part])
     inverse_ref[...] = short_dot(last, step)
 
 
-def sweeps(mine, other):
-    chips, half, piece = mine.shape
-    rank, width = 2 * half, chips * piece
+def sweeps(layout, mine, other):
+    count, half, piece = mine.shape
+    rank, width = 2 * half, count * piece
     return pl.pallas_call(
-        sweep_kernel,
+        functools.partial(sweep_kernel, layout),
         out_shape=[
             jax.ShapeDtypeStruct((rank, width), F32),
             jax.ShapeDtypeStruct((rank, rank), F32),
@@ -326,21 +363,29 @@
     )(merged, basis, inverse, mine, other)
 
 
-def local(chips, rest, count, workers, *arguments):
+def local(chips, rest, sizes, workers, *arguments):
     inputs, cotangent, error_prev, seed_q = (
         pltpu.with_memory_space_constraint(value, pltpu.HBM) for value in arguments)
+    count, rounds, stride = 1, [], 1
+    for axis, size in zip(chips[::-1], sizes[::-1]):
+        bits = [1 << i for i in range(size.bit_length() - 1)]
+        rounds = [(axis, size, bit, bit * stride) for bit in bits[::-1]] + rounds
+        stride *= size
+    count = stride
+    layout = (chips, sizes, masks_of(rounds))
     pieces = term_pieces(inputs, cotangent, error_prev, seed_q, count)
-    merged = merge(inputs, cotangent, error_prev)
+    merged = merge(inputs, cotangent, error_prev, pieces)
     merged_other = across(merged)
     if rest:
         pieces = lax.psum(pieces, rest)
     chunk = jnp.sum(swap(pieces, chips + ("pair",)), axis=0)
-    half = swap(jnp.broadcast_to(chunk[None], (count,) + chunk.shape), chips)
+    chunk, merged = lax.optimization_barrier((chunk, merged))
+    half = gathered(chunk, rounds)
     half_other = across(half)
-    copies = product_copies(half, merged, merged_other)
+    copies = product_copies(layout, half, merged, merged_other)
     if rest:
         copies = lax.psum(copies, rest)
-    basis, inverse = sweeps(half, half_other)
+    basis, inverse = sweeps(layout, half, half_other)
     product = jnp.sum(swap(copies, chips), axis=0)
     product, basis, inverse = lax.optimization_barrier((product, basis, inverse))
     product_other = across(product)
@@ -349,13 +394,13 @@
 
 
 def solution(mesh):
-    chips, rest, count = split_axes(mesh)
+    chips, rest, sizes = split_axes(mesh)
     workers = 1
     for axis in AXES:
         workers *= mesh.shape[axis]
 
     def run(*args):
-        return local(chips, rest, count, workers, *args)
+        return local(chips, rest, sizes, workers, *args)
 
     return jax.shard_map(
         run,

time: 54.7 us -> 53.5 us (0.978)
  waiting for transfers between devices: 4.9 us -> 16.6 us
  blocking collectives: 26.9 us -> 16.9 us
  Pallas kernels: 17.9 us -> 13.8 us
  starting transfers between devices: 3.96 us -> 5.2 us
    ppermute x0 -> x3, waiting for transfers between devices: none -> 11.7 us  [gathered(): other = lax.ppermute(blocks, axis, [(i, i ^ bit) for i in range(size)])]
    all_to_all x2 -> x1, blocking collectives: 26.9 us -> 16.9 us  [swap(): return lax.all_to_all(pieces, axes, 0, 0, tiled=True)]
    pallas_call x4, Pallas kernels: 15.9 us -> 11.7 us  [the longest x1 4.14 us: sweeps(): pl.pallas_call(functools.partial(sweep_kernel, layout), out_shape=[jax.Sh...]
    ppermute x0 -> x3, starting transfers between devices: none -> 1.15 us  [gathered(): other = lax.ppermute(blocks, axis, [(i, i ^ bit) for i in range(size)])]
  transfers between devices with their start and end apart: 4 -> 7, of which waited for: 2 -> 5; matrix products, arithmetic and copies ran while one was open for 0% -> 0% of each run, Pallas kernels for 21% -> 13%
where the time goes in v7:
time: 53.5 us; the launch traced here: 53.2 us
  blocking collectives  16.9 us (32%)
  waiting for transfers between devices  16.6 us (31%)
  Pallas kernels  13.8 us (26%)
  starting transfers between devices  5.2 us (10%)
  between operations  0.71 us (1%)
    all_to_all x1, blocking collectives, swap(): return lax.all_to_all(pieces, axes, 0, 0, tiled=True)  16.9 us
    ppermute x3, waiting for transfers between devices, gathered(): other = lax.ppermute(blocks, axis, [(i, i ^ bit) for i in range(size)])  11.7 us
    pallas_call x1, Pallas kernels, sweeps(): pl.pallas_call(functools.partial(sweep_kernel, layout), out_shape=[jax.Sh...  4.14 us
    all_to_all x1, waiting for transfers between devices, swap(): return lax.all_to_all(pieces, axes, 0, 0, tiled=True)  3.69 us
    all_to_all x1, starting transfers between devices, swap(): return lax.all_to_all(pieces, axes, 0, 0, tiled=True)  3.38 us
    pallas_call x1, Pallas kernels, merge(): pl.pallas_call(merge_kernel, in_specs=[HBM] * 3 + [ANY], out_specs=VMEM,...  2.74 us
    pallas_call x1, Pallas kernels, product_copies(): pl.pallas_call(functools.partial(product_kernel, layout), in_specs=[VMEM,...  2.53 us
    pallas_call x1, Pallas kernels, term_pieces(): pl.pallas_call(term_kernel, in_specs=[HBM] * 4, out_specs=VMEM, out_shape...  2.32 us
  transfers between devices with their start and end apart: 7, of which 5 were waited for; matrix products, arithmetic and copies ran while one was open for 0% of the time, Pallas kernels for 13%

profile of v7, /device:TPU:0, one launch (start us, length us, event | category | flops | bytes accessed | tf_op | source)
XLA Modules:
  0.0 53.2 jit_solution(7188595563128967601)
XLA Ops:
  0.6 2.3 %term.1.after_hbm = f32[16,16,256]{2,1,0:T(8,128)S(1)} custom-call(bf16[512,2048]{1,0:T(8,128)(2,1)} %x_hbm.3, bf16[512,256]{1,0:T(8,128)(2,1)} %c_hbm.3, bf16[1,2048,256]{2,1,0:T(8,128)(2,1)} %e_hbm.3, f32[32,256]{1,0:T(8,128)} %seed_hbm.1), custom_call_target="tpu_custom_call" | custom-call | flops 201326592 | bytes 3145728 | tf_op jit(solution)/shard_map/term/pallas_call | solution.py:116
  3.0 2.7 %merge.1.mine_ref.merged_ref = f32[2048,256]{1,0:T(8,128)S(1)} custom-call(bf16[512,2048]{1,0:T(8,128)(2,1)} %x_hbm.3, bf16[512,256]{1,0:T(8,128)(2,1)} %c_hbm.3, bf16[1,2048,256]{2,1,0:T(8,128)(2,1)} %e_hbm.3, f32[16,16,256]{2,1,0:T(8,128)S(1)} %term.1.after_hbm), custom_call_target="tpu_custom_call" | custom-call | flops 1000000000 | bytes 10000000 | tf_op jit(solution)/shard_map/merge/pallas_call | solution.py:150
  5.7 0.5 collective-permute-start.3
  6.2 16.9 %all_to_all.10 = f32[16,16,256]{2,1,0:T(8,128)S(1)} all-to-all(f32[16,16,256]{2,1,0:T(8,128)S(1)} %term.1.after_hbm), channel_id=1, replica_groups=mesh['groups'=2,'dp'=4,'sub'=2,'pair'=2] {'dp','sub','pair'}, dimensions={0} | all-to-all | bytes 524288 | tf_op jit(solution)/shard_map/all_to_all | solution.py:33
  23.1 1.1 %collective-permute-start = (f32[1,16,256]{2,1,0:T(8,128)S(1)}, f32[1,16,256]{2,1,0:T(8,128)S(1)}, u32[]{:S(2)}, u32[]{:S(2)}) collective-permute-start(f32[1,16,256]{2,1,0:T(8,128)S(1)} %bitcast.1), channel_id=1, source_target_pairs={{0,8},{4,12},{8,0},{12,4},{1,9},{5,13},{9,1},{13,5},{2,10},{6,14},... | collective-permute-start | bytes 49160 | tf_op jit(solution)/shard_map/ppermute | solution.py:170
  24.2 3.6 %collective-permute-done = f32[1,16,256]{2,1,0:T(8,128)S(1)} collective-permute-done((f32[1,16,256]{2,1,0:T(8,128)S(1)}, f32[1,16,256]{2,1,0:T(8,128)S(1)}, u32[]{:S(2)}, u32[]{:S(2)}) %collective-permute-start) | collective-permute-done | bytes 16416 | tf_op jit(solution)/shard_map/ppermute | solution.py:170
  27.8 0.0 collective-permute-start.1
  27.8 3.9 %collective-permute-done.1 = f32[2,16,256]{2,1,0:T(8,128)S(1)} collective-permute-done((f32[2,16,256]{2,1,0:T(8,128)S(1)}, f32[2,16,256]{2,1,0:T(8,128)S(1)}, u32[]{:S(2)}, u32[]{:S(2)}) %collective-permute-start.1) | collective-permute-done | bytes 32800 | tf_op jit(solution)/shard_map/ppermute | solution.py:170
  31.7 0.0 collective-permute-start.2
  31.7 4.3 %collective-permute-done.2 = f32[4,16,256]{2,1,0:T(8,128)S(1)} collective-permute-done((f32[4,16,256]{2,1,0:T(8,128)S(1)}, f32[4,16,256]{2,1,0:T(8,128)S(1)}, u32[]{:S(2)}, u32[]{:S(2)}) %collective-permute-start.2) | collective-permute-done | bytes 65568 | tf_op jit(solution)/shard_map/ppermute | solution.py:170
  36.0 0.1 collective-permute-start.4
  36.1 0.0 collective-permute-done.3.other_hbm
  36.1 2.5 %product.1 = f32[8,16,256]{2,1,0:T(8,128)} custom-call(f32[8,16,256]{2,1,0:T(8,128)S(1)} %pad_maximum_fusion.pieces_ref.mine_ref, f32[2048,256]{1,0:T(8,128)S(1)} %merge.1.mine_ref.merged_ref, f32[2048,256]{1,0:T(8,128)} %collective-permute-done.3.other_hbm), custom_call_target="tpu_custom_call" | custom-call | flops 16777216 | bytes 4194304 | tf_op jit(solution)/shard_map/product/pallas_call | solution.py:216
  38.6 3.4 %all-to-all-start.1 = ((f32[8,16,256]{2,1,0:T(8,128)}), f32[8,16,256]{2,1,0:T(8,128)S(1)}, u32[]{:S(2)}, u32[]{:S(2)}) async-start(f32[8,16,256]{2,1,0:T(8,128)} %product.1), calls=%async_computation.1 | async-start | bytes 262144 | tf_op jit(solution)/shard_map/all_to_all | solution.py:33
  42.0 0.0 collective-permute-done.4.other_ref
  42.0 4.1 %sweeps.1 = (f32[32,2048]{1,0:T(8,128)S(1)}, f32[32,32]{1,0:T(8,128)S(1)}) custom-call(f32[8,16,256]{2,1,0:T(8,128)S(1)} %pad_maximum_fusion.pieces_ref.mine_ref, f32[8,16,256]{2,1,0:T(8,128)S(1)} %collective-permute-done.4.other_ref), custom_call_target="tpu_custom_call" | custom-call | flops 10000000000 | bytes 10000000 | tf_op jit(solution)/shard_map/sweeps/pallas_call | solution.py:305
  46.2 3.7 %all-to-all-done.1 = f32[8,16,256]{2,1,0:T(8,128)S(1)} async-done(((f32[8,16,256]{2,1,0:T(8,128)}), f32[8,16,256]{2,1,0:T(8,128)S(1)}, u32[]{:S(2)}, u32[]{:S(2)}) %all-to-all-start.1) | async-done | bytes 131104 | tf_op jit(solution)/shard_map/all_to_all | solution.py:33
  49.9 0.1 collective-permute-start.5
  50.0 1.2 %collective-permute-done.5.other_ref = f32[16,256]{1,0:T(8,128)S(1)} collective-permute-done((f32[16,256]{1,0:T(8,128)S(1)}, f32[16,256]{1,0:T(8,128)S(1)}, u32[]{:S(2)}, u32[]{:S(2)}) %collective-permute-start.5) | collective-permute-done | bytes 16416 | tf_op jit(solution)/shard_map/ppermute | solution.py:37
  51.1 2.0 %error_next.1 = (bf16[1,2048,256]{2,1,0:T(8,128)(2,1)}, f32[32,2048]{1,0:T(8,128)}, f32[32,256]{1,0:T(8,128)}) custom-call(f32[2048,256]{1,0:T(8,128)S(1)} %merge.1.mine_ref.merged_ref, f32[32,2048]{1,0:T(8,128)S(1)} %get-tuple-element.14.basis_ref, f32[32,32]{1,0:T(8,128)S(1)} %get-tuple-element.15.inverse_ref, f32[16,256]{1,0:T(8,128)S(1)} %reduce_sum.19.mine_ref, ...), custom_call_target="tpu_custom_call" | custom-call | flops 33554432 | bytes 3145728 | tf_op jit(solution)/shard_map/error_next/pallas_call | solution.py:346
  (5 shorter events, 0.1 us)
Async XLA Ops:
  5.7 30.4 %collective-permute-start.3 = (f32[2048,256]{1,0:T(8,128)S(1)}, f32[2048,256]{1,0:T(8,128)}, u32[]{:S(2)}, u32[]{:S(2)}) collective-permute-start(f32[2048,256]{1,0:T(8,128)S(1)} %merge.1.mine_ref.merged_ref), channel_id=1, source_target_pairs={{0,1},{1,0},{2,3},{3,2},{4,5},{5,4},{6,7},{7,6},{8,9},{9,8},{10,11... | collective-permute-start | bytes 6291464 | tf_op jit(solution)/shard_map/ppermute | solution.py:37
  23.1 4.7 %collective-permute-start = (f32[1,16,256]{2,1,0:T(8,128)S(1)}, f32[1,16,256]{2,1,0:T(8,128)S(1)}, u32[]{:S(2)}, u32[]{:S(2)}) collective-permute-start(f32[1,16,256]{2,1,0:T(8,128)S(1)} %bitcast.1), channel_id=1, source_target_pairs={{0,8},{4,12},{8,0},{12,4},{1,9},{5,13},{9,1},{13,5},{2,10},{6,14},... | collective-permute-start | bytes 49160 | tf_op jit(solution)/shard_map/ppermute | solution.py:170
  27.8 3.9 %collective-permute-start.1 = (f32[2,16,256]{2,1,0:T(8,128)S(1)}, f32[2,16,256]{2,1,0:T(8,128)S(1)}, u32[]{:S(2)}, u32[]{:S(2)}) collective-permute-start(f32[2,16,256]{2,1,0:T(8,128)S(1)} %pad_maximum_fusion.2), channel_id=1, source_target_pairs={{0,4},{4,0},{8,12},{12,8},{1,5},{5,1},{9,13},{13,9},{2,6},{6,2},{1... | collective-permute-start | bytes 98312 | tf_op jit(solution)/shard_map/ppermute | solution.py:170
  31.7 4.3 %collective-permute-start.2 = (f32[4,16,256]{2,1,0:T(8,128)S(1)}, f32[4,16,256]{2,1,0:T(8,128)S(1)}, u32[]{:S(2)}, u32[]{:S(2)}) collective-permute-start(f32[4,16,256]{2,1,0:T(8,128)S(1)} %pad_maximum_fusion.1), channel_id=1, source_target_pairs={{0,2},{2,0},{1,3},{3,1},{4,6},{6,4},{5,7},{7,5},{8,10},{10,8},{9,1... | collective-permute-start | bytes 196616 | tf_op jit(solution)/shard_map/ppermute | solution.py:170
  36.0 6.0 %collective-permute-start.4 = (f32[8,16,256]{2,1,0:T(8,128)S(1)}, f32[8,16,256]{2,1,0:T(8,128)S(1)}, u32[]{:S(2)}, u32[]{:S(2)}) collective-permute-start(f32[8,16,256]{2,1,0:T(8,128)S(1)} %pad_maximum_fusion.pieces_ref.mine_ref), channel_id=1, source_target_pairs={{0,1},{1,0},{2,3},{3,2},{4,5},{5,4},{6,7},{7,6},{8,9},{9,8},{10,11... | collective-permute-start | bytes 393224 | tf_op jit(solution)/shard_map/ppermute | solution.py:37
  38.6 11.2 %all-to-all-start.1 = ((f32[8,16,256]{2,1,0:T(8,128)}), f32[8,16,256]{2,1,0:T(8,128)S(1)}, u32[]{:S(2)}, u32[]{:S(2)}) async-start(f32[8,16,256]{2,1,0:T(8,128)} %product.1), calls=%async_computation.1 | async-start | bytes 262144 | tf_op jit(solution)/shard_map/all_to_all | solution.py:33
  49.9 1.2 %collective-permute-start.5 = (f32[16,256]{1,0:T(8,128)S(1)}, f32[16,256]{1,0:T(8,128)S(1)}, u32[]{:S(2)}, u32[]{:S(2)}) collective-permute-start(f32[16,256]{1,0:T(8,128)S(1)} %reduce_sum.19.mine_ref), channel_id=1, source_target_pairs={{0,1},{1,0},{2,3},{3,2},{4,5},{5,4},{6,7},{7,6},{8,9},{9,8},{10,11... | collective-permute-start | bytes 49160 | tf_op jit(solution)/shard_map/ppermute | solution.py:37

commit v8 on v7

--- a/solution.py
+++ b/solution.py
@@ -18,23 +18,17 @@
 VMEM = pl.BlockSpec(memory_space=pltpu.VMEM)
 
 
-def split_axes(mesh):
-    count, chips = mesh.shape["pair"], []
-    for axis in ("dp", "sub"):
-        if count * mesh.shape[axis] <= 16:
-            chips.append(axis)
-            count *= mesh.shape[axis]
-    chips = tuple(chips)
-    rest = tuple(axis for axis in AXES if axis not in chips + ("pair",))
-    return chips, rest, tuple(mesh.shape[axis] for axis in chips)
-
-
-def swap(pieces, axes):
-    return lax.all_to_all(pieces, axes, 0, 0, tiled=True)
+def swapped(value, axis, size, bit):
+    return lax.ppermute(value, axis, [(i, i ^ bit) for i in range(size)])
 
 
 def across(value):
-    return lax.ppermute(value, "pair", [(0, 1), (1, 0)])
+    return swapped(value, "pair", 2, 1)
+
+
+def bits_of(axis, size):
+    assert size & (size - 1) == 0
+    return [(axis, size, 1 << i) for i in range(size.bit_length() - 1)]
 
 
 def parts_of(value, count):
@@ -68,7 +62,7 @@
     return [(source.at[part, :], target.at[part, :]) for part in rows]
 
 
-def term_kernel(x_hbm, c_hbm, e_hbm, seed_hbm, pieces_ref,
+def term_kernel(x_hbm, c_hbm, e_hbm, seed_hbm, keep_ref, send_ref,
                 x_ref, c_ref, e_ref, seed_ref, term_ref, sems):
     copies = whole_copies(
         [(seed_hbm, seed_ref), (c_hbm, c_ref)] + row_parts(e_hbm.at[0], e_ref, 2)
@@ -77,7 +71,7 @@
         copy.start()
     rank = seed_ref.shape[0]
     tokens, width = x_ref.shape
-    half, piece = pieces_ref.shape[1:]
+    half, piece = keep_ref.shape[1:]
     copies[0].wait()
     copies[1].wait()
     seed = jnp.concatenate(parts_of(seed_ref[...], 3), axis=0)
@@ -96,10 +90,17 @@
         for i in range(blocks):
             part = pl.ds(i * CHUNK, CHUNK)
             term_ref[:, part] += added(dot(own, x_ref[rows, part], ((1,), (0,))), rank)
-    for j in range(width // piece):
-        for k in range(rank // half):
-            pieces_ref[j * (rank // half) + k] = (
-                term_ref[k * half:(k + 1) * half, j * piece:(j + 1) * piece])
+    low = lax.axis_index("pair") == 0
+    for i in range(2):
+        part = side(i, piece)
+        top, bottom = term_ref[:half, part], term_ref[half:, part]
+        keep_ref[i] = jnp.where(low, top, bottom)
+        send_ref[i] = jnp.where(low, bottom, top)
+
+
+def side(i, piece, start=0, size=None):
+    chosen = (lax.axis_index("sub") & 1) ^ i
+    return pl.ds(pl.multiple_of(chosen * piece + start, CHUNK), size or piece)
 
 
 def added(stack, rank):
@@ -109,15 +110,15 @@
     return total
 
 
-def term_pieces(inputs, cotangent, error_prev, seed_q, chips):
+def term_halves(inputs, cotangent, error_prev, seed_q):
     tokens, width = inputs.shape
     out = cotangent.shape[1]
     rank = seed_q.shape[0]
     return pl.pallas_call(
         term_kernel,
         in_specs=[HBM] * 4,
-        out_specs=VMEM,
-        out_shape=jax.ShapeDtypeStruct((2 * chips, rank // 2, width // chips), F32),
+        out_specs=[VMEM] * 2,
+        out_shape=[jax.ShapeDtypeStruct((2, rank // 2, width // 2), F32)] * 2,
         scratch_shapes=[
             pltpu.VMEM((tokens, width), BF16),
             pltpu.VMEM((tokens, out), BF16),
@@ -164,64 +165,39 @@
     )(inputs, cotangent, error_prev, after)
 
 
-def gathered(block, rounds):
-    blocks = block[None]
-    for axis, size, bit, mask in rounds:
-        other = lax.ppermute(blocks, axis, [(i, i ^ bit) for i in range(size)])
-        blocks = jnp.concatenate([blocks, other], axis=0)
-    return blocks
-
-
-def masks_of(rounds):
-    masks = [0]
-    for axis, size, bit, mask in rounds:
-        masks = masks + [old ^ mask for old in masks]
-    return masks
-
-
-def chip_index(chips, sizes):
-    index = 0
-    for axis, size in zip(chips, sizes):
-        index = index * size + lax.axis_index(axis)
-    return index
-
-
-def place(chip, mask, piece):
-    return pl.ds(pl.multiple_of((chip ^ mask) * piece, piece), piece)
-
-
-def product_kernel(layout, pieces_ref, mine_ref, other_hbm, copies_ref, other_ref, sems):
-    chips, sizes, masks = layout
-    count, half, piece = pieces_ref.shape
-    chip = chip_index(chips, sizes)
-    parts = [place(chip, mask, piece) for mask in masks]
+def product_kernel(near_ref, far_ref, mine_ref, other_hbm, product_ref, other_ref, sems):
+    half, piece = near_ref.shape
+    per = piece // CHUNK
+    parts = [side(i, piece, j * CHUNK, CHUNK) for i in range(2) for j in range(per)]
     copies = whole_copies([(other_hbm.at[part, :], other_ref.at[part, :]) for part in parts], sems)
     for copy in copies:
         copy.start()
     product = None
     for i, part in enumerate(parts):
-        f_high, f_low = parts_of(pieces_ref[i], 2)
+        rows_ref = near_ref if i < per else far_ref
+        rows = rows_ref[:, (i % per) * CHUNK:(i % per + 1) * CHUNK]
+        f_high, f_low = parts_of(rows, 2)
         both = jnp.concatenate([f_high, f_low], axis=0)
         copies[i].wait()
         m_high, m_low = parts_of(mine_ref[part, :] + other_ref[part, :], 2)
         term = added(dot(both, m_high, ((1,), (0,))), half) + dot(f_high, m_low, ((1,), (0,)))
         product = term if product is None else product + term
-    for i in range(count):
-        copies_ref[i] = product
-
-
-def product_copies(layout, pieces, mine, other):
-    count, half, piece = pieces.shape
+    product_ref[...] = product
+
+
+def product_of(near, far, mine, other):
+    half = near.shape[0]
     width, out = mine.shape
     return pl.pallas_call(
-        functools.partial(product_kernel, layout),
-        in_specs=[VMEM, VMEM, ANY],
-        out_shape=jax.ShapeDtypeStruct((count, half, out), F32),
-        scratch_shapes=[pltpu.VMEM((width, out), F32), pltpu.SemaphoreType.DMA((count,))],
+        product_kernel,
+        in_specs=[VMEM, VMEM, VMEM, ANY],
+        out_shape=jax.ShapeDtypeStruct((half, out), F32),
+        scratch_shapes=[
+            pltpu.VMEM((width, out), F32), pltpu.SemaphoreType.DMA((width // CHUNK,))],
         compiler_params=params(),
         cost_estimate=cost(2 * half * width * out, 8 * width * out),
         name="product",
-    )(pieces, mine, other)
+    )(near, far, mine, other)
 
 
 def both_halves(mine, other):
@@ -273,45 +249,64 @@
     return dot(lefts, rights, ((1,), (0,)))
 
 
-def sweep_kernel(layout, mine_ref, other_ref, basis_ref, inverse_ref):
-    chips, sizes, masks = layout
-    count, half, piece = mine_ref.shape
+def first_sweep_kernel(mine_ref, other_ref, rows_ref, step_ref, gram_ref):
+    half, piece = mine_ref.shape[1:]
     rank = 2 * half
-    chip = chip_index(chips, sizes)
     blocks = None
-    for i, mask in enumerate(masks):
-        rows = both_halves(mine_ref[i], other_ref[i])
-        basis_ref[:, place(chip, mask, piece)] = rows
+    for i in range(2):
+        for j in range(piece // CHUNK):
+            part = slice(j * CHUNK, (j + 1) * CHUNK)
+            rows = both_halves(mine_ref[i, :, part], other_ref[i, :, part])
+            rows_ref[:, side(i, piece, j * CHUNK, CHUNK)] = rows
+            term = gram_blocks(rows)
+            blocks = term if blocks is None else blocks + term
+    step = inverse_factor(gram_of(blocks, rank))
+    step_ref[...] = step
+    blocks = None
+    for i in range(rows_ref.shape[1] // CHUNK):
+        part = slice(i * CHUNK, (i + 1) * CHUNK)
+        rows = short_dot(step, rows_ref[:, part])
+        rows_ref[:, part] = rows
         term = gram_blocks(rows)
         blocks = term if blocks is None else blocks + term
-    step = inverse_factor(gram_of(blocks, rank))
-    blocks = None
-    for i in range(count):
-        part = slice(i * piece, (i + 1) * piece)
-        rows = short_dot(step, basis_ref[:, part])
-        basis_ref[:, part] = rows
-        term = gram_blocks(rows)
-        blocks = term if blocks is None else blocks + term
-    last = inverse_factor(gram_of(blocks, rank))
-    for i in range(count):
-        part = slice(i * piece, (i + 1) * piece)
-        basis_ref[:, part] = short_dot(last, basis_ref[:, part])
-    inverse_ref[...] = short_dot(last, step)
-
-
-def sweeps(layout, mine, other):
-    count, half, piece = mine.shape
-    rank, width = 2 * half, count * piece
-    return pl.pallas_call(
-        functools.partial(sweep_kernel, layout),
+    gram_ref[...] = gram_of(blocks, rank)
+
+
+def first_sweep(mine, other):
+    _, half, piece = mine.shape
+    rank, width = 2 * half, 2 * piece
+    return pl.pallas_call(
+        first_sweep_kernel,
         out_shape=[
             jax.ShapeDtypeStruct((rank, width), F32),
             jax.ShapeDtypeStruct((rank, rank), F32),
-        ],
-        compiler_params=params(),
-        cost_estimate=cost(10 ** 10, 10 ** 7),
-        name="sweeps",
+            jax.ShapeDtypeStruct((rank, rank), F32),
+        ],
+        compiler_params=params(),
+        cost_estimate=cost(10 ** 9, 7 * 10 ** 6),
+        name="first_sweep",
     )(mine, other)
+
+
+def second_sweep_kernel(rows_ref, step_ref, gram_ref, basis_ref, inverse_ref):
+    last = inverse_factor(gram_ref[...])
+    for i in range(rows_ref.shape[1] // CHUNK):
+        part = slice(i * CHUNK, (i + 1) * CHUNK)
+        basis_ref[:, part] = short_dot(last, rows_ref[:, part])
+    inverse_ref[...] = short_dot(last, step_ref[...])
+
+
+def second_sweep(rows, step, gram):
+    return pl.pallas_call(
+        second_sweep_kernel,
+        out_shape=[
+            jax.ShapeDtypeStruct(rows.shape, F32),
+            jax.ShapeDtypeStruct(step.shape, F32),
+        ],
+        compiler_params=params(),
+        cost_estimate=cost(10 ** 9, 7 * 10 ** 6),
+        name="second_sweep",
+    )(rows, step, gram)
 
 
 def error_kernel(workers, steps, merged_ref, basis_ref, inverse_ref, mine_ref, other_ref,
@@ -363,44 +358,44 @@
     )(merged, basis, inverse, mine, other)
 
 
-def local(chips, rest, sizes, workers, *arguments):
+def local(sizes, *arguments):
     inputs, cotangent, error_prev, seed_q = (
         pltpu.with_memory_space_constraint(value, pltpu.HBM) for value in arguments)
-    count, rounds, stride = 1, [], 1
-    for axis, size in zip(chips[::-1], sizes[::-1]):
-        bits = [1 << i for i in range(size.bit_length() - 1)]
-        rounds = [(axis, size, bit, bit * stride) for bit in bits[::-1]] + rounds
-        stride *= size
-    count = stride
-    layout = (chips, sizes, masks_of(rounds))
-    pieces = term_pieces(inputs, cotangent, error_prev, seed_q, count)
-    merged = merge(inputs, cotangent, error_prev, pieces)
+    beside = ("sub", sizes["sub"], 1)
+    rounds = bits_of("sub", sizes["sub"]) + bits_of("dp", sizes["dp"])
+    workers = 2 * sizes["sub"] * sizes["dp"]
+
+    keep, send = term_halves(inputs, cotangent, error_prev, seed_q)
+    part = keep + across(send)
+    merged = merge(inputs, cotangent, error_prev, part)
     merged_other = across(merged)
-    if rest:
-        pieces = lax.psum(pieces, rest)
-    chunk = jnp.sum(swap(pieces, chips + ("pair",)), axis=0)
-    chunk, merged = lax.optimization_barrier((chunk, merged))
-    half = gathered(chunk, rounds)
-    half_other = across(half)
-    copies = product_copies(layout, half, merged, merged_other)
-    if rest:
-        copies = lax.psum(copies, rest)
-    basis, inverse = sweeps(layout, half, half_other)
-    product = jnp.sum(swap(copies, chips), axis=0)
-    product, basis, inverse = lax.optimization_barrier((product, basis, inverse))
+    near = part[0] + swapped(part[1], *beside)
+    for axis_bit in rounds[1:]:
+        near = near + swapped(near, *axis_bit)
+    far = swapped(near, *beside)
+    mine = jnp.stack([near, far])
+    other = across(mine)
+
+    product = product_of(near, far, merged, merged_other)
+    rows, step, gram = first_sweep(mine, other)
+    product = product + swapped(product, *rounds[0])
+    product, rows, step, gram = lax.optimization_barrier((product, rows, step, gram))
+    basis, inverse = second_sweep(rows, step, gram)
+    for i, axis_bit in enumerate(rounds[1:]):
+        product = product + swapped(product, *axis_bit)
+        if i == 0:
+            product, basis, inverse = lax.optimization_barrier((product, basis, inverse))
     product_other = across(product)
     error_next, basis, second = error_of(merged, basis, inverse, product, product_other, workers)
     return (error_next, basis, second)
 
 
 def solution(mesh):
-    chips, rest, sizes = split_axes(mesh)
-    workers = 1
-    for axis in AXES:
-        workers *= mesh.shape[axis]
+    sizes = {axis: mesh.shape[axis] for axis in AXES}
+    assert sizes["pair"] == 2 and sizes["sub"] > 1
 
     def run(*args):
-        return local(chips, rest, sizes, workers, *args)
+        return local(sizes, *args)
 
     return jax.shard_map(
         run,

time: 53.5 us -> 44.3 us (0.83)
  blocking collectives: 16.9 us -> 0 us
  starting transfers between devices: 5.2 us -> 16.5 us
  waiting for transfers between devices: 16.6 us -> 14.5 us
  Pallas kernels: 13.8 us -> 12.4 us
    all_to_all x1 -> x0, blocking collectives: 16.9 us -> none  [swap(): return lax.all_to_all(pieces, axes, 0, 0, tiled=True)]
    ppermute x6 -> x11, starting transfers between devices: 1.81 us -> 16.5 us  [swapped(): return lax.ppermute(value, axis, [(i, i ^ bit) for i in range(size)])]
    all_to_all x1 -> x0, waiting for transfers between devices: 3.69 us -> none  [swap(): return lax.all_to_all(pieces, axes, 0, 0, tiled=True)]
    all_to_all x1 -> x0, starting transfers between devices: 3.38 us -> none  [swap(): return lax.all_to_all(pieces, axes, 0, 0, tiled=True)]
    ppermute x6 -> x11, waiting for transfers between devices: 12.9 us -> 14.5 us  [swapped(): return lax.ppermute(value, axis, [(i, i ^ bit) for i in range(size)])]
    pallas_call x3 -> x4, Pallas kernels: 8.99 us -> 7.6 us  [the longest x1 2.57 us: first_sweep(): pl.pallas_call(first_sweep_kernel, out_shape=[jax.ShapeDtypeStruct((rank,...]
  transfers between devices with their start and end apart: 7 -> 11, of which waited for: 5 -> 8; matrix products, arithmetic and copies ran while one was open for 0% -> 0% of each run, Pallas kernels for 13% -> 12%
where the time goes in v8:
time: 44.3 us; the launch traced here: 44.1 us
  starting transfers between devices  16.5 us (37%)
  waiting for transfers between devices  14.5 us (33%)
  Pallas kernels  12.4 us (28%)
  between operations  0.73 us (2%)
    ppermute x11, starting transfers between devices, swapped(): return lax.ppermute(value, axis, [(i, i ^ bit) for i in range(size)])  16.5 us
    ppermute x11, waiting for transfers between devices, swapped(): return lax.ppermute(value, axis, [(i, i ^ bit) for i in range(size)])  14.5 us
    pallas_call x1, Pallas kernels, merge(): pl.pallas_call(merge_kernel, in_specs=[HBM] * 3 + [ANY], out_specs=VMEM,...  2.74 us
    pallas_call x1, Pallas kernels, first_sweep(): pl.pallas_call(first_sweep_kernel, out_shape=[jax.ShapeDtypeStruct((rank,...  2.57 us
    pallas_call x1, Pallas kernels, term_halves(): pl.pallas_call(term_kernel, in_specs=[HBM] * 4, out_specs=[VMEM] * 2, out...  2.34 us
    pallas_call x1, Pallas kernels, error_of(): pl.pallas_call(functools.partial(error_kernel, workers, steps), in_specs=...  2.05 us
    pallas_call x1, Pallas kernels, second_sweep(): pl.pallas_call(second_sweep_kernel, out_shape=[jax.ShapeDtypeStruct(rows....  1.63 us
    pallas_call x1, Pallas kernels, product_of(): pl.pallas_call(product_kernel, in_specs=[VMEM, VMEM, VMEM, ANY], out_shap...  1.07 us
  transfers between devices with their start and end apart: 11, of which 8 were waited for; matrix products, arithmetic and copies ran while one was open for 0% of the time, Pallas kernels for 12%

profile of v8, /device:TPU:0, one launch (start us, length us, event | category | flops | bytes accessed | tf_op | source)
XLA Modules:
  0.0 44.1 jit_solution(14414263633507333120)
XLA Ops:
  0.6 2.3 %term.1 = (f32[2,16,1024]{2,1,0:T(8,128)S(1)}, f32[2,16,1024]{2,1,0:T(8,128)S(1)}) custom-call(bf16[512,2048]{1,0:T(8,128)(2,1)} %x_hbm.3, bf16[512,256]{1,0:T(8,128)(2,1)} %c_hbm.3, bf16[1,2048,256]{2,1,0:T(8,128)(2,1)} %e_hbm.3, f32[32,256]{1,0:T(8,128)} %seed_hbm.1), custom_call_target="tpu_custom_call" | custom-call | flops 201326592 | bytes 3145728 | tf_op jit(solution)/shard_map/term/pallas_call | solution.py:117
  3.0 0.5 %collective-permute-start = (f32[2,16,1024]{2,1,0:T(8,128)S(1)}, f32[2,16,1024]{2,1,0:T(8,128)S(1)}, u32[]{:S(2)}, u32[]{:S(2)}) collective-permute-start(f32[2,16,1024]{2,1,0:T(8,128)S(1)} %get-tuple-element.18), channel_id=1, source_target_pairs={{0,1},{1,0},{2,3},{3,2},{4,5},{5,4},{6,7},{7,6},{8,9},{9,8},{10,11... | collective-permute-start | bytes 393224 | tf_op jit(solution)/shard_map/ppermute | solution.py:22
  3.5 1.0 %collective-permute-done = f32[2,16,1024]{2,1,0:T(8,128)S(1)} collective-permute-done((f32[2,16,1024]{2,1,0:T(8,128)S(1)}, f32[2,16,1024]{2,1,0:T(8,128)S(1)}, u32[]{:S(2)}, u32[]{:S(2)}) %collective-permute-start) | collective-permute-done | bytes 131104 | tf_op jit(solution)/shard_map/ppermute | solution.py:22
  4.5 2.7 %merge.1.mine_ref.merged_ref = f32[2048,256]{1,0:T(8,128)S(1)} custom-call(bf16[512,2048]{1,0:T(8,128)(2,1)} %x_hbm.3, bf16[512,256]{1,0:T(8,128)(2,1)} %c_hbm.3, bf16[1,2048,256]{2,1,0:T(8,128)(2,1)} %e_hbm.3, f32[2,16,1024]{2,1,0:T(8,128)S(1)} %add.21.after_hbm), custom_call_target="tpu_custom_call" | custom-call | flops 1000000000 | bytes 10000000 | tf_op jit(solution)/shard_map/merge/pallas_call | solution.py:151
  7.3 0.4 collective-permute-start.5
  7.7 2.6 %collective-permute-start.1 = (f32[16,1024]{1,0:T(8,128)S(1)}, f32[16,1024]{1,0:T(8,128)S(1)}, u32[]{:S(2)}, u32[]{:S(2)}) collective-permute-start(f32[16,1024]{1,0:T(8,128)S(1)} %slice_bitcast_fusion), channel_id=1, source_target_pairs={{0,2},{2,0},{1,3},{3,1},{4,6},{6,4},{5,7},{7,5},{8,10},{10,8},{9,1... | collective-permute-start | bytes 196616 | tf_op jit(solution)/shard_map/ppermute | solution.py:22
  10.3 2.6 %collective-permute-done.1 = f32[16,1024]{1,0:T(8,128)S(1)} collective-permute-done((f32[16,1024]{1,0:T(8,128)S(1)}, f32[16,1024]{1,0:T(8,128)S(1)}, u32[]{:S(2)}, u32[]{:S(2)}) %collective-permute-start.1) | collective-permute-done | bytes 65568 | tf_op jit(solution)/shard_map/ppermute | solution.py:22
  13.0 1.9 %collective-permute-start.2 = (f32[16,1024]{1,0:T(8,128)S(1)}, f32[16,1024]{1,0:T(8,128)S(1)}, u32[]{:S(2)}, u32[]{:S(2)}) collective-permute-start(f32[16,1024]{1,0:T(8,128)S(1)} %fusion), channel_id=1, source_target_pairs={{0,4},{4,0},{8,12},{12,8},{1,5},{5,1},{9,13},{13,9},{2,6},{6,2},{1... | collective-permute-start | bytes 196616 | tf_op jit(solution)/shard_map/ppermute | solution.py:22
  14.8 2.4 %collective-permute-done.2 = f32[16,1024]{1,0:T(8,128)S(1)} collective-permute-done((f32[16,1024]{1,0:T(8,128)S(1)}, f32[16,1024]{1,0:T(8,128)S(1)}, u32[]{:S(2)}, u32[]{:S(2)}) %collective-permute-start.2) | collective-permute-done | bytes 65568 | tf_op jit(solution)/shard_map/ppermute | solution.py:22
  17.3 2.9 %collective-permute-start.3 = (f32[16,1024]{1,0:T(8,128)S(1)}, f32[16,1024]{1,0:T(8,128)S(1)}, u32[]{:S(2)}, u32[]{:S(2)}) collective-permute-start(f32[16,1024]{1,0:T(8,128)S(1)} %add.23), channel_id=1, source_target_pairs={{0,8},{4,12},{8,0},{12,4},{1,9},{5,13},{9,1},{13,5},{2,10},{6,14},... | collective-permute-start | bytes 196616 | tf_op jit(solution)/shard_map/ppermute | solution.py:22
  20.2 2.3 %collective-permute-done.3 = f32[16,1024]{1,0:T(8,128)S(1)} collective-permute-done((f32[16,1024]{1,0:T(8,128)S(1)}, f32[16,1024]{1,0:T(8,128)S(1)}, u32[]{:S(2)}, u32[]{:S(2)}) %collective-permute-start.3) | collective-permute-done | bytes 65568 | tf_op jit(solution)/shard_map/ppermute | solution.py:22
  22.5 1.8 %collective-permute-start.4 = (f32[16,1024]{1,0:T(8,128)S(1)}, f32[16,1024]{1,0:T(8,128)S(1)}, u32[]{:S(2)}, u32[]{:S(2)}) collective-permute-start(f32[16,1024]{1,0:T(8,128)S(1)} %add.24.near_ref), channel_id=1, source_target_pairs={{0,2},{2,0},{1,3},{3,1},{4,6},{6,4},{5,7},{7,5},{8,10},{10,8},{9,1... | collective-permute-start | bytes 196616 | tf_op jit(solution)/shard_map/ppermute | solution.py:22
  24.3 2.5 %collective-permute-done.4.far_ref = f32[16,1024]{1,0:T(8,128)S(1)} collective-permute-done((f32[16,1024]{1,0:T(8,128)S(1)}, f32[16,1024]{1,0:T(8,128)S(1)}, u32[]{:S(2)}, u32[]{:S(2)}) %collective-permute-start.4) | collective-permute-done | bytes 65568 | tf_op jit(solution)/shard_map/ppermute | solution.py:22
  26.9 0.1 collective-permute-start.7
  27.0 0.0 collective-permute-done.5.other_hbm
  27.0 1.1 %product.1 = f32[16,256]{1,0:T(8,128)S(1)} custom-call(f32[16,1024]{1,0:T(8,128)S(1)} %add.24.near_ref, f32[16,1024]{1,0:T(8,128)S(1)} %collective-permute-done.4.far_ref, f32[2048,256]{1,0:T(8,128)S(1)} %merge.1.mine_ref.merged_ref, f32[2048,256]{1,0:T(8,128)S(1)} %collective-permute-done.5.other_hbm), custom_call_target="tpu_custom_call" | custom-call | flops 16777216 | bytes 4194304 | tf_op jit(solution)/shard_map/product/pallas_call | solution.py:191
  28.0 1.8 %collective-permute-start.6 = (f32[16,256]{1,0:T(8,128)S(1)}, f32[16,256]{1,0:T(8,128)S(1)}, u32[]{:S(2)}, u32[]{:S(2)}) collective-permute-start(f32[16,256]{1,0:T(8,128)S(1)} %product.1), channel_id=1, source_target_pairs={{0,2},{2,0},{1,3},{3,1},{4,6},{6,4},{5,7},{7,5},{8,10},{10,8},{9,1... | collective-permute-start | bytes 49160 | tf_op jit(solution)/shard_map/ppermute | solution.py:22
  29.9 0.0 collective-permute-done.7.other_ref
  29.9 2.6 %first_sweep.1 = (f32[32,2048]{1,0:T(8,128)S(1)}, f32[32,32]{1,0:T(8,128)S(1)}, f32[32,32]{1,0:T(8,128)S(1)}) custom-call(f32[2,16,1024]{2,1,0:T(8,128)S(1)} %pad_maximum_fusion.mine_ref, f32[2,16,1024]{2,1,0:T(8,128)S(1)} %collective-permute-done.7.other_ref), custom_call_target="tpu_custom_call" | custom-call | flops 1000000000 | bytes 7000000 | tf_op jit(solution)/shard_map/first_sweep/pallas_call | solution.py:278
  32.4 0.0 collective-permute-done.6
  32.5 1.6 %collective-permute-start.8 = (f32[16,256]{1,0:T(8,128)S(1)}, f32[16,256]{1,0:T(8,128)S(1)}, u32[]{:S(2)}, u32[]{:S(2)}) collective-permute-start(f32[16,256]{1,0:T(8,128)S(1)} %add.25), channel_id=1, source_target_pairs={{0,4},{4,0},{8,12},{12,8},{1,5},{5,1},{9,13},{13,9},{2,6},{6,2},{1... | collective-permute-start | bytes 49160 | tf_op jit(solution)/shard_map/ppermute | solution.py:22
  34.1 1.6 %second_sweep.1 = (f32[32,2048]{1,0:T(8,128)S(1)}, f32[32,32]{1,0:T(8,128)S(1)}) custom-call(f32[32,2048]{1,0:T(8,128)S(1)} %get-tuple-element.23.rows_ref, f32[32,32]{1,0:T(8,128)S(1)} %get-tuple-element.24.step_ref, f32[32,32]{1,0:T(8,128)S(1)} %get-tuple-element.25.gram_ref), custom_call_target="tpu_custom_call" | custom-call | flops 1000000000 | bytes 7000000 | tf_op jit(solution)/shard_map/second_sweep/pallas_call | solution.py:300
  35.7 0.5 %collective-permute-done.8 = f32[16,256]{1,0:T(8,128)S(1)} collective-permute-done((f32[16,256]{1,0:T(8,128)S(1)}, f32[16,256]{1,0:T(8,128)S(1)}, u32[]{:S(2)}, u32[]{:S(2)}) %collective-permute-start.8) | collective-permute-done | bytes 16416 | tf_op jit(solution)/shard_map/ppermute | solution.py:22
  36.3 2.7 %collective-permute-start.9 = (f32[16,256]{1,0:T(8,128)S(1)}, f32[16,256]{1,0:T(8,128)S(1)}, u32[]{:S(2)}, u32[]{:S(2)}) collective-permute-start(f32[16,256]{1,0:T(8,128)S(1)} %add.26), channel_id=1, source_target_pairs={{0,8},{4,12},{8,0},{12,4},{1,9},{5,13},{9,1},{13,5},{2,10},{6,14},... | collective-permute-start | bytes 49160 | tf_op jit(solution)/shard_map/ppermute | solution.py:22
  39.0 1.9 %collective-permute-done.9 = f32[16,256]{1,0:T(8,128)S(1)} collective-permute-done((f32[16,256]{1,0:T(8,128)S(1)}, f32[16,256]{1,0:T(8,128)S(1)}, u32[]{:S(2)}, u32[]{:S(2)}) %collective-permute-start.9) | collective-permute-done | bytes 16416 | tf_op jit(solution)/shard_map/ppermute | solution.py:22
  40.9 0.0 collective-permute-start.10
  40.9 1.2 %collective-permute-done.10.other_ref = f32[16,256]{1,0:T(8,128)S(1)} collective-permute-done((f32[16,256]{1,0:T(8,128)S(1)}, f32[16,256]{1,0:T(8,128)S(1)}, u32[]{:S(2)}, u32[]{:S(2)}) %collective-permute-start.10) | collective-permute-done | bytes 16416 | tf_op jit(solution)/shard_map/ppermute | solution.py:22
  42.1 2.0 %error_next.1 = (bf16[1,2048,256]{2,1,0:T(8,128)(2,1)}, f32[32,2048]{1,0:T(8,128)}, f32[32,256]{1,0:T(8,128)}) custom-call(f32[2048,256]{1,0:T(8,128)S(1)} %merge.1.mine_ref.merged_ref, f32[32,2048]{1,0:T(8,128)S(1)} %get-tuple-element.28.basis_ref, f32[32,32]{1,0:T(8,128)S(1)} %get-tuple-element.29.inverse_ref, f32[16,256]{1,0:T(8,128)S(1)} %add.27.mine_ref, ...), custom_call_target="tpu_custom_call" | custom-call | flops 33554432 | bytes 3145728 | tf_op jit(solution)/shard_map/error_next/pallas_call | solution.py:341
  (9 shorter events, 0.1 us)
Async XLA Ops:
  3.0 1.5 %collective-permute-start = (f32[2,16,1024]{2,1,0:T(8,128)S(1)}, f32[2,16,1024]{2,1,0:T(8,128)S(1)}, u32[]{:S(2)}, u32[]{:S(2)}) collective-permute-start(f32[2,16,1024]{2,1,0:T(8,128)S(1)} %get-tuple-element.18), channel_id=1, source_target_pairs={{0,1},{1,0},{2,3},{3,2},{4,5},{5,4},{6,7},{7,6},{8,9},{9,8},{10,11... | collective-permute-start | bytes 393224 | tf_op jit(solution)/shard_map/ppermute | solution.py:22
  7.3 19.7 %collective-permute-start.5 = (f32[2048,256]{1,0:T(8,128)S(1)}, f32[2048,256]{1,0:T(8,128)S(1)}, u32[]{:S(2)}, u32[]{:S(2)}) collective-permute-start(f32[2048,256]{1,0:T(8,128)S(1)} %merge.1.mine_ref.merged_ref), channel_id=1, source_target_pairs={{0,1},{1,0},{2,3},{3,2},{4,5},{5,4},{6,7},{7,6},{8,9},{9,8},{10,11... | collective-permute-start | bytes 6291464 | tf_op jit(solution)/shard_map/ppermute | solution.py:22
  7.7 5.3 %collective-permute-start.1 = (f32[16,1024]{1,0:T(8,128)S(1)}, f32[16,1024]{1,0:T(8,128)S(1)}, u32[]{:S(2)}, u32[]{:S(2)}) collective-permute-start(f32[16,1024]{1,0:T(8,128)S(1)} %slice_bitcast_fusion), channel_id=1, source_target_pairs={{0,2},{2,0},{1,3},{3,1},{4,6},{6,4},{5,7},{7,5},{8,10},{10,8},{9,1... | collective-permute-start | bytes 196616 | tf_op jit(solution)/shard_map/ppermute | solution.py:22
  13.0 4.3 %collective-permute-start.2 = (f32[16,1024]{1,0:T(8,128)S(1)}, f32[16,1024]{1,0:T(8,128)S(1)}, u32[]{:S(2)}, u32[]{:S(2)}) collective-permute-start(f32[16,1024]{1,0:T(8,128)S(1)} %fusion), channel_id=1, source_target_pairs={{0,4},{4,0},{8,12},{12,8},{1,5},{5,1},{9,13},{13,9},{2,6},{6,2},{1... | collective-permute-start | bytes 196616 | tf_op jit(solution)/shard_map/ppermute | solution.py:22
  17.3 5.2 %collective-permute-start.3 = (f32[16,1024]{1,0:T(8,128)S(1)}, f32[16,1024]{1,0:T(8,128)S(1)}, u32[]{:S(2)}, u32[]{:S(2)}) collective-permute-start(f32[16,1024]{1,0:T(8,128)S(1)} %add.23), channel_id=1, source_target_pairs={{0,8},{4,12},{8,0},{12,4},{1,9},{5,13},{9,1},{13,5},{2,10},{6,14},... | collective-permute-start | bytes 196616 | tf_op jit(solution)/shard_map/ppermute | solution.py:22
  22.5 4.3 %collective-permute-start.4 = (f32[16,1024]{1,0:T(8,128)S(1)}, f32[16,1024]{1,0:T(8,128)S(1)}, u32[]{:S(2)}, u32[]{:S(2)}) collective-permute-start(f32[16,1024]{1,0:T(8,128)S(1)} %add.24.near_ref), channel_id=1, source_target_pairs={{0,2},{2,0},{1,3},{3,1},{4,6},{6,4},{5,7},{7,5},{8,10},{10,8},{9,1... | collective-permute-start | bytes 196616 | tf_op jit(solution)/shard_map/ppermute | solution.py:22
  26.9 3.0 %collective-permute-start.7 = (f32[2,16,1024]{2,1,0:T(8,128)S(1)}, f32[2,16,1024]{2,1,0:T(8,128)S(1)}, u32[]{:S(2)}, u32[]{:S(2)}) collective-permute-start(f32[2,16,1024]{2,1,0:T(8,128)S(1)} %pad_maximum_fusion.mine_ref), channel_id=1, source_target_pairs={{0,1},{1,0},{2,3},{3,2},{4,5},{5,4},{6,7},{7,6},{8,9},{9,8},{10,11... | collective-permute-start | bytes 393224 | tf_op jit(solution)/shard_map/ppermute | solution.py:22
  28.0 4.4 %collective-permute-start.6 = (f32[16,256]{1,0:T(8,128)S(1)}, f32[16,256]{1,0:T(8,128)S(1)}, u32[]{:S(2)}, u32[]{:S(2)}) collective-permute-start(f32[16,256]{1,0:T(8,128)S(1)} %product.1), channel_id=1, source_target_pairs={{0,2},{2,0},{1,3},{3,1},{4,6},{6,4},{5,7},{7,5},{8,10},{10,8},{9,1... | collective-permute-start | bytes 49160 | tf_op jit(solution)/shard_map/ppermute | solution.py:22
  32.5 3.8 %collective-permute-start.8 = (f32[16,256]{1,0:T(8,128)S(1)}, f32[16,256]{1,0:T(8,128)S(1)}, u32[]{:S(2)}, u32[]{:S(2)}) collective-permute-start(f32[16,256]{1,0:T(8,128)S(1)} %add.25), channel_id=1, source_target_pairs={{0,4},{4,0},{8,12},{12,8},{1,5},{5,1},{9,13},{13,9},{2,6},{6,2},{1... | collective-permute-start | bytes 49160 | tf_op jit(solution)/shard_map/ppermute | solution.py:22
  36.3 4.6 %collective-permute-start.9 = (f32[16,256]{1,0:T(8,128)S(1)}, f32[16,256]{1,0:T(8,128)S(1)}, u32[]{:S(2)}, u32[]{:S(2)}) collective-permute-start(f32[16,256]{1,0:T(8,128)S(1)} %add.26), channel_id=1, source_target_pairs={{0,8},{4,12},{8,0},{12,4},{1,9},{5,13},{9,1},{13,5},{2,10},{6,14},... | collective-permute-start | bytes 49160 | tf_op jit(solution)/shard_map/ppermute | solution.py:22
  40.9 1.2 %collective-permute-start.10 = (f32[16,256]{1,0:T(8,128)S(1)}, f32[16,256]{1,0:T(8,128)S(1)}, u32[]{:S(2)}, u32[]{:S(2)}) collective-permute-start(f32[16,256]{1,0:T(8,128)S(1)} %add.27.mine_ref), channel_id=1, source_target_pairs={{0,1},{1,0},{2,3},{3,2},{4,5},{5,4},{6,7},{7,6},{8,9},{9,8},{10,11... | collective-permute-start | bytes 49160 | tf_op jit(solution)/shard_map/ppermute | solution.py:22

commit v9 on v8

--- a/solution.py
+++ b/solution.py
@@ -12,23 +12,43 @@
 VMEM_BYTES = 24 * 1024 * 1024
 CHUNK = 256
 GROUP = 4
+PARTS = 4
 BF16, F32 = jnp.bfloat16, jnp.float32
 HBM = pl.BlockSpec(memory_space=pltpu.HBM)
 ANY = pl.BlockSpec(memory_space=pl.ANY)
 VMEM = pl.BlockSpec(memory_space=pltpu.VMEM)
 
 
-def swapped(value, axis, size, bit):
-    return lax.ppermute(value, axis, [(i, i ^ bit) for i in range(size)])
+def bits_of(axis, size):
+    assert size > 1 and size & (size - 1) == 0
+    return [(axis, 1 << i) for i in range(size.bit_length() - 1)]
+
+
+def swapped(value, sizes, ways):
+    pairs = []
+    for dp in range(sizes["dp"]):
+        for sub in range(sizes["sub"]):
+            for pair in range(2):
+                here = {"dp": dp, "sub": sub, "pair": pair}
+                axis, bit = ways[pair]
+                there = {**here, axis: here[axis] ^ bit}
+                pairs.append(tuple(
+                    (c["dp"] * sizes["sub"] + c["sub"]) * 2 + c["pair"] for c in (here, there)))
+    return lax.ppermute(value, AXES, pairs)
 
 
 def across(value):
-    return swapped(value, "pair", 2, 1)
-
-
-def bits_of(axis, size):
-    assert size & (size - 1) == 0
-    return [(axis, size, 1 << i) for i in range(size.bit_length() - 1)]
+    return lax.ppermute(value, "pair", [(0, 1), (1, 0)])
+
+
+def sides():
+    sub, dp = lax.axis_index("sub") & 1, lax.axis_index("dp") & 1
+    pair = lax.axis_index("pair")
+    return sub + pair * (dp - sub), dp + pair * (sub - dp)
+
+
+def half_of(chosen, piece, start=0, size=None):
+    return pl.ds(pl.multiple_of(chosen * piece + start, CHUNK), size or piece)
 
 
 def parts_of(value, count):
@@ -91,16 +111,12 @@
             part = pl.ds(i * CHUNK, CHUNK)
             term_ref[:, part] += added(dot(own, x_ref[rows, part], ((1,), (0,))), rank)
     low = lax.axis_index("pair") == 0
+    mine, other = sides()
     for i in range(2):
-        part = side(i, piece)
-        top, bottom = term_ref[:half, part], term_ref[half:, part]
-        keep_ref[i] = jnp.where(low, top, bottom)
-        send_ref[i] = jnp.where(low, bottom, top)
-
-
-def side(i, piece, start=0, size=None):
-    chosen = (lax.axis_index("sub") & 1) ^ i
-    return pl.ds(pl.multiple_of(chosen * piece + start, CHUNK), size or piece)
+        part = half_of(mine ^ i, piece)
+        keep_ref[i] = jnp.where(low, term_ref[:half, part], term_ref[half:, part])
+        part = half_of(other ^ i, piece)
+        send_ref[i] = jnp.where(low, term_ref[half:, part], term_ref[:half, part])
 
 
 def added(stack, rank):
@@ -133,71 +149,83 @@
     )(inputs, cotangent, error_prev, seed_q)
 
 
-def merge_kernel(x_hbm, c_hbm, e_hbm, after_hbm, merged_ref, x_ref, c_ref, e_ref, sems):
-    copies = whole_copies([(c_hbm, c_ref), (x_hbm, x_ref), (e_hbm.at[0], e_ref)], sems)
+def merge_kernel(index, x_hbm, c_hbm, e_hbm, after_hbm, merged_ref, x_ref, c_ref, e_ref, sems):
+    size = merged_ref.shape[0]
+    rows = pl.ds(index * size, size)
+    copies = whole_copies(
+        [(c_hbm, c_ref), (x_hbm.at[:, rows], x_ref), (e_hbm.at[0, rows, :], e_ref)], sems)
     for copy in copies:
         copy.start()
     for copy in copies:
         copy.wait()
-    for i in range(merged_ref.shape[0] // CHUNK):
+    for i in range(size // CHUNK):
         part = pl.ds(i * CHUNK, CHUNK)
         merged_ref[part, :] = (
             dot(x_ref[:, part], c_ref[...], ((0,), (0,))) + e_ref[part, :].astype(F32))
 
 
-def merge(inputs, cotangent, error_prev, after):
+def merge(inputs, cotangent, error_prev, after, index):
     tokens, width = inputs.shape
-    out = cotangent.shape[1]
-    return pl.pallas_call(
-        merge_kernel,
+    size, out = width // PARTS, cotangent.shape[1]
+    return pl.pallas_call(
+        functools.partial(merge_kernel, index),
         in_specs=[HBM] * 3 + [ANY],
         out_specs=VMEM,
-        out_shape=jax.ShapeDtypeStruct((width, out), F32),
+        out_shape=jax.ShapeDtypeStruct((size, out), F32),
         scratch_shapes=[
-            pltpu.VMEM((tokens, width), BF16),
+            pltpu.VMEM((tokens, size), BF16),
             pltpu.VMEM((tokens, out), BF16),
-            pltpu.VMEM((width, out), BF16),
+            pltpu.VMEM((size, out), BF16),
             pltpu.SemaphoreType.DMA((3,)),
         ],
         compiler_params=params(),
-        cost_estimate=cost(10 ** 9, 10 ** 7),
+        cost_estimate=cost(10 ** 8 // PARTS, 10 ** 6 // PARTS),
         name="merge",
     )(inputs, cotangent, error_prev, after)
 
 
-def product_kernel(near_ref, far_ref, mine_ref, other_hbm, product_ref, other_ref, sems):
+def product_kernel(near_ref, far_ref, *refs):
+    mine_refs, other_hbms = refs[:PARTS], refs[PARTS:2 * PARTS]
+    product_ref, other_ref, sems = refs[2 * PARTS:]
     half, piece = near_ref.shape
-    per = piece // CHUNK
-    parts = [side(i, piece, j * CHUNK, CHUNK) for i in range(2) for j in range(per)]
-    copies = whole_copies([(other_hbm.at[part, :], other_ref.at[part, :]) for part in parts], sems)
+    size = mine_refs[0].shape[0]
+    copies = whole_copies(
+        [(other, other_ref.at[pl.ds(i * size, size), :]) for i, other in enumerate(other_hbms)],
+        sems)
     for copy in copies:
         copy.start()
+    straight = sides()[0] == 0
     product = None
-    for i, part in enumerate(parts):
-        rows_ref = near_ref if i < per else far_ref
-        rows = rows_ref[:, (i % per) * CHUNK:(i % per + 1) * CHUNK]
+    for i in range(2 * piece // CHUNK):
+        start = i * CHUNK
+        part = slice(start % piece, start % piece + CHUNK)
+        near, far = near_ref[:, part], far_ref[:, part]
+        rows = jnp.where(straight, near, far) if start < piece else jnp.where(straight, far, near)
         f_high, f_low = parts_of(rows, 2)
         both = jnp.concatenate([f_high, f_low], axis=0)
-        copies[i].wait()
-        m_high, m_low = parts_of(mine_ref[part, :] + other_ref[part, :], 2)
+        if start % size == 0:
+            copies[start // size].wait()
+        merged = (mine_refs[start // size][start % size:start % size + CHUNK, :]
+                  + other_ref[start:start + CHUNK, :])
+        m_high, m_low = parts_of(merged, 2)
         term = added(dot(both, m_high, ((1,), (0,))), half) + dot(f_high, m_low, ((1,), (0,)))
         product = term if product is None else product + term
     product_ref[...] = product
 
 
 def product_of(near, far, mine, other):
-    half = near.shape[0]
-    width, out = mine.shape
+    half, piece = near.shape
+    out = mine[0].shape[1]
+    width = 2 * piece
     return pl.pallas_call(
         product_kernel,
-        in_specs=[VMEM, VMEM, VMEM, ANY],
+        in_specs=[VMEM] * (2 + PARTS) + [ANY] * PARTS,
         out_shape=jax.ShapeDtypeStruct((half, out), F32),
-        scratch_shapes=[
-            pltpu.VMEM((width, out), F32), pltpu.SemaphoreType.DMA((width // CHUNK,))],
+        scratch_shapes=[pltpu.VMEM((width, out), F32), pltpu.SemaphoreType.DMA((PARTS,))],
         compiler_params=params(),
         cost_estimate=cost(2 * half * width * out, 8 * width * out),
         name="product",
-    )(near, far, mine, other)
+    )(near, far, *mine, *other)
 
 
 def both_halves(mine, other):
@@ -253,11 +281,12 @@
     half, piece = mine_ref.shape[1:]
     rank = 2 * half
     blocks = None
+    mine, other = sides()
     for i in range(2):
         for j in range(piece // CHUNK):
             part = slice(j * CHUNK, (j + 1) * CHUNK)
-            rows = both_halves(mine_ref[i, :, part], other_ref[i, :, part])
-            rows_ref[:, side(i, piece, j * CHUNK, CHUNK)] = rows
+            rows = both_halves(mine_ref[i, :, part], other_ref[i ^ mine ^ other, :, part])
+            rows_ref[:, half_of(mine ^ i, piece, j * CHUNK, CHUNK)] = rows
             term = gram_blocks(rows)
             blocks = term if blocks is None else blocks + term
     step = inverse_factor(gram_of(blocks, rank))
@@ -288,11 +317,16 @@
     )(mine, other)
 
 
-def second_sweep_kernel(rows_ref, step_ref, gram_ref, basis_ref, inverse_ref):
+def second_sweep_kernel(rows_ref, step_ref, gram_ref, basis_ref, inverse_ref, lefts_ref):
     last = inverse_factor(gram_ref[...])
+    rank = last.shape[0]
     for i in range(rows_ref.shape[1] // CHUNK):
         part = slice(i * CHUNK, (i + 1) * CHUNK)
-        basis_ref[:, part] = short_dot(last, rows_ref[:, part])
+        basis = short_dot(last, rows_ref[:, part])
+        basis_ref[:, part] = basis
+        high, low = parts_of(basis, 2)
+        zeros = jnp.zeros((lefts_ref.shape[1] - 3 * rank, CHUNK), BF16)
+        lefts_ref[part, :] = jnp.concatenate([high, high, low, zeros], axis=0).T
     inverse_ref[...] = short_dot(last, step_ref[...])
 
 
@@ -302,6 +336,7 @@
         out_shape=[
             jax.ShapeDtypeStruct(rows.shape, F32),
             jax.ShapeDtypeStruct(step.shape, F32),
+            jax.ShapeDtypeStruct((rows.shape[1], 128), BF16),
         ],
         compiler_params=params(),
         cost_estimate=cost(10 ** 9, 7 * 10 ** 6),
@@ -309,24 +344,25 @@
     )(rows, step, gram)
 
 
-def error_kernel(workers, steps, merged_ref, basis_ref, inverse_ref, mine_ref, other_ref,
-                 error_hbm, basis_hbm, second_ref, error_ref, error_sem, basis_sem):
-    width = merged_ref.shape[0]
-    block = width // steps
+def error_kernel(workers, basis_ref, lefts_ref, inverse_ref, mine_ref, other_ref, *refs):
+    merged_refs = refs[:PARTS]
+    error_hbm, basis_hbm, second_ref, error_ref, error_sem, basis_sem = refs[PARTS:]
+    size = merged_refs[0].shape[0]
     keep = pltpu.make_async_copy(basis_ref, basis_hbm, basis_sem)
     keep.start()
     product = both_halves(mine_ref[...], other_ref[...])
     second = short_dot(inverse_ref[...], product) * (1.0 / workers)
     second_ref[...] = second
-    s_high, s_low = parts_of(second, 2)
-    rights = jnp.concatenate([s_high, s_low, s_high], axis=0)
+    high, low = parts_of(second, 2)
+    zeros = jnp.zeros((lefts_ref.shape[1] - 3 * high.shape[0], high.shape[1]), BF16)
+    rights = jnp.concatenate([high, low, high, zeros], axis=0)
     copies = []
-    for i in range(steps):
-        part = pl.ds(i * block, block)
-        b_high, b_low = parts_of(basis_ref[:, part], 2)
-        lefts = jnp.concatenate([b_high, b_high, b_low], axis=0)
-        approx = dot(lefts, rights, ((0,), (0,)))
-        error_ref[part, :] = (merged_ref[part, :] - approx).astype(BF16)
+    for i in range(lefts_ref.shape[0] // CHUNK):
+        start = i * CHUNK
+        part = pl.ds(start, CHUNK)
+        approx = dot(lefts_ref[part, :], rights, ((1,), (0,)))
+        merged = merged_refs[start // size][start % size:start % size + CHUNK, :]
+        error_ref[part, :] = (merged - approx).astype(BF16)
         copies.append(pltpu.make_async_copy(
             error_ref.at[part, :], error_hbm.at[0, part, :], error_sem.at[i]))
         copies[i].start()
@@ -334,13 +370,12 @@
         copy.wait()
 
 
-def error_of(merged, basis, inverse, mine, other, workers):
-    width, out = merged.shape
-    rank = basis.shape[0]
-    steps = width // CHUNK
-    return pl.pallas_call(
-        functools.partial(error_kernel, workers, steps),
-        in_specs=[VMEM] * 5,
+def error_of(merged, basis, lefts, inverse, mine, other, workers):
+    rank, width = basis.shape
+    out = mine.shape[1]
+    return pl.pallas_call(
+        functools.partial(error_kernel, workers),
+        in_specs=[VMEM] * (5 + PARTS),
         out_specs=[HBM, HBM, VMEM],
         out_shape=[
             jax.ShapeDtypeStruct((1, width, out), BF16),
@@ -349,53 +384,55 @@
         ],
         scratch_shapes=[
             pltpu.VMEM((width, out), BF16),
-            pltpu.SemaphoreType.DMA((steps,)),
+            pltpu.SemaphoreType.DMA((width // CHUNK,)),
             pltpu.SemaphoreType.DMA,
         ],
         compiler_params=params(),
         cost_estimate=cost(2 * rank * width * out, 6 * width * out),
         name="error_next",
-    )(merged, basis, inverse, mine, other)
+    )(basis, lefts, inverse, mine, other, *merged)
 
 
 def local(sizes, *arguments):
     inputs, cotangent, error_prev, seed_q = (
         pltpu.with_memory_space_constraint(value, pltpu.HBM) for value in arguments)
-    beside = ("sub", sizes["sub"], 1)
-    rounds = bits_of("sub", sizes["sub"]) + bits_of("dp", sizes["dp"])
+    sub, dp = bits_of("sub", sizes["sub"]), bits_of("dp", sizes["dp"])
+    rounds = list(zip(sub[:1] + dp + sub[1:], dp + sub))
     workers = 2 * sizes["sub"] * sizes["dp"]
 
     keep, send = term_halves(inputs, cotangent, error_prev, seed_q)
     part = keep + across(send)
-    merged = merge(inputs, cotangent, error_prev, part)
-    merged_other = across(merged)
-    near = part[0] + swapped(part[1], *beside)
-    for axis_bit in rounds[1:]:
-        near = near + swapped(near, *axis_bit)
-    far = swapped(near, *beside)
+    near = part[0] + swapped(part[1], sizes, rounds[0])
+    merged = [
+        merge(inputs, cotangent, error_prev, part if i < PARTS // 2 else near, i)
+        for i in range(PARTS)]
+    merged_other = [across(rows) for rows in merged]
+    for ways in rounds[1:]:
+        near = near + swapped(near, sizes, ways)
+    far = swapped(near, sizes, rounds[0])
     mine = jnp.stack([near, far])
     other = across(mine)
 
     product = product_of(near, far, merged, merged_other)
     rows, step, gram = first_sweep(mine, other)
-    product = product + swapped(product, *rounds[0])
+    product = product + swapped(product, sizes, rounds[0])
     product, rows, step, gram = lax.optimization_barrier((product, rows, step, gram))
-    basis, inverse = second_sweep(rows, step, gram)
-    for i, axis_bit in enumerate(rounds[1:]):
-        product = product + swapped(product, *axis_bit)
+    basis, inverse, lefts = second_sweep(rows, step, gram)
+    for i, ways in enumerate(rounds[1:]):
+        product = product + swapped(product, sizes, ways)
         if i == 0:
-            product, basis, inverse = lax.optimization_barrier((product, basis, inverse))
+            product, basis, inverse, lefts = lax.optimization_barrier(
+                (product, basis, inverse, lefts))
     product_other = across(product)
-    error_next, basis, second = error_of(merged, basis, inverse, product, product_other, workers)
-    return (error_next, basis, second)
+    return error_of(merged, basis, lefts, inverse, product, product_other, workers)
 
 
 def solution(mesh):
     sizes = {axis: mesh.shape[axis] for axis in AXES}
-    assert sizes["pair"] == 2 and sizes["sub"] > 1
+    assert sizes["pair"] == 2
 
     def run(*args):
-        return local(sizes, *args)
+        return tuple(local(sizes, *args))
 
     return jax.shard_map(
         run,

time: 44.3 us -> 46.4 us (1.047)
  Pallas kernels: 12.4 us -> 16.1 us
  starting transfers between devices: 16.5 us -> 13.3 us
  waiting for transfers between devices: 14.5 us -> 16 us
    pallas_call x3 -> x6, Pallas kernels: 5.86 us -> 9.43 us  [the longest x4 6.29 us: merge(): pl.pallas_call(functools.partial(merge_kernel, index), in_specs=[HBM] * 3...]
    ppermute x11 -> x14, starting transfers between devices: 16.5 us -> 13.3 us  [the longest x7 11.5 us: swapped(): return lax.ppermute(value, AXES, pairs)]
    ppermute x11 -> x14, waiting for transfers between devices: 14.5 us -> 16 us  [the longest x7 13.8 us: swapped(): return lax.ppermute(value, AXES, pairs)]
  transfers between devices with their start and end apart: 11 -> 14, of which waited for: 8 -> 8; matrix products, arithmetic and copies ran while one was open for 0% -> 0% of each run, Pallas kernels for 12% -> 25%
where the time goes in v9:
time: 46.4 us; the launch traced here: 46.2 us
  Pallas kernels  16.1 us (35%)
  waiting for transfers between devices  16 us (34%)
  starting transfers between devices  13.3 us (29%)
  between operations  0.78 us (2%)
    ppermute x7, waiting for transfers between devices, swapped(): return lax.ppermute(value, AXES, pairs)  13.8 us
    ppermute x7, starting transfers between devices, swapped(): return lax.ppermute(value, AXES, pairs)  11.5 us
    pallas_call x4, Pallas kernels, merge(): pl.pallas_call(functools.partial(merge_kernel, index), in_specs=[HBM] * 3...  6.29 us
    pallas_call x1, Pallas kernels, first_sweep(): pl.pallas_call(first_sweep_kernel, out_shape=[jax.ShapeDtypeStruct((rank,...  2.56 us
    pallas_call x1, Pallas kernels, term_halves(): pl.pallas_call(term_kernel, in_specs=[HBM] * 4, out_specs=[VMEM] * 2, out...  2.34 us
    ppermute x7, waiting for transfers between devices, across(): return lax.ppermute(value, 'pair', [(0, 1), (1, 0)])  2.18 us
    pallas_call x1, Pallas kernels, error_of(): pl.pallas_call(functools.partial(error_kernel, workers), in_specs=[VMEM]...  2.14 us
    ppermute x7, starting transfers between devices, across(): return lax.ppermute(value, 'pair', [(0, 1), (1, 0)])  1.79 us
  transfers between devices with their start and end apart: 14, of which 8 were waited for; matrix products, arithmetic and copies ran while one was open for 0% of the time, Pallas kernels for 25%

profile of v9, /device:TPU:0, one launch (start us, length us, event | category | flops | bytes accessed | tf_op | source)
XLA Modules:
  0.0 46.2 jit_solution(16118118037723313739)
XLA Ops:
  0.6 2.3 %term.1 = (f32[2,16,1024]{2,1,0:T(8,128)S(1)}, f32[2,16,1024]{2,1,0:T(8,128)S(1)}) custom-call(bf16[512,2048]{1,0:T(8,128)(2,1)} %x_hbm.9, bf16[512,256]{1,0:T(8,128)(2,1)} %c_hbm.9, bf16[1,2048,256]{2,1,0:T(8,128)(2,1)} %e_hbm.9, f32[32,256]{1,0:T(8,128)} %seed_hbm.1), custom_call_target="tpu_custom_call" | custom-call | flops 201326592 | bytes 3145728 | tf_op jit(solution)/shard_map/term/pallas_call | solution.py:133
  3.0 0.5 %collective-permute-start = (f32[2,16,1024]{2,1,0:T(8,128)S(1)}, f32[2,16,1024]{2,1,0:T(8,128)S(1)}, u32[]{:S(2)}, u32[]{:S(2)}) collective-permute-start(f32[2,16,1024]{2,1,0:T(8,128)S(1)} %get-tuple-element.20), channel_id=1, source_target_pairs={{0,1},{1,0},{2,3},{3,2},{4,5},{5,4},{6,7},{7,6},{8,9},{9,8},{10,11... | collective-permute-start | bytes 393224 | tf_op jit(solution)/shard_map/ppermute | solution.py:41
  3.5 1.0 %collective-permute-done = f32[2,16,1024]{2,1,0:T(8,128)S(1)} collective-permute-done((f32[2,16,1024]{2,1,0:T(8,128)S(1)}, f32[2,16,1024]{2,1,0:T(8,128)S(1)}, u32[]{:S(2)}, u32[]{:S(2)}) %collective-permute-start) | collective-permute-done | bytes 131104 | tf_op jit(solution)/shard_map/ppermute | solution.py:41
  4.5 2.9 %collective-permute-start.1 = (f32[16,1024]{1,0:T(8,128)S(1)}, f32[16,1024]{1,0:T(8,128)S(1)}, u32[]{:S(2)}, u32[]{:S(2)}) collective-permute-start(f32[16,1024]{1,0:T(8,128)S(1)} %slice_bitcast_fusion), channel_id=1, source_target_pairs={{0,2},{1,5},{2,0},{3,7},{4,6},{5,1},{6,4},{7,3},{8,10},{9,13},{10,... | collective-permute-start | bytes 196616 | tf_op jit(solution)/shard_map/ppermute | solution.py:37
  7.4 1.6 %merge.4.refs_0_ = f32[512,256]{1,0:T(8,128)S(1)} custom-call(bf16[512,2048]{1,0:T(8,128)(2,1)} %x_hbm.9, bf16[512,256]{1,0:T(8,128)(2,1)} %c_hbm.9, bf16[1,2048,256]{2,1,0:T(8,128)(2,1)} %e_hbm.9, f32[2,16,1024]{2,1,0:T(8,128)S(1)} %add.21.after_hbm), custom_call_target="tpu_custom_call" | custom-call | flops 25000000 | bytes 250000 | tf_op jit(solution)/shard_map/merge/pallas_call | solution.py:170
  9.0 0.1 collective-permute-start.5
  9.1 1.6 %merge.5.refs_1_ = f32[512,256]{1,0:T(8,128)S(1)} custom-call(bf16[512,2048]{1,0:T(8,128)(2,1)} %x_hbm.9, bf16[512,256]{1,0:T(8,128)(2,1)} %c_hbm.9, bf16[1,2048,256]{2,1,0:T(8,128)(2,1)} %e_hbm.9, f32[2,16,1024]{2,1,0:T(8,128)S(1)} %add.21.after_hbm), custom_call_target="tpu_custom_call" | custom-call | flops 25000000 | bytes 250000 | tf_op jit(solution)/shard_map/merge/pallas_call | solution.py:170
  10.7 0.6 %collective-permute-start.6 = (f32[512,256]{1,0:T(8,128)S(1)}, f32[512,256]{1,0:T(8,128)S(1)}, u32[]{:S(2)}, u32[]{:S(2)}) collective-permute-start(f32[512,256]{1,0:T(8,128)S(1)} %merge.5.refs_1_), channel_id=1, source_target_pairs={{0,1},{1,0},{2,3},{3,2},{4,5},{5,4},{6,7},{7,6},{8,9},{9,8},{10,11... | collective-permute-start | bytes 1572872 | tf_op jit(solution)/shard_map/ppermute | solution.py:41
  11.2 0.0 collective-permute-done.1
  11.2 1.6 %merge.6.refs_2_ = f32[512,256]{1,0:T(8,128)S(1)} custom-call(bf16[512,2048]{1,0:T(8,128)(2,1)} %x_hbm.9, bf16[512,256]{1,0:T(8,128)(2,1)} %c_hbm.9, bf16[1,2048,256]{2,1,0:T(8,128)(2,1)} %e_hbm.9, f32[16,1024]{1,0:T(8,128)S(1)} %fusion.after_hbm), custom_call_target="tpu_custom_call" | custom-call | flops 25000000 | bytes 250000 | tf_op jit(solution)/shard_map/merge/pallas_call | solution.py:170
  12.8 1.6 %merge.7.refs_3_ = f32[512,256]{1,0:T(8,128)S(1)} custom-call(bf16[512,2048]{1,0:T(8,128)(2,1)} %x_hbm.9, bf16[512,256]{1,0:T(8,128)(2,1)} %c_hbm.9, bf16[1,2048,256]{2,1,0:T(8,128)(2,1)} %e_hbm.9, f32[16,1024]{1,0:T(8,128)S(1)} %fusion.after_hbm), custom_call_target="tpu_custom_call" | custom-call | flops 25000000 | bytes 250000 | tf_op jit(solution)/shard_map/merge/pallas_call | solution.py:170
  14.4 0.1 collective-permute-start.7
  14.5 0.5 %collective-permute-start.8 = (f32[512,256]{1,0:T(8,128)S(1)}, f32[512,256]{1,0:T(8,128)S(1)}, u32[]{:S(2)}, u32[]{:S(2)}) collective-permute-start(f32[512,256]{1,0:T(8,128)S(1)} %merge.7.refs_3_), channel_id=1, source_target_pairs={{0,1},{1,0},{2,3},{3,2},{4,5},{5,4},{6,7},{7,6},{8,9},{9,8},{10,11... | collective-permute-start | bytes 1572872 | tf_op jit(solution)/shard_map/ppermute | solution.py:41
  15.0 1.6 %collective-permute-start.2 = (f32[16,1024]{1,0:T(8,128)S(1)}, f32[16,1024]{1,0:T(8,128)S(1)}, u32[]{:S(2)}, u32[]{:S(2)}) collective-permute-start(f32[16,1024]{1,0:T(8,128)S(1)} %fusion.after_hbm), channel_id=1, source_target_pairs={{0,4},{1,9},{2,6},{3,11},{4,0},{5,13},{6,2},{7,15},{8,12},{9,1},{1... | collective-permute-start | bytes 196616 | tf_op jit(solution)/shard_map/ppermute | solution.py:37
  16.6 3.4 %collective-permute-done.2 = f32[16,1024]{1,0:T(8,128)S(1)} collective-permute-done((f32[16,1024]{1,0:T(8,128)S(1)}, f32[16,1024]{1,0:T(8,128)S(1)}, u32[]{:S(2)}, u32[]{:S(2)}) %collective-permute-start.2) | collective-permute-done | bytes 65568 | tf_op jit(solution)/shard_map/ppermute | solution.py:37
  20.0 2.0 %collective-permute-start.3 = (f32[16,1024]{1,0:T(8,128)S(1)}, f32[16,1024]{1,0:T(8,128)S(1)}, u32[]{:S(2)}, u32[]{:S(2)}) collective-permute-start(f32[16,1024]{1,0:T(8,128)S(1)} %add.23), channel_id=1, source_target_pairs={{0,8},{1,3},{2,10},{3,1},{4,12},{5,7},{6,14},{7,5},{8,0},{9,11},{1... | collective-permute-start | bytes 196616 | tf_op jit(solution)/shard_map/ppermute | solution.py:37
  21.9 3.3 %collective-permute-done.3 = f32[16,1024]{1,0:T(8,128)S(1)} collective-permute-done((f32[16,1024]{1,0:T(8,128)S(1)}, f32[16,1024]{1,0:T(8,128)S(1)}, u32[]{:S(2)}, u32[]{:S(2)}) %collective-permute-start.3) | collective-permute-done | bytes 65568 | tf_op jit(solution)/shard_map/ppermute | solution.py:37
  25.2 0.7 %collective-permute-start.4 = (f32[16,1024]{1,0:T(8,128)S(1)}, f32[16,1024]{1,0:T(8,128)S(1)}, u32[]{:S(2)}, u32[]{:S(2)}) collective-permute-start(f32[16,1024]{1,0:T(8,128)S(1)} %add.24.near_ref), channel_id=1, source_target_pairs={{0,2},{1,5},{2,0},{3,7},{4,6},{5,1},{6,4},{7,3},{8,10},{9,13},{10,... | collective-permute-start | bytes 196616 | tf_op jit(solution)/shard_map/ppermute | solution.py:37
  25.9 3.7 %collective-permute-done.4.far_ref = f32[16,1024]{1,0:T(8,128)S(1)} collective-permute-done((f32[16,1024]{1,0:T(8,128)S(1)}, f32[16,1024]{1,0:T(8,128)S(1)}, u32[]{:S(2)}, u32[]{:S(2)}) %collective-permute-start.4) | collective-permute-done | bytes 65568 | tf_op jit(solution)/shard_map/ppermute | solution.py:37
  29.6 0.1 collective-permute-start.10
  29.6 0.0 collective-permute-done.5.refs_4_
  29.6 0.0 collective-permute-done.6.refs_5_
  29.7 0.0 collective-permute-done.7.refs_6_
  29.7 0.0 collective-permute-done.8.refs_7_
  29.7 1.0 %product.1 = f32[16,256]{1,0:T(8,128)S(1)} custom-call(f32[16,1024]{1,0:T(8,128)S(1)} %add.24.near_ref, f32[16,1024]{1,0:T(8,128)S(1)} %collective-permute-done.4.far_ref, f32[512,256]{1,0:T(8,128)S(1)} %merge.4.refs_0_, f32[512,256]{1,0:T(8,128)S(1)} %merge.5.refs_1_, f32[512,256]{1,0:T(8,128)S(1)} %merge.6.refs_2_, f32[512,256]{1,0:T(8,128)S(1)} %merge.7.refs_3_, ...), custom_call_target="tpu_custom_call" | custom-call | flops 16777216 | bytes 4194304 | tf_op jit(solution)/shard_map/product/pallas_call | solution.py:220
  30.7 0.7 %collective-permute-start.9 = (f32[16,256]{1,0:T(8,128)S(1)}, f32[16,256]{1,0:T(8,128)S(1)}, u32[]{:S(2)}, u32[]{:S(2)}) collective-permute-start(f32[16,256]{1,0:T(8,128)S(1)} %product.1), channel_id=1, source_target_pairs={{0,2},{1,5},{2,0},{3,7},{4,6},{5,1},{6,4},{7,3},{8,10},{9,13},{10,... | collective-permute-start | bytes 49160 | tf_op jit(solution)/shard_map/ppermute | solution.py:37
  31.4 0.0 collective-permute-done.10.other_ref
  31.4 2.6 %first_sweep.1 = (f32[32,2048]{1,0:T(8,128)S(1)}, f32[32,32]{1,0:T(8,128)S(1)}, f32[32,32]{1,0:T(8,128)S(1)}) custom-call(f32[2,16,1024]{2,1,0:T(8,128)S(1)} %pad_maximum_fusion.mine_ref, f32[2,16,1024]{2,1,0:T(8,128)S(1)} %collective-permute-done.10.other_ref), custom_call_target="tpu_custom_call" | custom-call | flops 1000000000 | bytes 7000000 | tf_op jit(solution)/shard_map/first_sweep/pallas_call | solution.py:307
  33.9 0.6 %collective-permute-done.9 = f32[16,256]{1,0:T(8,128)S(1)} collective-permute-done((f32[16,256]{1,0:T(8,128)S(1)}, f32[16,256]{1,0:T(8,128)S(1)}, u32[]{:S(2)}, u32[]{:S(2)}) %collective-permute-start.9) | collective-permute-done | bytes 16416 | tf_op jit(solution)/shard_map/ppermute | solution.py:37
  34.5 1.5 %collective-permute-start.11 = (f32[16,256]{1,0:T(8,128)S(1)}, f32[16,256]{1,0:T(8,128)S(1)}, u32[]{:S(2)}, u32[]{:S(2)}) collective-permute-start(f32[16,256]{1,0:T(8,128)S(1)} %add.25), channel_id=1, source_target_pairs={{0,4},{1,9},{2,6},{3,11},{4,0},{5,13},{6,2},{7,15},{8,12},{9,1},{1... | collective-permute-start | bytes 49160 | tf_op jit(solution)/shard_map/ppermute | solution.py:37
  35.9 1.7 %second_sweep.1 = (f32[32,2048]{1,0:T(8,128)S(1)}, f32[32,32]{1,0:T(8,128)S(1)}, bf16[2048,128]{1,0:T(8,128)(2,1)S(1)}) custom-call(f32[32,2048]{1,0:T(8,128)S(1)} %get-tuple-element.25.rows_ref, f32[32,32]{1,0:T(8,128)S(1)} %get-tuple-element.26.step_ref, f32[32,32]{1,0:T(8,128)S(1)} %get-tuple-element.27.gram_ref), custom_call_target="tpu_custom_call" | custom-call | flops 1000000000 | bytes 7000000 | tf_op jit(solution)/shard_map/second_sweep/pallas_call | solution.py:334
  37.7 0.6 %collective-permute-done.11 = f32[16,256]{1,0:T(8,128)S(1)} collective-permute-done((f32[16,256]{1,0:T(8,128)S(1)}, f32[16,256]{1,0:T(8,128)S(1)}, u32[]{:S(2)}, u32[]{:S(2)}) %collective-permute-start.11) | collective-permute-done | bytes 16416 | tf_op jit(solution)/shard_map/ppermute | solution.py:37
  38.2 2.2 %collective-permute-start.12 = (f32[16,256]{1,0:T(8,128)S(1)}, f32[16,256]{1,0:T(8,128)S(1)}, u32[]{:S(2)}, u32[]{:S(2)}) collective-permute-start(f32[16,256]{1,0:T(8,128)S(1)} %add.26), channel_id=1, source_target_pairs={{0,8},{1,3},{2,10},{3,1},{4,12},{5,7},{6,14},{7,5},{8,0},{9,11},{1... | collective-permute-start | bytes 49160 | tf_op jit(solution)/shard_map/ppermute | solution.py:37
  40.5 2.4 %collective-permute-done.12 = f32[16,256]{1,0:T(8,128)S(1)} collective-permute-done((f32[16,256]{1,0:T(8,128)S(1)}, f32[16,256]{1,0:T(8,128)S(1)}, u32[]{:S(2)}, u32[]{:S(2)}) %collective-permute-start.12) | collective-permute-done | bytes 16416 | tf_op jit(solution)/shard_map/ppermute | solution.py:37
  42.9 0.0 collective-permute-start.13
  42.9 1.2 %collective-permute-done.13.other_ref = f32[16,256]{1,0:T(8,128)S(1)} collective-permute-done((f32[16,256]{1,0:T(8,128)S(1)}, f32[16,256]{1,0:T(8,128)S(1)}, u32[]{:S(2)}, u32[]{:S(2)}) %collective-permute-start.13) | collective-permute-done | bytes 16416 | tf_op jit(solution)/shard_map/ppermute | solution.py:41
  44.1 2.1 %error_next.1 = (bf16[1,2048,256]{2,1,0:T(8,128)(2,1)}, f32[32,2048]{1,0:T(8,128)}, f32[32,256]{1,0:T(8,128)}) custom-call(f32[32,2048]{1,0:T(8,128)S(1)} %get-tuple-element.31.basis_ref, bf16[2048,128]{1,0:T(8,128)(2,1)S(1)} %get-tuple-element.32.lefts_ref, f32[32,32]{1,0:T(8,128)S(1)} %get-tuple-element.33.inverse_ref, f32[16,256]{1,0:T(8,128)S(1)} %add.27.mine_ref, ...), custom_call_target="tpu_custom_call" | custom-call | flops 33554432 | bytes 3145728 | tf_op jit(solution)/shard_map/error_next/pallas_call | solution.py:376
  (9 shorter events, 0.1 us)
Async XLA Ops:
  3.0 1.5 %collective-permute-start = (f32[2,16,1024]{2,1,0:T(8,128)S(1)}, f32[2,16,1024]{2,1,0:T(8,128)S(1)}, u32[]{:S(2)}, u32[]{:S(2)}) collective-permute-start(f32[2,16,1024]{2,1,0:T(8,128)S(1)} %get-tuple-element.20), channel_id=1, source_target_pairs={{0,1},{1,0},{2,3},{3,2},{4,5},{5,4},{6,7},{7,6},{8,9},{9,8},{10,11... | collective-permute-start | bytes 393224 | tf_op jit(solution)/shard_map/ppermute | solution.py:41
  4.5 6.7 %collective-permute-start.1 = (f32[16,1024]{1,0:T(8,128)S(1)}, f32[16,1024]{1,0:T(8,128)S(1)}, u32[]{:S(2)}, u32[]{:S(2)}) collective-permute-start(f32[16,1024]{1,0:T(8,128)S(1)} %slice_bitcast_fusion), channel_id=1, source_target_pairs={{0,2},{1,5},{2,0},{3,7},{4,6},{5,1},{6,4},{7,3},{8,10},{9,13},{10,... | collective-permute-start | bytes 196616 | tf_op jit(solution)/shard_map/ppermute | solution.py:37
  9.0 20.6 %collective-permute-start.5 = (f32[512,256]{1,0:T(8,128)S(1)}, f32[512,256]{1,0:T(8,128)S(1)}, u32[]{:S(2)}, u32[]{:S(2)}) collective-permute-start(f32[512,256]{1,0:T(8,128)S(1)} %merge.4.refs_0_), channel_id=1, source_target_pairs={{0,1},{1,0},{2,3},{3,2},{4,5},{5,4},{6,7},{7,6},{8,9},{9,8},{10,11... | collective-permute-start | bytes 1572872 | tf_op jit(solution)/shard_map/ppermute | solution.py:41
  10.7 19.0 %collective-permute-start.6 = (f32[512,256]{1,0:T(8,128)S(1)}, f32[512,256]{1,0:T(8,128)S(1)}, u32[]{:S(2)}, u32[]{:S(2)}) collective-permute-start(f32[512,256]{1,0:T(8,128)S(1)} %merge.5.refs_1_), channel_id=1, source_target_pairs={{0,1},{1,0},{2,3},{3,2},{4,5},{5,4},{6,7},{7,6},{8,9},{9,8},{10,11... | collective-permute-start | bytes 1572872 | tf_op jit(solution)/shard_map/ppermute | solution.py:41
  14.4 15.2 %collective-permute-start.7 = (f32[512,256]{1,0:T(8,128)S(1)}, f32[512,256]{1,0:T(8,128)S(1)}, u32[]{:S(2)}, u32[]{:S(2)}) collective-permute-start(f32[512,256]{1,0:T(8,128)S(1)} %merge.6.refs_2_), channel_id=1, source_target_pairs={{0,1},{1,0},{2,3},{3,2},{4,5},{5,4},{6,7},{7,6},{8,9},{9,8},{10,11... | collective-permute-start | bytes 1572872 | tf_op jit(solution)/shard_map/ppermute | solution.py:41
  14.5 15.2 %collective-permute-start.8 = (f32[512,256]{1,0:T(8,128)S(1)}, f32[512,256]{1,0:T(8,128)S(1)}, u32[]{:S(2)}, u32[]{:S(2)}) collective-permute-start(f32[512,256]{1,0:T(8,128)S(1)} %merge.7.refs_3_), channel_id=1, source_target_pairs={{0,1},{1,0},{2,3},{3,2},{4,5},{5,4},{6,7},{7,6},{8,9},{9,8},{10,11... | collective-permute-start | bytes 1572872 | tf_op jit(solution)/shard_map/ppermute | solution.py:41
  15.0 5.0 %collective-permute-start.2 = (f32[16,1024]{1,0:T(8,128)S(1)}, f32[16,1024]{1,0:T(8,128)S(1)}, u32[]{:S(2)}, u32[]{:S(2)}) collective-permute-start(f32[16,1024]{1,0:T(8,128)S(1)} %fusion.after_hbm), channel_id=1, source_target_pairs={{0,4},{1,9},{2,6},{3,11},{4,0},{5,13},{6,2},{7,15},{8,12},{9,1},{1... | collective-permute-start | bytes 196616 | tf_op jit(solution)/shard_map/ppermute | solution.py:37
  20.0 5.2 %collective-permute-start.3 = (f32[16,1024]{1,0:T(8,128)S(1)}, f32[16,1024]{1,0:T(8,128)S(1)}, u32[]{:S(2)}, u32[]{:S(2)}) collective-permute-start(f32[16,1024]{1,0:T(8,128)S(1)} %add.23), channel_id=1, source_target_pairs={{0,8},{1,3},{2,10},{3,1},{4,12},{5,7},{6,14},{7,5},{8,0},{9,11},{1... | collective-permute-start | bytes 196616 | tf_op jit(solution)/shard_map/ppermute | solution.py:37
  25.2 4.3 %collective-permute-start.4 = (f32[16,1024]{1,0:T(8,128)S(1)}, f32[16,1024]{1,0:T(8,128)S(1)}, u32[]{:S(2)}, u32[]{:S(2)}) collective-permute-start(f32[16,1024]{1,0:T(8,128)S(1)} %add.24.near_ref), channel_id=1, source_target_pairs={{0,2},{1,5},{2,0},{3,7},{4,6},{5,1},{6,4},{7,3},{8,10},{9,13},{10,... | collective-permute-start | bytes 196616 | tf_op jit(solution)/shard_map/ppermute | solution.py:37
  29.6 1.8 %collective-permute-start.10 = (f32[2,16,1024]{2,1,0:T(8,128)S(1)}, f32[2,16,1024]{2,1,0:T(8,128)S(1)}, u32[]{:S(2)}, u32[]{:S(2)}) collective-permute-start(f32[2,16,1024]{2,1,0:T(8,128)S(1)} %pad_maximum_fusion.mine_ref), channel_id=1, source_target_pairs={{0,1},{1,0},{2,3},{3,2},{4,5},{5,4},{6,7},{7,6},{8,9},{9,8},{10,11... | collective-permute-start | bytes 393224 | tf_op jit(solution)/shard_map/ppermute | solution.py:41
  30.7 3.8 %collective-permute-start.9 = (f32[16,256]{1,0:T(8,128)S(1)}, f32[16,256]{1,0:T(8,128)S(1)}, u32[]{:S(2)}, u32[]{:S(2)}) collective-permute-start(f32[16,256]{1,0:T(8,128)S(1)} %product.1), channel_id=1, source_target_pairs={{0,2},{1,5},{2,0},{3,7},{4,6},{5,1},{6,4},{7,3},{8,10},{9,13},{10,... | collective-permute-start | bytes 49160 | tf_op jit(solution)/shard_map/ppermute | solution.py:37
  34.5 3.7 %collective-permute-start.11 = (f32[16,256]{1,0:T(8,128)S(1)}, f32[16,256]{1,0:T(8,128)S(1)}, u32[]{:S(2)}, u32[]{:S(2)}) collective-permute-start(f32[16,256]{1,0:T(8,128)S(1)} %add.25), channel_id=1, source_target_pairs={{0,4},{1,9},{2,6},{3,11},{4,0},{5,13},{6,2},{7,15},{8,12},{9,1},{1... | collective-permute-start | bytes 49160 | tf_op jit(solution)/shard_map/ppermute | solution.py:37
  38.2 4.6 %collective-permute-start.12 = (f32[16,256]{1,0:T(8,128)S(1)}, f32[16,256]{1,0:T(8,128)S(1)}, u32[]{:S(2)}, u32[]{:S(2)}) collective-permute-start(f32[16,256]{1,0:T(8,128)S(1)} %add.26), channel_id=1, source_target_pairs={{0,8},{1,3},{2,10},{3,1},{4,12},{5,7},{6,14},{7,5},{8,0},{9,11},{1... | collective-permute-start | bytes 49160 | tf_op jit(solution)/shard_map/ppermute | solution.py:37
  42.9 1.2 %collective-permute-start.13 = (f32[16,256]{1,0:T(8,128)S(1)}, f32[16,256]{1,0:T(8,128)S(1)}, u32[]{:S(2)}, u32[]{:S(2)}) collective-permute-start(f32[16,256]{1,0:T(8,128)S(1)} %add.27.mine_ref), channel_id=1, source_target_pairs={{0,1},{1,0},{2,3},{3,2},{4,5},{5,4},{6,7},{7,6},{8,9},{9,8},{10,11... | collective-permute-start | bytes 49160 | tf_op jit(solution)/shard_map/ppermute | solution.py:41

commit v10 on v9

--- a/solution.py
+++ b/solution.py
@@ -24,27 +24,31 @@
     return [(axis, 1 << i) for i in range(size.bit_length() - 1)]
 
 
-def swapped(value, sizes, ways):
+def swapped(value, sizes, way):
+    axis, bit = way
     pairs = []
     for dp in range(sizes["dp"]):
         for sub in range(sizes["sub"]):
-            for pair in range(2):
-                here = {"dp": dp, "sub": sub, "pair": pair}
-                axis, bit = ways[pair]
-                there = {**here, axis: here[axis] ^ bit}
-                pairs.append(tuple(
-                    (c["dp"] * sizes["sub"] + c["sub"]) * 2 + c["pair"] for c in (here, there)))
+            here = {"dp": dp, "sub": sub}
+            there = {**here, axis: here[axis] ^ bit}
+            pairs.append(tuple((c["dp"] * sizes["sub"] + c["sub"]) * 2 + 1 for c in (here, there)))
     return lax.ppermute(value, AXES, pairs)
 
 
-def across(value):
-    return lax.ppermute(value, "pair", [(0, 1), (1, 0)])
-
-
-def sides():
-    sub, dp = lax.axis_index("sub") & 1, lax.axis_index("dp") & 1
-    pair = lax.axis_index("pair")
-    return sub + pair * (dp - sub), dp + pair * (sub - dp)
+def to_first(value):
+    return lax.ppermute(value, "pair", [(1, 0)])
+
+
+def to_second(value):
+    return lax.ppermute(value, "pair", [(0, 1)])
+
+
+def of_second(mine, got):
+    return jnp.where(lax.axis_index("pair") == 1, mine, got)
+
+
+def side():
+    return lax.axis_index("sub") & 1
 
 
 def half_of(chosen, piece, start=0, size=None):
@@ -82,7 +86,7 @@
     return [(source.at[part, :], target.at[part, :]) for part in rows]
 
 
-def term_kernel(x_hbm, c_hbm, e_hbm, seed_hbm, keep_ref, send_ref,
+def term_kernel(x_hbm, c_hbm, e_hbm, seed_hbm, halves_ref,
                 x_ref, c_ref, e_ref, seed_ref, term_ref, sems):
     copies = whole_copies(
         [(seed_hbm, seed_ref), (c_hbm, c_ref)] + row_parts(e_hbm.at[0], e_ref, 2)
@@ -91,7 +95,7 @@
         copy.start()
     rank = seed_ref.shape[0]
     tokens, width = x_ref.shape
-    half, piece = keep_ref.shape[1:]
+    piece = halves_ref.shape[2]
     copies[0].wait()
     copies[1].wait()
     seed = jnp.concatenate(parts_of(seed_ref[...], 3), axis=0)
@@ -110,13 +114,8 @@
         for i in range(blocks):
             part = pl.ds(i * CHUNK, CHUNK)
             term_ref[:, part] += added(dot(own, x_ref[rows, part], ((1,), (0,))), rank)
-    low = lax.axis_index("pair") == 0
-    mine, other = sides()
     for i in range(2):
-        part = half_of(mine ^ i, piece)
-        keep_ref[i] = jnp.where(low, term_ref[:half, part], term_ref[half:, part])
-        part = half_of(other ^ i, piece)
-        send_ref[i] = jnp.where(low, term_ref[half:, part], term_ref[:half, part])
+        halves_ref[i] = term_ref[:, half_of(side() ^ i, piece)]
 
 
 def added(stack, rank):
@@ -133,8 +132,8 @@
     return pl.pallas_call(
         term_kernel,
         in_specs=[HBM] * 4,
-        out_specs=[VMEM] * 2,
-        out_shape=[jax.ShapeDtypeStruct((2, rank // 2, width // 2), F32)] * 2,
+        out_specs=VMEM,
+        out_shape=jax.ShapeDtypeStruct((2, rank, width // 2), F32),
         scratch_shapes=[
             pltpu.VMEM((tokens, width), BF16),
             pltpu.VMEM((tokens, out), BF16),
@@ -149,37 +148,38 @@
     )(inputs, cotangent, error_prev, seed_q)
 
 
-def merge_kernel(index, x_hbm, c_hbm, e_hbm, after_hbm, merged_ref, x_ref, c_ref, e_ref, sems):
-    size = merged_ref.shape[0]
-    rows = pl.ds(index * size, size)
-    copies = whole_copies(
-        [(c_hbm, c_ref), (x_hbm.at[:, rows], x_ref), (e_hbm.at[0, rows, :], e_ref)], sems)
+def merge_kernel(x_hbm, c_hbm, e_hbm, after_hbm, *refs):
+    merged_refs = refs[:PARTS]
+    x_ref, c_ref, e_ref, sems = refs[PARTS:]
+    size = merged_refs[0].shape[0]
+    copies = whole_copies([(c_hbm, c_ref), (x_hbm, x_ref), (e_hbm.at[0], e_ref)], sems)
     for copy in copies:
         copy.start()
     for copy in copies:
         copy.wait()
-    for i in range(size // CHUNK):
-        part = pl.ds(i * CHUNK, CHUNK)
-        merged_ref[part, :] = (
+    for i in range(e_ref.shape[0] // CHUNK):
+        start = i * CHUNK
+        part = pl.ds(start, CHUNK)
+        merged_refs[start // size][start % size:start % size + CHUNK, :] = (
             dot(x_ref[:, part], c_ref[...], ((0,), (0,))) + e_ref[part, :].astype(F32))
 
 
-def merge(inputs, cotangent, error_prev, after, index):
+def merge(inputs, cotangent, error_prev, after):
     tokens, width = inputs.shape
-    size, out = width // PARTS, cotangent.shape[1]
-    return pl.pallas_call(
-        functools.partial(merge_kernel, index),
+    out = cotangent.shape[1]
+    return pl.pallas_call(
+        merge_kernel,
         in_specs=[HBM] * 3 + [ANY],
-        out_specs=VMEM,
-        out_shape=jax.ShapeDtypeStruct((size, out), F32),
+        out_specs=[VMEM] * PARTS,
+        out_shape=[jax.ShapeDtypeStruct((width // PARTS, out), F32)] * PARTS,
         scratch_shapes=[
-            pltpu.VMEM((tokens, size), BF16),
+            pltpu.VMEM((tokens, width), BF16),
             pltpu.VMEM((tokens, out), BF16),
-            pltpu.VMEM((size, out), BF16),
+            pltpu.VMEM((width, out), BF16),
             pltpu.SemaphoreType.DMA((3,)),
         ],
         compiler_params=params(),
-        cost_estimate=cost(10 ** 8 // PARTS, 10 ** 6 // PARTS),
+        cost_estimate=cost(10 ** 8, 10 ** 6),
         name="merge",
     )(inputs, cotangent, error_prev, after)
 
@@ -187,14 +187,14 @@
 def product_kernel(near_ref, far_ref, *refs):
     mine_refs, other_hbms = refs[:PARTS], refs[PARTS:2 * PARTS]
     product_ref, other_ref, sems = refs[2 * PARTS:]
-    half, piece = near_ref.shape
+    rank, piece = near_ref.shape
     size = mine_refs[0].shape[0]
     copies = whole_copies(
         [(other, other_ref.at[pl.ds(i * size, size), :]) for i, other in enumerate(other_hbms)],
         sems)
     for copy in copies:
         copy.start()
-    straight = sides()[0] == 0
+    straight = side() == 0
     product = None
     for i in range(2 * piece // CHUNK):
         start = i * CHUNK
@@ -208,29 +208,24 @@
         merged = (mine_refs[start // size][start % size:start % size + CHUNK, :]
                   + other_ref[start:start + CHUNK, :])
         m_high, m_low = parts_of(merged, 2)
-        term = added(dot(both, m_high, ((1,), (0,))), half) + dot(f_high, m_low, ((1,), (0,)))
+        term = added(dot(both, m_high, ((1,), (0,))), rank) + dot(f_high, m_low, ((1,), (0,)))
         product = term if product is None else product + term
     product_ref[...] = product
 
 
 def product_of(near, far, mine, other):
-    half, piece = near.shape
+    rank, piece = near.shape
     out = mine[0].shape[1]
     width = 2 * piece
     return pl.pallas_call(
         product_kernel,
         in_specs=[VMEM] * (2 + PARTS) + [ANY] * PARTS,
-        out_shape=jax.ShapeDtypeStruct((half, out), F32),
+        out_shape=jax.ShapeDtypeStruct((rank, out), F32),
         scratch_shapes=[pltpu.VMEM((width, out), F32), pltpu.SemaphoreType.DMA((PARTS,))],
         compiler_params=params(),
-        cost_estimate=cost(2 * half * width * out, 8 * width * out),
+        cost_estimate=cost(2 * rank * width * out, 8 * width * out),
         name="product",
     )(near, far, *mine, *other)
-
-
-def both_halves(mine, other):
-    low = lax.axis_index("pair") == 0
-    return jnp.concatenate([jnp.where(low, mine, other), jnp.where(low, other, mine)], axis=0)
 
 
 def gram_blocks(rows):
@@ -277,16 +272,14 @@
     return dot(lefts, rights, ((1,), (0,)))
 
 
-def first_sweep_kernel(mine_ref, other_ref, rows_ref, step_ref, gram_ref):
-    half, piece = mine_ref.shape[1:]
-    rank = 2 * half
+def first_sweep_kernel(near_ref, far_ref, got_near_ref, got_far_ref, rows_ref, step_ref, gram_ref):
+    rank, piece = near_ref.shape
     blocks = None
-    mine, other = sides()
-    for i in range(2):
+    for i, (mine_ref, got_ref) in enumerate([(near_ref, got_near_ref), (far_ref, got_far_ref)]):
         for j in range(piece // CHUNK):
             part = slice(j * CHUNK, (j + 1) * CHUNK)
-            rows = both_halves(mine_ref[i, :, part], other_ref[i ^ mine ^ other, :, part])
-            rows_ref[:, half_of(mine ^ i, piece, j * CHUNK, CHUNK)] = rows
+            rows = of_second(mine_ref[:, part], got_ref[:, part])
+            rows_ref[:, half_of(side() ^ i, piece, j * CHUNK, CHUNK)] = rows
             term = gram_blocks(rows)
             blocks = term if blocks is None else blocks + term
     step = inverse_factor(gram_of(blocks, rank))
@@ -301,9 +294,9 @@
     gram_ref[...] = gram_of(blocks, rank)
 
 
-def first_sweep(mine, other):
-    _, half, piece = mine.shape
-    rank, width = 2 * half, 2 * piece
+def first_sweep(near, far, got_near, got_far):
+    rank, piece = near.shape
+    width = 2 * piece
     return pl.pallas_call(
         first_sweep_kernel,
         out_shape=[
@@ -314,7 +307,7 @@
         compiler_params=params(),
         cost_estimate=cost(10 ** 9, 7 * 10 ** 6),
         name="first_sweep",
-    )(mine, other)
+    )(near, far, got_near, got_far)
 
 
 def second_sweep_kernel(rows_ref, step_ref, gram_ref, basis_ref, inverse_ref, lefts_ref):
@@ -344,13 +337,13 @@
     )(rows, step, gram)
 
 
-def error_kernel(workers, basis_ref, lefts_ref, inverse_ref, mine_ref, other_ref, *refs):
+def error_kernel(workers, basis_ref, lefts_ref, inverse_ref, mine_ref, got_ref, *refs):
     merged_refs = refs[:PARTS]
     error_hbm, basis_hbm, second_ref, error_ref, error_sem, basis_sem = refs[PARTS:]
     size = merged_refs[0].shape[0]
     keep = pltpu.make_async_copy(basis_ref, basis_hbm, basis_sem)
     keep.start()
-    product = both_halves(mine_ref[...], other_ref[...])
+    product = of_second(mine_ref[...], got_ref[...])
     second = short_dot(inverse_ref[...], product) * (1.0 / workers)
     second_ref[...] = second
     high, low = parts_of(second, 2)
@@ -370,7 +363,7 @@
         copy.wait()
 
 
-def error_of(merged, basis, lefts, inverse, mine, other, workers):
+def error_of(merged, basis, lefts, inverse, mine, got, workers):
     rank, width = basis.shape
     out = mine.shape[1]
     return pl.pallas_call(
@@ -390,41 +383,36 @@
         compiler_params=params(),
         cost_estimate=cost(2 * rank * width * out, 6 * width * out),
         name="error_next",
-    )(basis, lefts, inverse, mine, other, *merged)
+    )(basis, lefts, inverse, mine, got, *merged)
 
 
 def local(sizes, *arguments):
     inputs, cotangent, error_prev, seed_q = (
         pltpu.with_memory_space_constraint(value, pltpu.HBM) for value in arguments)
-    sub, dp = bits_of("sub", sizes["sub"]), bits_of("dp", sizes["dp"])
-    rounds = list(zip(sub[:1] + dp + sub[1:], dp + sub))
+    rounds = bits_of("sub", sizes["sub"]) + bits_of("dp", sizes["dp"])
     workers = 2 * sizes["sub"] * sizes["dp"]
 
-    keep, send = term_halves(inputs, cotangent, error_prev, seed_q)
-    part = keep + across(send)
-    near = part[0] + swapped(part[1], sizes, rounds[0])
-    merged = [
-        merge(inputs, cotangent, error_prev, part if i < PARTS // 2 else near, i)
-        for i in range(PARTS)]
-    merged_other = [across(rows) for rows in merged]
-    for ways in rounds[1:]:
-        near = near + swapped(near, sizes, ways)
+    halves = term_halves(inputs, cotangent, error_prev, seed_q)
+    halves = halves + to_second(halves)
+    merged = merge(inputs, cotangent, error_prev, halves)
+    merged_other = [to_second(rows) for rows in merged]
+    near = halves[0] + swapped(halves[1], sizes, rounds[0])
+    for way in rounds[1:]:
+        near = near + swapped(near, sizes, way)
     far = swapped(near, sizes, rounds[0])
-    mine = jnp.stack([near, far])
-    other = across(mine)
+    got_near, got_far = to_first(near), to_first(far)
 
     product = product_of(near, far, merged, merged_other)
-    rows, step, gram = first_sweep(mine, other)
+    product, got_near, got_far = lax.optimization_barrier((product, got_near, got_far))
+    rows, step, gram = first_sweep(near, far, got_near, got_far)
     product = product + swapped(product, sizes, rounds[0])
     product, rows, step, gram = lax.optimization_barrier((product, rows, step, gram))
     basis, inverse, lefts = second_sweep(rows, step, gram)
-    for i, ways in enumerate(rounds[1:]):
-        product = product + swapped(product, sizes, ways)
-        if i == 0:
-            product, basis, inverse, lefts = lax.optimization_barrier(
-                (product, basis, inverse, lefts))
-    product_other = across(product)
-    return error_of(merged, basis, lefts, inverse, product, product_other, workers)
+    product = product + swapped(product, sizes, rounds[1])
+    product, basis, inverse, lefts = lax.optimization_barrier((product, basis, inverse, lefts))
+    for way in rounds[2:]:
+        product = product + swapped(product, sizes, way)
+    return error_of(merged, basis, lefts, inverse, product, to_first(product), workers)
 
 
 def solution(mesh):

time: 46.4 us -> 60.4 us (1.30)
  waiting for transfers between devices: 16 us -> 25.9 us
  starting transfers between devices: 13.3 us -> 20.5 us
  Pallas kernels: 16.1 us -> 12.6 us
    ppermute x7 -> x8, waiting for transfers between devices: 2.18 us -> 25.9 us  [the longest x3 24.8 us: to_first(): return lax.ppermute(value, 'pair', [(1, 0)])]
    ppermute x7 -> x8, starting transfers between devices: 1.79 us -> 15.8 us  [the longest x5 11.9 us: to_second(): return lax.ppermute(value, 'pair', [(0, 1)])]
    ppermute x7, waiting for transfers between devices: 13.8 us -> 0.02 us  [swapped(): return lax.ppermute(value, AXES, pairs)]
    ppermute x7, starting transfers between devices: 11.5 us -> 4.65 us  [swapped(): return lax.ppermute(value, AXES, pairs)]
    pallas_call x5 -> x2, Pallas kernels: 8.63 us -> 5.08 us  [the longest x1 2.74 us: merge(): pl.pallas_call(merge_kernel, in_specs=[HBM] * 3 + [ANY], out_specs=[VMEM]...]
  transfers between devices with their start and end apart: 14 -> 15, of which waited for: 8 -> 4; matrix products, arithmetic and copies ran while one was open for 0% -> 0% of each run, Pallas kernels for 25% -> 13%
where the time goes in v10:
time: 60.4 us; the launch traced here: 60 us
  waiting for transfers between devices  25.9 us (43%)
  starting transfers between devices  20.5 us (34%)
  Pallas kernels  12.6 us (21%)
  between operations  0.94 us (2%)
    ppermute x3, waiting for transfers between devices, to_first(): return lax.ppermute(value, 'pair', [(1, 0)])  24.8 us
    ppermute x5, starting transfers between devices, to_second(): return lax.ppermute(value, 'pair', [(0, 1)])  11.9 us
    ppermute x7, starting transfers between devices, swapped(): return lax.ppermute(value, AXES, pairs)  4.65 us
    ppermute x3, starting transfers between devices, to_first(): return lax.ppermute(value, 'pair', [(1, 0)])  3.88 us
    pallas_call x1, Pallas kernels, merge(): pl.pallas_call(merge_kernel, in_specs=[HBM] * 3 + [ANY], out_specs=[VMEM]...  2.74 us
    pallas_call x1, Pallas kernels, first_sweep(): pl.pallas_call(first_sweep_kernel, out_shape=[jax.ShapeDtypeStruct((rank,...  2.57 us
    pallas_call x1, Pallas kernels, term_halves(): pl.pallas_call(term_kernel, in_specs=[HBM] * 4, out_specs=VMEM, out_shape...  2.34 us
    pallas_call x1, Pallas kernels, error_of(): pl.pallas_call(functools.partial(error_kernel, workers), in_specs=[VMEM]...  2.13 us
  transfers between devices with their start and end apart: 15, of which 4 were waited for; matrix products, arithmetic and copies ran while one was open for 0% of the time, Pallas kernels for 13%

profile of v10, /device:TPU:0, one launch (start us, length us, event | category | flops | bytes accessed | tf_op | source)
XLA Modules:
  0.0 60.0 jit_solution(3547814653018137496)
XLA Ops:
  0.6 2.3 %term.1 = f32[2,32,1024]{2,1,0:T(8,128)S(1)} custom-call(bf16[512,2048]{1,0:T(8,128)(2,1)} %x_hbm.3, bf16[512,256]{1,0:T(8,128)(2,1)} %c_hbm.3, bf16[1,2048,256]{2,1,0:T(8,128)(2,1)} %e_hbm.3, f32[32,256]{1,0:T(8,128)} %seed_hbm.1), custom_call_target="tpu_custom_call" | custom-call | flops 201326592 | bytes 3145728 | tf_op jit(solution)/shard_map/term/pallas_call | solution.py:132
  3.0 2.4 %collective-permute-start = (f32[2,32,1024]{2,1,0:T(8,128)S(1)}, f32[2,32,1024]{2,1,0:T(8,128)S(1)}, u32[]{:S(2)}, u32[]{:S(2)}) collective-permute-start(f32[2,32,1024]{2,1,0:T(8,128)S(1)} %term.1), channel_id=1, source_target_pairs={{0,1},{2,3},{4,5},{6,7},{8,9},{10,11},{12,13},{14,15},{16,17},{18,... | collective-permute-start | bytes 786440 | tf_op jit(solution)/shard_map/ppermute | solution.py:43
  5.4 1.1 %collective-permute-done = f32[2,32,1024]{2,1,0:T(8,128)S(1)} collective-permute-done((f32[2,32,1024]{2,1,0:T(8,128)S(1)}, f32[2,32,1024]{2,1,0:T(8,128)S(1)}, u32[]{:S(2)}, u32[]{:S(2)}) %collective-permute-start) | collective-permute-done | bytes 262176 | tf_op jit(solution)/shard_map/ppermute | solution.py:43
  6.5 0.7 %collective-permute-start.1 = (f32[32,1024]{1,0:T(8,128)S(1)}, f32[32,1024]{1,0:T(8,128)S(1)}, u32[]{:S(2)}, u32[]{:S(2)}) collective-permute-start(f32[32,1024]{1,0:T(8,128)S(1)} %slice_bitcast_fusion), channel_id=1, source_target_pairs={{1,3},{3,1},{5,7},{7,5},{9,11},{11,9},{13,15},{15,13},{17,19},{19,... | collective-permute-start | bytes 393224 | tf_op jit(solution)/shard_map/ppermute | solution.py:35
  7.2 2.7 %merge.1 = (f32[512,256]{1,0:T(8,128)S(1)}, f32[512,256]{1,0:T(8,128)S(1)}, f32[512,256]{1,0:T(8,128)S(1)}, f32[512,256]{1,0:T(8,128)S(1)}) custom-call(bf16[512,2048]{1,0:T(8,128)(2,1)} %x_hbm.3, bf16[512,256]{1,0:T(8,128)(2,1)} %c_hbm.3, bf16[1,2048,256]{2,1,0:T(8,128)(2,1)} %e_hbm.3, f32[2,32,1024]{2,1,0:T(8,128)S(1)} %add.21.after_hbm), custom_call_target="tpu_custom_call" | custom-call | flops 100000000 | bytes 1000000 | tf_op jit(solution)/shard_map/merge/pallas_call | solution.py:170
  10.0 5.6 %collective-permute-start.5 = (f32[512,256]{1,0:T(8,128)S(1)}, f32[512,256]{1,0:T(8,128)S(1)}, u32[]{:S(2)}, u32[]{:S(2)}) collective-permute-start(f32[512,256]{1,0:T(8,128)S(1)} %get-tuple-element.24.refs_0_), channel_id=1, source_target_pairs={{0,1},{2,3},{4,5},{6,7},{8,9},{10,11},{12,13},{14,15},{16,17},{18,... | collective-permute-start | bytes 1572872 | tf_op jit(solution)/shard_map/ppermute | solution.py:43
  15.6 1.3 %collective-permute-start.6 = (f32[512,256]{1,0:T(8,128)S(1)}, f32[512,256]{1,0:T(8,128)S(1)}, u32[]{:S(2)}, u32[]{:S(2)}) collective-permute-start(f32[512,256]{1,0:T(8,128)S(1)} %get-tuple-element.25.refs_1_), channel_id=1, source_target_pairs={{0,1},{2,3},{4,5},{6,7},{8,9},{10,11},{12,13},{14,15},{16,17},{18,... | collective-permute-start | bytes 1572872 | tf_op jit(solution)/shard_map/ppermute | solution.py:43
  16.9 1.3 %collective-permute-start.7 = (f32[512,256]{1,0:T(8,128)S(1)}, f32[512,256]{1,0:T(8,128)S(1)}, u32[]{:S(2)}, u32[]{:S(2)}) collective-permute-start(f32[512,256]{1,0:T(8,128)S(1)} %get-tuple-element.26.refs_2_), channel_id=1, source_target_pairs={{0,1},{2,3},{4,5},{6,7},{8,9},{10,11},{12,13},{14,15},{16,17},{18,... | collective-permute-start | bytes 1572872 | tf_op jit(solution)/shard_map/ppermute | solution.py:43
  18.2 1.3 %collective-permute-start.8 = (f32[512,256]{1,0:T(8,128)S(1)}, f32[512,256]{1,0:T(8,128)S(1)}, u32[]{:S(2)}, u32[]{:S(2)}) collective-permute-start(f32[512,256]{1,0:T(8,128)S(1)} %get-tuple-element.27.refs_3_), channel_id=1, source_target_pairs={{0,1},{2,3},{4,5},{6,7},{8,9},{10,11},{12,13},{14,15},{16,17},{18,... | collective-permute-start | bytes 1572872 | tf_op jit(solution)/shard_map/ppermute | solution.py:43
  19.6 0.0 collective-permute-done.1
  19.6 0.7 %collective-permute-start.2 = (f32[32,1024]{1,0:T(8,128)S(1)}, f32[32,1024]{1,0:T(8,128)S(1)}, u32[]{:S(2)}, u32[]{:S(2)}) collective-permute-start(f32[32,1024]{1,0:T(8,128)S(1)} %fusion), channel_id=1, source_target_pairs={{1,5},{3,7},{5,1},{7,3},{9,13},{11,15},{13,9},{15,11},{17,21},{19,... | collective-permute-start | bytes 393224 | tf_op jit(solution)/shard_map/ppermute | solution.py:35
  20.3 0.0 collective-permute-done.2
  20.3 0.7 %collective-permute-start.3 = (f32[32,1024]{1,0:T(8,128)S(1)}, f32[32,1024]{1,0:T(8,128)S(1)}, u32[]{:S(2)}, u32[]{:S(2)}) collective-permute-start(f32[32,1024]{1,0:T(8,128)S(1)} %add.23), channel_id=1, source_target_pairs={{1,9},{3,11},{5,13},{7,15},{9,1},{11,3},{13,5},{15,7},{17,25},{19,... | collective-permute-start | bytes 393224 | tf_op jit(solution)/shard_map/ppermute | solution.py:35
  21.0 0.0 collective-permute-done.3
  21.0 0.7 %collective-permute-start.4 = (f32[32,1024]{1,0:T(8,128)S(1)}, f32[32,1024]{1,0:T(8,128)S(1)}, u32[]{:S(2)}, u32[]{:S(2)}) collective-permute-start(f32[32,1024]{1,0:T(8,128)S(1)} %add.24.near_ref), channel_id=1, source_target_pairs={{1,3},{3,1},{5,7},{7,5},{9,11},{11,9},{13,15},{15,13},{17,19},{19,... | collective-permute-start | bytes 393224 | tf_op jit(solution)/shard_map/ppermute | solution.py:35
  21.7 0.0 collective-permute-done.5.refs_4_
  21.7 1.3 %collective-permute-start.9 = (f32[32,1024]{1,0:T(8,128)S(1)}, f32[32,1024]{1,0:T(8,128)S(1)}, u32[]{:S(2)}, u32[]{:S(2)}) collective-permute-start(f32[32,1024]{1,0:T(8,128)S(1)} %add.24.near_ref), channel_id=1, source_target_pairs={{1,0},{3,2},{5,4},{7,6},{9,8},{11,10},{13,12},{15,14},{17,16},{19,... | collective-permute-start | bytes 393224 | tf_op jit(solution)/shard_map/ppermute | solution.py:39
  23.0 0.0 collective-permute-done.4.far_ref
  23.0 1.3 %collective-permute-start.10 = (f32[32,1024]{1,0:T(8,128)S(1)}, f32[32,1024]{1,0:T(8,128)S(1)}, u32[]{:S(2)}, u32[]{:S(2)}) collective-permute-start(f32[32,1024]{1,0:T(8,128)S(1)} %collective-permute-done.4.far_ref), channel_id=1, source_target_pairs={{1,0},{3,2},{5,4},{7,6},{9,8},{11,10},{13,12},{15,14},{17,16},{19,... | collective-permute-start | bytes 393224 | tf_op jit(solution)/shard_map/ppermute | solution.py:39
  24.3 0.0 collective-permute-done.6.refs_5_
  24.3 0.0 collective-permute-done.7.refs_6_
  24.3 0.0 collective-permute-done.8.refs_7_
  24.3 1.1 %product.1 = f32[32,256]{1,0:T(8,128)S(1)} custom-call(f32[32,1024]{1,0:T(8,128)S(1)} %add.24.near_ref, f32[32,1024]{1,0:T(8,128)S(1)} %collective-permute-done.4.far_ref, f32[512,256]{1,0:T(8,128)S(1)} %get-tuple-element.24.refs_0_, f32[512,256]{1,0:T(8,128)S(1)} %get-tuple-element.25.refs_1_, f32[512,256]{1,0:T(8,128)S(1)} %get-tuple-element.26.refs_2_, ...), custom_call_target="tpu_custom_call" | custom-call | flops 33554432 | bytes 4194304 | tf_op jit(solution)/shard_map/product/pallas_call | solution.py:220
  25.4 11.5 %collective-permute-done.9.got_near_ref = f32[32,1024]{1,0:T(8,128)S(1)} collective-permute-done((f32[32,1024]{1,0:T(8,128)S(1)}, f32[32,1024]{1,0:T(8,128)S(1)}, u32[]{:S(2)}, u32[]{:S(2)}) %collective-permute-start.9) | collective-permute-done | bytes 131104 | tf_op jit(solution)/shard_map/ppermute | solution.py:39
  36.9 3.6 %collective-permute-done.10.got_far_ref = f32[32,1024]{1,0:T(8,128)S(1)} collective-permute-done((f32[32,1024]{1,0:T(8,128)S(1)}, f32[32,1024]{1,0:T(8,128)S(1)}, u32[]{:S(2)}, u32[]{:S(2)}) %collective-permute-start.10) | collective-permute-done | bytes 131104 | tf_op jit(solution)/shard_map/ppermute | solution.py:39
  40.4 0.7 %collective-permute-start.11 = (f32[32,256]{1,0:T(8,128)S(1)}, f32[32,256]{1,0:T(8,128)S(1)}, u32[]{:S(2)}, u32[]{:S(2)}) collective-permute-start(f32[32,256]{1,0:T(8,128)S(1)} %product.1), channel_id=1, source_target_pairs={{1,3},{3,1},{5,7},{7,5},{9,11},{11,9},{13,15},{15,13},{17,19},{19,... | collective-permute-start | bytes 98312 | tf_op jit(solution)/shard_map/ppermute | solution.py:35
  41.1 2.6 %first_sweep.1 = (f32[32,2048]{1,0:T(8,128)S(1)}, f32[32,32]{1,0:T(8,128)S(1)}, f32[32,32]{1,0:T(8,128)S(1)}) custom-call(f32[32,1024]{1,0:T(8,128)S(1)} %add.24.near_ref, f32[32,1024]{1,0:T(8,128)S(1)} %collective-permute-done.4.far_ref, f32[32,1024]{1,0:T(8,128)S(1)} %collective-permute-done.9.got_near_ref, f32[32,1024]{1,0:T(8,128)S(1)} %collective-permute-done.10.got_far_ref), custom_call_target="tpu_custom_call" | custom-call | flops 1000000000 | bytes 7000000 | tf_op jit(solution)/shard_map/first_sweep/pallas_call | solution.py:300
  43.7 0.0 collective-permute-done.11
  43.7 0.7 %collective-permute-start.12 = (f32[32,256]{1,0:T(8,128)S(1)}, f32[32,256]{1,0:T(8,128)S(1)}, u32[]{:S(2)}, u32[]{:S(2)}) collective-permute-start(f32[32,256]{1,0:T(8,128)S(1)} %add.25), channel_id=1, source_target_pairs={{1,5},{3,7},{5,1},{7,3},{9,13},{11,15},{13,9},{15,11},{17,21},{19,... | collective-permute-start | bytes 98312 | tf_op jit(solution)/shard_map/ppermute | solution.py:35
  44.4 1.7 %second_sweep.1 = (f32[32,2048]{1,0:T(8,128)S(1)}, f32[32,32]{1,0:T(8,128)S(1)}, bf16[2048,128]{1,0:T(8,128)(2,1)S(1)}) custom-call(f32[32,2048]{1,0:T(8,128)S(1)} %get-tuple-element.35.rows_ref, f32[32,32]{1,0:T(8,128)S(1)} %get-tuple-element.36.step_ref, f32[32,32]{1,0:T(8,128)S(1)} %get-tuple-element.37.gram_ref), custom_call_target="tpu_custom_call" | custom-call | flops 1000000000 | bytes 7000000 | tf_op jit(solution)/shard_map/second_sweep/pallas_call | solution.py:327
  46.1 0.0 collective-permute-done.12
  46.1 0.7 %collective-permute-start.13 = (f32[32,256]{1,0:T(8,128)S(1)}, f32[32,256]{1,0:T(8,128)S(1)}, u32[]{:S(2)}, u32[]{:S(2)}) collective-permute-start(f32[32,256]{1,0:T(8,128)S(1)} %add.26), channel_id=1, source_target_pairs={{1,9},{3,11},{5,13},{7,15},{9,1},{11,3},{13,5},{15,7},{17,25},{19,... | collective-permute-start | bytes 98312 | tf_op jit(solution)/shard_map/ppermute | solution.py:35
  46.8 0.0 collective-permute-done.13
  46.8 1.3 %collective-permute-start.14 = (f32[32,256]{1,0:T(8,128)S(1)}, f32[32,256]{1,0:T(8,128)S(1)}, u32[]{:S(2)}, u32[]{:S(2)}) collective-permute-start(f32[32,256]{1,0:T(8,128)S(1)} %add.27.mine_ref), channel_id=1, source_target_pairs={{1,0},{3,2},{5,4},{7,6},{9,8},{11,10},{13,12},{15,14},{17,16},{19,... | collective-permute-start | bytes 98312 | tf_op jit(solution)/shard_map/ppermute | solution.py:39
  48.1 9.7 %collective-permute-done.14.got_ref = f32[32,256]{1,0:T(8,128)S(1)} collective-permute-done((f32[32,256]{1,0:T(8,128)S(1)}, f32[32,256]{1,0:T(8,128)S(1)}, u32[]{:S(2)}, u32[]{:S(2)}) %collective-permute-start.14) | collective-permute-done | bytes 32800 | tf_op jit(solution)/shard_map/ppermute | solution.py:39
  57.9 2.1 %error_next.1 = (bf16[1,2048,256]{2,1,0:T(8,128)(2,1)}, f32[32,2048]{1,0:T(8,128)}, f32[32,256]{1,0:T(8,128)}) custom-call(f32[32,2048]{1,0:T(8,128)S(1)} %get-tuple-element.41.basis_ref, bf16[2048,128]{1,0:T(8,128)(2,1)S(1)} %get-tuple-element.42.lefts_ref, f32[32,32]{1,0:T(8,128)S(1)} %get-tuple-element.43.inverse_ref, f32[32,256]{1,0:T(8,128)S(1)} %add.27.mine_ref, ...), custom_call_target="tpu_custom_call" | custom-call | flops 33554432 | bytes 3145728 | tf_op jit(solution)/shard_map/error_next/pallas_call | solution.py:369
  (8 shorter events, 0.1 us)
Async XLA Ops:
  3.0 3.5 %collective-permute-start = (f32[2,32,1024]{2,1,0:T(8,128)S(1)}, f32[2,32,1024]{2,1,0:T(8,128)S(1)}, u32[]{:S(2)}, u32[]{:S(2)}) collective-permute-start(f32[2,32,1024]{2,1,0:T(8,128)S(1)} %term.1), channel_id=1, source_target_pairs={{0,1},{2,3},{4,5},{6,7},{8,9},{10,11},{12,13},{14,15},{16,17},{18,... | collective-permute-start | bytes 786440 | tf_op jit(solution)/shard_map/ppermute | solution.py:43
  6.5 13.0 %collective-permute-start.1 = (f32[32,1024]{1,0:T(8,128)S(1)}, f32[32,1024]{1,0:T(8,128)S(1)}, u32[]{:S(2)}, u32[]{:S(2)}) collective-permute-start(f32[32,1024]{1,0:T(8,128)S(1)} %slice_bitcast_fusion), channel_id=1, source_target_pairs={{1,3},{3,1},{5,7},{7,5},{9,11},{11,9},{13,15},{15,13},{17,19},{19,... | collective-permute-start | bytes 393224 | tf_op jit(solution)/shard_map/ppermute | solution.py:35
  10.0 11.7 %collective-permute-start.5 = (f32[512,256]{1,0:T(8,128)S(1)}, f32[512,256]{1,0:T(8,128)S(1)}, u32[]{:S(2)}, u32[]{:S(2)}) collective-permute-start(f32[512,256]{1,0:T(8,128)S(1)} %get-tuple-element.24.refs_0_), channel_id=1, source_target_pairs={{0,1},{2,3},{4,5},{6,7},{8,9},{10,11},{12,13},{14,15},{16,17},{18,... | collective-permute-start | bytes 1572872 | tf_op jit(solution)/shard_map/ppermute | solution.py:43
  15.6 8.8 %collective-permute-start.6 = (f32[512,256]{1,0:T(8,128)S(1)}, f32[512,256]{1,0:T(8,128)S(1)}, u32[]{:S(2)}, u32[]{:S(2)}) collective-permute-start(f32[512,256]{1,0:T(8,128)S(1)} %get-tuple-element.25.refs_1_), channel_id=1, source_target_pairs={{0,1},{2,3},{4,5},{6,7},{8,9},{10,11},{12,13},{14,15},{16,17},{18,... | collective-permute-start | bytes 1572872 | tf_op jit(solution)/shard_map/ppermute | solution.py:43
  16.9 7.4 %collective-permute-start.7 = (f32[512,256]{1,0:T(8,128)S(1)}, f32[512,256]{1,0:T(8,128)S(1)}, u32[]{:S(2)}, u32[]{:S(2)}) collective-permute-start(f32[512,256]{1,0:T(8,128)S(1)} %get-tuple-element.26.refs_2_), channel_id=1, source_target_pairs={{0,1},{2,3},{4,5},{6,7},{8,9},{10,11},{12,13},{14,15},{16,17},{18,... | collective-permute-start | bytes 1572872 | tf_op jit(solution)/shard_map/ppermute | solution.py:43
  18.2 6.1 %collective-permute-start.8 = (f32[512,256]{1,0:T(8,128)S(1)}, f32[512,256]{1,0:T(8,128)S(1)}, u32[]{:S(2)}, u32[]{:S(2)}) collective-permute-start(f32[512,256]{1,0:T(8,128)S(1)} %get-tuple-element.27.refs_3_), channel_id=1, source_target_pairs={{0,1},{2,3},{4,5},{6,7},{8,9},{10,11},{12,13},{14,15},{16,17},{18,... | collective-permute-start | bytes 1572872 | tf_op jit(solution)/shard_map/ppermute | solution.py:43
  19.6 0.7 %collective-permute-start.2 = (f32[32,1024]{1,0:T(8,128)S(1)}, f32[32,1024]{1,0:T(8,128)S(1)}, u32[]{:S(2)}, u32[]{:S(2)}) collective-permute-start(f32[32,1024]{1,0:T(8,128)S(1)} %fusion), channel_id=1, source_target_pairs={{1,5},{3,7},{5,1},{7,3},{9,13},{11,15},{13,9},{15,11},{17,21},{19,... | collective-permute-start | bytes 393224 | tf_op jit(solution)/shard_map/ppermute | solution.py:35
  20.3 0.7 %collective-permute-start.3 = (f32[32,1024]{1,0:T(8,128)S(1)}, f32[32,1024]{1,0:T(8,128)S(1)}, u32[]{:S(2)}, u32[]{:S(2)}) collective-permute-start(f32[32,1024]{1,0:T(8,128)S(1)} %add.23), channel_id=1, source_target_pairs={{1,9},{3,11},{5,13},{7,15},{9,1},{11,3},{13,5},{15,7},{17,25},{19,... | collective-permute-start | bytes 393224 | tf_op jit(solution)/shard_map/ppermute | solution.py:35
  21.0 2.0 %collective-permute-start.4 = (f32[32,1024]{1,0:T(8,128)S(1)}, f32[32,1024]{1,0:T(8,128)S(1)}, u32[]{:S(2)}, u32[]{:S(2)}) collective-permute-start(f32[32,1024]{1,0:T(8,128)S(1)} %add.24.near_ref), channel_id=1, source_target_pairs={{1,3},{3,1},{5,7},{7,5},{9,11},{11,9},{13,15},{15,13},{17,19},{19,... | collective-permute-start | bytes 393224 | tf_op jit(solution)/shard_map/ppermute | solution.py:35
  21.7 15.2 %collective-permute-start.9 = (f32[32,1024]{1,0:T(8,128)S(1)}, f32[32,1024]{1,0:T(8,128)S(1)}, u32[]{:S(2)}, u32[]{:S(2)}) collective-permute-start(f32[32,1024]{1,0:T(8,128)S(1)} %add.24.near_ref), channel_id=1, source_target_pairs={{1,0},{3,2},{5,4},{7,6},{9,8},{11,10},{13,12},{15,14},{17,16},{19,... | collective-permute-start | bytes 393224 | tf_op jit(solution)/shard_map/ppermute | solution.py:39
  23.0 17.4 %collective-permute-start.10 = (f32[32,1024]{1,0:T(8,128)S(1)}, f32[32,1024]{1,0:T(8,128)S(1)}, u32[]{:S(2)}, u32[]{:S(2)}) collective-permute-start(f32[32,1024]{1,0:T(8,128)S(1)} %collective-permute-done.4.far_ref), channel_id=1, source_target_pairs={{1,0},{3,2},{5,4},{7,6},{9,8},{11,10},{13,12},{15,14},{17,16},{19,... | collective-permute-start | bytes 393224 | tf_op jit(solution)/shard_map/ppermute | solution.py:39
  40.4 3.2 %collective-permute-start.11 = (f32[32,256]{1,0:T(8,128)S(1)}, f32[32,256]{1,0:T(8,128)S(1)}, u32[]{:S(2)}, u32[]{:S(2)}) collective-permute-start(f32[32,256]{1,0:T(8,128)S(1)} %product.1), channel_id=1, source_target_pairs={{1,3},{3,1},{5,7},{7,5},{9,11},{11,9},{13,15},{15,13},{17,19},{19,... | collective-permute-start | bytes 98312 | tf_op jit(solution)/shard_map/ppermute | solution.py:35
  43.7 2.4 %collective-permute-start.12 = (f32[32,256]{1,0:T(8,128)S(1)}, f32[32,256]{1,0:T(8,128)S(1)}, u32[]{:S(2)}, u32[]{:S(2)}) collective-permute-start(f32[32,256]{1,0:T(8,128)S(1)} %add.25), channel_id=1, source_target_pairs={{1,5},{3,7},{5,1},{7,3},{9,13},{11,15},{13,9},{15,11},{17,21},{19,... | collective-permute-start | bytes 98312 | tf_op jit(solution)/shard_map/ppermute | solution.py:35
  46.1 0.7 %collective-permute-start.13 = (f32[32,256]{1,0:T(8,128)S(1)}, f32[32,256]{1,0:T(8,128)S(1)}, u32[]{:S(2)}, u32[]{:S(2)}) collective-permute-start(f32[32,256]{1,0:T(8,128)S(1)} %add.26), channel_id=1, source_target_pairs={{1,9},{3,11},{5,13},{7,15},{9,1},{11,3},{13,5},{15,7},{17,25},{19,... | collective-permute-start | bytes 98312 | tf_op jit(solution)/shard_map/ppermute | solution.py:35
  46.8 11.0 %collective-permute-start.14 = (f32[32,256]{1,0:T(8,128)S(1)}, f32[32,256]{1,0:T(8,128)S(1)}, u32[]{:S(2)}, u32[]{:S(2)}) collective-permute-start(f32[32,256]{1,0:T(8,128)S(1)} %add.27.mine_ref), channel_id=1, source_target_pairs={{1,0},{3,2},{5,4},{7,6},{9,8},{11,10},{13,12},{15,14},{17,16},{19,... | collective-permute-start | bytes 98312 | tf_op jit(solution)/shard_map/ppermute | solution.py:39

commit v11 on v10

--- a/solution.py
+++ b/solution.py
@@ -19,40 +19,36 @@
 VMEM = pl.BlockSpec(memory_space=pltpu.VMEM)
 
 
-def bits_of(axis, size):
-    assert size > 1 and size & (size - 1) == 0
-    return [(axis, 1 << i) for i in range(size.bit_length() - 1)]
-
-
-def swapped(value, sizes, way):
-    axis, bit = way
+def swapped(value, sizes, bits):
     pairs = []
     for dp in range(sizes["dp"]):
         for sub in range(sizes["sub"]):
-            here = {"dp": dp, "sub": sub}
-            there = {**here, axis: here[axis] ^ bit}
-            pairs.append(tuple((c["dp"] * sizes["sub"] + c["sub"]) * 2 + 1 for c in (here, there)))
+            for pair in range(2):
+                pairs.append(tuple(
+                    (z * sizes["sub"] + x) * 2 + pair
+                    for z, x in ((dp, sub), (dp ^ bits["dp"], sub ^ bits["sub"]))))
     return lax.ppermute(value, AXES, pairs)
 
 
-def to_first(value):
-    return lax.ppermute(value, "pair", [(1, 0)])
-
-
-def to_second(value):
-    return lax.ppermute(value, "pair", [(0, 1)])
-
-
-def of_second(mine, got):
-    return jnp.where(lax.axis_index("pair") == 1, mine, got)
-
-
-def side():
-    return lax.axis_index("sub") & 1
-
-
-def half_of(chosen, piece, start=0, size=None):
-    return pl.ds(pl.multiple_of(chosen * piece + start, CHUNK), size or piece)
+def across(value):
+    return lax.ppermute(value, "pair", [(0, 1), (1, 0)])
+
+
+def bits_of(axis, size):
+    assert size > 1 and size & (size - 1) == 0
+    return [{"dp": 0, "sub": 0, axis: 1 << i} for i in range(size.bit_length() - 1)]
+
+
+def both_bits(a, b):
+    return {axis: a[axis] ^ b[axis] for axis in a}
+
+
+def summed(value, sizes, group):
+    if len(group) == 1:
+        return value + swapped(value, sizes, group[0])
+    one, two, three = (
+        swapped(value, sizes, bits) for bits in (group[0], group[1], both_bits(*group)))
+    return (value + one) + (two + three)
 
 
 def parts_of(value, count):
@@ -86,7 +82,7 @@
     return [(source.at[part, :], target.at[part, :]) for part in rows]
 
 
-def term_kernel(x_hbm, c_hbm, e_hbm, seed_hbm, halves_ref,
+def term_kernel(x_hbm, c_hbm, e_hbm, seed_hbm, keep_ref, send_ref,
                 x_ref, c_ref, e_ref, seed_ref, term_ref, sems):
     copies = whole_copies(
         [(seed_hbm, seed_ref), (c_hbm, c_ref)] + row_parts(e_hbm.at[0], e_ref, 2)
@@ -95,7 +91,7 @@
         copy.start()
     rank = seed_ref.shape[0]
     tokens, width = x_ref.shape
-    piece = halves_ref.shape[2]
+    half, piece = keep_ref.shape[1:]
     copies[0].wait()
     copies[1].wait()
     seed = jnp.concatenate(parts_of(seed_ref[...], 3), axis=0)
@@ -114,8 +110,20 @@
         for i in range(blocks):
             part = pl.ds(i * CHUNK, CHUNK)
             term_ref[:, part] += added(dot(own, x_ref[rows, part], ((1,), (0,))), rank)
+    low = lax.axis_index("pair") == 0
     for i in range(2):
-        halves_ref[i] = term_ref[:, half_of(side() ^ i, piece)]
+        part = half_of(side() ^ i, piece)
+        top, bottom = term_ref[:half, part], term_ref[half:, part]
+        keep_ref[i] = jnp.where(low, top, bottom)
+        send_ref[i] = jnp.where(low, bottom, top)
+
+
+def side():
+    return lax.axis_index("sub") & 1
+
+
+def half_of(chosen, piece, start=0, size=None):
+    return pl.ds(pl.multiple_of(chosen * piece + start, CHUNK), size or piece)
 
 
 def added(stack, rank):
@@ -132,8 +140,8 @@
     return pl.pallas_call(
         term_kernel,
         in_specs=[HBM] * 4,
-        out_specs=VMEM,
-        out_shape=jax.ShapeDtypeStruct((2, rank, width // 2), F32),
+        out_specs=[VMEM] * 2,
+        out_shape=[jax.ShapeDtypeStruct((2, rank // 2, width // 2), F32)] * 2,
         scratch_shapes=[
             pltpu.VMEM((tokens, width), BF16),
             pltpu.VMEM((tokens, out), BF16),
@@ -228,6 +236,11 @@
     )(near, far, *mine, *other)
 
 
+def both_halves(mine, other):
+    low = lax.axis_index("pair") == 0
+    return jnp.concatenate([jnp.where(low, mine, other), jnp.where(low, other, mine)], axis=0)
+
+
 def gram_blocks(rows):
     stack = jnp.concatenate(parts_of(rows, 3), axis=0)
     return dot(stack, stack, ((1,), (1,)))
@@ -272,13 +285,14 @@
     return dot(lefts, rights, ((1,), (0,)))
 
 
-def first_sweep_kernel(near_ref, far_ref, got_near_ref, got_far_ref, rows_ref, step_ref, gram_ref):
-    rank, piece = near_ref.shape
+def first_sweep_kernel(mine_ref, other_ref, rows_ref, step_ref, gram_ref):
+    half, piece = mine_ref.shape[1:]
+    rank = 2 * half
     blocks = None
-    for i, (mine_ref, got_ref) in enumerate([(near_ref, got_near_ref), (far_ref, got_far_ref)]):
+    for i in range(2):
         for j in range(piece // CHUNK):
             part = slice(j * CHUNK, (j + 1) * CHUNK)
-            rows = of_second(mine_ref[:, part], got_ref[:, part])
+            rows = both_halves(mine_ref[i, :, part], other_ref[i, :, part])
             rows_ref[:, half_of(side() ^ i, piece, j * CHUNK, CHUNK)] = rows
             term = gram_blocks(rows)
             blocks = term if blocks is None else blocks + term
@@ -294,9 +308,9 @@
     gram_ref[...] = gram_of(blocks, rank)
 
 
-def first_sweep(near, far, got_near, got_far):
-    rank, piece = near.shape
-    width = 2 * piece
+def first_sweep(mine, other):
+    _, half, piece = mine.shape
+    rank, width = 2 * half, 2 * piece
     return pl.pallas_call(
         first_sweep_kernel,
         out_shape=[
@@ -307,19 +321,14 @@
         compiler_params=params(),
         cost_estimate=cost(10 ** 9, 7 * 10 ** 6),
         name="first_sweep",
-    )(near, far, got_near, got_far)
-
-
-def second_sweep_kernel(rows_ref, step_ref, gram_ref, basis_ref, inverse_ref, lefts_ref):
+    )(mine, other)
+
+
+def second_sweep_kernel(rows_ref, step_ref, gram_ref, basis_ref, inverse_ref):
     last = inverse_factor(gram_ref[...])
-    rank = last.shape[0]
     for i in range(rows_ref.shape[1] // CHUNK):
         part = slice(i * CHUNK, (i + 1) * CHUNK)
-        basis = short_dot(last, rows_ref[:, part])
-        basis_ref[:, part] = basis
-        high, low = parts_of(basis, 2)
-        zeros = jnp.zeros((lefts_ref.shape[1] - 3 * rank, CHUNK), BF16)
-        lefts_ref[part, :] = jnp.concatenate([high, high, low, zeros], axis=0).T
+        basis_ref[:, part] = short_dot(last, rows_ref[:, part])
     inverse_ref[...] = short_dot(last, step_ref[...])
 
 
@@ -329,7 +338,6 @@
         out_shape=[
             jax.ShapeDtypeStruct(rows.shape, F32),
             jax.ShapeDtypeStruct(step.shape, F32),
-            jax.ShapeDtypeStruct((rows.shape[1], 128), BF16),
         ],
         compiler_params=params(),
         cost_estimate=cost(10 ** 9, 7 * 10 ** 6),
@@ -337,23 +345,24 @@
     )(rows, step, gram)
 
 
-def error_kernel(workers, basis_ref, lefts_ref, inverse_ref, mine_ref, got_ref, *refs):
+def error_kernel(workers, basis_ref, inverse_ref, mine_ref, other_ref, *refs):
     merged_refs = refs[:PARTS]
     error_hbm, basis_hbm, second_ref, error_ref, error_sem, basis_sem = refs[PARTS:]
     size = merged_refs[0].shape[0]
     keep = pltpu.make_async_copy(basis_ref, basis_hbm, basis_sem)
     keep.start()
-    product = of_second(mine_ref[...], got_ref[...])
+    product = both_halves(mine_ref[...], other_ref[...])
     second = short_dot(inverse_ref[...], product) * (1.0 / workers)
     second_ref[...] = second
-    high, low = parts_of(second, 2)
-    zeros = jnp.zeros((lefts_ref.shape[1] - 3 * high.shape[0], high.shape[1]), BF16)
-    rights = jnp.concatenate([high, low, high, zeros], axis=0)
+    s_high, s_low = parts_of(second, 2)
+    rights = jnp.concatenate([s_high, s_low, s_high], axis=0)
     copies = []
-    for i in range(lefts_ref.shape[0] // CHUNK):
+    for i in range(error_ref.shape[0] // CHUNK):
         start = i * CHUNK
         part = pl.ds(start, CHUNK)
-        approx = dot(lefts_ref[part, :], rights, ((1,), (0,)))
+        b_high, b_low = parts_of(basis_ref[:, part], 2)
+        lefts = jnp.concatenate([b_high, b_high, b_low], axis=0)
+        approx = dot(lefts, rights, ((0,), (0,)))
         merged = merged_refs[start // size][start % size:start % size + CHUNK, :]
         error_ref[part, :] = (merged - approx).astype(BF16)
         copies.append(pltpu.make_async_copy(
@@ -363,12 +372,12 @@
         copy.wait()
 
 
-def error_of(merged, basis, lefts, inverse, mine, got, workers):
+def error_of(merged, basis, inverse, mine, other, workers):
     rank, width = basis.shape
     out = mine.shape[1]
     return pl.pallas_call(
         functools.partial(error_kernel, workers),
-        in_specs=[VMEM] * (5 + PARTS),
+        in_specs=[VMEM] * (4 + PARTS),
         out_specs=[HBM, HBM, VMEM],
         out_shape=[
             jax.ShapeDtypeStruct((1, width, out), BF16),
@@ -383,36 +392,36 @@
         compiler_params=params(),
         cost_estimate=cost(2 * rank * width * out, 6 * width * out),
         name="error_next",
-    )(basis, lefts, inverse, mine, got, *merged)
+    )(basis, inverse, mine, other, *merged)
 
 
 def local(sizes, *arguments):
     inputs, cotangent, error_prev, seed_q = (
         pltpu.with_memory_space_constraint(value, pltpu.HBM) for value in arguments)
     rounds = bits_of("sub", sizes["sub"]) + bits_of("dp", sizes["dp"])
+    beside, others = rounds[0], rounds[1:]
     workers = 2 * sizes["sub"] * sizes["dp"]
 
-    halves = term_halves(inputs, cotangent, error_prev, seed_q)
-    halves = halves + to_second(halves)
-    merged = merge(inputs, cotangent, error_prev, halves)
-    merged_other = [to_second(rows) for rows in merged]
-    near = halves[0] + swapped(halves[1], sizes, rounds[0])
-    for way in rounds[1:]:
-        near = near + swapped(near, sizes, way)
-    far = swapped(near, sizes, rounds[0])
-    got_near, got_far = to_first(near), to_first(far)
+    keep, send = term_halves(inputs, cotangent, error_prev, seed_q)
+    part = keep + across(send)
+    merged = merge(inputs, cotangent, error_prev, part)
+    merged_other = [across(rows) for rows in merged]
+    near = part[0] + swapped(part[1], sizes, beside)
+    for bits in others:
+        near = near + swapped(near, sizes, bits)
+    far = swapped(near, sizes, beside)
+    mine = jnp.stack([near, far])
+    other = across(mine)
 
     product = product_of(near, far, merged, merged_other)
-    product, got_near, got_far = lax.optimization_barrier((product, got_near, got_far))
-    rows, step, gram = first_sweep(near, far, got_near, got_far)
-    product = product + swapped(product, sizes, rounds[0])
+    rows, step, gram = first_sweep(mine, other)
+    product = summed(product, sizes, [beside])
     product, rows, step, gram = lax.optimization_barrier((product, rows, step, gram))
-    basis, inverse, lefts = second_sweep(rows, step, gram)
-    product = product + swapped(product, sizes, rounds[1])
-    product, basis, inverse, lefts = lax.optimization_barrier((product, basis, inverse, lefts))
-    for way in rounds[2:]:
-        product = product + swapped(product, sizes, way)
-    return error_of(merged, basis, lefts, inverse, product, to_first(product), workers)
+    basis, inverse = second_sweep(rows, step, gram)
+    for i in range(0, len(others), 2):
+        product = summed(product, sizes, others[i:i + 2])
+    product, basis, inverse = lax.optimization_barrier((product, basis, inverse))
+    return error_of(merged, basis, inverse, product, across(product), workers)
 
 
 def solution(mesh):

time: 60.4 us -> 44 us (0.73)
  waiting for transfers between devices: 25.9 us -> 15.9 us
  starting transfers between devices: 20.5 us -> 14.7 us
    ppermute x8 -> x7, waiting for transfers between devices: 25.9 us -> 2.17 us  [across(): return lax.ppermute(value, 'pair', [(0, 1), (1, 0)])]
    ppermute x8 -> x7, starting transfers between devices: 15.8 us -> 1.73 us  [across(): return lax.ppermute(value, 'pair', [(0, 1), (1, 0)])]
    ppermute x7 -> x8, waiting for transfers between devices: 0.02 us -> 13.7 us  [swapped(): return lax.ppermute(value, AXES, pairs)]
    ppermute x7 -> x8, starting transfers between devices: 4.65 us -> 13 us  [swapped(): return lax.ppermute(value, AXES, pairs)]
  transfers between devices with their start and end apart: 15 -> 15, of which waited for: 4 -> 8; matrix products, arithmetic and copies ran while one was open for 0% -> 0% of each run, Pallas kernels for 13% -> 18%
where the time goes in v11:
time: 44 us; the launch traced here: 43.8 us
  waiting for transfers between devices  15.9 us (36%)
  starting transfers between devices  14.7 us (33%)
  Pallas kernels  12.4 us (28%)
  between operations  0.75 us (2%)
    ppermute x8, waiting for transfers between devices, swapped(): return lax.ppermute(value, AXES, pairs)  13.7 us
    ppermute x8, starting transfers between devices, swapped(): return lax.ppermute(value, AXES, pairs)  13 us
    pallas_call x1, Pallas kernels, merge(): pl.pallas_call(merge_kernel, in_specs=[HBM] * 3 + [ANY], out_specs=[VMEM]...  2.74 us
    pallas_call x1, Pallas kernels, first_sweep(): pl.pallas_call(first_sweep_kernel, out_shape=[jax.ShapeDtypeStruct((rank,...  2.56 us
    pallas_call x1, Pallas kernels, term_halves(): pl.pallas_call(term_kernel, in_specs=[HBM] * 4, out_specs=[VMEM] * 2, out...  2.34 us
    ppermute x7, waiting for transfers between devices, across(): return lax.ppermute(value, 'pair', [(0, 1), (1, 0)])  2.17 us
    pallas_call x1, Pallas kernels, error_of(): pl.pallas_call(functools.partial(error_kernel, workers), in_specs=[VMEM]...  2.13 us
    ppermute x7, starting transfers between devices, across(): return lax.ppermute(value, 'pair', [(0, 1), (1, 0)])  1.73 us
  transfers between devices with their start and end apart: 15, of which 8 were waited for; matrix products, arithmetic and copies ran while one was open for 0% of the time, Pallas kernels for 18%

profile of v11, /device:TPU:0, one launch (start us, length us, event | category | flops | bytes accessed | tf_op | source)
XLA Modules:
  0.0 43.8 jit_solution(10998573267209889072)
XLA Ops:
  0.6 2.3 %term.1 = (f32[2,16,1024]{2,1,0:T(8,128)S(1)}, f32[2,16,1024]{2,1,0:T(8,128)S(1)}) custom-call(bf16[512,2048]{1,0:T(8,128)(2,1)} %x_hbm.3, bf16[512,256]{1,0:T(8,128)(2,1)} %c_hbm.3, bf16[1,2048,256]{2,1,0:T(8,128)(2,1)} %e_hbm.3, f32[32,256]{1,0:T(8,128)} %seed_hbm.1), custom_call_target="tpu_custom_call" | custom-call | flops 201326592 | bytes 3145728 | tf_op jit(solution)/shard_map/term/pallas_call | solution.py:140
  3.0 0.5 %collective-permute-start = (f32[2,16,1024]{2,1,0:T(8,128)S(1)}, f32[2,16,1024]{2,1,0:T(8,128)S(1)}, u32[]{:S(2)}, u32[]{:S(2)}) collective-permute-start(f32[2,16,1024]{2,1,0:T(8,128)S(1)} %get-tuple-element.22), channel_id=1, source_target_pairs={{0,1},{1,0},{2,3},{3,2},{4,5},{5,4},{6,7},{7,6},{8,9},{9,8},{10,11... | collective-permute-start | bytes 393224 | tf_op jit(solution)/shard_map/ppermute | solution.py:34
  3.5 1.0 %collective-permute-done = f32[2,16,1024]{2,1,0:T(8,128)S(1)} collective-permute-done((f32[2,16,1024]{2,1,0:T(8,128)S(1)}, f32[2,16,1024]{2,1,0:T(8,128)S(1)}, u32[]{:S(2)}, u32[]{:S(2)}) %collective-permute-start) | collective-permute-done | bytes 131104 | tf_op jit(solution)/shard_map/ppermute | solution.py:34
  4.5 2.9 %collective-permute-start.1 = (f32[16,1024]{1,0:T(8,128)S(1)}, f32[16,1024]{1,0:T(8,128)S(1)}, u32[]{:S(2)}, u32[]{:S(2)}) collective-permute-start(f32[16,1024]{1,0:T(8,128)S(1)} %slice_bitcast_fusion), channel_id=1, source_target_pairs={{0,2},{1,3},{2,0},{3,1},{4,6},{5,7},{6,4},{7,5},{8,10},{9,11},{10,... | collective-permute-start | bytes 196616 | tf_op jit(solution)/shard_map/ppermute | solution.py:30
  7.4 2.7 %merge.1 = (f32[512,256]{1,0:T(8,128)S(1)}, f32[512,256]{1,0:T(8,128)S(1)}, f32[512,256]{1,0:T(8,128)S(1)}, f32[512,256]{1,0:T(8,128)S(1)}) custom-call(bf16[512,2048]{1,0:T(8,128)(2,1)} %x_hbm.3, bf16[512,256]{1,0:T(8,128)(2,1)} %c_hbm.3, bf16[1,2048,256]{2,1,0:T(8,128)(2,1)} %e_hbm.3, f32[2,16,1024]{2,1,0:T(8,128)S(1)} %add.24.after_hbm), custom_call_target="tpu_custom_call" | custom-call | flops 100000000 | bytes 1000000 | tf_op jit(solution)/shard_map/merge/pallas_call | solution.py:178
  10.2 0.1 collective-permute-start.5
  10.3 0.5 %collective-permute-start.6 = (f32[512,256]{1,0:T(8,128)S(1)}, f32[512,256]{1,0:T(8,128)S(1)}, u32[]{:S(2)}, u32[]{:S(2)}) collective-permute-start(f32[512,256]{1,0:T(8,128)S(1)} %get-tuple-element.24.refs_1_), channel_id=1, source_target_pairs={{0,1},{1,0},{2,3},{3,2},{4,5},{5,4},{6,7},{7,6},{8,9},{9,8},{10,11... | collective-permute-start | bytes 1572872 | tf_op jit(solution)/shard_map/ppermute | solution.py:34
  10.8 0.1 collective-permute-start.7
  10.8 0.4 collective-permute-start.8
  11.3 0.0 collective-permute-done.1
  11.3 1.6 %collective-permute-start.2 = (f32[16,1024]{1,0:T(8,128)S(1)}, f32[16,1024]{1,0:T(8,128)S(1)}, u32[]{:S(2)}, u32[]{:S(2)}) collective-permute-start(f32[16,1024]{1,0:T(8,128)S(1)} %fusion), channel_id=1, source_target_pairs={{0,4},{1,5},{2,6},{3,7},{4,0},{5,1},{6,2},{7,3},{8,12},{9,13},{10,... | collective-permute-start | bytes 196616 | tf_op jit(solution)/shard_map/ppermute | solution.py:30
  12.9 2.7 %collective-permute-done.2 = f32[16,1024]{1,0:T(8,128)S(1)} collective-permute-done((f32[16,1024]{1,0:T(8,128)S(1)}, f32[16,1024]{1,0:T(8,128)S(1)}, u32[]{:S(2)}, u32[]{:S(2)}) %collective-permute-start.2) | collective-permute-done | bytes 65568 | tf_op jit(solution)/shard_map/ppermute | solution.py:30
  15.6 2.7 %collective-permute-start.3 = (f32[16,1024]{1,0:T(8,128)S(1)}, f32[16,1024]{1,0:T(8,128)S(1)}, u32[]{:S(2)}, u32[]{:S(2)}) collective-permute-start(f32[16,1024]{1,0:T(8,128)S(1)} %add.26), channel_id=1, source_target_pairs={{0,8},{1,9},{2,10},{3,11},{4,12},{5,13},{6,14},{7,15},{8,0},{9,1},... | collective-permute-start | bytes 196616 | tf_op jit(solution)/shard_map/ppermute | solution.py:30
  18.3 2.6 %collective-permute-done.3 = f32[16,1024]{1,0:T(8,128)S(1)} collective-permute-done((f32[16,1024]{1,0:T(8,128)S(1)}, f32[16,1024]{1,0:T(8,128)S(1)}, u32[]{:S(2)}, u32[]{:S(2)}) %collective-permute-start.3) | collective-permute-done | bytes 65568 | tf_op jit(solution)/shard_map/ppermute | solution.py:30
  20.9 0.5 %collective-permute-start.4 = (f32[16,1024]{1,0:T(8,128)S(1)}, f32[16,1024]{1,0:T(8,128)S(1)}, u32[]{:S(2)}, u32[]{:S(2)}) collective-permute-start(f32[16,1024]{1,0:T(8,128)S(1)} %add.27.near_ref), channel_id=1, source_target_pairs={{0,2},{1,3},{2,0},{3,1},{4,6},{5,7},{6,4},{7,5},{8,10},{9,11},{10,... | collective-permute-start | bytes 196616 | tf_op jit(solution)/shard_map/ppermute | solution.py:30
  21.4 3.8 %collective-permute-done.4.far_ref = f32[16,1024]{1,0:T(8,128)S(1)} collective-permute-done((f32[16,1024]{1,0:T(8,128)S(1)}, f32[16,1024]{1,0:T(8,128)S(1)}, u32[]{:S(2)}, u32[]{:S(2)}) %collective-permute-start.4) | collective-permute-done | bytes 65568 | tf_op jit(solution)/shard_map/ppermute | solution.py:30
  25.2 0.1 collective-permute-start.10
  25.3 0.0 collective-permute-done.5.refs_4_
  25.3 0.0 collective-permute-done.6.refs_5_
  25.3 0.0 collective-permute-done.7.refs_6_
  25.3 0.0 collective-permute-done.8.refs_7_
  25.3 1.0 %product.1 = f32[16,256]{1,0:T(8,128)S(1)} custom-call(f32[16,1024]{1,0:T(8,128)S(1)} %add.27.near_ref, f32[16,1024]{1,0:T(8,128)S(1)} %collective-permute-done.4.far_ref, f32[512,256]{1,0:T(8,128)S(1)} %get-tuple-element.23.refs_0_, f32[512,256]{1,0:T(8,128)S(1)} %get-tuple-element.24.refs_1_, f32[512,256]{1,0:T(8,128)S(1)} %get-tuple-element.25.refs_2_, ...), custom_call_target="tpu_custom_call" | custom-call | flops 16777216 | bytes 4194304 | tf_op jit(solution)/shard_map/product/pallas_call | solution.py:228
  26.3 0.5 %collective-permute-start.9 = (f32[16,256]{1,0:T(8,128)S(1)}, f32[16,256]{1,0:T(8,128)S(1)}, u32[]{:S(2)}, u32[]{:S(2)}) collective-permute-start(f32[16,256]{1,0:T(8,128)S(1)} %product.1), channel_id=1, source_target_pairs={{0,2},{1,3},{2,0},{3,1},{4,6},{5,7},{6,4},{7,5},{8,10},{9,11},{10,... | collective-permute-start | bytes 49160 | tf_op jit(solution)/shard_map/ppermute | solution.py:30
  26.8 0.0 collective-permute-done.10.other_ref
  26.8 2.6 %first_sweep.1 = (f32[32,2048]{1,0:T(8,128)S(1)}, f32[32,32]{1,0:T(8,128)S(1)}, f32[32,32]{1,0:T(8,128)S(1)}) custom-call(f32[2,16,1024]{2,1,0:T(8,128)S(1)} %pad_maximum_fusion.mine_ref, f32[2,16,1024]{2,1,0:T(8,128)S(1)} %collective-permute-done.10.other_ref), custom_call_target="tpu_custom_call" | custom-call | flops 1000000000 | bytes 7000000 | tf_op jit(solution)/shard_map/first_sweep/pallas_call | solution.py:314
  29.4 0.7 %collective-permute-done.9 = f32[16,256]{1,0:T(8,128)S(1)} collective-permute-done((f32[16,256]{1,0:T(8,128)S(1)}, f32[16,256]{1,0:T(8,128)S(1)}, u32[]{:S(2)}, u32[]{:S(2)}) %collective-permute-start.9) | collective-permute-done | bytes 16416 | tf_op jit(solution)/shard_map/ppermute | solution.py:30
  30.1 1.6 %collective-permute-start.11 = (f32[16,256]{1,0:T(8,128)S(1)}, f32[16,256]{1,0:T(8,128)S(1)}, u32[]{:S(2)}, u32[]{:S(2)}) collective-permute-start(f32[16,256]{1,0:T(8,128)S(1)} %add.28), channel_id=1, source_target_pairs={{0,4},{1,5},{2,6},{3,7},{4,0},{5,1},{6,2},{7,3},{8,12},{9,13},{10,... | collective-permute-start | bytes 49160 | tf_op jit(solution)/shard_map/ppermute | solution.py:30
  31.7 3.2 %collective-permute-start.12 = (f32[16,256]{1,0:T(8,128)S(1)}, f32[16,256]{1,0:T(8,128)S(1)}, u32[]{:S(2)}, u32[]{:S(2)}) collective-permute-start(f32[16,256]{1,0:T(8,128)S(1)} %add.28), channel_id=1, source_target_pairs={{0,8},{1,9},{2,10},{3,11},{4,12},{5,13},{6,14},{7,15},{8,0},{9,1},... | collective-permute-start | bytes 49160 | tf_op jit(solution)/shard_map/ppermute | solution.py:30
  34.9 0.0 collective-permute-start.13
  34.9 1.6 %second_sweep.1 = (f32[32,2048]{1,0:T(8,128)S(1)}, f32[32,32]{1,0:T(8,128)S(1)}) custom-call(f32[32,2048]{1,0:T(8,128)S(1)} %get-tuple-element.31.rows_ref, f32[32,32]{1,0:T(8,128)S(1)} %get-tuple-element.32.step_ref, f32[32,32]{1,0:T(8,128)S(1)} %get-tuple-element.33.gram_ref), custom_call_target="tpu_custom_call" | custom-call | flops 1000000000 | bytes 7000000 | tf_op jit(solution)/shard_map/second_sweep/pallas_call | solution.py:336
  36.5 0.0 collective-permute-done.11
  36.5 0.2 collective-permute-done.12
  36.7 3.7 %collective-permute-done.13 = f32[16,256]{1,0:T(8,128)S(1)} collective-permute-done((f32[16,256]{1,0:T(8,128)S(1)}, f32[16,256]{1,0:T(8,128)S(1)}, u32[]{:S(2)}, u32[]{:S(2)}) %collective-permute-start.13) | collective-permute-done | bytes 16416 | tf_op jit(solution)/shard_map/ppermute | solution.py:30
  40.4 0.1 collective-permute-start.14
  40.5 1.2 %collective-permute-done.14.other_ref = f32[16,256]{1,0:T(8,128)S(1)} collective-permute-done((f32[16,256]{1,0:T(8,128)S(1)}, f32[16,256]{1,0:T(8,128)S(1)}, u32[]{:S(2)}, u32[]{:S(2)}) %collective-permute-start.14) | collective-permute-done | bytes 16416 | tf_op jit(solution)/shard_map/ppermute | solution.py:34
  41.7 2.1 %error_next.1 = (bf16[1,2048,256]{2,1,0:T(8,128)(2,1)}, f32[32,2048]{1,0:T(8,128)}, f32[32,256]{1,0:T(8,128)}) custom-call(f32[32,2048]{1,0:T(8,128)S(1)} %get-tuple-element.36.basis_ref, f32[32,32]{1,0:T(8,128)S(1)} %get-tuple-element.37.inverse_ref, f32[16,256]{1,0:T(8,128)S(1)} %add_add_fusion.mine_ref, f32[16,256]{1,0:T(8,128)S(1)} %collective-permute-done.14.other_ref, ...), custom_call_target="tpu_custom_call" | custom-call | flops 33554432 | bytes 3145728 | tf_op jit(solution)/shard_map/error_next/pallas_call | solution.py:378
  (8 shorter events, 0.1 us)
Async XLA Ops:
  3.0 1.5 %collective-permute-start = (f32[2,16,1024]{2,1,0:T(8,128)S(1)}, f32[2,16,1024]{2,1,0:T(8,128)S(1)}, u32[]{:S(2)}, u32[]{:S(2)}) collective-permute-start(f32[2,16,1024]{2,1,0:T(8,128)S(1)} %get-tuple-element.22), channel_id=1, source_target_pairs={{0,1},{1,0},{2,3},{3,2},{4,5},{5,4},{6,7},{7,6},{8,9},{9,8},{10,11... | collective-permute-start | bytes 393224 | tf_op jit(solution)/shard_map/ppermute | solution.py:34
  4.5 6.8 %collective-permute-start.1 = (f32[16,1024]{1,0:T(8,128)S(1)}, f32[16,1024]{1,0:T(8,128)S(1)}, u32[]{:S(2)}, u32[]{:S(2)}) collective-permute-start(f32[16,1024]{1,0:T(8,128)S(1)} %slice_bitcast_fusion), channel_id=1, source_target_pairs={{0,2},{1,3},{2,0},{3,1},{4,6},{5,7},{6,4},{7,5},{8,10},{9,11},{10,... | collective-permute-start | bytes 196616 | tf_op jit(solution)/shard_map/ppermute | solution.py:30
  10.2 15.1 %collective-permute-start.5 = (f32[512,256]{1,0:T(8,128)S(1)}, f32[512,256]{1,0:T(8,128)S(1)}, u32[]{:S(2)}, u32[]{:S(2)}) collective-permute-start(f32[512,256]{1,0:T(8,128)S(1)} %get-tuple-element.23.refs_0_), channel_id=1, source_target_pairs={{0,1},{1,0},{2,3},{3,2},{4,5},{5,4},{6,7},{7,6},{8,9},{9,8},{10,11... | collective-permute-start | bytes 1572872 | tf_op jit(solution)/shard_map/ppermute | solution.py:34
  10.3 15.0 %collective-permute-start.6 = (f32[512,256]{1,0:T(8,128)S(1)}, f32[512,256]{1,0:T(8,128)S(1)}, u32[]{:S(2)}, u32[]{:S(2)}) collective-permute-start(f32[512,256]{1,0:T(8,128)S(1)} %get-tuple-element.24.refs_1_), channel_id=1, source_target_pairs={{0,1},{1,0},{2,3},{3,2},{4,5},{5,4},{6,7},{7,6},{8,9},{9,8},{10,11... | collective-permute-start | bytes 1572872 | tf_op jit(solution)/shard_map/ppermute | solution.py:34
  10.8 14.6 %collective-permute-start.7 = (f32[512,256]{1,0:T(8,128)S(1)}, f32[512,256]{1,0:T(8,128)S(1)}, u32[]{:S(2)}, u32[]{:S(2)}) collective-permute-start(f32[512,256]{1,0:T(8,128)S(1)} %get-tuple-element.25.refs_2_), channel_id=1, source_target_pairs={{0,1},{1,0},{2,3},{3,2},{4,5},{5,4},{6,7},{7,6},{8,9},{9,8},{10,11... | collective-permute-start | bytes 1572872 | tf_op jit(solution)/shard_map/ppermute | solution.py:34
  10.8 14.5 %collective-permute-start.8 = (f32[512,256]{1,0:T(8,128)S(1)}, f32[512,256]{1,0:T(8,128)S(1)}, u32[]{:S(2)}, u32[]{:S(2)}) collective-permute-start(f32[512,256]{1,0:T(8,128)S(1)} %get-tuple-element.26.refs_3_), channel_id=1, source_target_pairs={{0,1},{1,0},{2,3},{3,2},{4,5},{5,4},{6,7},{7,6},{8,9},{9,8},{10,11... | collective-permute-start | bytes 1572872 | tf_op jit(solution)/shard_map/ppermute | solution.py:34
  11.3 4.3 %collective-permute-start.2 = (f32[16,1024]{1,0:T(8,128)S(1)}, f32[16,1024]{1,0:T(8,128)S(1)}, u32[]{:S(2)}, u32[]{:S(2)}) collective-permute-start(f32[16,1024]{1,0:T(8,128)S(1)} %fusion), channel_id=1, source_target_pairs={{0,4},{1,5},{2,6},{3,7},{4,0},{5,1},{6,2},{7,3},{8,12},{9,13},{10,... | collective-permute-start | bytes 196616 | tf_op jit(solution)/shard_map/ppermute | solution.py:30
  15.6 5.2 %collective-permute-start.3 = (f32[16,1024]{1,0:T(8,128)S(1)}, f32[16,1024]{1,0:T(8,128)S(1)}, u32[]{:S(2)}, u32[]{:S(2)}) collective-permute-start(f32[16,1024]{1,0:T(8,128)S(1)} %add.26), channel_id=1, source_target_pairs={{0,8},{1,9},{2,10},{3,11},{4,12},{5,13},{6,14},{7,15},{8,0},{9,1},... | collective-permute-start | bytes 196616 | tf_op jit(solution)/shard_map/ppermute | solution.py:30
  20.9 4.3 %collective-permute-start.4 = (f32[16,1024]{1,0:T(8,128)S(1)}, f32[16,1024]{1,0:T(8,128)S(1)}, u32[]{:S(2)}, u32[]{:S(2)}) collective-permute-start(f32[16,1024]{1,0:T(8,128)S(1)} %add.27.near_ref), channel_id=1, source_target_pairs={{0,2},{1,3},{2,0},{3,1},{4,6},{5,7},{6,4},{7,5},{8,10},{9,11},{10,... | collective-permute-start | bytes 196616 | tf_op jit(solution)/shard_map/ppermute | solution.py:30
  25.2 1.6 %collective-permute-start.10 = (f32[2,16,1024]{2,1,0:T(8,128)S(1)}, f32[2,16,1024]{2,1,0:T(8,128)S(1)}, u32[]{:S(2)}, u32[]{:S(2)}) collective-permute-start(f32[2,16,1024]{2,1,0:T(8,128)S(1)} %pad_maximum_fusion.mine_ref), channel_id=1, source_target_pairs={{0,1},{1,0},{2,3},{3,2},{4,5},{5,4},{6,7},{7,6},{8,9},{9,8},{10,11... | collective-permute-start | bytes 393224 | tf_op jit(solution)/shard_map/ppermute | solution.py:34
  26.3 3.8 %collective-permute-start.9 = (f32[16,256]{1,0:T(8,128)S(1)}, f32[16,256]{1,0:T(8,128)S(1)}, u32[]{:S(2)}, u32[]{:S(2)}) collective-permute-start(f32[16,256]{1,0:T(8,128)S(1)} %product.1), channel_id=1, source_target_pairs={{0,2},{1,3},{2,0},{3,1},{4,6},{5,7},{6,4},{7,5},{8,10},{9,11},{10,... | collective-permute-start | bytes 49160 | tf_op jit(solution)/shard_map/ppermute | solution.py:30
  30.1 6.4 %collective-permute-start.11 = (f32[16,256]{1,0:T(8,128)S(1)}, f32[16,256]{1,0:T(8,128)S(1)}, u32[]{:S(2)}, u32[]{:S(2)}) collective-permute-start(f32[16,256]{1,0:T(8,128)S(1)} %add.28), channel_id=1, source_target_pairs={{0,4},{1,5},{2,6},{3,7},{4,0},{5,1},{6,2},{7,3},{8,12},{9,13},{10,... | collective-permute-start | bytes 49160 | tf_op jit(solution)/shard_map/ppermute | solution.py:30
  31.7 5.0 %collective-permute-start.12 = (f32[16,256]{1,0:T(8,128)S(1)}, f32[16,256]{1,0:T(8,128)S(1)}, u32[]{:S(2)}, u32[]{:S(2)}) collective-permute-start(f32[16,256]{1,0:T(8,128)S(1)} %add.28), channel_id=1, source_target_pairs={{0,8},{1,9},{2,10},{3,11},{4,12},{5,13},{6,14},{7,15},{8,0},{9,1},... | collective-permute-start | bytes 49160 | tf_op jit(solution)/shard_map/ppermute | solution.py:30
  34.9 5.5 %collective-permute-start.13 = (f32[16,256]{1,0:T(8,128)S(1)}, f32[16,256]{1,0:T(8,128)S(1)}, u32[]{:S(2)}, u32[]{:S(2)}) collective-permute-start(f32[16,256]{1,0:T(8,128)S(1)} %add.28), channel_id=1, source_target_pairs={{0,12},{1,13},{2,14},{3,15},{4,8},{5,9},{6,10},{7,11},{8,4},{9,5},... | collective-permute-start | bytes 49160 | tf_op jit(solution)/shard_map/ppermute | solution.py:30
  40.4 1.2 %collective-permute-start.14 = (f32[16,256]{1,0:T(8,128)S(1)}, f32[16,256]{1,0:T(8,128)S(1)}, u32[]{:S(2)}, u32[]{:S(2)}) collective-permute-start(f32[16,256]{1,0:T(8,128)S(1)} %add_add_fusion.mine_ref), channel_id=1, source_target_pairs={{0,1},{1,0},{2,3},{3,2},{4,5},{5,4},{6,7},{7,6},{8,9},{9,8},{10,11... | collective-permute-start | bytes 49160 | tf_op jit(solution)/shard_map/ppermute | solution.py:34

commit v12 on v11

--- a/solution.py
+++ b/solution.py
@@ -39,18 +39,6 @@
     return [{"dp": 0, "sub": 0, axis: 1 << i} for i in range(size.bit_length() - 1)]
 
 
-def both_bits(a, b):
-    return {axis: a[axis] ^ b[axis] for axis in a}
-
-
-def summed(value, sizes, group):
-    if len(group) == 1:
-        return value + swapped(value, sizes, group[0])
-    one, two, three = (
-        swapped(value, sizes, bits) for bits in (group[0], group[1], both_bits(*group)))
-    return (value + one) + (two + three)
-
-
 def parts_of(value, count):
     parts = []
     for _ in range(count):
@@ -82,8 +70,8 @@
     return [(source.at[part, :], target.at[part, :]) for part in rows]
 
 
-def term_kernel(x_hbm, c_hbm, e_hbm, seed_hbm, keep_ref, send_ref,
-                x_ref, c_ref, e_ref, seed_ref, term_ref, sems):
+def term_kernel(x_hbm, c_hbm, e_hbm, seed_hbm, keep_ref, send_ref, x_ref, c_ref, e_ref,
+                seed_ref, term_ref, sems):
     copies = whole_copies(
         [(seed_hbm, seed_ref), (c_hbm, c_ref)] + row_parts(e_hbm.at[0], e_ref, 2)
         + row_parts(x_hbm, x_ref, 2), sems)
@@ -140,12 +128,15 @@
     return pl.pallas_call(
         term_kernel,
         in_specs=[HBM] * 4,
-        out_specs=[VMEM] * 2,
-        out_shape=[jax.ShapeDtypeStruct((2, rank // 2, width // 2), F32)] * 2,
+        out_specs=[VMEM] * 5,
+        out_shape=[
+            jax.ShapeDtypeStruct((2, rank // 2, width // 2), F32),
+            jax.ShapeDtypeStruct((2, rank // 2, width // 2), F32),
+            jax.ShapeDtypeStruct((tokens, width), BF16),
+            jax.ShapeDtypeStruct((tokens, out), BF16),
+            jax.ShapeDtypeStruct((width, out), BF16),
+        ],
         scratch_shapes=[
-            pltpu.VMEM((tokens, width), BF16),
-            pltpu.VMEM((tokens, out), BF16),
-            pltpu.VMEM((width, out), BF16),
             pltpu.VMEM((rank, out), F32),
             pltpu.VMEM((rank, width), F32),
             pltpu.SemaphoreType.DMA((6,)),
@@ -156,15 +147,8 @@
     )(inputs, cotangent, error_prev, seed_q)
 
 
-def merge_kernel(x_hbm, c_hbm, e_hbm, after_hbm, *refs):
-    merged_refs = refs[:PARTS]
-    x_ref, c_ref, e_ref, sems = refs[PARTS:]
+def merge_kernel(x_ref, c_ref, e_ref, after_ref, *merged_refs):
     size = merged_refs[0].shape[0]
-    copies = whole_copies([(c_hbm, c_ref), (x_hbm, x_ref), (e_hbm.at[0], e_ref)], sems)
-    for copy in copies:
-        copy.start()
-    for copy in copies:
-        copy.wait()
     for i in range(e_ref.shape[0] // CHUNK):
         start = i * CHUNK
         part = pl.ds(start, CHUNK)
@@ -172,36 +156,23 @@
             dot(x_ref[:, part], c_ref[...], ((0,), (0,))) + e_ref[part, :].astype(F32))
 
 
-def merge(inputs, cotangent, error_prev, after):
-    tokens, width = inputs.shape
-    out = cotangent.shape[1]
+def merge(x, c, e, after):
+    width, out = e.shape
     return pl.pallas_call(
         merge_kernel,
-        in_specs=[HBM] * 3 + [ANY],
+        in_specs=[VMEM] * 3 + [ANY],
         out_specs=[VMEM] * PARTS,
         out_shape=[jax.ShapeDtypeStruct((width // PARTS, out), F32)] * PARTS,
-        scratch_shapes=[
-            pltpu.VMEM((tokens, width), BF16),
-            pltpu.VMEM((tokens, out), BF16),
-            pltpu.VMEM((width, out), BF16),
-            pltpu.SemaphoreType.DMA((3,)),
-        ],
         compiler_params=params(),
         cost_estimate=cost(10 ** 8, 10 ** 6),
         name="merge",
-    )(inputs, cotangent, error_prev, after)
+    )(x, c, e, after)
 
 
 def product_kernel(near_ref, far_ref, *refs):
-    mine_refs, other_hbms = refs[:PARTS], refs[PARTS:2 * PARTS]
-    product_ref, other_ref, sems = refs[2 * PARTS:]
+    mine_refs, other_refs, product_ref = refs[:PARTS], refs[PARTS:2 * PARTS], refs[2 * PARTS]
     rank, piece = near_ref.shape
     size = mine_refs[0].shape[0]
-    copies = whole_copies(
-        [(other, other_ref.at[pl.ds(i * size, size), :]) for i, other in enumerate(other_hbms)],
-        sems)
-    for copy in copies:
-        copy.start()
     straight = side() == 0
     product = None
     for i in range(2 * piece // CHUNK):
@@ -211,10 +182,8 @@
         rows = jnp.where(straight, near, far) if start < piece else jnp.where(straight, far, near)
         f_high, f_low = parts_of(rows, 2)
         both = jnp.concatenate([f_high, f_low], axis=0)
-        if start % size == 0:
-            copies[start // size].wait()
-        merged = (mine_refs[start // size][start % size:start % size + CHUNK, :]
-                  + other_ref[start:start + CHUNK, :])
+        rows_here = slice(start % size, start % size + CHUNK)
+        merged = mine_refs[start // size][rows_here, :] + other_refs[start // size][rows_here, :]
         m_high, m_low = parts_of(merged, 2)
         term = added(dot(both, m_high, ((1,), (0,))), rank) + dot(f_high, m_low, ((1,), (0,)))
         product = term if product is None else product + term
@@ -223,13 +192,11 @@
 
 def product_of(near, far, mine, other):
     rank, piece = near.shape
-    out = mine[0].shape[1]
+    size, out = mine[0].shape
     width = 2 * piece
     return pl.pallas_call(
         product_kernel,
-        in_specs=[VMEM] * (2 + PARTS) + [ANY] * PARTS,
         out_shape=jax.ShapeDtypeStruct((rank, out), F32),
-        scratch_shapes=[pltpu.VMEM((width, out), F32), pltpu.SemaphoreType.DMA((PARTS,))],
         compiler_params=params(),
         cost_estimate=cost(2 * rank * width * out, 8 * width * out),
         name="product",
@@ -402,11 +369,11 @@
     beside, others = rounds[0], rounds[1:]
     workers = 2 * sizes["sub"] * sizes["dp"]
 
-    keep, send = term_halves(inputs, cotangent, error_prev, seed_q)
+    keep, send, x, c, e = term_halves(inputs, cotangent, error_prev, seed_q)
     part = keep + across(send)
-    merged = merge(inputs, cotangent, error_prev, part)
+    near = part[0] + swapped(part[1], sizes, beside)
+    merged = merge(x, c, e, part)
     merged_other = [across(rows) for rows in merged]
-    near = part[0] + swapped(part[1], sizes, beside)
     for bits in others:
         near = near + swapped(near, sizes, bits)
     far = swapped(near, sizes, beside)
@@ -415,12 +382,13 @@
 
     product = product_of(near, far, merged, merged_other)
     rows, step, gram = first_sweep(mine, other)
-    product = summed(product, sizes, [beside])
+    product = product + swapped(product, sizes, beside)
     product, rows, step, gram = lax.optimization_barrier((product, rows, step, gram))
     basis, inverse = second_sweep(rows, step, gram)
-    for i in range(0, len(others), 2):
-        product = summed(product, sizes, others[i:i + 2])
+    product = product + swapped(product, sizes, others[0])
     product, basis, inverse = lax.optimization_barrier((product, basis, inverse))
+    for bits in others[1:]:
+        product = product + swapped(product, sizes, bits)
     return error_of(merged, basis, inverse, product, across(product), workers)
 
 

time: 44 us -> 40.8 us (0.927)
  waiting for transfers between devices: 15.9 us -> 12.2 us
  starting transfers between devices: 14.7 us -> 17.7 us
  Pallas kernels: 12.4 us -> 9.95 us
    ppermute x8 -> x7, waiting for transfers between devices: 13.7 us -> 9.98 us  [swapped(): return lax.ppermute(value, AXES, pairs)]
    ppermute x8 -> x7, starting transfers between devices: 13 us -> 16 us  [swapped(): return lax.ppermute(value, AXES, pairs)]
    pallas_call x3, Pallas kernels: 6.07 us -> 3.62 us  [the longest x1 2.34 us: term_halves(): pl.pallas_call(term_kernel, in_specs=[HBM] * 4, out_specs=[VMEM] * 5, out...]
  transfers between devices with their start and end apart: 15 -> 14, of which waited for: 8 -> 8; matrix products, arithmetic and copies ran while one was open for 0% -> 0% of each run, Pallas kernels for 18% -> 13%
where the time goes in v12:
time: 40.8 us; the launch traced here: 40.7 us
  starting transfers between devices  17.7 us (43%)
  waiting for transfers between devices  12.2 us (30%)
  Pallas kernels  9.95 us (24%)
  between operations  0.76 us (2%)
    ppermute x7, starting transfers between devices, swapped(): return lax.ppermute(value, AXES, pairs)  16 us
    ppermute x7, waiting for transfers between devices, swapped(): return lax.ppermute(value, AXES, pairs)  9.98 us
    pallas_call x1, Pallas kernels, first_sweep(): pl.pallas_call(first_sweep_kernel, out_shape=[jax.ShapeDtypeStruct((rank,...  2.57 us
    pallas_call x1, Pallas kernels, term_halves(): pl.pallas_call(term_kernel, in_specs=[HBM] * 4, out_specs=[VMEM] * 5, out...  2.34 us
    ppermute x7, waiting for transfers between devices, across(): return lax.ppermute(value, 'pair', [(0, 1), (1, 0)])  2.18 us
    pallas_call x1, Pallas kernels, error_of(): pl.pallas_call(functools.partial(error_kernel, workers), in_specs=[VMEM]...  2.13 us
    ppermute x7, starting transfers between devices, across(): return lax.ppermute(value, 'pair', [(0, 1), (1, 0)])  1.67 us
    pallas_call x1, Pallas kernels, second_sweep(): pl.pallas_call(second_sweep_kernel, out_shape=[jax.ShapeDtypeStruct(rows....  1.63 us
  transfers between devices with their start and end apart: 14, of which 8 were waited for; matrix products, arithmetic and copies ran while one was open for 0% of the time, Pallas kernels for 13%

profile of v12, /device:TPU:0, one launch (start us, length us, event | category | flops | bytes accessed | tf_op | source)
XLA Modules:
  0.0 40.7 jit_solution(11831617317208635108)
XLA Ops:
  0.6 2.3 %term.1 = (f32[2,16,1024]{2,1,0:T(8,128)S(1)}, f32[2,16,1024]{2,1,0:T(8,128)S(1)}, bf16[512,2048]{1,0:T(8,128)(2,1)S(1)}, bf16[512,256]{1,0:T(8,128)(2,1)S(1)}, bf16[2048,256]{1,0:T(8,128)(2,1)S(1)}) custom-call(bf16[512,2048]{1,0:T(8,128)(2,1)} %x_hbm.1, bf16[512,256]{1,0:T(8,128)(2,1)} %c_hbm.1, bf16[1,2048,256]{2,1,0:T(8,128)(2,1)} %e_hbm.1, ...), custom_call_target="tpu_custom_call" | custom-call | flops 201326592 | bytes 3145728 | tf_op jit(solution)/shard_map/term/pallas_call | solution.py:128
  3.0 0.5 %collective-permute-start = (f32[2,16,1024]{2,1,0:T(8,128)S(1)}, f32[2,16,1024]{2,1,0:T(8,128)S(1)}, u32[]{:S(2)}, u32[]{:S(2)}) collective-permute-start(f32[2,16,1024]{2,1,0:T(8,128)S(1)} %get-tuple-element.25), channel_id=1, source_target_pairs={{0,1},{1,0},{2,3},{3,2},{4,5},{5,4},{6,7},{7,6},{8,9},{9,8},{10,11... | collective-permute-start | bytes 393224 | tf_op jit(solution)/shard_map/ppermute | solution.py:34
  3.5 1.0 %collective-permute-done = f32[2,16,1024]{2,1,0:T(8,128)S(1)} collective-permute-done((f32[2,16,1024]{2,1,0:T(8,128)S(1)}, f32[2,16,1024]{2,1,0:T(8,128)S(1)}, u32[]{:S(2)}, u32[]{:S(2)}) %collective-permute-start) | collective-permute-done | bytes 131104 | tf_op jit(solution)/shard_map/ppermute | solution.py:34
  4.5 2.9 %collective-permute-start.1 = (f32[16,1024]{1,0:T(8,128)S(1)}, f32[16,1024]{1,0:T(8,128)S(1)}, u32[]{:S(2)}, u32[]{:S(2)}) collective-permute-start(f32[16,1024]{1,0:T(8,128)S(1)} %slice_bitcast_fusion), channel_id=1, source_target_pairs={{0,2},{1,3},{2,0},{3,1},{4,6},{5,7},{6,4},{7,5},{8,10},{9,11},{10,... | collective-permute-start | bytes 196616 | tf_op jit(solution)/shard_map/ppermute | solution.py:30
  7.4 0.8 %merge.1 = (f32[512,256]{1,0:T(8,128)S(1)}, f32[512,256]{1,0:T(8,128)S(1)}, f32[512,256]{1,0:T(8,128)S(1)}, f32[512,256]{1,0:T(8,128)S(1)}) custom-call(bf16[512,2048]{1,0:T(8,128)(2,1)S(1)} %get-tuple-element.26.x_ref, bf16[512,256]{1,0:T(8,128)(2,1)S(1)} %get-tuple-element.27.c_ref, bf16[2048,256]{1,0:T(8,128)(2,1)S(1)} %get-tuple-element.28.e_ref, ...), custom_call_target="tpu_custom_call" | custom-call | flops 100000000 | bytes 1000000 | tf_op jit(solution)/shard_map/merge/pallas_call | solution.py:161
  8.2 0.1 collective-permute-start.5
  8.3 0.5 %collective-permute-start.6 = (f32[512,256]{1,0:T(8,128)S(1)}, f32[512,256]{1,0:T(8,128)S(1)}, u32[]{:S(2)}, u32[]{:S(2)}) collective-permute-start(f32[512,256]{1,0:T(8,128)S(1)} %get-tuple-element.30.refs_1_), channel_id=1, source_target_pairs={{0,1},{1,0},{2,3},{3,2},{4,5},{5,4},{6,7},{7,6},{8,9},{9,8},{10,11... | collective-permute-start | bytes 1572872 | tf_op jit(solution)/shard_map/ppermute | solution.py:34
  8.8 0.1 collective-permute-start.7
  8.9 0.4 %collective-permute-start.8 = (f32[512,256]{1,0:T(8,128)S(1)}, f32[512,256]{1,0:T(8,128)S(1)}, u32[]{:S(2)}, u32[]{:S(2)}) collective-permute-start(f32[512,256]{1,0:T(8,128)S(1)} %get-tuple-element.32.refs_3_), channel_id=1, source_target_pairs={{0,1},{1,0},{2,3},{3,2},{4,5},{5,4},{6,7},{7,6},{8,9},{9,8},{10,11... | collective-permute-start | bytes 1572872 | tf_op jit(solution)/shard_map/ppermute | solution.py:34
  9.3 0.5 %collective-permute-done.1 = f32[16,1024]{1,0:T(8,128)S(1)} collective-permute-done((f32[16,1024]{1,0:T(8,128)S(1)}, f32[16,1024]{1,0:T(8,128)S(1)}, u32[]{:S(2)}, u32[]{:S(2)}) %collective-permute-start.1) | collective-permute-done | bytes 65568 | tf_op jit(solution)/shard_map/ppermute | solution.py:30
  9.8 2.0 %collective-permute-start.2 = (f32[16,1024]{1,0:T(8,128)S(1)}, f32[16,1024]{1,0:T(8,128)S(1)}, u32[]{:S(2)}, u32[]{:S(2)}) collective-permute-start(f32[16,1024]{1,0:T(8,128)S(1)} %fusion), channel_id=1, source_target_pairs={{0,4},{1,5},{2,6},{3,7},{4,0},{5,1},{6,2},{7,3},{8,12},{9,13},{10,... | collective-permute-start | bytes 196616 | tf_op jit(solution)/shard_map/ppermute | solution.py:30
  11.9 2.3 %collective-permute-done.2 = f32[16,1024]{1,0:T(8,128)S(1)} collective-permute-done((f32[16,1024]{1,0:T(8,128)S(1)}, f32[16,1024]{1,0:T(8,128)S(1)}, u32[]{:S(2)}, u32[]{:S(2)}) %collective-permute-start.2) | collective-permute-done | bytes 65568 | tf_op jit(solution)/shard_map/ppermute | solution.py:30
  14.2 3.0 %collective-permute-start.3 = (f32[16,1024]{1,0:T(8,128)S(1)}, f32[16,1024]{1,0:T(8,128)S(1)}, u32[]{:S(2)}, u32[]{:S(2)}) collective-permute-start(f32[16,1024]{1,0:T(8,128)S(1)} %add.23), channel_id=1, source_target_pairs={{0,8},{1,9},{2,10},{3,11},{4,12},{5,13},{6,14},{7,15},{8,0},{9,1},... | collective-permute-start | bytes 196616 | tf_op jit(solution)/shard_map/ppermute | solution.py:30
  17.2 2.2 %collective-permute-done.3 = f32[16,1024]{1,0:T(8,128)S(1)} collective-permute-done((f32[16,1024]{1,0:T(8,128)S(1)}, f32[16,1024]{1,0:T(8,128)S(1)}, u32[]{:S(2)}, u32[]{:S(2)}) %collective-permute-start.3) | collective-permute-done | bytes 65568 | tf_op jit(solution)/shard_map/ppermute | solution.py:30
  19.5 1.9 %collective-permute-start.4 = (f32[16,1024]{1,0:T(8,128)S(1)}, f32[16,1024]{1,0:T(8,128)S(1)}, u32[]{:S(2)}, u32[]{:S(2)}) collective-permute-start(f32[16,1024]{1,0:T(8,128)S(1)} %add.24.near_ref), channel_id=1, source_target_pairs={{0,2},{1,3},{2,0},{3,1},{4,6},{5,7},{6,4},{7,5},{8,10},{9,11},{10,... | collective-permute-start | bytes 196616 | tf_op jit(solution)/shard_map/ppermute | solution.py:30
  21.4 2.4 %collective-permute-done.4.far_ref = f32[16,1024]{1,0:T(8,128)S(1)} collective-permute-done((f32[16,1024]{1,0:T(8,128)S(1)}, f32[16,1024]{1,0:T(8,128)S(1)}, u32[]{:S(2)}, u32[]{:S(2)}) %collective-permute-start.4) | collective-permute-done | bytes 65568 | tf_op jit(solution)/shard_map/ppermute | solution.py:30
  23.8 0.1 collective-permute-start.10
  23.9 0.0 collective-permute-done.5.refs_4_
  23.9 0.0 collective-permute-done.6.refs_5_
  23.9 0.0 collective-permute-done.7.refs_6_
  23.9 0.0 collective-permute-done.8.refs_7_
  23.9 0.5 %product.1 = f32[16,256]{1,0:T(8,128)S(1)} custom-call(f32[16,1024]{1,0:T(8,128)S(1)} %add.24.near_ref, f32[16,1024]{1,0:T(8,128)S(1)} %collective-permute-done.4.far_ref, f32[512,256]{1,0:T(8,128)S(1)} %get-tuple-element.29.refs_0_, f32[512,256]{1,0:T(8,128)S(1)} %get-tuple-element.30.refs_1_, f32[512,256]{1,0:T(8,128)S(1)} %get-tuple-element.31.refs_2_, ...), custom_call_target="tpu_custom_call" | custom-call | flops 16777216 | bytes 4194304 | tf_op jit(solution)/shard_map/product/pallas_call | solution.py:197
  24.5 1.8 %collective-permute-start.9 = (f32[16,256]{1,0:T(8,128)S(1)}, f32[16,256]{1,0:T(8,128)S(1)}, u32[]{:S(2)}, u32[]{:S(2)}) collective-permute-start(f32[16,256]{1,0:T(8,128)S(1)} %product.1), channel_id=1, source_target_pairs={{0,2},{1,3},{2,0},{3,1},{4,6},{5,7},{6,4},{7,5},{8,10},{9,11},{10,... | collective-permute-start | bytes 49160 | tf_op jit(solution)/shard_map/ppermute | solution.py:30
  26.3 0.0 collective-permute-done.10.other_ref
  26.3 2.6 %first_sweep.1 = (f32[32,2048]{1,0:T(8,128)S(1)}, f32[32,32]{1,0:T(8,128)S(1)}, f32[32,32]{1,0:T(8,128)S(1)}) custom-call(f32[2,16,1024]{2,1,0:T(8,128)S(1)} %pad_maximum_fusion.mine_ref, f32[2,16,1024]{2,1,0:T(8,128)S(1)} %collective-permute-done.10.other_ref), custom_call_target="tpu_custom_call" | custom-call | flops 1000000000 | bytes 7000000 | tf_op jit(solution)/shard_map/first_sweep/pallas_call | solution.py:281
  28.9 0.0 collective-permute-done.9
  28.9 1.6 %collective-permute-start.11 = (f32[16,256]{1,0:T(8,128)S(1)}, f32[16,256]{1,0:T(8,128)S(1)}, u32[]{:S(2)}, u32[]{:S(2)}) collective-permute-start(f32[16,256]{1,0:T(8,128)S(1)} %add.25), channel_id=1, source_target_pairs={{0,4},{1,5},{2,6},{3,7},{4,0},{5,1},{6,2},{7,3},{8,12},{9,13},{10,... | collective-permute-start | bytes 49160 | tf_op jit(solution)/shard_map/ppermute | solution.py:30
  30.5 1.6 %second_sweep.1 = (f32[32,2048]{1,0:T(8,128)S(1)}, f32[32,32]{1,0:T(8,128)S(1)}) custom-call(f32[32,2048]{1,0:T(8,128)S(1)} %get-tuple-element.37.rows_ref, f32[32,32]{1,0:T(8,128)S(1)} %get-tuple-element.38.step_ref, f32[32,32]{1,0:T(8,128)S(1)} %get-tuple-element.39.gram_ref), custom_call_target="tpu_custom_call" | custom-call | flops 1000000000 | bytes 7000000 | tf_op jit(solution)/shard_map/second_sweep/pallas_call | solution.py:303
  32.2 0.5 %collective-permute-done.11 = f32[16,256]{1,0:T(8,128)S(1)} collective-permute-done((f32[16,256]{1,0:T(8,128)S(1)}, f32[16,256]{1,0:T(8,128)S(1)}, u32[]{:S(2)}, u32[]{:S(2)}) %collective-permute-start.11) | collective-permute-done | bytes 16416 | tf_op jit(solution)/shard_map/ppermute | solution.py:30
  32.7 2.7 %collective-permute-start.12 = (f32[16,256]{1,0:T(8,128)S(1)}, f32[16,256]{1,0:T(8,128)S(1)}, u32[]{:S(2)}, u32[]{:S(2)}) collective-permute-start(f32[16,256]{1,0:T(8,128)S(1)} %add.26), channel_id=1, source_target_pairs={{0,8},{1,9},{2,10},{3,11},{4,12},{5,13},{6,14},{7,15},{8,0},{9,1},... | collective-permute-start | bytes 49160 | tf_op jit(solution)/shard_map/ppermute | solution.py:30
  35.4 1.9 %collective-permute-done.12 = f32[16,256]{1,0:T(8,128)S(1)} collective-permute-done((f32[16,256]{1,0:T(8,128)S(1)}, f32[16,256]{1,0:T(8,128)S(1)}, u32[]{:S(2)}, u32[]{:S(2)}) %collective-permute-start.12) | collective-permute-done | bytes 16416 | tf_op jit(solution)/shard_map/ppermute | solution.py:30
  37.3 0.0 collective-permute-start.13
  37.3 1.2 %collective-permute-done.13.other_ref = f32[16,256]{1,0:T(8,128)S(1)} collective-permute-done((f32[16,256]{1,0:T(8,128)S(1)}, f32[16,256]{1,0:T(8,128)S(1)}, u32[]{:S(2)}, u32[]{:S(2)}) %collective-permute-start.13) | collective-permute-done | bytes 16416 | tf_op jit(solution)/shard_map/ppermute | solution.py:34
  38.5 2.1 %error_next.1 = (bf16[1,2048,256]{2,1,0:T(8,128)(2,1)}, f32[32,2048]{1,0:T(8,128)}, f32[32,256]{1,0:T(8,128)}) custom-call(f32[32,2048]{1,0:T(8,128)S(1)} %get-tuple-element.42.basis_ref, f32[32,32]{1,0:T(8,128)S(1)} %get-tuple-element.43.inverse_ref, f32[16,256]{1,0:T(8,128)S(1)} %add.27.mine_ref, f32[16,256]{1,0:T(8,128)S(1)} %collective-permute-done.13.other_ref, ...), custom_call_target="tpu_custom_call" | custom-call | flops 33554432 | bytes 3145728 | tf_op jit(solution)/shard_map/error_next/pallas_call | solution.py:345
  (9 shorter events, 0.1 us)
Async XLA Ops:
  3.0 1.5 %collective-permute-start = (f32[2,16,1024]{2,1,0:T(8,128)S(1)}, f32[2,16,1024]{2,1,0:T(8,128)S(1)}, u32[]{:S(2)}, u32[]{:S(2)}) collective-permute-start(f32[2,16,1024]{2,1,0:T(8,128)S(1)} %get-tuple-element.25), channel_id=1, source_target_pairs={{0,1},{1,0},{2,3},{3,2},{4,5},{5,4},{6,7},{7,6},{8,9},{9,8},{10,11... | collective-permute-start | bytes 393224 | tf_op jit(solution)/shard_map/ppermute | solution.py:34
  4.5 5.3 %collective-permute-start.1 = (f32[16,1024]{1,0:T(8,128)S(1)}, f32[16,1024]{1,0:T(8,128)S(1)}, u32[]{:S(2)}, u32[]{:S(2)}) collective-permute-start(f32[16,1024]{1,0:T(8,128)S(1)} %slice_bitcast_fusion), channel_id=1, source_target_pairs={{0,2},{1,3},{2,0},{3,1},{4,6},{5,7},{6,4},{7,5},{8,10},{9,11},{10,... | collective-permute-start | bytes 196616 | tf_op jit(solution)/shard_map/ppermute | solution.py:30
  8.2 15.7 %collective-permute-start.5 = (f32[512,256]{1,0:T(8,128)S(1)}, f32[512,256]{1,0:T(8,128)S(1)}, u32[]{:S(2)}, u32[]{:S(2)}) collective-permute-start(f32[512,256]{1,0:T(8,128)S(1)} %get-tuple-element.29.refs_0_), channel_id=1, source_target_pairs={{0,1},{1,0},{2,3},{3,2},{4,5},{5,4},{6,7},{7,6},{8,9},{9,8},{10,11... | collective-permute-start | bytes 1572872 | tf_op jit(solution)/shard_map/ppermute | solution.py:34
  8.3 15.6 %collective-permute-start.6 = (f32[512,256]{1,0:T(8,128)S(1)}, f32[512,256]{1,0:T(8,128)S(1)}, u32[]{:S(2)}, u32[]{:S(2)}) collective-permute-start(f32[512,256]{1,0:T(8,128)S(1)} %get-tuple-element.30.refs_1_), channel_id=1, source_target_pairs={{0,1},{1,0},{2,3},{3,2},{4,5},{5,4},{6,7},{7,6},{8,9},{9,8},{10,11... | collective-permute-start | bytes 1572872 | tf_op jit(solution)/shard_map/ppermute | solution.py:34
  8.8 15.1 %collective-permute-start.7 = (f32[512,256]{1,0:T(8,128)S(1)}, f32[512,256]{1,0:T(8,128)S(1)}, u32[]{:S(2)}, u32[]{:S(2)}) collective-permute-start(f32[512,256]{1,0:T(8,128)S(1)} %get-tuple-element.31.refs_2_), channel_id=1, source_target_pairs={{0,1},{1,0},{2,3},{3,2},{4,5},{5,4},{6,7},{7,6},{8,9},{9,8},{10,11... | collective-permute-start | bytes 1572872 | tf_op jit(solution)/shard_map/ppermute | solution.py:34
  8.9 15.1 %collective-permute-start.8 = (f32[512,256]{1,0:T(8,128)S(1)}, f32[512,256]{1,0:T(8,128)S(1)}, u32[]{:S(2)}, u32[]{:S(2)}) collective-permute-start(f32[512,256]{1,0:T(8,128)S(1)} %get-tuple-element.32.refs_3_), channel_id=1, source_target_pairs={{0,1},{1,0},{2,3},{3,2},{4,5},{5,4},{6,7},{7,6},{8,9},{9,8},{10,11... | collective-permute-start | bytes 1572872 | tf_op jit(solution)/shard_map/ppermute | solution.py:34
  9.8 4.3 %collective-permute-start.2 = (f32[16,1024]{1,0:T(8,128)S(1)}, f32[16,1024]{1,0:T(8,128)S(1)}, u32[]{:S(2)}, u32[]{:S(2)}) collective-permute-start(f32[16,1024]{1,0:T(8,128)S(1)} %fusion), channel_id=1, source_target_pairs={{0,4},{1,5},{2,6},{3,7},{4,0},{5,1},{6,2},{7,3},{8,12},{9,13},{10,... | collective-permute-start | bytes 196616 | tf_op jit(solution)/shard_map/ppermute | solution.py:30
  14.2 5.3 %collective-permute-start.3 = (f32[16,1024]{1,0:T(8,128)S(1)}, f32[16,1024]{1,0:T(8,128)S(1)}, u32[]{:S(2)}, u32[]{:S(2)}) collective-permute-start(f32[16,1024]{1,0:T(8,128)S(1)} %add.23), channel_id=1, source_target_pairs={{0,8},{1,9},{2,10},{3,11},{4,12},{5,13},{6,14},{7,15},{8,0},{9,1},... | collective-permute-start | bytes 196616 | tf_op jit(solution)/shard_map/ppermute | solution.py:30
  19.5 4.3 %collective-permute-start.4 = (f32[16,1024]{1,0:T(8,128)S(1)}, f32[16,1024]{1,0:T(8,128)S(1)}, u32[]{:S(2)}, u32[]{:S(2)}) collective-permute-start(f32[16,1024]{1,0:T(8,128)S(1)} %add.24.near_ref), channel_id=1, source_target_pairs={{0,2},{1,3},{2,0},{3,1},{4,6},{5,7},{6,4},{7,5},{8,10},{9,11},{10,... | collective-permute-start | bytes 196616 | tf_op jit(solution)/shard_map/ppermute | solution.py:30
  23.8 2.5 %collective-permute-start.10 = (f32[2,16,1024]{2,1,0:T(8,128)S(1)}, f32[2,16,1024]{2,1,0:T(8,128)S(1)}, u32[]{:S(2)}, u32[]{:S(2)}) collective-permute-start(f32[2,16,1024]{2,1,0:T(8,128)S(1)} %pad_maximum_fusion.mine_ref), channel_id=1, source_target_pairs={{0,1},{1,0},{2,3},{3,2},{4,5},{5,4},{6,7},{7,6},{8,9},{9,8},{10,11... | collective-permute-start | bytes 393224 | tf_op jit(solution)/shard_map/ppermute | solution.py:34
  24.5 4.4 %collective-permute-start.9 = (f32[16,256]{1,0:T(8,128)S(1)}, f32[16,256]{1,0:T(8,128)S(1)}, u32[]{:S(2)}, u32[]{:S(2)}) collective-permute-start(f32[16,256]{1,0:T(8,128)S(1)} %product.1), channel_id=1, source_target_pairs={{0,2},{1,3},{2,0},{3,1},{4,6},{5,7},{6,4},{7,5},{8,10},{9,11},{10,... | collective-permute-start | bytes 49160 | tf_op jit(solution)/shard_map/ppermute | solution.py:30
  28.9 3.8 %collective-permute-start.11 = (f32[16,256]{1,0:T(8,128)S(1)}, f32[16,256]{1,0:T(8,128)S(1)}, u32[]{:S(2)}, u32[]{:S(2)}) collective-permute-start(f32[16,256]{1,0:T(8,128)S(1)} %add.25), channel_id=1, source_target_pairs={{0,4},{1,5},{2,6},{3,7},{4,0},{5,1},{6,2},{7,3},{8,12},{9,13},{10,... | collective-permute-start | bytes 49160 | tf_op jit(solution)/shard_map/ppermute | solution.py:30
  32.7 4.6 %collective-permute-start.12 = (f32[16,256]{1,0:T(8,128)S(1)}, f32[16,256]{1,0:T(8,128)S(1)}, u32[]{:S(2)}, u32[]{:S(2)}) collective-permute-start(f32[16,256]{1,0:T(8,128)S(1)} %add.26), channel_id=1, source_target_pairs={{0,8},{1,9},{2,10},{3,11},{4,12},{5,13},{6,14},{7,15},{8,0},{9,1},... | collective-permute-start | bytes 49160 | tf_op jit(solution)/shard_map/ppermute | solution.py:30
  37.3 1.2 %collective-permute-start.13 = (f32[16,256]{1,0:T(8,128)S(1)}, f32[16,256]{1,0:T(8,128)S(1)}, u32[]{:S(2)}, u32[]{:S(2)}) collective-permute-start(f32[16,256]{1,0:T(8,128)S(1)} %add.27.mine_ref), channel_id=1, source_target_pairs={{0,1},{1,0},{2,3},{3,2},{4,5},{5,4},{6,7},{7,6},{8,9},{9,8},{10,11... | collective-permute-start | bytes 49160 | tf_op jit(solution)/shard_map/ppermute | solution.py:34

commit v13 on v12

--- a/solution.py
+++ b/solution.py
@@ -19,14 +19,15 @@
 VMEM = pl.BlockSpec(memory_space=pltpu.VMEM)
 
 
-def swapped(value, sizes, bits):
+def swapped(value, sizes, bits, cores=(0, 1)):
     pairs = []
     for dp in range(sizes["dp"]):
         for sub in range(sizes["sub"]):
             for pair in range(2):
                 pairs.append(tuple(
                     (z * sizes["sub"] + x) * 2 + pair
-                    for z, x in ((dp, sub), (dp ^ bits["dp"], sub ^ bits["sub"]))))
+                    for z, x in ((dp, sub), (dp ^ bits["dp"], sub ^ bits["sub"])
+                                 if pair in cores else (dp, sub))))
     return lax.ppermute(value, AXES, pairs)
 
 
@@ -169,16 +170,18 @@
     )(x, c, e, after)
 
 
-def product_kernel(near_ref, far_ref, *refs):
+def product_kernel(mine_ref, other_ref, *refs):
     mine_refs, other_refs, product_ref = refs[:PARTS], refs[PARTS:2 * PARTS], refs[2 * PARTS]
-    rank, piece = near_ref.shape
+    half, piece = mine_ref.shape[1:]
+    rank = 2 * half
     size = mine_refs[0].shape[0]
     straight = side() == 0
     product = None
     for i in range(2 * piece // CHUNK):
         start = i * CHUNK
         part = slice(start % piece, start % piece + CHUNK)
-        near, far = near_ref[:, part], far_ref[:, part]
+        near = both_halves(mine_ref[0, :, part], other_ref[0, :, part])
+        far = both_halves(mine_ref[1, :, part], other_ref[1, :, part])
         rows = jnp.where(straight, near, far) if start < piece else jnp.where(straight, far, near)
         f_high, f_low = parts_of(rows, 2)
         both = jnp.concatenate([f_high, f_low], axis=0)
@@ -190,17 +193,16 @@
     product_ref[...] = product
 
 
-def product_of(near, far, mine, other):
-    rank, piece = near.shape
-    size, out = mine[0].shape
-    width = 2 * piece
+def product_of(mine, other, merged, merged_other):
+    _, half, piece = mine.shape
+    rank, width, out = 2 * half, 2 * piece, merged[0].shape[1]
     return pl.pallas_call(
         product_kernel,
         out_shape=jax.ShapeDtypeStruct((rank, out), F32),
         compiler_params=params(),
         cost_estimate=cost(2 * rank * width * out, 8 * width * out),
         name="product",
-    )(near, far, *mine, *other)
+    )(mine, other, *merged, *merged_other)
 
 
 def both_halves(mine, other):
@@ -318,7 +320,7 @@
     size = merged_refs[0].shape[0]
     keep = pltpu.make_async_copy(basis_ref, basis_hbm, basis_sem)
     keep.start()
-    product = both_halves(mine_ref[...], other_ref[...])
+    product = jnp.where(lax.axis_index("pair") == 1, mine_ref[...], other_ref[...])
     second = short_dot(inverse_ref[...], product) * (1.0 / workers)
     second_ref[...] = second
     s_high, s_low = parts_of(second, 2)
@@ -380,15 +382,15 @@
     mine = jnp.stack([near, far])
     other = across(mine)
 
-    product = product_of(near, far, merged, merged_other)
+    product = product_of(mine, other, merged, merged_other)
     rows, step, gram = first_sweep(mine, other)
-    product = product + swapped(product, sizes, beside)
+    product = product + swapped(product, sizes, beside, (1,))
     product, rows, step, gram = lax.optimization_barrier((product, rows, step, gram))
     basis, inverse = second_sweep(rows, step, gram)
-    product = product + swapped(product, sizes, others[0])
+    product = product + swapped(product, sizes, others[0], (1,))
     product, basis, inverse = lax.optimization_barrier((product, basis, inverse))
     for bits in others[1:]:
-        product = product + swapped(product, sizes, bits)
+        product = product + swapped(product, sizes, bits, (1,))
     return error_of(merged, basis, inverse, product, across(product), workers)
 
 

time: 40.8 us -> 46.2 us (1.13)
  starting transfers between devices: 17.7 us -> 24.4 us
  waiting for transfers between devices: 12.2 us -> 10.7 us
    ppermute x7, starting transfers between devices: 1.67 us -> 12.6 us  [across(): return lax.ppermute(value, 'pair', [(0, 1), (1, 0)])]
    ppermute x7, starting transfers between devices: 16 us -> 11.8 us  [swapped(): return lax.ppermute(value, AXES, pairs)]
    ppermute x7, waiting for transfers between devices: 9.98 us -> 7.55 us  [swapped(): return lax.ppermute(value, AXES, pairs)]
    ppermute x7, waiting for transfers between devices: 2.18 us -> 3.19 us  [across(): return lax.ppermute(value, 'pair', [(0, 1), (1, 0)])]
  transfers between devices with their start and end apart: 14 -> 14, of which waited for: 8 -> 7; matrix products, arithmetic and copies ran while one was open for 0% -> 0% of each run, Pallas kernels for 13% -> 11%
where the time goes in v13:
time: 46.2 us; the launch traced here: 46 us
  starting transfers between devices  24.4 us (53%)
  waiting for transfers between devices  10.7 us (23%)
  Pallas kernels  10 us (22%)
  between operations  0.78 us (2%)
    ppermute x7, starting transfers between devices, across(): return lax.ppermute(value, 'pair', [(0, 1), (1, 0)])  12.6 us
    ppermute x7, starting transfers between devices, swapped(): return lax.ppermute(value, AXES, pairs)  11.8 us
    ppermute x7, waiting for transfers between devices, swapped(): return lax.ppermute(value, AXES, pairs)  7.55 us
    ppermute x7, waiting for transfers between devices, across(): return lax.ppermute(value, 'pair', [(0, 1), (1, 0)])  3.19 us
    pallas_call x1, Pallas kernels, first_sweep(): pl.pallas_call(first_sweep_kernel, out_shape=[jax.ShapeDtypeStruct((rank,...  2.57 us
    pallas_call x1, Pallas kernels, term_halves(): pl.pallas_call(term_kernel, in_specs=[HBM] * 4, out_specs=[VMEM] * 5, out...  2.34 us
    pallas_call x1, Pallas kernels, error_of(): pl.pallas_call(functools.partial(error_kernel, workers), in_specs=[VMEM]...  2.13 us
    pallas_call x1, Pallas kernels, second_sweep(): pl.pallas_call(second_sweep_kernel, out_shape=[jax.ShapeDtypeStruct(rows....  1.63 us
  transfers between devices with their start and end apart: 14, of which 7 were waited for; matrix products, arithmetic and copies ran while one was open for 0% of the time, Pallas kernels for 11%

profile of v13, /device:TPU:0, one launch (start us, length us, event | category | flops | bytes accessed | tf_op | source)
XLA Modules:
  0.0 46.0 jit_solution(3075465457691359023)
XLA Ops:
  0.6 2.3 %term.1 = (f32[2,16,1024]{2,1,0:T(8,128)S(1)}, f32[2,16,1024]{2,1,0:T(8,128)S(1)}, bf16[512,2048]{1,0:T(8,128)(2,1)S(1)}, bf16[512,256]{1,0:T(8,128)(2,1)S(1)}, bf16[2048,256]{1,0:T(8,128)(2,1)S(1)}) custom-call(bf16[512,2048]{1,0:T(8,128)(2,1)} %x_hbm.1, bf16[512,256]{1,0:T(8,128)(2,1)} %c_hbm.1, bf16[1,2048,256]{2,1,0:T(8,128)(2,1)} %e_hbm.1, ...), custom_call_target="tpu_custom_call" | custom-call | flops 201326592 | bytes 3145728 | tf_op jit(solution)/shard_map/term/pallas_call | solution.py:129
  3.0 0.5 %collective-permute-start = (f32[2,16,1024]{2,1,0:T(8,128)S(1)}, f32[2,16,1024]{2,1,0:T(8,128)S(1)}, u32[]{:S(2)}, u32[]{:S(2)}) collective-permute-start(f32[2,16,1024]{2,1,0:T(8,128)S(1)} %get-tuple-element.25), channel_id=1, source_target_pairs={{0,1},{1,0},{2,3},{3,2},{4,5},{5,4},{6,7},{7,6},{8,9},{9,8},{10,11... | collective-permute-start | bytes 393224 | tf_op jit(solution)/shard_map/ppermute | solution.py:35
  3.5 1.0 %collective-permute-done = f32[2,16,1024]{2,1,0:T(8,128)S(1)} collective-permute-done((f32[2,16,1024]{2,1,0:T(8,128)S(1)}, f32[2,16,1024]{2,1,0:T(8,128)S(1)}, u32[]{:S(2)}, u32[]{:S(2)}) %collective-permute-start) | collective-permute-done | bytes 131104 | tf_op jit(solution)/shard_map/ppermute | solution.py:35
  4.5 2.9 %collective-permute-start.1 = (f32[16,1024]{1,0:T(8,128)S(1)}, f32[16,1024]{1,0:T(8,128)S(1)}, u32[]{:S(2)}, u32[]{:S(2)}) collective-permute-start(f32[16,1024]{1,0:T(8,128)S(1)} %slice_bitcast_fusion), channel_id=1, source_target_pairs={{0,2},{1,3},{2,0},{3,1},{4,6},{5,7},{6,4},{7,5},{8,10},{9,11},{10,... | collective-permute-start | bytes 196616 | tf_op jit(solution)/shard_map/ppermute | solution.py:31
  7.4 0.8 %merge.1 = (f32[512,256]{1,0:T(8,128)S(1)}, f32[512,256]{1,0:T(8,128)S(1)}, f32[512,256]{1,0:T(8,128)S(1)}, f32[512,256]{1,0:T(8,128)S(1)}) custom-call(bf16[512,2048]{1,0:T(8,128)(2,1)S(1)} %get-tuple-element.26.x_ref, bf16[512,256]{1,0:T(8,128)(2,1)S(1)} %get-tuple-element.27.c_ref, bf16[2048,256]{1,0:T(8,128)(2,1)S(1)} %get-tuple-element.28.e_ref, ...), custom_call_target="tpu_custom_call" | custom-call | flops 100000000 | bytes 1000000 | tf_op jit(solution)/shard_map/merge/pallas_call | solution.py:162
  8.2 0.1 collective-permute-start.6
  8.3 0.5 %collective-permute-start.7 = (f32[512,256]{1,0:T(8,128)S(1)}, f32[512,256]{1,0:T(8,128)S(1)}, u32[]{:S(2)}, u32[]{:S(2)}) collective-permute-start(f32[512,256]{1,0:T(8,128)S(1)} %get-tuple-element.30.refs_1_), channel_id=1, source_target_pairs={{0,1},{1,0},{2,3},{3,2},{4,5},{5,4},{6,7},{7,6},{8,9},{9,8},{10,11... | collective-permute-start | bytes 1572872 | tf_op jit(solution)/shard_map/ppermute | solution.py:35
  8.8 0.1 collective-permute-start.8
  8.9 0.4 collective-permute-start.9
  9.3 0.5 %collective-permute-done.1 = f32[16,1024]{1,0:T(8,128)S(1)} collective-permute-done((f32[16,1024]{1,0:T(8,128)S(1)}, f32[16,1024]{1,0:T(8,128)S(1)}, u32[]{:S(2)}, u32[]{:S(2)}) %collective-permute-start.1) | collective-permute-done | bytes 65568 | tf_op jit(solution)/shard_map/ppermute | solution.py:31
  9.8 2.0 %collective-permute-start.2 = (f32[16,1024]{1,0:T(8,128)S(1)}, f32[16,1024]{1,0:T(8,128)S(1)}, u32[]{:S(2)}, u32[]{:S(2)}) collective-permute-start(f32[16,1024]{1,0:T(8,128)S(1)} %fusion), channel_id=1, source_target_pairs={{0,4},{1,5},{2,6},{3,7},{4,0},{5,1},{6,2},{7,3},{8,12},{9,13},{10,... | collective-permute-start | bytes 196616 | tf_op jit(solution)/shard_map/ppermute | solution.py:31
  11.9 2.3 %collective-permute-done.2 = f32[16,1024]{1,0:T(8,128)S(1)} collective-permute-done((f32[16,1024]{1,0:T(8,128)S(1)}, f32[16,1024]{1,0:T(8,128)S(1)}, u32[]{:S(2)}, u32[]{:S(2)}) %collective-permute-start.2) | collective-permute-done | bytes 65568 | tf_op jit(solution)/shard_map/ppermute | solution.py:31
  14.2 3.0 %collective-permute-start.3 = (f32[16,1024]{1,0:T(8,128)S(1)}, f32[16,1024]{1,0:T(8,128)S(1)}, u32[]{:S(2)}, u32[]{:S(2)}) collective-permute-start(f32[16,1024]{1,0:T(8,128)S(1)} %add.23), channel_id=1, source_target_pairs={{0,8},{1,9},{2,10},{3,11},{4,12},{5,13},{6,14},{7,15},{8,0},{9,1},... | collective-permute-start | bytes 196616 | tf_op jit(solution)/shard_map/ppermute | solution.py:31
  17.2 2.2 %collective-permute-done.3 = f32[16,1024]{1,0:T(8,128)S(1)} collective-permute-done((f32[16,1024]{1,0:T(8,128)S(1)}, f32[16,1024]{1,0:T(8,128)S(1)}, u32[]{:S(2)}, u32[]{:S(2)}) %collective-permute-start.3) | collective-permute-done | bytes 65568 | tf_op jit(solution)/shard_map/ppermute | solution.py:31
  19.5 1.9 %collective-permute-start.4 = (f32[16,1024]{1,0:T(8,128)S(1)}, f32[16,1024]{1,0:T(8,128)S(1)}, u32[]{:S(2)}, u32[]{:S(2)}) collective-permute-start(f32[16,1024]{1,0:T(8,128)S(1)} %add.24), channel_id=1, source_target_pairs={{0,2},{1,3},{2,0},{3,1},{4,6},{5,7},{6,4},{7,5},{8,10},{9,11},{10,... | collective-permute-start | bytes 196616 | tf_op jit(solution)/shard_map/ppermute | solution.py:31
  21.4 2.4 %collective-permute-done.4 = f32[16,1024]{1,0:T(8,128)S(1)} collective-permute-done((f32[16,1024]{1,0:T(8,128)S(1)}, f32[16,1024]{1,0:T(8,128)S(1)}, u32[]{:S(2)}, u32[]{:S(2)}) %collective-permute-start.4) | collective-permute-done | bytes 65568 | tf_op jit(solution)/shard_map/ppermute | solution.py:31
  23.8 0.1 collective-permute-start.5
  23.9 1.3 %collective-permute-done.5.other_ref = f32[2,16,1024]{2,1,0:T(8,128)S(1)} collective-permute-done((f32[2,16,1024]{2,1,0:T(8,128)S(1)}, f32[2,16,1024]{2,1,0:T(8,128)S(1)}, u32[]{:S(2)}, u32[]{:S(2)}) %collective-permute-start.5) | collective-permute-done | bytes 131104 | tf_op jit(solution)/shard_map/ppermute | solution.py:35
  25.2 0.0 collective-permute-done.6.refs_4_
  25.2 0.0 collective-permute-done.7.refs_5_
  25.2 0.0 collective-permute-done.8.refs_6_
  25.2 0.0 collective-permute-done.9.refs_7_
  25.3 0.6 %product.1 = f32[32,256]{1,0:T(8,128)S(1)} custom-call(f32[2,16,1024]{2,1,0:T(8,128)S(1)} %pad_maximum_fusion.mine_ref, f32[2,16,1024]{2,1,0:T(8,128)S(1)} %collective-permute-done.5.other_ref, f32[512,256]{1,0:T(8,128)S(1)} %get-tuple-element.29.refs_0_, f32[512,256]{1,0:T(8,128)S(1)} %get-tuple-element.30.refs_1_, ...), custom_call_target="tpu_custom_call" | custom-call | flops 33554432 | bytes 4194304 | tf_op jit(solution)/shard_map/product/pallas_call | solution.py:199
  25.8 0.7 %collective-permute-start.10 = (f32[32,256]{1,0:T(8,128)S(1)}, f32[32,256]{1,0:T(8,128)S(1)}, u32[]{:S(2)}, u32[]{:S(2)}) collective-permute-start(f32[32,256]{1,0:T(8,128)S(1)} %product.1), channel_id=1, source_target_pairs={{0,0},{1,3},{2,2},{3,1},{4,4},{5,7},{6,6},{7,5},{8,8},{9,11},{10,1... | collective-permute-start | bytes 98312 | tf_op jit(solution)/shard_map/ppermute | solution.py:31
  26.5 2.6 %first_sweep.1 = (f32[32,2048]{1,0:T(8,128)S(1)}, f32[32,32]{1,0:T(8,128)S(1)}, f32[32,32]{1,0:T(8,128)S(1)}) custom-call(f32[2,16,1024]{2,1,0:T(8,128)S(1)} %pad_maximum_fusion.mine_ref, f32[2,16,1024]{2,1,0:T(8,128)S(1)} %collective-permute-done.5.other_ref), custom_call_target="tpu_custom_call" | custom-call | flops 1000000000 | bytes 7000000 | tf_op jit(solution)/shard_map/first_sweep/pallas_call | solution.py:283
  29.1 0.0 collective-permute-done.10
  29.1 0.7 %collective-permute-start.11 = (f32[32,256]{1,0:T(8,128)S(1)}, f32[32,256]{1,0:T(8,128)S(1)}, u32[]{:S(2)}, u32[]{:S(2)}) collective-permute-start(f32[32,256]{1,0:T(8,128)S(1)} %add.25), channel_id=1, source_target_pairs={{0,0},{1,5},{2,2},{3,7},{4,4},{5,1},{6,6},{7,3},{8,8},{9,13},{10,1... | collective-permute-start | bytes 98312 | tf_op jit(solution)/shard_map/ppermute | solution.py:31
  29.8 1.6 %second_sweep.1 = (f32[32,2048]{1,0:T(8,128)S(1)}, f32[32,32]{1,0:T(8,128)S(1)}) custom-call(f32[32,2048]{1,0:T(8,128)S(1)} %get-tuple-element.37.rows_ref, f32[32,32]{1,0:T(8,128)S(1)} %get-tuple-element.38.step_ref, f32[32,32]{1,0:T(8,128)S(1)} %get-tuple-element.39.gram_ref), custom_call_target="tpu_custom_call" | custom-call | flops 1000000000 | bytes 7000000 | tf_op jit(solution)/shard_map/second_sweep/pallas_call | solution.py:305
  31.4 0.0 collective-permute-done.11
  31.4 0.7 %collective-permute-start.12 = (f32[32,256]{1,0:T(8,128)S(1)}, f32[32,256]{1,0:T(8,128)S(1)}, u32[]{:S(2)}, u32[]{:S(2)}) collective-permute-start(f32[32,256]{1,0:T(8,128)S(1)} %add.26), channel_id=1, source_target_pairs={{0,0},{1,9},{2,2},{3,11},{4,4},{5,13},{6,6},{7,15},{8,8},{9,1},{10... | collective-permute-start | bytes 98312 | tf_op jit(solution)/shard_map/ppermute | solution.py:31
  32.1 0.0 collective-permute-done.12
  32.1 10.9 %collective-permute-start.13 = (f32[32,256]{1,0:T(8,128)S(1)}, f32[32,256]{1,0:T(8,128)S(1)}, u32[]{:S(2)}, u32[]{:S(2)}) collective-permute-start(f32[32,256]{1,0:T(8,128)S(1)} %add.27.mine_ref), channel_id=1, source_target_pairs={{0,1},{1,0},{2,3},{3,2},{4,5},{5,4},{6,7},{7,6},{8,9},{9,8},{10,11... | collective-permute-start | bytes 98312 | tf_op jit(solution)/shard_map/ppermute | solution.py:35
  43.0 0.9 %collective-permute-done.13.other_ref = f32[32,256]{1,0:T(8,128)S(1)} collective-permute-done((f32[32,256]{1,0:T(8,128)S(1)}, f32[32,256]{1,0:T(8,128)S(1)}, u32[]{:S(2)}, u32[]{:S(2)}) %collective-permute-start.13) | collective-permute-done | bytes 32800 | tf_op jit(solution)/shard_map/ppermute | solution.py:35
  43.9 2.1 %error_next.1 = (bf16[1,2048,256]{2,1,0:T(8,128)(2,1)}, f32[32,2048]{1,0:T(8,128)}, f32[32,256]{1,0:T(8,128)}) custom-call(f32[32,2048]{1,0:T(8,128)S(1)} %get-tuple-element.42.basis_ref, f32[32,32]{1,0:T(8,128)S(1)} %get-tuple-element.43.inverse_ref, f32[32,256]{1,0:T(8,128)S(1)} %add.27.mine_ref, f32[32,256]{1,0:T(8,128)S(1)} %collective-permute-done.13.other_ref, ...), custom_call_target="tpu_custom_call" | custom-call | flops 33554432 | bytes 3145728 | tf_op jit(solution)/shard_map/error_next/pallas_call | solution.py:347
  (9 shorter events, 0.1 us)
Async XLA Ops:
  3.0 1.5 %collective-permute-start = (f32[2,16,1024]{2,1,0:T(8,128)S(1)}, f32[2,16,1024]{2,1,0:T(8,128)S(1)}, u32[]{:S(2)}, u32[]{:S(2)}) collective-permute-start(f32[2,16,1024]{2,1,0:T(8,128)S(1)} %get-tuple-element.25), channel_id=1, source_target_pairs={{0,1},{1,0},{2,3},{3,2},{4,5},{5,4},{6,7},{7,6},{8,9},{9,8},{10,11... | collective-permute-start | bytes 393224 | tf_op jit(solution)/shard_map/ppermute | solution.py:35
  4.5 5.3 %collective-permute-start.1 = (f32[16,1024]{1,0:T(8,128)S(1)}, f32[16,1024]{1,0:T(8,128)S(1)}, u32[]{:S(2)}, u32[]{:S(2)}) collective-permute-start(f32[16,1024]{1,0:T(8,128)S(1)} %slice_bitcast_fusion), channel_id=1, source_target_pairs={{0,2},{1,3},{2,0},{3,1},{4,6},{5,7},{6,4},{7,5},{8,10},{9,11},{10,... | collective-permute-start | bytes 196616 | tf_op jit(solution)/shard_map/ppermute | solution.py:31
  8.2 17.0 %collective-permute-start.6 = (f32[512,256]{1,0:T(8,128)S(1)}, f32[512,256]{1,0:T(8,128)S(1)}, u32[]{:S(2)}, u32[]{:S(2)}) collective-permute-start(f32[512,256]{1,0:T(8,128)S(1)} %get-tuple-element.29.refs_0_), channel_id=1, source_target_pairs={{0,1},{1,0},{2,3},{3,2},{4,5},{5,4},{6,7},{7,6},{8,9},{9,8},{10,11... | collective-permute-start | bytes 1572872 | tf_op jit(solution)/shard_map/ppermute | solution.py:35
  8.3 16.9 %collective-permute-start.7 = (f32[512,256]{1,0:T(8,128)S(1)}, f32[512,256]{1,0:T(8,128)S(1)}, u32[]{:S(2)}, u32[]{:S(2)}) collective-permute-start(f32[512,256]{1,0:T(8,128)S(1)} %get-tuple-element.30.refs_1_), channel_id=1, source_target_pairs={{0,1},{1,0},{2,3},{3,2},{4,5},{5,4},{6,7},{7,6},{8,9},{9,8},{10,11... | collective-permute-start | bytes 1572872 | tf_op jit(solution)/shard_map/ppermute | solution.py:35
  8.8 16.5 %collective-permute-start.8 = (f32[512,256]{1,0:T(8,128)S(1)}, f32[512,256]{1,0:T(8,128)S(1)}, u32[]{:S(2)}, u32[]{:S(2)}) collective-permute-start(f32[512,256]{1,0:T(8,128)S(1)} %get-tuple-element.31.refs_2_), channel_id=1, source_target_pairs={{0,1},{1,0},{2,3},{3,2},{4,5},{5,4},{6,7},{7,6},{8,9},{9,8},{10,11... | collective-permute-start | bytes 1572872 | tf_op jit(solution)/shard_map/ppermute | solution.py:35
  8.9 16.4 %collective-permute-start.9 = (f32[512,256]{1,0:T(8,128)S(1)}, f32[512,256]{1,0:T(8,128)S(1)}, u32[]{:S(2)}, u32[]{:S(2)}) collective-permute-start(f32[512,256]{1,0:T(8,128)S(1)} %get-tuple-element.32.refs_3_), channel_id=1, source_target_pairs={{0,1},{1,0},{2,3},{3,2},{4,5},{5,4},{6,7},{7,6},{8,9},{9,8},{10,11... | collective-permute-start | bytes 1572872 | tf_op jit(solution)/shard_map/ppermute | solution.py:35
  9.8 4.3 %collective-permute-start.2 = (f32[16,1024]{1,0:T(8,128)S(1)}, f32[16,1024]{1,0:T(8,128)S(1)}, u32[]{:S(2)}, u32[]{:S(2)}) collective-permute-start(f32[16,1024]{1,0:T(8,128)S(1)} %fusion), channel_id=1, source_target_pairs={{0,4},{1,5},{2,6},{3,7},{4,0},{5,1},{6,2},{7,3},{8,12},{9,13},{10,... | collective-permute-start | bytes 196616 | tf_op jit(solution)/shard_map/ppermute | solution.py:31
  14.2 5.3 %collective-permute-start.3 = (f32[16,1024]{1,0:T(8,128)S(1)}, f32[16,1024]{1,0:T(8,128)S(1)}, u32[]{:S(2)}, u32[]{:S(2)}) collective-permute-start(f32[16,1024]{1,0:T(8,128)S(1)} %add.23), channel_id=1, source_target_pairs={{0,8},{1,9},{2,10},{3,11},{4,12},{5,13},{6,14},{7,15},{8,0},{9,1},... | collective-permute-start | bytes 196616 | tf_op jit(solution)/shard_map/ppermute | solution.py:31
  19.5 4.3 %collective-permute-start.4 = (f32[16,1024]{1,0:T(8,128)S(1)}, f32[16,1024]{1,0:T(8,128)S(1)}, u32[]{:S(2)}, u32[]{:S(2)}) collective-permute-start(f32[16,1024]{1,0:T(8,128)S(1)} %add.24), channel_id=1, source_target_pairs={{0,2},{1,3},{2,0},{3,1},{4,6},{5,7},{6,4},{7,5},{8,10},{9,11},{10,... | collective-permute-start | bytes 196616 | tf_op jit(solution)/shard_map/ppermute | solution.py:31
  23.8 1.4 %collective-permute-start.5 = (f32[2,16,1024]{2,1,0:T(8,128)S(1)}, f32[2,16,1024]{2,1,0:T(8,128)S(1)}, u32[]{:S(2)}, u32[]{:S(2)}) collective-permute-start(f32[2,16,1024]{2,1,0:T(8,128)S(1)} %pad_maximum_fusion.mine_ref), channel_id=1, source_target_pairs={{0,1},{1,0},{2,3},{3,2},{4,5},{5,4},{6,7},{7,6},{8,9},{9,8},{10,11... | collective-permute-start | bytes 393224 | tf_op jit(solution)/shard_map/ppermute | solution.py:35
  25.8 3.3 %collective-permute-start.10 = (f32[32,256]{1,0:T(8,128)S(1)}, f32[32,256]{1,0:T(8,128)S(1)}, u32[]{:S(2)}, u32[]{:S(2)}) collective-permute-start(f32[32,256]{1,0:T(8,128)S(1)} %product.1), channel_id=1, source_target_pairs={{0,0},{1,3},{2,2},{3,1},{4,4},{5,7},{6,6},{7,5},{8,8},{9,11},{10,1... | collective-permute-start | bytes 98312 | tf_op jit(solution)/shard_map/ppermute | solution.py:31
  29.1 2.3 %collective-permute-start.11 = (f32[32,256]{1,0:T(8,128)S(1)}, f32[32,256]{1,0:T(8,128)S(1)}, u32[]{:S(2)}, u32[]{:S(2)}) collective-permute-start(f32[32,256]{1,0:T(8,128)S(1)} %add.25), channel_id=1, source_target_pairs={{0,0},{1,5},{2,2},{3,7},{4,4},{5,1},{6,6},{7,3},{8,8},{9,13},{10,1... | collective-permute-start | bytes 98312 | tf_op jit(solution)/shard_map/ppermute | solution.py:31
  31.4 0.7 %collective-permute-start.12 = (f32[32,256]{1,0:T(8,128)S(1)}, f32[32,256]{1,0:T(8,128)S(1)}, u32[]{:S(2)}, u32[]{:S(2)}) collective-permute-start(f32[32,256]{1,0:T(8,128)S(1)} %add.26), channel_id=1, source_target_pairs={{0,0},{1,9},{2,2},{3,11},{4,4},{5,13},{6,6},{7,15},{8,8},{9,1},{10... | collective-permute-start | bytes 98312 | tf_op jit(solution)/shard_map/ppermute | solution.py:31
  32.1 11.8 %collective-permute-start.13 = (f32[32,256]{1,0:T(8,128)S(1)}, f32[32,256]{1,0:T(8,128)S(1)}, u32[]{:S(2)}, u32[]{:S(2)}) collective-permute-start(f32[32,256]{1,0:T(8,128)S(1)} %add.27.mine_ref), channel_id=1, source_target_pairs={{0,1},{1,0},{2,3},{3,2},{4,5},{5,4},{6,7},{7,6},{8,9},{9,8},{10,11... | collective-permute-start | bytes 98312 | tf_op jit(solution)/shard_map/ppermute | solution.py:35

commit v14 on v12

--- a/solution.py
+++ b/solution.py
@@ -73,8 +73,8 @@
 def term_kernel(x_hbm, c_hbm, e_hbm, seed_hbm, keep_ref, send_ref, x_ref, c_ref, e_ref,
                 seed_ref, term_ref, sems):
     copies = whole_copies(
-        [(seed_hbm, seed_ref), (c_hbm, c_ref)] + row_parts(e_hbm.at[0], e_ref, 2)
-        + row_parts(x_hbm, x_ref, 2), sems)
+        [(seed_hbm, seed_ref), (c_hbm, c_ref)] + row_parts(x_hbm, x_ref, 2)
+        + row_parts(e_hbm.at[0], e_ref, 2), sems)
     for copy in copies:
         copy.start()
     rank = seed_ref.shape[0]
@@ -86,18 +86,19 @@
     mixed = added(dot(seed, c_ref[...], ((1,), (1,))), rank)
     mixed = jnp.concatenate(parts_of(mixed, 3), axis=0)
     blocks = width // CHUNK
-    for i in range(blocks):
-        if i % (blocks // 2) == 0:
-            copies[2 + i // (blocks // 2)].wait()
-        part = pl.ds(i * CHUNK, CHUNK)
-        term_ref[:, part] = added(dot(seed, e_ref[part, :], ((1,), (1,))), rank)
     for t in range(2):
-        copies[4 + t].wait()
+        copies[2 + t].wait()
         own = mixed[:, t * (tokens // 2):(t + 1) * (tokens // 2)]
         rows = pl.ds(t * (tokens // 2), tokens // 2)
         for i in range(blocks):
             part = pl.ds(i * CHUNK, CHUNK)
-            term_ref[:, part] += added(dot(own, x_ref[rows, part], ((1,), (0,))), rank)
+            term = added(dot(own, x_ref[rows, part], ((1,), (0,))), rank)
+            term_ref[:, part] = term if t == 0 else term_ref[:, part] + term
+    for i in range(blocks):
+        if i % (blocks // 2) == 0:
+            copies[4 + i // (blocks // 2)].wait()
+        part = pl.ds(i * CHUNK, CHUNK)
+        term_ref[:, part] += added(dot(seed, e_ref[part, :], ((1,), (1,))), rank)
     low = lax.axis_index("pair") == 0
     for i in range(2):
         part = half_of(side() ^ i, piece)
@@ -252,7 +253,7 @@
     return dot(lefts, rights, ((1,), (0,)))
 
 
-def first_sweep_kernel(mine_ref, other_ref, rows_ref, step_ref, gram_ref):
+def first_sweep_kernel(mine_ref, other_ref, rows_ref, step_ref):
     half, piece = mine_ref.shape[1:]
     rank = 2 * half
     blocks = None
@@ -263,16 +264,7 @@
             rows_ref[:, half_of(side() ^ i, piece, j * CHUNK, CHUNK)] = rows
             term = gram_blocks(rows)
             blocks = term if blocks is None else blocks + term
-    step = inverse_factor(gram_of(blocks, rank))
-    step_ref[...] = step
-    blocks = None
-    for i in range(rows_ref.shape[1] // CHUNK):
-        part = slice(i * CHUNK, (i + 1) * CHUNK)
-        rows = short_dot(step, rows_ref[:, part])
-        rows_ref[:, part] = rows
-        term = gram_blocks(rows)
-        blocks = term if blocks is None else blocks + term
-    gram_ref[...] = gram_of(blocks, rank)
+    step_ref[...] = inverse_factor(gram_of(blocks, rank))
 
 
 def first_sweep(mine, other):
@@ -283,7 +275,6 @@
         out_shape=[
             jax.ShapeDtypeStruct((rank, width), F32),
             jax.ShapeDtypeStruct((rank, rank), F32),
-            jax.ShapeDtypeStruct((rank, rank), F32),
         ],
         compiler_params=params(),
         cost_estimate=cost(10 ** 9, 7 * 10 ** 6),
@@ -291,36 +282,63 @@
     )(mine, other)
 
 
-def second_sweep_kernel(rows_ref, step_ref, gram_ref, basis_ref, inverse_ref):
-    last = inverse_factor(gram_ref[...])
+def second_sweep_kernel(first_ref, step_ref, rows_ref, last_ref):
+    rank, width = rows_ref.shape
+    step = step_ref[...]
+    blocks = None
+    for i in range(width // CHUNK):
+        part = slice(i * CHUNK, (i + 1) * CHUNK)
+        rows = short_dot(step, first_ref[:, part])
+        rows_ref[:, part] = rows
+        term = gram_blocks(rows)
+        blocks = term if blocks is None else blocks + term
+    last_ref[...] = inverse_factor(gram_of(blocks, rank))
+
+
+def second_sweep(rows, step):
+    return pl.pallas_call(
+        second_sweep_kernel,
+        out_shape=[
+            jax.ShapeDtypeStruct(rows.shape, F32),
+            jax.ShapeDtypeStruct(step.shape, F32),
+        ],
+        compiler_params=params(),
+        cost_estimate=cost(10 ** 9, 7 * 10 ** 6),
+        name="second_sweep",
+    )(rows, step)
+
+
+def basis_kernel(rows_ref, step_ref, last_ref, basis_ref, inverse_ref):
+    last = last_ref[...]
     for i in range(rows_ref.shape[1] // CHUNK):
         part = slice(i * CHUNK, (i + 1) * CHUNK)
         basis_ref[:, part] = short_dot(last, rows_ref[:, part])
     inverse_ref[...] = short_dot(last, step_ref[...])
 
 
-def second_sweep(rows, step, gram):
-    return pl.pallas_call(
-        second_sweep_kernel,
+def basis_of(rows, step, last):
+    return pl.pallas_call(
+        basis_kernel,
         out_shape=[
             jax.ShapeDtypeStruct(rows.shape, F32),
             jax.ShapeDtypeStruct(step.shape, F32),
         ],
         compiler_params=params(),
         cost_estimate=cost(10 ** 9, 7 * 10 ** 6),
-        name="second_sweep",
-    )(rows, step, gram)
+        name="basis",
+    )(rows, step, last)
 
 
 def error_kernel(workers, basis_ref, inverse_ref, mine_ref, other_ref, *refs):
     merged_refs = refs[:PARTS]
-    error_hbm, basis_hbm, second_ref, error_ref, error_sem, basis_sem = refs[PARTS:]
+    error_hbm, basis_hbm, second_hbm, error_ref, second_ref, error_sem, small_sem = refs[PARTS:]
     size = merged_refs[0].shape[0]
-    keep = pltpu.make_async_copy(basis_ref, basis_hbm, basis_sem)
-    keep.start()
+    small = whole_copies([(basis_ref, basis_hbm), (second_ref, second_hbm)], small_sem)
+    small[0].start()
     product = both_halves(mine_ref[...], other_ref[...])
     second = short_dot(inverse_ref[...], product) * (1.0 / workers)
     second_ref[...] = second
+    small[1].start()
     s_high, s_low = parts_of(second, 2)
     rights = jnp.concatenate([s_high, s_low, s_high], axis=0)
     copies = []
@@ -335,7 +353,7 @@
         copies.append(pltpu.make_async_copy(
             error_ref.at[part, :], error_hbm.at[0, part, :], error_sem.at[i]))
         copies[i].start()
-    for copy in copies + [keep]:
+    for copy in copies + small:
         copy.wait()
 
 
@@ -345,7 +363,7 @@
     return pl.pallas_call(
         functools.partial(error_kernel, workers),
         in_specs=[VMEM] * (4 + PARTS),
-        out_specs=[HBM, HBM, VMEM],
+        out_specs=[HBM] * 3,
         out_shape=[
             jax.ShapeDtypeStruct((1, width, out), BF16),
             jax.ShapeDtypeStruct((rank, width), F32),
@@ -353,8 +371,9 @@
         ],
         scratch_shapes=[
             pltpu.VMEM((width, out), BF16),
+            pltpu.VMEM((rank, out), F32),
             pltpu.SemaphoreType.DMA((width // CHUNK,)),
-            pltpu.SemaphoreType.DMA,
+            pltpu.SemaphoreType.DMA((2,)),
         ],
         compiler_params=params(),
         cost_estimate=cost(2 * rank * width * out, 6 * width * out),
@@ -381,14 +400,16 @@
     other = across(mine)
 
     product = product_of(near, far, merged, merged_other)
-    rows, step, gram = first_sweep(mine, other)
+    rows, step = first_sweep(mine, other)
     product = product + swapped(product, sizes, beside)
-    product, rows, step, gram = lax.optimization_barrier((product, rows, step, gram))
-    basis, inverse = second_sweep(rows, step, gram)
+    product, rows, step = lax.optimization_barrier((product, rows, step))
+    rows, last = second_sweep(rows, step)
     product = product + swapped(product, sizes, others[0])
-    product, basis, inverse = lax.optimization_barrier((product, basis, inverse))
+    product, rows, step, last = lax.optimization_barrier((product, rows, step, last))
+    basis, inverse = basis_of(rows, step, last)
     for bits in others[1:]:
         product = product + swapped(product, sizes, bits)
+    product, basis, inverse = lax.optimization_barrier((product, basis, inverse))
     return error_of(merged, basis, inverse, product, across(product), workers)
 
 

time: 40.8 us -> 40 us (0.980)
  starting transfers between devices: 17.7 us -> 18.5 us
  waiting for transfers between devices: 12.2 us -> 11.4 us
  Pallas kernels: 9.95 us -> 9.2 us
    pallas_call x1, Pallas kernels: 2.57 us -> 1.63 us  [first_sweep(): pl.pallas_call(first_sweep_kernel, out_shape=[jax.ShapeDtypeStruct((rank,...]
    ppermute x7, starting transfers between devices: 16 us -> 16.8 us  [swapped(): return lax.ppermute(value, AXES, pairs)]
    ppermute x7, waiting for transfers between devices: 9.98 us -> 9.22 us  [swapped(): return lax.ppermute(value, AXES, pairs)]
    pallas_call x1, Pallas kernels: 2.13 us -> 1.55 us  [error_of(): pl.pallas_call(functools.partial(error_kernel, workers), in_specs=[VMEM]...]
where the time goes in v14:
time: 40 us; the launch traced here: 39.9 us
  starting transfers between devices  18.5 us (46%)
  waiting for transfers between devices  11.4 us (28%)
  Pallas kernels  9.2 us (23%)
  between operations  0.75 us (2%)
    ppermute x7, starting transfers between devices, swapped(): return lax.ppermute(value, AXES, pairs)  16.8 us
    ppermute x7, waiting for transfers between devices, swapped(): return lax.ppermute(value, AXES, pairs)  9.22 us
    pallas_call x1, Pallas kernels, term_halves(): pl.pallas_call(term_kernel, in_specs=[HBM] * 4, out_specs=[VMEM] * 5, out...  2.5 us
    ppermute x7, waiting for transfers between devices, across(): return lax.ppermute(value, 'pair', [(0, 1), (1, 0)])  2.18 us
    pallas_call x1, Pallas kernels, second_sweep(): pl.pallas_call(second_sweep_kernel, out_shape=[jax.ShapeDtypeStruct(rows....  1.91 us
    ppermute x7, starting transfers between devices, across(): return lax.ppermute(value, 'pair', [(0, 1), (1, 0)])  1.66 us
    pallas_call x1, Pallas kernels, first_sweep(): pl.pallas_call(first_sweep_kernel, out_shape=[jax.ShapeDtypeStruct((rank,...  1.63 us
    pallas_call x1, Pallas kernels, error_of(): pl.pallas_call(functools.partial(error_kernel, workers), in_specs=[VMEM]...  1.55 us
  transfers between devices with their start and end apart: 14, of which 8 were waited for; matrix products, arithmetic and copies ran while one was open for 0% of the time, Pallas kernels for 13%

profile of v14, /device:TPU:0, one launch (start us, length us, event | category | flops | bytes accessed | tf_op | source)
XLA Modules:
  0.0 39.9 jit_solution(71711985817304294)
XLA Ops:
  0.6 2.5 %term.1 = (f32[2,16,1024]{2,1,0:T(8,128)S(1)}, f32[2,16,1024]{2,1,0:T(8,128)S(1)}, bf16[512,2048]{1,0:T(8,128)(2,1)S(1)}, bf16[512,256]{1,0:T(8,128)(2,1)S(1)}, bf16[2048,256]{1,0:T(8,128)(2,1)S(1)}) custom-call(bf16[512,2048]{1,0:T(8,128)(2,1)} %x_hbm.1, bf16[512,256]{1,0:T(8,128)(2,1)} %c_hbm.1, bf16[1,2048,256]{2,1,0:T(8,128)(2,1)} %e_hbm.1, ...), custom_call_target="tpu_custom_call" | custom-call | flops 201326592 | bytes 3145728 | tf_op jit(solution)/shard_map/term/pallas_call | solution.py:129
  3.1 0.5 %collective-permute-start = (f32[2,16,1024]{2,1,0:T(8,128)S(1)}, f32[2,16,1024]{2,1,0:T(8,128)S(1)}, u32[]{:S(2)}, u32[]{:S(2)}) collective-permute-start(f32[2,16,1024]{2,1,0:T(8,128)S(1)} %get-tuple-element.29), channel_id=1, source_target_pairs={{0,1},{1,0},{2,3},{3,2},{4,5},{5,4},{6,7},{7,6},{8,9},{9,8},{10,11... | collective-permute-start | bytes 393224 | tf_op jit(solution)/shard_map/ppermute | solution.py:34
  3.7 1.0 %collective-permute-done = f32[2,16,1024]{2,1,0:T(8,128)S(1)} collective-permute-done((f32[2,16,1024]{2,1,0:T(8,128)S(1)}, f32[2,16,1024]{2,1,0:T(8,128)S(1)}, u32[]{:S(2)}, u32[]{:S(2)}) %collective-permute-start) | collective-permute-done | bytes 131104 | tf_op jit(solution)/shard_map/ppermute | solution.py:34
  4.7 2.9 %collective-permute-start.1 = (f32[16,1024]{1,0:T(8,128)S(1)}, f32[16,1024]{1,0:T(8,128)S(1)}, u32[]{:S(2)}, u32[]{:S(2)}) collective-permute-start(f32[16,1024]{1,0:T(8,128)S(1)} %slice_bitcast_fusion), channel_id=1, source_target_pairs={{0,2},{1,3},{2,0},{3,1},{4,6},{5,7},{6,4},{7,5},{8,10},{9,11},{10,... | collective-permute-start | bytes 196616 | tf_op jit(solution)/shard_map/ppermute | solution.py:30
  7.6 0.8 %merge.1 = (f32[512,256]{1,0:T(8,128)S(1)}, f32[512,256]{1,0:T(8,128)S(1)}, f32[512,256]{1,0:T(8,128)S(1)}, f32[512,256]{1,0:T(8,128)S(1)}) custom-call(bf16[512,2048]{1,0:T(8,128)(2,1)S(1)} %get-tuple-element.30.x_ref, bf16[512,256]{1,0:T(8,128)(2,1)S(1)} %get-tuple-element.31.c_ref, bf16[2048,256]{1,0:T(8,128)(2,1)S(1)} %get-tuple-element.32.e_ref, ...), custom_call_target="tpu_custom_call" | custom-call | flops 100000000 | bytes 1000000 | tf_op jit(solution)/shard_map/merge/pallas_call | solution.py:162
  8.4 0.1 collective-permute-start.5
  8.4 0.5 %collective-permute-start.6 = (f32[512,256]{1,0:T(8,128)S(1)}, f32[512,256]{1,0:T(8,128)S(1)}, u32[]{:S(2)}, u32[]{:S(2)}) collective-permute-start(f32[512,256]{1,0:T(8,128)S(1)} %get-tuple-element.34.refs_1_), channel_id=1, source_target_pairs={{0,1},{1,0},{2,3},{3,2},{4,5},{5,4},{6,7},{7,6},{8,9},{9,8},{10,11... | collective-permute-start | bytes 1572872 | tf_op jit(solution)/shard_map/ppermute | solution.py:34
  8.9 0.1 collective-permute-start.7
  9.0 0.4 %collective-permute-start.8 = (f32[512,256]{1,0:T(8,128)S(1)}, f32[512,256]{1,0:T(8,128)S(1)}, u32[]{:S(2)}, u32[]{:S(2)}) collective-permute-start(f32[512,256]{1,0:T(8,128)S(1)} %get-tuple-element.36.refs_3_), channel_id=1, source_target_pairs={{0,1},{1,0},{2,3},{3,2},{4,5},{5,4},{6,7},{7,6},{8,9},{9,8},{10,11... | collective-permute-start | bytes 1572872 | tf_op jit(solution)/shard_map/ppermute | solution.py:34
  9.5 0.5 %collective-permute-done.1 = f32[16,1024]{1,0:T(8,128)S(1)} collective-permute-done((f32[16,1024]{1,0:T(8,128)S(1)}, f32[16,1024]{1,0:T(8,128)S(1)}, u32[]{:S(2)}, u32[]{:S(2)}) %collective-permute-start.1) | collective-permute-done | bytes 65568 | tf_op jit(solution)/shard_map/ppermute | solution.py:30
  10.0 2.0 %collective-permute-start.2 = (f32[16,1024]{1,0:T(8,128)S(1)}, f32[16,1024]{1,0:T(8,128)S(1)}, u32[]{:S(2)}, u32[]{:S(2)}) collective-permute-start(f32[16,1024]{1,0:T(8,128)S(1)} %fusion), channel_id=1, source_target_pairs={{0,4},{1,5},{2,6},{3,7},{4,0},{5,1},{6,2},{7,3},{8,12},{9,13},{10,... | collective-permute-start | bytes 196616 | tf_op jit(solution)/shard_map/ppermute | solution.py:30
  12.0 2.3 %collective-permute-done.2 = f32[16,1024]{1,0:T(8,128)S(1)} collective-permute-done((f32[16,1024]{1,0:T(8,128)S(1)}, f32[16,1024]{1,0:T(8,128)S(1)}, u32[]{:S(2)}, u32[]{:S(2)}) %collective-permute-start.2) | collective-permute-done | bytes 65568 | tf_op jit(solution)/shard_map/ppermute | solution.py:30
  14.4 3.0 %collective-permute-start.3 = (f32[16,1024]{1,0:T(8,128)S(1)}, f32[16,1024]{1,0:T(8,128)S(1)}, u32[]{:S(2)}, u32[]{:S(2)}) collective-permute-start(f32[16,1024]{1,0:T(8,128)S(1)} %add.23), channel_id=1, source_target_pairs={{0,8},{1,9},{2,10},{3,11},{4,12},{5,13},{6,14},{7,15},{8,0},{9,1},... | collective-permute-start | bytes 196616 | tf_op jit(solution)/shard_map/ppermute | solution.py:30
  17.4 2.2 %collective-permute-done.3 = f32[16,1024]{1,0:T(8,128)S(1)} collective-permute-done((f32[16,1024]{1,0:T(8,128)S(1)}, f32[16,1024]{1,0:T(8,128)S(1)}, u32[]{:S(2)}, u32[]{:S(2)}) %collective-permute-start.3) | collective-permute-done | bytes 65568 | tf_op jit(solution)/shard_map/ppermute | solution.py:30
  19.6 1.9 %collective-permute-start.4 = (f32[16,1024]{1,0:T(8,128)S(1)}, f32[16,1024]{1,0:T(8,128)S(1)}, u32[]{:S(2)}, u32[]{:S(2)}) collective-permute-start(f32[16,1024]{1,0:T(8,128)S(1)} %add.24.near_ref), channel_id=1, source_target_pairs={{0,2},{1,3},{2,0},{3,1},{4,6},{5,7},{6,4},{7,5},{8,10},{9,11},{10,... | collective-permute-start | bytes 196616 | tf_op jit(solution)/shard_map/ppermute | solution.py:30
  21.5 2.4 %collective-permute-done.4.far_ref = f32[16,1024]{1,0:T(8,128)S(1)} collective-permute-done((f32[16,1024]{1,0:T(8,128)S(1)}, f32[16,1024]{1,0:T(8,128)S(1)}, u32[]{:S(2)}, u32[]{:S(2)}) %collective-permute-start.4) | collective-permute-done | bytes 65568 | tf_op jit(solution)/shard_map/ppermute | solution.py:30
  24.0 0.1 collective-permute-start.10
  24.1 0.0 collective-permute-done.5.refs_4_
  24.1 0.0 collective-permute-done.6.refs_5_
  24.1 0.0 collective-permute-done.7.refs_6_
  24.1 0.0 collective-permute-done.8.refs_7_
  24.1 0.5 %product.1 = f32[16,256]{1,0:T(8,128)S(1)} custom-call(f32[16,1024]{1,0:T(8,128)S(1)} %add.24.near_ref, f32[16,1024]{1,0:T(8,128)S(1)} %collective-permute-done.4.far_ref, f32[512,256]{1,0:T(8,128)S(1)} %get-tuple-element.33.refs_0_, f32[512,256]{1,0:T(8,128)S(1)} %get-tuple-element.34.refs_1_, f32[512,256]{1,0:T(8,128)S(1)} %get-tuple-element.35.refs_2_, ...), custom_call_target="tpu_custom_call" | custom-call | flops 16777216 | bytes 4194304 | tf_op jit(solution)/shard_map/product/pallas_call | solution.py:198
  24.6 1.8 %collective-permute-start.9 = (f32[16,256]{1,0:T(8,128)S(1)}, f32[16,256]{1,0:T(8,128)S(1)}, u32[]{:S(2)}, u32[]{:S(2)}) collective-permute-start(f32[16,256]{1,0:T(8,128)S(1)} %product.1), channel_id=1, source_target_pairs={{0,2},{1,3},{2,0},{3,1},{4,6},{5,7},{6,4},{7,5},{8,10},{9,11},{10,... | collective-permute-start | bytes 49160 | tf_op jit(solution)/shard_map/ppermute | solution.py:30
  26.4 0.0 collective-permute-done.10.other_ref
  26.4 1.6 %first_sweep.1 = (f32[32,2048]{1,0:T(8,128)S(1)}, f32[32,32]{1,0:T(8,128)S(1)}) custom-call(f32[2,16,1024]{2,1,0:T(8,128)S(1)} %pad_maximum_fusion.mine_ref, f32[2,16,1024]{2,1,0:T(8,128)S(1)} %collective-permute-done.10.other_ref), custom_call_target="tpu_custom_call" | custom-call | flops 1000000000 | bytes 7000000 | tf_op jit(solution)/shard_map/first_sweep/pallas_call | solution.py:273
  28.1 0.3 collective-permute-done.9
  28.4 1.9 %collective-permute-start.11 = (f32[16,256]{1,0:T(8,128)S(1)}, f32[16,256]{1,0:T(8,128)S(1)}, u32[]{:S(2)}, u32[]{:S(2)}) collective-permute-start(f32[16,256]{1,0:T(8,128)S(1)} %add.25), channel_id=1, source_target_pairs={{0,4},{1,5},{2,6},{3,7},{4,0},{5,1},{6,2},{7,3},{8,12},{9,13},{10,... | collective-permute-start | bytes 49160 | tf_op jit(solution)/shard_map/ppermute | solution.py:30
  30.3 1.9 %second_sweep.1 = (f32[32,2048]{1,0:T(8,128)S(1)}, f32[32,32]{1,0:T(8,128)S(1)}) custom-call(f32[32,2048]{1,0:T(8,128)S(1)} %get-tuple-element.40.first_ref, f32[32,32]{1,0:T(8,128)S(1)} %get-tuple-element.46.step_ref), custom_call_target="tpu_custom_call" | custom-call | flops 1000000000 | bytes 7000000 | tf_op jit(solution)/shard_map/second_sweep/pallas_call | solution.py:299
  32.2 0.0 collective-permute-done.11
  32.2 3.2 %collective-permute-start.12 = (f32[16,256]{1,0:T(8,128)S(1)}, f32[16,256]{1,0:T(8,128)S(1)}, u32[]{:S(2)}, u32[]{:S(2)}) collective-permute-start(f32[16,256]{1,0:T(8,128)S(1)} %add.26), channel_id=1, source_target_pairs={{0,8},{1,9},{2,10},{3,11},{4,12},{5,13},{6,14},{7,15},{8,0},{9,1},... | collective-permute-start | bytes 49160 | tf_op jit(solution)/shard_map/ppermute | solution.py:30
  35.4 0.3 basis.1
  35.8 1.4 %collective-permute-done.12 = f32[16,256]{1,0:T(8,128)S(1)} collective-permute-done((f32[16,256]{1,0:T(8,128)S(1)}, f32[16,256]{1,0:T(8,128)S(1)}, u32[]{:S(2)}, u32[]{:S(2)}) %collective-permute-start.12) | collective-permute-done | bytes 16416 | tf_op jit(solution)/shard_map/ppermute | solution.py:30
  37.2 0.0 collective-permute-start.13
  37.2 1.2 %collective-permute-done.13.other_ref = f32[16,256]{1,0:T(8,128)S(1)} collective-permute-done((f32[16,256]{1,0:T(8,128)S(1)}, f32[16,256]{1,0:T(8,128)S(1)}, u32[]{:S(2)}, u32[]{:S(2)}) %collective-permute-start.13) | collective-permute-done | bytes 16416 | tf_op jit(solution)/shard_map/ppermute | solution.py:34
  38.3 1.5 %error_next.1 = (bf16[1,2048,256]{2,1,0:T(8,128)(2,1)}, f32[32,2048]{1,0:T(8,128)}, f32[32,256]{1,0:T(8,128)}) custom-call(f32[32,2048]{1,0:T(8,128)S(1)} %get-tuple-element.50.basis_ref, f32[32,32]{1,0:T(8,128)S(1)} %get-tuple-element.51.inverse_ref, f32[16,256]{1,0:T(8,128)S(1)} %add.27.mine_ref, f32[16,256]{1,0:T(8,128)S(1)} %collective-permute-done.13.other_ref, ...), custom_call_target="tpu_custom_call" | custom-call | flops 33554432 | bytes 3145728 | tf_op jit(solution)/shard_map/error_next/pallas_call | solution.py:363
  (9 shorter events, 0.1 us)
Async XLA Ops:
  3.1 1.5 %collective-permute-start = (f32[2,16,1024]{2,1,0:T(8,128)S(1)}, f32[2,16,1024]{2,1,0:T(8,128)S(1)}, u32[]{:S(2)}, u32[]{:S(2)}) collective-permute-start(f32[2,16,1024]{2,1,0:T(8,128)S(1)} %get-tuple-element.29), channel_id=1, source_target_pairs={{0,1},{1,0},{2,3},{3,2},{4,5},{5,4},{6,7},{7,6},{8,9},{9,8},{10,11... | collective-permute-start | bytes 393224 | tf_op jit(solution)/shard_map/ppermute | solution.py:34
  4.7 5.3 %collective-permute-start.1 = (f32[16,1024]{1,0:T(8,128)S(1)}, f32[16,1024]{1,0:T(8,128)S(1)}, u32[]{:S(2)}, u32[]{:S(2)}) collective-permute-start(f32[16,1024]{1,0:T(8,128)S(1)} %slice_bitcast_fusion), channel_id=1, source_target_pairs={{0,2},{1,3},{2,0},{3,1},{4,6},{5,7},{6,4},{7,5},{8,10},{9,11},{10,... | collective-permute-start | bytes 196616 | tf_op jit(solution)/shard_map/ppermute | solution.py:30
  8.4 15.7 %collective-permute-start.5 = (f32[512,256]{1,0:T(8,128)S(1)}, f32[512,256]{1,0:T(8,128)S(1)}, u32[]{:S(2)}, u32[]{:S(2)}) collective-permute-start(f32[512,256]{1,0:T(8,128)S(1)} %get-tuple-element.33.refs_0_), channel_id=1, source_target_pairs={{0,1},{1,0},{2,3},{3,2},{4,5},{5,4},{6,7},{7,6},{8,9},{9,8},{10,11... | collective-permute-start | bytes 1572872 | tf_op jit(solution)/shard_map/ppermute | solution.py:34
  8.4 15.6 %collective-permute-start.6 = (f32[512,256]{1,0:T(8,128)S(1)}, f32[512,256]{1,0:T(8,128)S(1)}, u32[]{:S(2)}, u32[]{:S(2)}) collective-permute-start(f32[512,256]{1,0:T(8,128)S(1)} %get-tuple-element.34.refs_1_), channel_id=1, source_target_pairs={{0,1},{1,0},{2,3},{3,2},{4,5},{5,4},{6,7},{7,6},{8,9},{9,8},{10,11... | collective-permute-start | bytes 1572872 | tf_op jit(solution)/shard_map/ppermute | solution.py:34
  8.9 15.1 %collective-permute-start.7 = (f32[512,256]{1,0:T(8,128)S(1)}, f32[512,256]{1,0:T(8,128)S(1)}, u32[]{:S(2)}, u32[]{:S(2)}) collective-permute-start(f32[512,256]{1,0:T(8,128)S(1)} %get-tuple-element.35.refs_2_), channel_id=1, source_target_pairs={{0,1},{1,0},{2,3},{3,2},{4,5},{5,4},{6,7},{7,6},{8,9},{9,8},{10,11... | collective-permute-start | bytes 1572872 | tf_op jit(solution)/shard_map/ppermute | solution.py:34
  9.0 15.1 %collective-permute-start.8 = (f32[512,256]{1,0:T(8,128)S(1)}, f32[512,256]{1,0:T(8,128)S(1)}, u32[]{:S(2)}, u32[]{:S(2)}) collective-permute-start(f32[512,256]{1,0:T(8,128)S(1)} %get-tuple-element.36.refs_3_), channel_id=1, source_target_pairs={{0,1},{1,0},{2,3},{3,2},{4,5},{5,4},{6,7},{7,6},{8,9},{9,8},{10,11... | collective-permute-start | bytes 1572872 | tf_op jit(solution)/shard_map/ppermute | solution.py:34
  10.0 4.3 %collective-permute-start.2 = (f32[16,1024]{1,0:T(8,128)S(1)}, f32[16,1024]{1,0:T(8,128)S(1)}, u32[]{:S(2)}, u32[]{:S(2)}) collective-permute-start(f32[16,1024]{1,0:T(8,128)S(1)} %fusion), channel_id=1, source_target_pairs={{0,4},{1,5},{2,6},{3,7},{4,0},{5,1},{6,2},{7,3},{8,12},{9,13},{10,... | collective-permute-start | bytes 196616 | tf_op jit(solution)/shard_map/ppermute | solution.py:30
  14.4 5.3 %collective-permute-start.3 = (f32[16,1024]{1,0:T(8,128)S(1)}, f32[16,1024]{1,0:T(8,128)S(1)}, u32[]{:S(2)}, u32[]{:S(2)}) collective-permute-start(f32[16,1024]{1,0:T(8,128)S(1)} %add.23), channel_id=1, source_target_pairs={{0,8},{1,9},{2,10},{3,11},{4,12},{5,13},{6,14},{7,15},{8,0},{9,1},... | collective-permute-start | bytes 196616 | tf_op jit(solution)/shard_map/ppermute | solution.py:30
  19.6 4.3 %collective-permute-start.4 = (f32[16,1024]{1,0:T(8,128)S(1)}, f32[16,1024]{1,0:T(8,128)S(1)}, u32[]{:S(2)}, u32[]{:S(2)}) collective-permute-start(f32[16,1024]{1,0:T(8,128)S(1)} %add.24.near_ref), channel_id=1, source_target_pairs={{0,2},{1,3},{2,0},{3,1},{4,6},{5,7},{6,4},{7,5},{8,10},{9,11},{10,... | collective-permute-start | bytes 196616 | tf_op jit(solution)/shard_map/ppermute | solution.py:30
  24.0 2.5 %collective-permute-start.10 = (f32[2,16,1024]{2,1,0:T(8,128)S(1)}, f32[2,16,1024]{2,1,0:T(8,128)S(1)}, u32[]{:S(2)}, u32[]{:S(2)}) collective-permute-start(f32[2,16,1024]{2,1,0:T(8,128)S(1)} %pad_maximum_fusion.mine_ref), channel_id=1, source_target_pairs={{0,1},{1,0},{2,3},{3,2},{4,5},{5,4},{6,7},{7,6},{8,9},{9,8},{10,11... | collective-permute-start | bytes 393224 | tf_op jit(solution)/shard_map/ppermute | solution.py:34
  24.6 3.7 %collective-permute-start.9 = (f32[16,256]{1,0:T(8,128)S(1)}, f32[16,256]{1,0:T(8,128)S(1)}, u32[]{:S(2)}, u32[]{:S(2)}) collective-permute-start(f32[16,256]{1,0:T(8,128)S(1)} %product.1), channel_id=1, source_target_pairs={{0,2},{1,3},{2,0},{3,1},{4,6},{5,7},{6,4},{7,5},{8,10},{9,11},{10,... | collective-permute-start | bytes 49160 | tf_op jit(solution)/shard_map/ppermute | solution.py:30
  28.4 3.8 %collective-permute-start.11 = (f32[16,256]{1,0:T(8,128)S(1)}, f32[16,256]{1,0:T(8,128)S(1)}, u32[]{:S(2)}, u32[]{:S(2)}) collective-permute-start(f32[16,256]{1,0:T(8,128)S(1)} %add.25), channel_id=1, source_target_pairs={{0,4},{1,5},{2,6},{3,7},{4,0},{5,1},{6,2},{7,3},{8,12},{9,13},{10,... | collective-permute-start | bytes 49160 | tf_op jit(solution)/shard_map/ppermute | solution.py:30
  32.2 5.0 %collective-permute-start.12 = (f32[16,256]{1,0:T(8,128)S(1)}, f32[16,256]{1,0:T(8,128)S(1)}, u32[]{:S(2)}, u32[]{:S(2)}) collective-permute-start(f32[16,256]{1,0:T(8,128)S(1)} %add.26), channel_id=1, source_target_pairs={{0,8},{1,9},{2,10},{3,11},{4,12},{5,13},{6,14},{7,15},{8,0},{9,1},... | collective-permute-start | bytes 49160 | tf_op jit(solution)/shard_map/ppermute | solution.py:30
  37.2 1.2 %collective-permute-start.13 = (f32[16,256]{1,0:T(8,128)S(1)}, f32[16,256]{1,0:T(8,128)S(1)}, u32[]{:S(2)}, u32[]{:S(2)}) collective-permute-start(f32[16,256]{1,0:T(8,128)S(1)} %add.27.mine_ref), channel_id=1, source_target_pairs={{0,1},{1,0},{2,3},{3,2},{4,5},{5,4},{6,7},{7,6},{8,9},{9,8},{10,11... | collective-permute-start | bytes 49160 | tf_op jit(solution)/shard_map/ppermute | solution.py:34

commit v15 on v14

--- a/solution.py
+++ b/solution.py
@@ -73,8 +73,8 @@
 def term_kernel(x_hbm, c_hbm, e_hbm, seed_hbm, keep_ref, send_ref, x_ref, c_ref, e_ref,
                 seed_ref, term_ref, sems):
     copies = whole_copies(
-        [(seed_hbm, seed_ref), (c_hbm, c_ref)] + row_parts(x_hbm, x_ref, 2)
-        + row_parts(e_hbm.at[0], e_ref, 2), sems)
+        [(seed_hbm, seed_ref), (c_hbm, c_ref)] + row_parts(e_hbm.at[0], e_ref, 2)
+        + row_parts(x_hbm, x_ref, 2), sems)
     for copy in copies:
         copy.start()
     rank = seed_ref.shape[0]
@@ -86,19 +86,18 @@
     mixed = added(dot(seed, c_ref[...], ((1,), (1,))), rank)
     mixed = jnp.concatenate(parts_of(mixed, 3), axis=0)
     blocks = width // CHUNK
+    for i in range(blocks):
+        if i % (blocks // 2) == 0:
+            copies[2 + i // (blocks // 2)].wait()
+        part = pl.ds(i * CHUNK, CHUNK)
+        term_ref[:, part] = added(dot(seed, e_ref[part, :], ((1,), (1,))), rank)
     for t in range(2):
-        copies[2 + t].wait()
+        copies[4 + t].wait()
         own = mixed[:, t * (tokens // 2):(t + 1) * (tokens // 2)]
         rows = pl.ds(t * (tokens // 2), tokens // 2)
         for i in range(blocks):
             part = pl.ds(i * CHUNK, CHUNK)
-            term = added(dot(own, x_ref[rows, part], ((1,), (0,))), rank)
-            term_ref[:, part] = term if t == 0 else term_ref[:, part] + term
-    for i in range(blocks):
-        if i % (blocks // 2) == 0:
-            copies[4 + i // (blocks // 2)].wait()
-        part = pl.ds(i * CHUNK, CHUNK)
-        term_ref[:, part] += added(dot(seed, e_ref[part, :], ((1,), (1,))), rank)
+            term_ref[:, part] += added(dot(own, x_ref[rows, part], ((1,), (0,))), rank)
     low = lax.axis_index("pair") == 0
     for i in range(2):
         part = half_of(side() ^ i, piece)
@@ -171,7 +170,7 @@
 
 
 def product_kernel(near_ref, far_ref, *refs):
-    mine_refs, other_refs, product_ref = refs[:PARTS], refs[PARTS:2 * PARTS], refs[2 * PARTS]
+    mine_refs, other_refs, copies_ref = refs[:PARTS], refs[PARTS:2 * PARTS], refs[2 * PARTS]
     rank, piece = near_ref.shape
     size = mine_refs[0].shape[0]
     straight = side() == 0
@@ -188,16 +187,17 @@
         m_high, m_low = parts_of(merged, 2)
         term = added(dot(both, m_high, ((1,), (0,))), rank) + dot(f_high, m_low, ((1,), (0,)))
         product = term if product is None else product + term
-    product_ref[...] = product
-
-
-def product_of(near, far, mine, other):
+    for i in range(copies_ref.shape[0]):
+        copies_ref[i] = product
+
+
+def product_copies(count, near, far, mine, other):
     rank, piece = near.shape
     size, out = mine[0].shape
     width = 2 * piece
     return pl.pallas_call(
         product_kernel,
-        out_shape=jax.ShapeDtypeStruct((rank, out), F32),
+        out_shape=jax.ShapeDtypeStruct((count, rank, out), F32),
         compiler_params=params(),
         cost_estimate=cost(2 * rank * width * out, 8 * width * out),
         name="product",
@@ -399,16 +399,12 @@
     mine = jnp.stack([near, far])
     other = across(mine)
 
-    product = product_of(near, far, merged, merged_other)
+    copies = product_copies(workers // 2, near, far, merged, merged_other)
     rows, step = first_sweep(mine, other)
-    product = product + swapped(product, sizes, beside)
-    product, rows, step = lax.optimization_barrier((product, rows, step))
     rows, last = second_sweep(rows, step)
-    product = product + swapped(product, sizes, others[0])
-    product, rows, step, last = lax.optimization_barrier((product, rows, step, last))
     basis, inverse = basis_of(rows, step, last)
-    for bits in others[1:]:
-        product = product + swapped(product, sizes, bits)
+    products = lax.all_to_all(copies, ("dp", "sub"), 0, 0, tiled=True)
+    product = jnp.sum(products, axis=0)
     product, basis, inverse = lax.optimization_barrier((product, basis, inverse))
     return error_of(merged, basis, inverse, product, across(product), workers)
 

time: 40 us -> 42.6 us (1.065)
  waiting for transfers between devices: 11.4 us -> 13.4 us
  Pallas kernels: 9.2 us -> 9.72 us
    ppermute x7 -> x4, starting transfers between devices: 16.8 us -> 9.83 us  [swapped(): return lax.ppermute(value, AXES, pairs)]
    all_to_all x0 -> x1, starting transfers between devices: none -> 6.73 us  [local(): products = lax.all_to_all(copies, ('dp', 'sub'), 0, 0, tiled=True)]
    all_to_all x0 -> x1, waiting for transfers between devices: none -> 3.73 us  [local(): products = lax.all_to_all(copies, ('dp', 'sub'), 0, 0, tiled=True)]
    ppermute x7 -> x4, waiting for transfers between devices: 9.22 us -> 7.54 us  [swapped(): return lax.ppermute(value, AXES, pairs)]
    pallas_call x1, Pallas kernels: 0.51 us -> 1.18 us  [product_copies(): pl.pallas_call(product_kernel, out_shape=jax.ShapeDtypeStruct((count, ran...]
  transfers between devices with their start and end apart: 14 -> 12, of which waited for: 8 -> 7; matrix products, arithmetic and copies ran while one was open for 0% -> 0% of each run, Pallas kernels for 13% -> 14%
where the time goes in v15:
time: 42.6 us; the launch traced here: 42.3 us
  starting transfers between devices  18.3 us (43%)
  waiting for transfers between devices  13.4 us (31%)
  Pallas kernels  9.72 us (23%)
  between operations  0.74 us (2%)
    ppermute x4, starting transfers between devices, swapped(): return lax.ppermute(value, AXES, pairs)  9.83 us
    ppermute x4, waiting for transfers between devices, swapped(): return lax.ppermute(value, AXES, pairs)  7.54 us
    all_to_all x1, starting transfers between devices, local(): products = lax.all_to_all(copies, ('dp', 'sub'), 0, 0, tiled=True)  6.73 us
    all_to_all x1, waiting for transfers between devices, local(): products = lax.all_to_all(copies, ('dp', 'sub'), 0, 0, tiled=True)  3.73 us
    pallas_call x1, Pallas kernels, term_halves(): pl.pallas_call(term_kernel, in_specs=[HBM] * 4, out_specs=[VMEM] * 5, out...  2.34 us
    ppermute x7, waiting for transfers between devices, across(): return lax.ppermute(value, 'pair', [(0, 1), (1, 0)])  2.17 us
    pallas_call x1, Pallas kernels, second_sweep(): pl.pallas_call(second_sweep_kernel, out_shape=[jax.ShapeDtypeStruct(rows....  1.92 us
    ppermute x7, starting transfers between devices, across(): return lax.ppermute(value, 'pair', [(0, 1), (1, 0)])  1.74 us
  transfers between devices with their start and end apart: 12, of which 7 were waited for; matrix products, arithmetic and copies ran while one was open for 0% of the time, Pallas kernels for 14%

profile of v15, /device:TPU:0, one launch (start us, length us, event | category | flops | bytes accessed | tf_op | source)
XLA Modules:
  0.0 42.3 jit_solution(14702367388117021569)
XLA Ops:
  0.6 2.3 %term.1 = (f32[2,16,1024]{2,1,0:T(8,128)S(1)}, f32[2,16,1024]{2,1,0:T(8,128)S(1)}, bf16[512,2048]{1,0:T(8,128)(2,1)S(1)}, bf16[512,256]{1,0:T(8,128)(2,1)S(1)}, bf16[2048,256]{1,0:T(8,128)(2,1)S(1)}) custom-call(bf16[512,2048]{1,0:T(8,128)(2,1)} %x_hbm.1, bf16[512,256]{1,0:T(8,128)(2,1)} %c_hbm.1, bf16[1,2048,256]{2,1,0:T(8,128)(2,1)} %e_hbm.1, ...), custom_call_target="tpu_custom_call" | custom-call | flops 201326592 | bytes 3145728 | tf_op jit(solution)/shard_map/term/pallas_call | solution.py:128
  3.0 0.5 %collective-permute-start = (f32[2,16,1024]{2,1,0:T(8,128)S(1)}, f32[2,16,1024]{2,1,0:T(8,128)S(1)}, u32[]{:S(2)}, u32[]{:S(2)}) collective-permute-start(f32[2,16,1024]{2,1,0:T(8,128)S(1)} %get-tuple-element.22), channel_id=1, source_target_pairs={{0,1},{1,0},{2,3},{3,2},{4,5},{5,4},{6,7},{7,6},{8,9},{9,8},{10,11... | collective-permute-start | bytes 393224 | tf_op jit(solution)/shard_map/ppermute | solution.py:34
  3.5 1.0 %collective-permute-done = f32[2,16,1024]{2,1,0:T(8,128)S(1)} collective-permute-done((f32[2,16,1024]{2,1,0:T(8,128)S(1)}, f32[2,16,1024]{2,1,0:T(8,128)S(1)}, u32[]{:S(2)}, u32[]{:S(2)}) %collective-permute-start) | collective-permute-done | bytes 131104 | tf_op jit(solution)/shard_map/ppermute | solution.py:34
  4.5 2.9 %collective-permute-start.1 = (f32[16,1024]{1,0:T(8,128)S(1)}, f32[16,1024]{1,0:T(8,128)S(1)}, u32[]{:S(2)}, u32[]{:S(2)}) collective-permute-start(f32[16,1024]{1,0:T(8,128)S(1)} %slice_bitcast_fusion), channel_id=1, source_target_pairs={{0,2},{1,3},{2,0},{3,1},{4,6},{5,7},{6,4},{7,5},{8,10},{9,11},{10,... | collective-permute-start | bytes 196616 | tf_op jit(solution)/shard_map/ppermute | solution.py:30
  7.4 0.8 %merge.1 = (f32[512,256]{1,0:T(8,128)S(1)}, f32[512,256]{1,0:T(8,128)S(1)}, f32[512,256]{1,0:T(8,128)S(1)}, f32[512,256]{1,0:T(8,128)S(1)}) custom-call(bf16[512,2048]{1,0:T(8,128)(2,1)S(1)} %get-tuple-element.23.x_ref, bf16[512,256]{1,0:T(8,128)(2,1)S(1)} %get-tuple-element.24.c_ref, bf16[2048,256]{1,0:T(8,128)(2,1)S(1)} %get-tuple-element.25.e_ref, ...), custom_call_target="tpu_custom_call" | custom-call | flops 100000000 | bytes 1000000 | tf_op jit(solution)/shard_map/merge/pallas_call | solution.py:161
  8.2 0.1 collective-permute-start.5
  8.3 0.5 %collective-permute-start.6 = (f32[512,256]{1,0:T(8,128)S(1)}, f32[512,256]{1,0:T(8,128)S(1)}, u32[]{:S(2)}, u32[]{:S(2)}) collective-permute-start(f32[512,256]{1,0:T(8,128)S(1)} %get-tuple-element.27.refs_1_), channel_id=1, source_target_pairs={{0,1},{1,0},{2,3},{3,2},{4,5},{5,4},{6,7},{7,6},{8,9},{9,8},{10,11... | collective-permute-start | bytes 1572872 | tf_op jit(solution)/shard_map/ppermute | solution.py:34
  8.8 0.1 collective-permute-start.7
  8.9 0.4 %collective-permute-start.8 = (f32[512,256]{1,0:T(8,128)S(1)}, f32[512,256]{1,0:T(8,128)S(1)}, u32[]{:S(2)}, u32[]{:S(2)}) collective-permute-start(f32[512,256]{1,0:T(8,128)S(1)} %get-tuple-element.29.refs_3_), channel_id=1, source_target_pairs={{0,1},{1,0},{2,3},{3,2},{4,5},{5,4},{6,7},{7,6},{8,9},{9,8},{10,11... | collective-permute-start | bytes 1572872 | tf_op jit(solution)/shard_map/ppermute | solution.py:34
  9.3 0.5 %collective-permute-done.1 = f32[16,1024]{1,0:T(8,128)S(1)} collective-permute-done((f32[16,1024]{1,0:T(8,128)S(1)}, f32[16,1024]{1,0:T(8,128)S(1)}, u32[]{:S(2)}, u32[]{:S(2)}) %collective-permute-start.1) | collective-permute-done | bytes 65568 | tf_op jit(solution)/shard_map/ppermute | solution.py:30
  9.8 2.0 %collective-permute-start.2 = (f32[16,1024]{1,0:T(8,128)S(1)}, f32[16,1024]{1,0:T(8,128)S(1)}, u32[]{:S(2)}, u32[]{:S(2)}) collective-permute-start(f32[16,1024]{1,0:T(8,128)S(1)} %fusion), channel_id=1, source_target_pairs={{0,4},{1,5},{2,6},{3,7},{4,0},{5,1},{6,2},{7,3},{8,12},{9,13},{10,... | collective-permute-start | bytes 196616 | tf_op jit(solution)/shard_map/ppermute | solution.py:30
  11.9 2.3 %collective-permute-done.2 = f32[16,1024]{1,0:T(8,128)S(1)} collective-permute-done((f32[16,1024]{1,0:T(8,128)S(1)}, f32[16,1024]{1,0:T(8,128)S(1)}, u32[]{:S(2)}, u32[]{:S(2)}) %collective-permute-start.2) | collective-permute-done | bytes 65568 | tf_op jit(solution)/shard_map/ppermute | solution.py:30
  14.2 3.0 %collective-permute-start.3 = (f32[16,1024]{1,0:T(8,128)S(1)}, f32[16,1024]{1,0:T(8,128)S(1)}, u32[]{:S(2)}, u32[]{:S(2)}) collective-permute-start(f32[16,1024]{1,0:T(8,128)S(1)} %add.14), channel_id=1, source_target_pairs={{0,8},{1,9},{2,10},{3,11},{4,12},{5,13},{6,14},{7,15},{8,0},{9,1},... | collective-permute-start | bytes 196616 | tf_op jit(solution)/shard_map/ppermute | solution.py:30
  17.2 2.2 %collective-permute-done.3 = f32[16,1024]{1,0:T(8,128)S(1)} collective-permute-done((f32[16,1024]{1,0:T(8,128)S(1)}, f32[16,1024]{1,0:T(8,128)S(1)}, u32[]{:S(2)}, u32[]{:S(2)}) %collective-permute-start.3) | collective-permute-done | bytes 65568 | tf_op jit(solution)/shard_map/ppermute | solution.py:30
  19.5 1.9 %collective-permute-start.4 = (f32[16,1024]{1,0:T(8,128)S(1)}, f32[16,1024]{1,0:T(8,128)S(1)}, u32[]{:S(2)}, u32[]{:S(2)}) collective-permute-start(f32[16,1024]{1,0:T(8,128)S(1)} %add.15.near_ref), channel_id=1, source_target_pairs={{0,2},{1,3},{2,0},{3,1},{4,6},{5,7},{6,4},{7,5},{8,10},{9,11},{10,... | collective-permute-start | bytes 196616 | tf_op jit(solution)/shard_map/ppermute | solution.py:30
  21.4 2.4 %collective-permute-done.4.far_ref = f32[16,1024]{1,0:T(8,128)S(1)} collective-permute-done((f32[16,1024]{1,0:T(8,128)S(1)}, f32[16,1024]{1,0:T(8,128)S(1)}, u32[]{:S(2)}, u32[]{:S(2)}) %collective-permute-start.4) | collective-permute-done | bytes 65568 | tf_op jit(solution)/shard_map/ppermute | solution.py:30
  23.8 0.1 collective-permute-start.9
  23.9 0.0 collective-permute-done.5.refs_4_
  23.9 0.0 collective-permute-done.6.refs_5_
  23.9 0.0 collective-permute-done.7.refs_6_
  23.9 0.0 collective-permute-done.8.refs_7_
  23.9 1.2 %product.1 = f32[8,16,256]{2,1,0:T(8,128)} custom-call(f32[16,1024]{1,0:T(8,128)S(1)} %add.15.near_ref, f32[16,1024]{1,0:T(8,128)S(1)} %collective-permute-done.4.far_ref, f32[512,256]{1,0:T(8,128)S(1)} %get-tuple-element.26.refs_0_, f32[512,256]{1,0:T(8,128)S(1)} %get-tuple-element.27.refs_1_, f32[512,256]{1,0:T(8,128)S(1)} %get-tuple-element.28.refs_2_, ...), custom_call_target="tpu_custom_call" | custom-call | flops 16777216 | bytes 4194304 | tf_op jit(solution)/shard_map/product/pallas_call | solution.py:198
  25.1 6.7 %all-to-all-start = ((f32[8,16,256]{2,1,0:T(8,128)}), f32[8,16,256]{2,1,0:T(8,128)S(1)}, u32[]{:S(2)}, u32[]{:S(2)}) async-start(f32[8,16,256]{2,1,0:T(8,128)} %product.1), calls=%async_computation | async-start | bytes 262144 | tf_op jit(solution)/shard_map/all_to_all | solution.py:406
  31.8 0.0 collective-permute-done.9.other_ref
  31.9 1.6 %first_sweep.1 = (f32[32,2048]{1,0:T(8,128)S(1)}, f32[32,32]{1,0:T(8,128)S(1)}) custom-call(f32[2,16,1024]{2,1,0:T(8,128)S(1)} %pad_maximum_fusion.mine_ref, f32[2,16,1024]{2,1,0:T(8,128)S(1)} %collective-permute-done.9.other_ref), custom_call_target="tpu_custom_call" | custom-call | flops 1000000000 | bytes 7000000 | tf_op jit(solution)/shard_map/first_sweep/pallas_call | solution.py:273
  33.5 1.9 %second_sweep.1 = (f32[32,2048]{1,0:T(8,128)S(1)}, f32[32,32]{1,0:T(8,128)S(1)}) custom-call(f32[32,2048]{1,0:T(8,128)S(1)} %get-tuple-element.30.first_ref, f32[32,32]{1,0:T(8,128)S(1)} %get-tuple-element.31.step_ref), custom_call_target="tpu_custom_call" | custom-call | flops 1000000000 | bytes 7000000 | tf_op jit(solution)/shard_map/second_sweep/pallas_call | solution.py:299
  35.4 0.3 basis.1
  35.7 3.7 %all-to-all-done = f32[8,16,256]{2,1,0:T(8,128)S(1)} async-done(((f32[8,16,256]{2,1,0:T(8,128)}), f32[8,16,256]{2,1,0:T(8,128)S(1)}, u32[]{:S(2)}, u32[]{:S(2)}) %all-to-all-start) | async-done | bytes 131104 | tf_op jit(solution)/shard_map/all_to_all | solution.py:406
  39.5 0.1 collective-permute-start.10
  39.6 1.2 %collective-permute-done.10.other_ref = f32[16,256]{1,0:T(8,128)S(1)} collective-permute-done((f32[16,256]{1,0:T(8,128)S(1)}, f32[16,256]{1,0:T(8,128)S(1)}, u32[]{:S(2)}, u32[]{:S(2)}) %collective-permute-start.10) | collective-permute-done | bytes 16416 | tf_op jit(solution)/shard_map/ppermute | solution.py:34
  40.7 1.5 %error_next.1 = (bf16[1,2048,256]{2,1,0:T(8,128)(2,1)}, f32[32,2048]{1,0:T(8,128)}, f32[32,256]{1,0:T(8,128)}) custom-call(f32[32,2048]{1,0:T(8,128)S(1)} %get-tuple-element.36.basis_ref, f32[32,32]{1,0:T(8,128)S(1)} %get-tuple-element.37.inverse_ref, f32[16,256]{1,0:T(8,128)S(1)} %reduce_sum.9.mine_ref, f32[16,256]{1,0:T(8,128)S(1)} %collective-permute-done.10.other_ref, ...), custom_call_target="tpu_custom_call" | custom-call | flops 33554432 | bytes 3145728 | tf_op jit(solution)/shard_map/error_next/pallas_call | solution.py:363
  (7 shorter events, 0.1 us)
Async XLA Ops:
  3.0 1.5 %collective-permute-start = (f32[2,16,1024]{2,1,0:T(8,128)S(1)}, f32[2,16,1024]{2,1,0:T(8,128)S(1)}, u32[]{:S(2)}, u32[]{:S(2)}) collective-permute-start(f32[2,16,1024]{2,1,0:T(8,128)S(1)} %get-tuple-element.22), channel_id=1, source_target_pairs={{0,1},{1,0},{2,3},{3,2},{4,5},{5,4},{6,7},{7,6},{8,9},{9,8},{10,11... | collective-permute-start | bytes 393224 | tf_op jit(solution)/shard_map/ppermute | solution.py:34
  4.5 5.3 %collective-permute-start.1 = (f32[16,1024]{1,0:T(8,128)S(1)}, f32[16,1024]{1,0:T(8,128)S(1)}, u32[]{:S(2)}, u32[]{:S(2)}) collective-permute-start(f32[16,1024]{1,0:T(8,128)S(1)} %slice_bitcast_fusion), channel_id=1, source_target_pairs={{0,2},{1,3},{2,0},{3,1},{4,6},{5,7},{6,4},{7,5},{8,10},{9,11},{10,... | collective-permute-start | bytes 196616 | tf_op jit(solution)/shard_map/ppermute | solution.py:30
  8.2 15.7 %collective-permute-start.5 = (f32[512,256]{1,0:T(8,128)S(1)}, f32[512,256]{1,0:T(8,128)S(1)}, u32[]{:S(2)}, u32[]{:S(2)}) collective-permute-start(f32[512,256]{1,0:T(8,128)S(1)} %get-tuple-element.26.refs_0_), channel_id=1, source_target_pairs={{0,1},{1,0},{2,3},{3,2},{4,5},{5,4},{6,7},{7,6},{8,9},{9,8},{10,11... | collective-permute-start | bytes 1572872 | tf_op jit(solution)/shard_map/ppermute | solution.py:34
  8.3 15.6 %collective-permute-start.6 = (f32[512,256]{1,0:T(8,128)S(1)}, f32[512,256]{1,0:T(8,128)S(1)}, u32[]{:S(2)}, u32[]{:S(2)}) collective-permute-start(f32[512,256]{1,0:T(8,128)S(1)} %get-tuple-element.27.refs_1_), channel_id=1, source_target_pairs={{0,1},{1,0},{2,3},{3,2},{4,5},{5,4},{6,7},{7,6},{8,9},{9,8},{10,11... | collective-permute-start | bytes 1572872 | tf_op jit(solution)/shard_map/ppermute | solution.py:34
  8.8 15.1 %collective-permute-start.7 = (f32[512,256]{1,0:T(8,128)S(1)}, f32[512,256]{1,0:T(8,128)S(1)}, u32[]{:S(2)}, u32[]{:S(2)}) collective-permute-start(f32[512,256]{1,0:T(8,128)S(1)} %get-tuple-element.28.refs_2_), channel_id=1, source_target_pairs={{0,1},{1,0},{2,3},{3,2},{4,5},{5,4},{6,7},{7,6},{8,9},{9,8},{10,11... | collective-permute-start | bytes 1572872 | tf_op jit(solution)/shard_map/ppermute | solution.py:34
  8.9 15.1 %collective-permute-start.8 = (f32[512,256]{1,0:T(8,128)S(1)}, f32[512,256]{1,0:T(8,128)S(1)}, u32[]{:S(2)}, u32[]{:S(2)}) collective-permute-start(f32[512,256]{1,0:T(8,128)S(1)} %get-tuple-element.29.refs_3_), channel_id=1, source_target_pairs={{0,1},{1,0},{2,3},{3,2},{4,5},{5,4},{6,7},{7,6},{8,9},{9,8},{10,11... | collective-permute-start | bytes 1572872 | tf_op jit(solution)/shard_map/ppermute | solution.py:34
  9.8 4.3 %collective-permute-start.2 = (f32[16,1024]{1,0:T(8,128)S(1)}, f32[16,1024]{1,0:T(8,128)S(1)}, u32[]{:S(2)}, u32[]{:S(2)}) collective-permute-start(f32[16,1024]{1,0:T(8,128)S(1)} %fusion), channel_id=1, source_target_pairs={{0,4},{1,5},{2,6},{3,7},{4,0},{5,1},{6,2},{7,3},{8,12},{9,13},{10,... | collective-permute-start | bytes 196616 | tf_op jit(solution)/shard_map/ppermute | solution.py:30
  14.2 5.3 %collective-permute-start.3 = (f32[16,1024]{1,0:T(8,128)S(1)}, f32[16,1024]{1,0:T(8,128)S(1)}, u32[]{:S(2)}, u32[]{:S(2)}) collective-permute-start(f32[16,1024]{1,0:T(8,128)S(1)} %add.14), channel_id=1, source_target_pairs={{0,8},{1,9},{2,10},{3,11},{4,12},{5,13},{6,14},{7,15},{8,0},{9,1},... | collective-permute-start | bytes 196616 | tf_op jit(solution)/shard_map/ppermute | solution.py:30
  19.5 4.3 %collective-permute-start.4 = (f32[16,1024]{1,0:T(8,128)S(1)}, f32[16,1024]{1,0:T(8,128)S(1)}, u32[]{:S(2)}, u32[]{:S(2)}) collective-permute-start(f32[16,1024]{1,0:T(8,128)S(1)} %add.15.near_ref), channel_id=1, source_target_pairs={{0,2},{1,3},{2,0},{3,1},{4,6},{5,7},{6,4},{7,5},{8,10},{9,11},{10,... | collective-permute-start | bytes 196616 | tf_op jit(solution)/shard_map/ppermute | solution.py:30
  23.8 8.0 %collective-permute-start.9 = (f32[2,16,1024]{2,1,0:T(8,128)S(1)}, f32[2,16,1024]{2,1,0:T(8,128)S(1)}, u32[]{:S(2)}, u32[]{:S(2)}) collective-permute-start(f32[2,16,1024]{2,1,0:T(8,128)S(1)} %pad_maximum_fusion.mine_ref), channel_id=1, source_target_pairs={{0,1},{1,0},{2,3},{3,2},{4,5},{5,4},{6,7},{7,6},{8,9},{9,8},{10,11... | collective-permute-start | bytes 393224 | tf_op jit(solution)/shard_map/ppermute | solution.py:34
  25.1 14.4 %all-to-all-start = ((f32[8,16,256]{2,1,0:T(8,128)}), f32[8,16,256]{2,1,0:T(8,128)S(1)}, u32[]{:S(2)}, u32[]{:S(2)}) async-start(f32[8,16,256]{2,1,0:T(8,128)} %product.1), calls=%async_computation | async-start | bytes 262144 | tf_op jit(solution)/shard_map/all_to_all | solution.py:406
  39.5 1.2 %collective-permute-start.10 = (f32[16,256]{1,0:T(8,128)S(1)}, f32[16,256]{1,0:T(8,128)S(1)}, u32[]{:S(2)}, u32[]{:S(2)}) collective-permute-start(f32[16,256]{1,0:T(8,128)S(1)} %reduce_sum.9.mine_ref), channel_id=1, source_target_pairs={{0,1},{1,0},{2,3},{3,2},{4,5},{5,4},{6,7},{7,6},{8,9},{9,8},{10,11... | collective-permute-start | bytes 49160 | tf_op jit(solution)/shard_map/ppermute | solution.py:34

commit v16 on v15

--- a/solution.py
+++ b/solution.py
@@ -12,7 +12,7 @@
 VMEM_BYTES = 24 * 1024 * 1024
 CHUNK = 256
 GROUP = 4
-PARTS = 4
+PARTS = 8
 BF16, F32 = jnp.bfloat16, jnp.float32
 HBM = pl.BlockSpec(memory_space=pltpu.HBM)
 ANY = pl.BlockSpec(memory_space=pl.ANY)
@@ -79,7 +79,7 @@
         copy.start()
     rank = seed_ref.shape[0]
     tokens, width = x_ref.shape
-    half, piece = keep_ref.shape[1:]
+    half = keep_ref.shape[0]
     copies[0].wait()
     copies[1].wait()
     seed = jnp.concatenate(parts_of(seed_ref[...], 3), axis=0)
@@ -99,19 +99,8 @@
             part = pl.ds(i * CHUNK, CHUNK)
             term_ref[:, part] += added(dot(own, x_ref[rows, part], ((1,), (0,))), rank)
     low = lax.axis_index("pair") == 0
-    for i in range(2):
-        part = half_of(side() ^ i, piece)
-        top, bottom = term_ref[:half, part], term_ref[half:, part]
-        keep_ref[i] = jnp.where(low, top, bottom)
-        send_ref[i] = jnp.where(low, bottom, top)
-
-
-def side():
-    return lax.axis_index("sub") & 1
-
-
-def half_of(chosen, piece, start=0, size=None):
-    return pl.ds(pl.multiple_of(chosen * piece + start, CHUNK), size or piece)
+    keep_ref[...] = jnp.where(low, term_ref[:half, :], term_ref[half:, :])
+    send_ref[...] = jnp.where(low, term_ref[half:, :], term_ref[:half, :])
 
 
 def added(stack, rank):
@@ -130,8 +119,8 @@
         in_specs=[HBM] * 4,
         out_specs=[VMEM] * 5,
         out_shape=[
-            jax.ShapeDtypeStruct((2, rank // 2, width // 2), F32),
-            jax.ShapeDtypeStruct((2, rank // 2, width // 2), F32),
+            jax.ShapeDtypeStruct((rank // 2, width), F32),
+            jax.ShapeDtypeStruct((rank // 2, width), F32),
             jax.ShapeDtypeStruct((tokens, width), BF16),
             jax.ShapeDtypeStruct((tokens, out), BF16),
             jax.ShapeDtypeStruct((width, out), BF16),
@@ -169,17 +158,14 @@
     )(x, c, e, after)
 
 
-def product_kernel(near_ref, far_ref, *refs):
-    mine_refs, other_refs, copies_ref = refs[:PARTS], refs[PARTS:2 * PARTS], refs[2 * PARTS]
-    rank, piece = near_ref.shape
+def product_kernel(first_ref, *refs):
+    mine_refs, other_refs, product_ref = refs[:PARTS], refs[PARTS:2 * PARTS], refs[2 * PARTS]
+    rank, width = first_ref.shape
     size = mine_refs[0].shape[0]
-    straight = side() == 0
     product = None
-    for i in range(2 * piece // CHUNK):
+    for i in range(width // CHUNK):
         start = i * CHUNK
-        part = slice(start % piece, start % piece + CHUNK)
-        near, far = near_ref[:, part], far_ref[:, part]
-        rows = jnp.where(straight, near, far) if start < piece else jnp.where(straight, far, near)
+        rows = first_ref[:, start:start + CHUNK]
         f_high, f_low = parts_of(rows, 2)
         both = jnp.concatenate([f_high, f_low], axis=0)
         rows_here = slice(start % size, start % size + CHUNK)
@@ -187,21 +173,19 @@
         m_high, m_low = parts_of(merged, 2)
         term = added(dot(both, m_high, ((1,), (0,))), rank) + dot(f_high, m_low, ((1,), (0,)))
         product = term if product is None else product + term
-    for i in range(copies_ref.shape[0]):
-        copies_ref[i] = product
-
-
-def product_copies(count, near, far, mine, other):
-    rank, piece = near.shape
-    size, out = mine[0].shape
-    width = 2 * piece
+    product_ref[...] = product
+
+
+def product_of(first, mine, other):
+    rank, width = first.shape
+    out = mine[0].shape[1]
     return pl.pallas_call(
         product_kernel,
-        out_shape=jax.ShapeDtypeStruct((count, rank, out), F32),
+        out_shape=jax.ShapeDtypeStruct((rank, out), F32),
         compiler_params=params(),
         cost_estimate=cost(2 * rank * width * out, 8 * width * out),
         name="product",
-    )(near, far, *mine, *other)
+    )(first, *mine, *other)
 
 
 def both_halves(mine, other):
@@ -254,22 +238,20 @@
 
 
 def first_sweep_kernel(mine_ref, other_ref, rows_ref, step_ref):
-    half, piece = mine_ref.shape[1:]
+    rank, width = rows_ref.shape
+    blocks = None
+    for i in range(width // CHUNK):
+        part = slice(i * CHUNK, (i + 1) * CHUNK)
+        rows = both_halves(mine_ref[:, part], other_ref[:, part])
+        rows_ref[:, part] = rows
+        term = gram_blocks(rows)
+        blocks = term if blocks is None else blocks + term
+    step_ref[...] = inverse_factor(gram_of(blocks, rank))
+
+
+def first_sweep(mine, other):
+    half, width = mine.shape
     rank = 2 * half
-    blocks = None
-    for i in range(2):
-        for j in range(piece // CHUNK):
-            part = slice(j * CHUNK, (j + 1) * CHUNK)
-            rows = both_halves(mine_ref[i, :, part], other_ref[i, :, part])
-            rows_ref[:, half_of(side() ^ i, piece, j * CHUNK, CHUNK)] = rows
-            term = gram_blocks(rows)
-            blocks = term if blocks is None else blocks + term
-    step_ref[...] = inverse_factor(gram_of(blocks, rank))
-
-
-def first_sweep(mine, other):
-    _, half, piece = mine.shape
-    rank, width = 2 * half, 2 * piece
     return pl.pallas_call(
         first_sweep_kernel,
         out_shape=[
@@ -385,26 +367,26 @@
     inputs, cotangent, error_prev, seed_q = (
         pltpu.with_memory_space_constraint(value, pltpu.HBM) for value in arguments)
     rounds = bits_of("sub", sizes["sub"]) + bits_of("dp", sizes["dp"])
-    beside, others = rounds[0], rounds[1:]
     workers = 2 * sizes["sub"] * sizes["dp"]
 
     keep, send, x, c, e = term_halves(inputs, cotangent, error_prev, seed_q)
-    part = keep + across(send)
-    near = part[0] + swapped(part[1], sizes, beside)
-    merged = merge(x, c, e, part)
+    first = keep + across(send)
+    merged = merge(x, c, e, first)
     merged_other = [across(rows) for rows in merged]
-    for bits in others:
-        near = near + swapped(near, sizes, bits)
-    far = swapped(near, sizes, beside)
-    mine = jnp.stack([near, far])
-    other = across(mine)
-
-    copies = product_copies(workers // 2, near, far, merged, merged_other)
-    rows, step = first_sweep(mine, other)
+    for bits in rounds:
+        first = first + swapped(first, sizes, bits)
+    other = across(first)
+
+    product = product_of(first, merged, merged_other)
+    rows, step = first_sweep(first, other)
+    product = product + swapped(product, sizes, rounds[0])
+    product, rows, step = lax.optimization_barrier((product, rows, step))
     rows, last = second_sweep(rows, step)
+    product = product + swapped(product, sizes, rounds[1])
+    product, rows, step, last = lax.optimization_barrier((product, rows, step, last))
     basis, inverse = basis_of(rows, step, last)
-    products = lax.all_to_all(copies, ("dp", "sub"), 0, 0, tiled=True)
-    product = jnp.sum(products, axis=0)
+    for bits in rounds[2:]:
+        product = product + swapped(product, sizes, bits)
     product, basis, inverse = lax.optimization_barrier((product, basis, inverse))
     return error_of(merged, basis, inverse, product, across(product), workers)
 

time: 42.6 us -> 42.9 us (level)
  waiting for transfers between devices: 13.4 us -> 19.3 us
  starting transfers between devices: 18.3 us -> 13.7 us
  Pallas kernels: 9.72 us -> 8.93 us
    ppermute x4 -> x6, waiting for transfers between devices: 7.54 us -> 16.2 us  [swapped(): return lax.ppermute(value, AXES, pairs)]
    all_to_all x1 -> x0, starting transfers between devices: 6.73 us -> none  [local(): products = lax.all_to_all(copies, ('dp', 'sub'), 0, 0, tiled=True)]
    all_to_all x1 -> x0, waiting for transfers between devices: 3.73 us -> none  [local(): products = lax.all_to_all(copies, ('dp', 'sub'), 0, 0, tiled=True)]
    ppermute x4 -> x6, starting transfers between devices: 9.83 us -> 10.9 us  [swapped(): return lax.ppermute(value, AXES, pairs)]
    ppermute x7 -> x11, starting transfers between devices: 1.74 us -> 2.76 us  [across(): return lax.ppermute(value, 'pair', [(0, 1), (1, 0)])]
    ppermute x7 -> x11, waiting for transfers between devices: 2.17 us -> 3.1 us  [across(): return lax.ppermute(value, 'pair', [(0, 1), (1, 0)])]
    pallas_call x1, Pallas kernels: 1.18 us -> 0.51 us  [product_of(): pl.pallas_call(product_kernel, out_shape=jax.ShapeDtypeStruct((rank, out)...]
  transfers between devices with their start and end apart: 12 -> 17, of which waited for: 7 -> 9; matrix products, arithmetic and copies ran while one was open for 0% -> 0% of each run, Pallas kernels for 14% -> 8%
where the time goes in v16:
time: 42.9 us; the launch traced here: 42.7 us
  waiting for transfers between devices  19.3 us (45%)
  starting transfers between devices  13.7 us (32%)
  Pallas kernels  8.93 us (21%)
  between operations  0.71 us (2%)
    ppermute x6, waiting for transfers between devices, swapped(): return lax.ppermute(value, AXES, pairs)  16.2 us
    ppermute x6, starting transfers between devices, swapped(): return lax.ppermute(value, AXES, pairs)  10.9 us
    ppermute x11, waiting for transfers between devices, across(): return lax.ppermute(value, 'pair', [(0, 1), (1, 0)])  3.1 us
    ppermute x11, starting transfers between devices, across(): return lax.ppermute(value, 'pair', [(0, 1), (1, 0)])  2.76 us
    pallas_call x1, Pallas kernels, term_halves(): pl.pallas_call(term_kernel, in_specs=[HBM] * 4, out_specs=[VMEM] * 5, out...  2.32 us
    pallas_call x1, Pallas kernels, second_sweep(): pl.pallas_call(second_sweep_kernel, out_shape=[jax.ShapeDtypeStruct(rows....  1.91 us
    pallas_call x1, Pallas kernels, first_sweep(): pl.pallas_call(first_sweep_kernel, out_shape=[jax.ShapeDtypeStruct((rank,...  1.63 us
    pallas_call x1, Pallas kernels, error_of(): pl.pallas_call(functools.partial(error_kernel, workers), in_specs=[VMEM]...  1.46 us
  transfers between devices with their start and end apart: 17, of which 9 were waited for; matrix products, arithmetic and copies ran while one was open for 0% of the time, Pallas kernels for 8%

profile of v16, /device:TPU:0, one launch (start us, length us, event | category | flops | bytes accessed | tf_op | source)
XLA Modules:
  0.0 42.7 jit_solution(16160949013465879287)
XLA Ops:
  0.6 2.3 %term.1 = (f32[16,2048]{1,0:T(8,128)S(1)}, f32[16,2048]{1,0:T(8,128)S(1)}, bf16[512,2048]{1,0:T(8,128)(2,1)S(1)}, bf16[512,256]{1,0:T(8,128)(2,1)S(1)}, bf16[2048,256]{1,0:T(8,128)(2,1)S(1)}) custom-call(bf16[512,2048]{1,0:T(8,128)(2,1)} %x_hbm.1, bf16[512,256]{1,0:T(8,128)(2,1)} %c_hbm.1, bf16[1,2048,256]{2,1,0:T(8,128)(2,1)} %e_hbm.1, f32[32,256]{1,0:T(8,128)} %seed_hbm.1), custom_call_target="tpu_custom_call" | custom-call | flops 201326592 | bytes 3145728 | tf_op jit(solution)/shard_map/term/pallas_call | solution.py:117
  3.0 0.5 %collective-permute-start = (f32[16,2048]{1,0:T(8,128)S(1)}, f32[16,2048]{1,0:T(8,128)S(1)}, u32[]{:S(2)}, u32[]{:S(2)}) collective-permute-start(f32[16,2048]{1,0:T(8,128)S(1)} %get-tuple-element.33), channel_id=1, source_target_pairs={{0,1},{1,0},{2,3},{3,2},{4,5},{5,4},{6,7},{7,6},{8,9},{9,8},{10,11... | collective-permute-start | bytes 393224 | tf_op jit(solution)/shard_map/ppermute | solution.py:34
  3.5 1.0 %collective-permute-done = f32[16,2048]{1,0:T(8,128)S(1)} collective-permute-done((f32[16,2048]{1,0:T(8,128)S(1)}, f32[16,2048]{1,0:T(8,128)S(1)}, u32[]{:S(2)}, u32[]{:S(2)}) %collective-permute-start) | collective-permute-done | bytes 131104 | tf_op jit(solution)/shard_map/ppermute | solution.py:34
  4.5 2.9 %collective-permute-start.1 = (f32[16,2048]{1,0:T(8,128)S(1)}, f32[16,2048]{1,0:T(8,128)S(1)}, u32[]{:S(2)}, u32[]{:S(2)}) collective-permute-start(f32[16,2048]{1,0:T(8,128)S(1)} %add.21.after_ref), channel_id=1, source_target_pairs={{0,2},{1,3},{2,0},{3,1},{4,6},{5,7},{6,4},{7,5},{8,10},{9,11},{10,... | collective-permute-start | bytes 393224 | tf_op jit(solution)/shard_map/ppermute | solution.py:30
  7.4 0.8 %merge.1 = (f32[256,256]{1,0:T(8,128)S(1)}, f32[256,256]{1,0:T(8,128)S(1)}, f32[256,256]{1,0:T(8,128)S(1)}, f32[256,256]{1,0:T(8,128)S(1)}, f32[256,256]{1,0:T(8...) custom-call(bf16[512,2048]{1,0:T(8,128)(2,1)S(1)} %get-tuple-element.34.x_ref, ...), custom_call_target="tpu_custom_call" | custom-call | flops 100000000 | bytes 1000000 | tf_op jit(solution)/shard_map/merge/pallas_call | solution.py:150
  8.2 0.1 collective-permute-start.4
  8.3 0.5 %collective-permute-start.5 = (f32[256,256]{1,0:T(8,128)S(1)}, f32[256,256]{1,0:T(8,128)S(1)}, u32[]{:S(2)}, u32[]{:S(2)}) collective-permute-start(f32[256,256]{1,0:T(8,128)S(1)} %get-tuple-element.38.refs_1_), channel_id=1, source_target_pairs={{0,1},{1,0},{2,3},{3,2},{4,5},{5,4},{6,7},{7,6},{8,9},{9,8},{10,11... | collective-permute-start | bytes 786440 | tf_op jit(solution)/shard_map/ppermute | solution.py:34
  8.8 0.1 collective-permute-start.6
  8.8 2.4 %collective-permute-done.1 = f32[16,2048]{1,0:T(8,128)S(1)} collective-permute-done((f32[16,2048]{1,0:T(8,128)S(1)}, f32[16,2048]{1,0:T(8,128)S(1)}, u32[]{:S(2)}, u32[]{:S(2)}) %collective-permute-start.1) | collective-permute-done | bytes 131104 | tf_op jit(solution)/shard_map/ppermute | solution.py:30
  11.2 1.9 %collective-permute-start.2 = (f32[16,2048]{1,0:T(8,128)S(1)}, f32[16,2048]{1,0:T(8,128)S(1)}, u32[]{:S(2)}, u32[]{:S(2)}) collective-permute-start(f32[16,2048]{1,0:T(8,128)S(1)} %add.22), channel_id=1, source_target_pairs={{0,4},{1,5},{2,6},{3,7},{4,0},{5,1},{6,2},{7,3},{8,12},{9,13},{10,... | collective-permute-start | bytes 393224 | tf_op jit(solution)/shard_map/ppermute | solution.py:30
  13.1 3.2 %collective-permute-done.2 = f32[16,2048]{1,0:T(8,128)S(1)} collective-permute-done((f32[16,2048]{1,0:T(8,128)S(1)}, f32[16,2048]{1,0:T(8,128)S(1)}, u32[]{:S(2)}, u32[]{:S(2)}) %collective-permute-start.2) | collective-permute-done | bytes 131104 | tf_op jit(solution)/shard_map/ppermute | solution.py:30
  16.4 2.8 %collective-permute-start.3 = (f32[16,2048]{1,0:T(8,128)S(1)}, f32[16,2048]{1,0:T(8,128)S(1)}, u32[]{:S(2)}, u32[]{:S(2)}) collective-permute-start(f32[16,2048]{1,0:T(8,128)S(1)} %add.23), channel_id=1, source_target_pairs={{0,8},{1,9},{2,10},{3,11},{4,12},{5,13},{6,14},{7,15},{8,0},{9,1},... | collective-permute-start | bytes 393224 | tf_op jit(solution)/shard_map/ppermute | solution.py:30
  19.2 0.0 collective-permute-start.7
  19.2 0.0 collective-permute-done.4.refs_8_
  19.2 0.5 %collective-permute-start.8 = (f32[256,256]{1,0:T(8,128)S(1)}, f32[256,256]{1,0:T(8,128)S(1)}, u32[]{:S(2)}, u32[]{:S(2)}) collective-permute-start(f32[256,256]{1,0:T(8,128)S(1)} %get-tuple-element.41.refs_4_), channel_id=1, source_target_pairs={{0,1},{1,0},{2,3},{3,2},{4,5},{5,4},{6,7},{7,6},{8,9},{9,8},{10,11... | collective-permute-start | bytes 786440 | tf_op jit(solution)/shard_map/ppermute | solution.py:34
  19.7 0.0 collective-permute-done.5.refs_9_
  19.7 0.1 collective-permute-start.9
  19.8 0.0 collective-permute-done.6.refs_10_
  19.8 0.4 %collective-permute-start.10 = (f32[256,256]{1,0:T(8,128)S(1)}, f32[256,256]{1,0:T(8,128)S(1)}, u32[]{:S(2)}, u32[]{:S(2)}) collective-permute-start(f32[256,256]{1,0:T(8,128)S(1)} %get-tuple-element.43.refs_6_), channel_id=1, source_target_pairs={{0,1},{1,0},{2,3},{3,2},{4,5},{5,4},{6,7},{7,6},{8,9},{9,8},{10,11... | collective-permute-start | bytes 786440 | tf_op jit(solution)/shard_map/ppermute | solution.py:34
  20.2 4.0 %collective-permute-done.3 = f32[16,2048]{1,0:T(8,128)S(1)} collective-permute-done((f32[16,2048]{1,0:T(8,128)S(1)}, f32[16,2048]{1,0:T(8,128)S(1)}, u32[]{:S(2)}, u32[]{:S(2)}) %collective-permute-start.3) | collective-permute-done | bytes 131104 | tf_op jit(solution)/shard_map/ppermute | solution.py:30
  24.3 0.0 collective-permute-start.11
  24.3 0.0 collective-permute-done.7.refs_11_
  24.3 0.6 %collective-permute-start.13 = (f32[16,2048]{1,0:T(8,128)S(1)}, f32[16,2048]{1,0:T(8,128)S(1)}, u32[]{:S(2)}, u32[]{:S(2)}) collective-permute-start(f32[16,2048]{1,0:T(8,128)S(1)} %add.24.first_ref.mine_ref), channel_id=1, source_target_pairs={{0,1},{1,0},{2,3},{3,2},{4,5},{5,4},{6,7},{7,6},{8,9},{9,8},{10,11... | collective-permute-start | bytes 393224 | tf_op jit(solution)/shard_map/ppermute | solution.py:34
  24.9 0.0 collective-permute-done.8.refs_12_
  24.9 0.0 collective-permute-done.9.refs_13_
  24.9 0.0 collective-permute-done.10.refs_14_
  24.9 0.9 %collective-permute-done.11.refs_15_ = f32[256,256]{1,0:T(8,128)S(1)} collective-permute-done((f32[256,256]{1,0:T(8,128)S(1)}, f32[256,256]{1,0:T(8,128)S(1)}, u32[]{:S(2)}, u32[]{:S(2)}) %collective-permute-start.11) | collective-permute-done | bytes 262176 | tf_op jit(solution)/shard_map/ppermute | solution.py:34
  25.8 0.5 %product.1 = f32[16,256]{1,0:T(8,128)S(1)} custom-call(f32[16,2048]{1,0:T(8,128)S(1)} %add.24.first_ref.mine_ref, f32[256,256]{1,0:T(8,128)S(1)} %get-tuple-element.37.refs_0_, f32[256,256]{1,0:T(8,128)S(1)} %get-tuple-element.38.refs_1_, f32[256,256]{1,0:T(8,128)S(1)} %get-tuple-element.39.refs_2_, f32[256,256]{1,0:T(8,128)S(1)} %get-tuple-element.40.refs_3_, ...), custom_call_target="tpu_custom_call" | custom-call | flops 16777216 | bytes 4194304 | tf_op jit(solution)/shard_map/product/pallas_call | solution.py:182
  26.3 1.1 %collective-permute-start.12 = (f32[16,256]{1,0:T(8,128)S(1)}, f32[16,256]{1,0:T(8,128)S(1)}, u32[]{:S(2)}, u32[]{:S(2)}) collective-permute-start(f32[16,256]{1,0:T(8,128)S(1)} %product.1), channel_id=1, source_target_pairs={{0,2},{1,3},{2,0},{3,1},{4,6},{5,7},{6,4},{7,5},{8,10},{9,11},{10,... | collective-permute-start | bytes 49160 | tf_op jit(solution)/shard_map/ppermute | solution.py:30
  27.4 2.6 %collective-permute-done.12 = f32[16,256]{1,0:T(8,128)S(1)} collective-permute-done((f32[16,256]{1,0:T(8,128)S(1)}, f32[16,256]{1,0:T(8,128)S(1)}, u32[]{:S(2)}, u32[]{:S(2)}) %collective-permute-start.12) | collective-permute-done | bytes 16416 | tf_op jit(solution)/shard_map/ppermute | solution.py:30
  30.1 0.0 collective-permute-done.13.other_ref
  30.1 1.6 %first_sweep.1 = (f32[32,2048]{1,0:T(8,128)S(1)}, f32[32,32]{1,0:T(8,128)S(1)}) custom-call(f32[16,2048]{1,0:T(8,128)S(1)} %add.24.first_ref.mine_ref, f32[16,2048]{1,0:T(8,128)S(1)} %collective-permute-done.13.other_ref), custom_call_target="tpu_custom_call" | custom-call | flops 1000000000 | bytes 7000000 | tf_op jit(solution)/shard_map/first_sweep/pallas_call | solution.py:255
  31.7 0.3 collective-permute-start.14
  32.0 1.9 %second_sweep.1 = (f32[32,2048]{1,0:T(8,128)S(1)}, f32[32,32]{1,0:T(8,128)S(1)}) custom-call(f32[32,2048]{1,0:T(8,128)S(1)} %get-tuple-element.48.first_ref, f32[32,32]{1,0:T(8,128)S(1)} %get-tuple-element.54.step_ref), custom_call_target="tpu_custom_call" | custom-call | flops 1000000000 | bytes 7000000 | tf_op jit(solution)/shard_map/second_sweep/pallas_call | solution.py:281
  33.9 1.5 %collective-permute-done.14 = f32[16,256]{1,0:T(8,128)S(1)} collective-permute-done((f32[16,256]{1,0:T(8,128)S(1)}, f32[16,256]{1,0:T(8,128)S(1)}, u32[]{:S(2)}, u32[]{:S(2)}) %collective-permute-start.14) | collective-permute-done | bytes 16416 | tf_op jit(solution)/shard_map/ppermute | solution.py:30
  35.5 1.9 %collective-permute-start.15 = (f32[16,256]{1,0:T(8,128)S(1)}, f32[16,256]{1,0:T(8,128)S(1)}, u32[]{:S(2)}, u32[]{:S(2)}) collective-permute-start(f32[16,256]{1,0:T(8,128)S(1)} %add.26), channel_id=1, source_target_pairs={{0,8},{1,9},{2,10},{3,11},{4,12},{5,13},{6,14},{7,15},{8,0},{9,1},... | collective-permute-start | bytes 49160 | tf_op jit(solution)/shard_map/ppermute | solution.py:30
  37.4 0.3 basis.1
  37.7 2.4 %collective-permute-done.15 = f32[16,256]{1,0:T(8,128)S(1)} collective-permute-done((f32[16,256]{1,0:T(8,128)S(1)}, f32[16,256]{1,0:T(8,128)S(1)}, u32[]{:S(2)}, u32[]{:S(2)}) %collective-permute-start.15) | collective-permute-done | bytes 16416 | tf_op jit(solution)/shard_map/ppermute | solution.py:30
  40.1 0.0 collective-permute-start.16
  40.1 1.2 %collective-permute-done.16.other_ref = f32[16,256]{1,0:T(8,128)S(1)} collective-permute-done((f32[16,256]{1,0:T(8,128)S(1)}, f32[16,256]{1,0:T(8,128)S(1)}, u32[]{:S(2)}, u32[]{:S(2)}) %collective-permute-start.16) | collective-permute-done | bytes 16416 | tf_op jit(solution)/shard_map/ppermute | solution.py:34
  41.3 1.5 %error_next.1 = (bf16[1,2048,256]{2,1,0:T(8,128)(2,1)}, f32[32,2048]{1,0:T(8,128)}, f32[32,256]{1,0:T(8,128)}) custom-call(f32[32,2048]{1,0:T(8,128)S(1)} %get-tuple-element.58.basis_ref, f32[32,32]{1,0:T(8,128)S(1)} %get-tuple-element.59.inverse_ref, f32[16,256]{1,0:T(8,128)S(1)} %add.27.mine_ref, f32[16,256]{1,0:T(8,128)S(1)} %collective-permute-done.16.other_ref, ...), custom_call_target="tpu_custom_call" | custom-call | flops 33554432 | bytes 3145728 | tf_op jit(solution)/shard_map/error_next/pallas_call | solution.py:345
  (7 shorter events, 0.1 us)
Async XLA Ops:
  3.0 1.5 %collective-permute-start = (f32[16,2048]{1,0:T(8,128)S(1)}, f32[16,2048]{1,0:T(8,128)S(1)}, u32[]{:S(2)}, u32[]{:S(2)}) collective-permute-start(f32[16,2048]{1,0:T(8,128)S(1)} %get-tuple-element.33), channel_id=1, source_target_pairs={{0,1},{1,0},{2,3},{3,2},{4,5},{5,4},{6,7},{7,6},{8,9},{9,8},{10,11... | collective-permute-start | bytes 393224 | tf_op jit(solution)/shard_map/ppermute | solution.py:34
  4.5 6.7 %collective-permute-start.1 = (f32[16,2048]{1,0:T(8,128)S(1)}, f32[16,2048]{1,0:T(8,128)S(1)}, u32[]{:S(2)}, u32[]{:S(2)}) collective-permute-start(f32[16,2048]{1,0:T(8,128)S(1)} %add.21.after_ref), channel_id=1, source_target_pairs={{0,2},{1,3},{2,0},{3,1},{4,6},{5,7},{6,4},{7,5},{8,10},{9,11},{10,... | collective-permute-start | bytes 393224 | tf_op jit(solution)/shard_map/ppermute | solution.py:30
  8.2 11.0 %collective-permute-start.4 = (f32[256,256]{1,0:T(8,128)S(1)}, f32[256,256]{1,0:T(8,128)S(1)}, u32[]{:S(2)}, u32[]{:S(2)}) collective-permute-start(f32[256,256]{1,0:T(8,128)S(1)} %get-tuple-element.37.refs_0_), channel_id=1, source_target_pairs={{0,1},{1,0},{2,3},{3,2},{4,5},{5,4},{6,7},{7,6},{8,9},{9,8},{10,11... | collective-permute-start | bytes 786440 | tf_op jit(solution)/shard_map/ppermute | solution.py:34
  8.3 11.4 %collective-permute-start.5 = (f32[256,256]{1,0:T(8,128)S(1)}, f32[256,256]{1,0:T(8,128)S(1)}, u32[]{:S(2)}, u32[]{:S(2)}) collective-permute-start(f32[256,256]{1,0:T(8,128)S(1)} %get-tuple-element.38.refs_1_), channel_id=1, source_target_pairs={{0,1},{1,0},{2,3},{3,2},{4,5},{5,4},{6,7},{7,6},{8,9},{9,8},{10,11... | collective-permute-start | bytes 786440 | tf_op jit(solution)/shard_map/ppermute | solution.py:34
  8.8 11.0 %collective-permute-start.6 = (f32[256,256]{1,0:T(8,128)S(1)}, f32[256,256]{1,0:T(8,128)S(1)}, u32[]{:S(2)}, u32[]{:S(2)}) collective-permute-start(f32[256,256]{1,0:T(8,128)S(1)} %get-tuple-element.39.refs_2_), channel_id=1, source_target_pairs={{0,1},{1,0},{2,3},{3,2},{4,5},{5,4},{6,7},{7,6},{8,9},{9,8},{10,11... | collective-permute-start | bytes 786440 | tf_op jit(solution)/shard_map/ppermute | solution.py:34
  11.2 5.1 %collective-permute-start.2 = (f32[16,2048]{1,0:T(8,128)S(1)}, f32[16,2048]{1,0:T(8,128)S(1)}, u32[]{:S(2)}, u32[]{:S(2)}) collective-permute-start(f32[16,2048]{1,0:T(8,128)S(1)} %add.22), channel_id=1, source_target_pairs={{0,4},{1,5},{2,6},{3,7},{4,0},{5,1},{6,2},{7,3},{8,12},{9,13},{10,... | collective-permute-start | bytes 393224 | tf_op jit(solution)/shard_map/ppermute | solution.py:30
  16.4 7.9 %collective-permute-start.3 = (f32[16,2048]{1,0:T(8,128)S(1)}, f32[16,2048]{1,0:T(8,128)S(1)}, u32[]{:S(2)}, u32[]{:S(2)}) collective-permute-start(f32[16,2048]{1,0:T(8,128)S(1)} %add.23), channel_id=1, source_target_pairs={{0,8},{1,9},{2,10},{3,11},{4,12},{5,13},{6,14},{7,15},{8,0},{9,1},... | collective-permute-start | bytes 393224 | tf_op jit(solution)/shard_map/ppermute | solution.py:30
  19.2 5.1 %collective-permute-start.7 = (f32[256,256]{1,0:T(8,128)S(1)}, f32[256,256]{1,0:T(8,128)S(1)}, u32[]{:S(2)}, u32[]{:S(2)}) collective-permute-start(f32[256,256]{1,0:T(8,128)S(1)} %get-tuple-element.40.refs_3_), channel_id=1, source_target_pairs={{0,1},{1,0},{2,3},{3,2},{4,5},{5,4},{6,7},{7,6},{8,9},{9,8},{10,11... | collective-permute-start | bytes 786440 | tf_op jit(solution)/shard_map/ppermute | solution.py:34
  19.2 5.7 %collective-permute-start.8 = (f32[256,256]{1,0:T(8,128)S(1)}, f32[256,256]{1,0:T(8,128)S(1)}, u32[]{:S(2)}, u32[]{:S(2)}) collective-permute-start(f32[256,256]{1,0:T(8,128)S(1)} %get-tuple-element.41.refs_4_), channel_id=1, source_target_pairs={{0,1},{1,0},{2,3},{3,2},{4,5},{5,4},{6,7},{7,6},{8,9},{9,8},{10,11... | collective-permute-start | bytes 786440 | tf_op jit(solution)/shard_map/ppermute | solution.py:34
  19.7 5.2 %collective-permute-start.9 = (f32[256,256]{1,0:T(8,128)S(1)}, f32[256,256]{1,0:T(8,128)S(1)}, u32[]{:S(2)}, u32[]{:S(2)}) collective-permute-start(f32[256,256]{1,0:T(8,128)S(1)} %get-tuple-element.42.refs_5_), channel_id=1, source_target_pairs={{0,1},{1,0},{2,3},{3,2},{4,5},{5,4},{6,7},{7,6},{8,9},{9,8},{10,11... | collective-permute-start | bytes 786440 | tf_op jit(solution)/shard_map/ppermute | solution.py:34
  19.8 5.1 %collective-permute-start.10 = (f32[256,256]{1,0:T(8,128)S(1)}, f32[256,256]{1,0:T(8,128)S(1)}, u32[]{:S(2)}, u32[]{:S(2)}) collective-permute-start(f32[256,256]{1,0:T(8,128)S(1)} %get-tuple-element.43.refs_6_), channel_id=1, source_target_pairs={{0,1},{1,0},{2,3},{3,2},{4,5},{5,4},{6,7},{7,6},{8,9},{9,8},{10,11... | collective-permute-start | bytes 786440 | tf_op jit(solution)/shard_map/ppermute | solution.py:34
  24.3 1.5 %collective-permute-start.11 = (f32[256,256]{1,0:T(8,128)S(1)}, f32[256,256]{1,0:T(8,128)S(1)}, u32[]{:S(2)}, u32[]{:S(2)}) collective-permute-start(f32[256,256]{1,0:T(8,128)S(1)} %get-tuple-element.44.refs_7_), channel_id=1, source_target_pairs={{0,1},{1,0},{2,3},{3,2},{4,5},{5,4},{6,7},{7,6},{8,9},{9,8},{10,11... | collective-permute-start | bytes 786440 | tf_op jit(solution)/shard_map/ppermute | solution.py:34
  24.3 5.8 %collective-permute-start.13 = (f32[16,2048]{1,0:T(8,128)S(1)}, f32[16,2048]{1,0:T(8,128)S(1)}, u32[]{:S(2)}, u32[]{:S(2)}) collective-permute-start(f32[16,2048]{1,0:T(8,128)S(1)} %add.24.first_ref.mine_ref), channel_id=1, source_target_pairs={{0,1},{1,0},{2,3},{3,2},{4,5},{5,4},{6,7},{7,6},{8,9},{9,8},{10,11... | collective-permute-start | bytes 393224 | tf_op jit(solution)/shard_map/ppermute | solution.py:34
  26.3 3.7 %collective-permute-start.12 = (f32[16,256]{1,0:T(8,128)S(1)}, f32[16,256]{1,0:T(8,128)S(1)}, u32[]{:S(2)}, u32[]{:S(2)}) collective-permute-start(f32[16,256]{1,0:T(8,128)S(1)} %product.1), channel_id=1, source_target_pairs={{0,2},{1,3},{2,0},{3,1},{4,6},{5,7},{6,4},{7,5},{8,10},{9,11},{10,... | collective-permute-start | bytes 49160 | tf_op jit(solution)/shard_map/ppermute | solution.py:30
  31.7 3.7 %collective-permute-start.14 = (f32[16,256]{1,0:T(8,128)S(1)}, f32[16,256]{1,0:T(8,128)S(1)}, u32[]{:S(2)}, u32[]{:S(2)}) collective-permute-start(f32[16,256]{1,0:T(8,128)S(1)} %add.25), channel_id=1, source_target_pairs={{0,4},{1,5},{2,6},{3,7},{4,0},{5,1},{6,2},{7,3},{8,12},{9,13},{10,... | collective-permute-start | bytes 49160 | tf_op jit(solution)/shard_map/ppermute | solution.py:30
  35.5 4.6 %collective-permute-start.15 = (f32[16,256]{1,0:T(8,128)S(1)}, f32[16,256]{1,0:T(8,128)S(1)}, u32[]{:S(2)}, u32[]{:S(2)}) collective-permute-start(f32[16,256]{1,0:T(8,128)S(1)} %add.26), channel_id=1, source_target_pairs={{0,8},{1,9},{2,10},{3,11},{4,12},{5,13},{6,14},{7,15},{8,0},{9,1},... | collective-permute-start | bytes 49160 | tf_op jit(solution)/shard_map/ppermute | solution.py:30
  40.1 1.2 %collective-permute-start.16 = (f32[16,256]{1,0:T(8,128)S(1)}, f32[16,256]{1,0:T(8,128)S(1)}, u32[]{:S(2)}, u32[]{:S(2)}) collective-permute-start(f32[16,256]{1,0:T(8,128)S(1)} %add.27.mine_ref), channel_id=1, source_target_pairs={{0,1},{1,0},{2,3},{3,2},{4,5},{5,4},{6,7},{7,6},{8,9},{9,8},{10,11... | collective-permute-start | bytes 49160 | tf_op jit(solution)/shard_map/ppermute | solution.py:34

commit v17 on v16

--- a/solution.py
+++ b/solution.py
@@ -378,6 +378,7 @@
     other = across(first)
 
     product = product_of(first, merged, merged_other)
+    product, other = lax.optimization_barrier((product, other))
     rows, step = first_sweep(first, other)
     product = product + swapped(product, sizes, rounds[0])
     product, rows, step = lax.optimization_barrier((product, rows, step))

time: 42.9 us -> 41.2 us (0.960)
  waiting for transfers between devices: 19.3 us -> 17.7 us
    ppermute x6, waiting for transfers between devices: 16.2 us -> 14.6 us  [swapped(): return lax.ppermute(value, AXES, pairs)]
  transfers between devices with their start and end apart: 17 -> 17, of which waited for: 9 -> 9; matrix products, arithmetic and copies ran while one was open for 0% -> 0% of each run, Pallas kernels for 8% -> 13%
where the time goes in v17:
time: 41.2 us; the launch traced here: 41.1 us
  waiting for transfers between devices  17.7 us (43%)
  starting transfers between devices  13.7 us (33%)
  Pallas kernels  8.93 us (22%)
  between operations  0.7 us (2%)
    ppermute x6, waiting for transfers between devices, swapped(): return lax.ppermute(value, AXES, pairs)  14.6 us
    ppermute x6, starting transfers between devices, swapped(): return lax.ppermute(value, AXES, pairs)  10.9 us
    ppermute x11, waiting for transfers between devices, across(): return lax.ppermute(value, 'pair', [(0, 1), (1, 0)])  3.1 us
    ppermute x11, starting transfers between devices, across(): return lax.ppermute(value, 'pair', [(0, 1), (1, 0)])  2.76 us
    pallas_call x1, Pallas kernels, term_halves(): pl.pallas_call(term_kernel, in_specs=[HBM] * 4, out_specs=[VMEM] * 5, out...  2.32 us
    pallas_call x1, Pallas kernels, second_sweep(): pl.pallas_call(second_sweep_kernel, out_shape=[jax.ShapeDtypeStruct(rows....  1.91 us
    pallas_call x1, Pallas kernels, first_sweep(): pl.pallas_call(first_sweep_kernel, out_shape=[jax.ShapeDtypeStruct((rank,...  1.63 us
    pallas_call x1, Pallas kernels, error_of(): pl.pallas_call(functools.partial(error_kernel, workers), in_specs=[VMEM]...  1.46 us
  transfers between devices with their start and end apart: 17, of which 9 were waited for; matrix products, arithmetic and copies ran while one was open for 0% of the time, Pallas kernels for 13%

profile of v17, /device:TPU:0, one launch (start us, length us, event | category | flops | bytes accessed | tf_op | source)
XLA Modules:
  0.0 41.1 jit_solution(2245153228493103366)
XLA Ops:
  0.6 2.3 %term.1 = (f32[16,2048]{1,0:T(8,128)S(1)}, f32[16,2048]{1,0:T(8,128)S(1)}, bf16[512,2048]{1,0:T(8,128)(2,1)S(1)}, bf16[512,256]{1,0:T(8,128)(2,1)S(1)}, bf16[2048,256]{1,0:T(8,128)(2,1)S(1)}) custom-call(bf16[512,2048]{1,0:T(8,128)(2,1)} %x_hbm.1, bf16[512,256]{1,0:T(8,128)(2,1)} %c_hbm.1, bf16[1,2048,256]{2,1,0:T(8,128)(2,1)} %e_hbm.1, f32[32,256]{1,0:T(8,128)} %seed_hbm.1), custom_call_target="tpu_custom_call" | custom-call | flops 201326592 | bytes 3145728 | tf_op jit(solution)/shard_map/term/pallas_call | solution.py:117
  3.0 0.5 %collective-permute-start = (f32[16,2048]{1,0:T(8,128)S(1)}, f32[16,2048]{1,0:T(8,128)S(1)}, u32[]{:S(2)}, u32[]{:S(2)}) collective-permute-start(f32[16,2048]{1,0:T(8,128)S(1)} %get-tuple-element.35), channel_id=1, source_target_pairs={{0,1},{1,0},{2,3},{3,2},{4,5},{5,4},{6,7},{7,6},{8,9},{9,8},{10,11... | collective-permute-start | bytes 393224 | tf_op jit(solution)/shard_map/ppermute | solution.py:34
  3.5 1.0 %collective-permute-done = f32[16,2048]{1,0:T(8,128)S(1)} collective-permute-done((f32[16,2048]{1,0:T(8,128)S(1)}, f32[16,2048]{1,0:T(8,128)S(1)}, u32[]{:S(2)}, u32[]{:S(2)}) %collective-permute-start) | collective-permute-done | bytes 131104 | tf_op jit(solution)/shard_map/ppermute | solution.py:34
  4.5 2.9 %collective-permute-start.1 = (f32[16,2048]{1,0:T(8,128)S(1)}, f32[16,2048]{1,0:T(8,128)S(1)}, u32[]{:S(2)}, u32[]{:S(2)}) collective-permute-start(f32[16,2048]{1,0:T(8,128)S(1)} %add.21.after_ref), channel_id=1, source_target_pairs={{0,2},{1,3},{2,0},{3,1},{4,6},{5,7},{6,4},{7,5},{8,10},{9,11},{10,... | collective-permute-start | bytes 393224 | tf_op jit(solution)/shard_map/ppermute | solution.py:30
  7.4 0.8 %merge.1 = (f32[256,256]{1,0:T(8,128)S(1)}, f32[256,256]{1,0:T(8,128)S(1)}, f32[256,256]{1,0:T(8,128)S(1)}, f32[256,256]{1,0:T(8,128)S(1)}, f32[256,256]{1,0:T(8...) custom-call(bf16[512,2048]{1,0:T(8,128)(2,1)S(1)} %get-tuple-element.36.x_ref, ...), custom_call_target="tpu_custom_call" | custom-call | flops 100000000 | bytes 1000000 | tf_op jit(solution)/shard_map/merge/pallas_call | solution.py:150
  8.2 0.1 collective-permute-start.4
  8.3 0.5 %collective-permute-start.5 = (f32[256,256]{1,0:T(8,128)S(1)}, f32[256,256]{1,0:T(8,128)S(1)}, u32[]{:S(2)}, u32[]{:S(2)}) collective-permute-start(f32[256,256]{1,0:T(8,128)S(1)} %get-tuple-element.40.refs_1_), channel_id=1, source_target_pairs={{0,1},{1,0},{2,3},{3,2},{4,5},{5,4},{6,7},{7,6},{8,9},{9,8},{10,11... | collective-permute-start | bytes 786440 | tf_op jit(solution)/shard_map/ppermute | solution.py:34
  8.8 0.1 collective-permute-start.6
  8.8 2.4 %collective-permute-done.1 = f32[16,2048]{1,0:T(8,128)S(1)} collective-permute-done((f32[16,2048]{1,0:T(8,128)S(1)}, f32[16,2048]{1,0:T(8,128)S(1)}, u32[]{:S(2)}, u32[]{:S(2)}) %collective-permute-start.1) | collective-permute-done | bytes 131104 | tf_op jit(solution)/shard_map/ppermute | solution.py:30
  11.2 1.9 %collective-permute-start.2 = (f32[16,2048]{1,0:T(8,128)S(1)}, f32[16,2048]{1,0:T(8,128)S(1)}, u32[]{:S(2)}, u32[]{:S(2)}) collective-permute-start(f32[16,2048]{1,0:T(8,128)S(1)} %add.22), channel_id=1, source_target_pairs={{0,4},{1,5},{2,6},{3,7},{4,0},{5,1},{6,2},{7,3},{8,12},{9,13},{10,... | collective-permute-start | bytes 393224 | tf_op jit(solution)/shard_map/ppermute | solution.py:30
  13.1 3.2 %collective-permute-done.2 = f32[16,2048]{1,0:T(8,128)S(1)} collective-permute-done((f32[16,2048]{1,0:T(8,128)S(1)}, f32[16,2048]{1,0:T(8,128)S(1)}, u32[]{:S(2)}, u32[]{:S(2)}) %collective-permute-start.2) | collective-permute-done | bytes 131104 | tf_op jit(solution)/shard_map/ppermute | solution.py:30
  16.4 2.8 %collective-permute-start.3 = (f32[16,2048]{1,0:T(8,128)S(1)}, f32[16,2048]{1,0:T(8,128)S(1)}, u32[]{:S(2)}, u32[]{:S(2)}) collective-permute-start(f32[16,2048]{1,0:T(8,128)S(1)} %add.23), channel_id=1, source_target_pairs={{0,8},{1,9},{2,10},{3,11},{4,12},{5,13},{6,14},{7,15},{8,0},{9,1},... | collective-permute-start | bytes 393224 | tf_op jit(solution)/shard_map/ppermute | solution.py:30
  19.2 0.0 collective-permute-start.7
  19.2 0.0 collective-permute-done.4.refs_8_
  19.2 0.5 %collective-permute-start.8 = (f32[256,256]{1,0:T(8,128)S(1)}, f32[256,256]{1,0:T(8,128)S(1)}, u32[]{:S(2)}, u32[]{:S(2)}) collective-permute-start(f32[256,256]{1,0:T(8,128)S(1)} %get-tuple-element.43.refs_4_), channel_id=1, source_target_pairs={{0,1},{1,0},{2,3},{3,2},{4,5},{5,4},{6,7},{7,6},{8,9},{9,8},{10,11... | collective-permute-start | bytes 786440 | tf_op jit(solution)/shard_map/ppermute | solution.py:34
  19.7 0.0 collective-permute-done.5.refs_9_
  19.7 0.1 collective-permute-start.9
  19.8 0.0 collective-permute-done.6.refs_10_
  19.8 0.4 %collective-permute-start.10 = (f32[256,256]{1,0:T(8,128)S(1)}, f32[256,256]{1,0:T(8,128)S(1)}, u32[]{:S(2)}, u32[]{:S(2)}) collective-permute-start(f32[256,256]{1,0:T(8,128)S(1)} %get-tuple-element.45.refs_6_), channel_id=1, source_target_pairs={{0,1},{1,0},{2,3},{3,2},{4,5},{5,4},{6,7},{7,6},{8,9},{9,8},{10,11... | collective-permute-start | bytes 786440 | tf_op jit(solution)/shard_map/ppermute | solution.py:34
  20.2 4.0 %collective-permute-done.3 = f32[16,2048]{1,0:T(8,128)S(1)} collective-permute-done((f32[16,2048]{1,0:T(8,128)S(1)}, f32[16,2048]{1,0:T(8,128)S(1)}, u32[]{:S(2)}, u32[]{:S(2)}) %collective-permute-start.3) | collective-permute-done | bytes 131104 | tf_op jit(solution)/shard_map/ppermute | solution.py:30
  24.3 0.0 collective-permute-start.11
  24.3 0.0 collective-permute-done.7.refs_11_
  24.3 0.6 %collective-permute-start.12 = (f32[16,2048]{1,0:T(8,128)S(1)}, f32[16,2048]{1,0:T(8,128)S(1)}, u32[]{:S(2)}, u32[]{:S(2)}) collective-permute-start(f32[16,2048]{1,0:T(8,128)S(1)} %add.24.first_ref.mine_ref), channel_id=1, source_target_pairs={{0,1},{1,0},{2,3},{3,2},{4,5},{5,4},{6,7},{7,6},{8,9},{9,8},{10,11... | collective-permute-start | bytes 393224 | tf_op jit(solution)/shard_map/ppermute | solution.py:34
  24.9 0.0 collective-permute-done.8.refs_12_
  24.9 0.0 collective-permute-done.9.refs_13_
  24.9 0.0 collective-permute-done.10.refs_14_
  24.9 0.9 %collective-permute-done.11.refs_15_ = f32[256,256]{1,0:T(8,128)S(1)} collective-permute-done((f32[256,256]{1,0:T(8,128)S(1)}, f32[256,256]{1,0:T(8,128)S(1)}, u32[]{:S(2)}, u32[]{:S(2)}) %collective-permute-start.11) | collective-permute-done | bytes 262176 | tf_op jit(solution)/shard_map/ppermute | solution.py:34
  25.8 0.5 %product.1 = f32[16,256]{1,0:T(8,128)S(1)} custom-call(f32[16,2048]{1,0:T(8,128)S(1)} %add.24.first_ref.mine_ref, f32[256,256]{1,0:T(8,128)S(1)} %get-tuple-element.39.refs_0_, f32[256,256]{1,0:T(8,128)S(1)} %get-tuple-element.40.refs_1_, f32[256,256]{1,0:T(8,128)S(1)} %get-tuple-element.41.refs_2_, f32[256,256]{1,0:T(8,128)S(1)} %get-tuple-element.42.refs_3_, ...), custom_call_target="tpu_custom_call" | custom-call | flops 16777216 | bytes 4194304 | tf_op jit(solution)/shard_map/product/pallas_call | solution.py:182
  26.3 0.0 collective-permute-done.12.other_ref
  26.3 1.1 %collective-permute-start.13 = (f32[16,256]{1,0:T(8,128)S(1)}, f32[16,256]{1,0:T(8,128)S(1)}, u32[]{:S(2)}, u32[]{:S(2)}) collective-permute-start(f32[16,256]{1,0:T(8,128)S(1)} %product.1), channel_id=1, source_target_pairs={{0,2},{1,3},{2,0},{3,1},{4,6},{5,7},{6,4},{7,5},{8,10},{9,11},{10,... | collective-permute-start | bytes 49160 | tf_op jit(solution)/shard_map/ppermute | solution.py:30
  27.4 1.6 %first_sweep.1 = (f32[32,2048]{1,0:T(8,128)S(1)}, f32[32,32]{1,0:T(8,128)S(1)}) custom-call(f32[16,2048]{1,0:T(8,128)S(1)} %add.24.first_ref.mine_ref, f32[16,2048]{1,0:T(8,128)S(1)} %collective-permute-done.12.other_ref), custom_call_target="tpu_custom_call" | custom-call | flops 1000000000 | bytes 7000000 | tf_op jit(solution)/shard_map/first_sweep/pallas_call | solution.py:255
  29.0 1.0 %collective-permute-done.13 = f32[16,256]{1,0:T(8,128)S(1)} collective-permute-done((f32[16,256]{1,0:T(8,128)S(1)}, f32[16,256]{1,0:T(8,128)S(1)}, u32[]{:S(2)}, u32[]{:S(2)}) %collective-permute-start.13) | collective-permute-done | bytes 16416 | tf_op jit(solution)/shard_map/ppermute | solution.py:30
  30.1 0.3 collective-permute-start.14
  30.3 1.9 %second_sweep.1 = (f32[32,2048]{1,0:T(8,128)S(1)}, f32[32,32]{1,0:T(8,128)S(1)}) custom-call(f32[32,2048]{1,0:T(8,128)S(1)} %get-tuple-element.52.first_ref, f32[32,32]{1,0:T(8,128)S(1)} %get-tuple-element.58.step_ref), custom_call_target="tpu_custom_call" | custom-call | flops 1000000000 | bytes 7000000 | tf_op jit(solution)/shard_map/second_sweep/pallas_call | solution.py:281
  32.3 1.5 %collective-permute-done.14 = f32[16,256]{1,0:T(8,128)S(1)} collective-permute-done((f32[16,256]{1,0:T(8,128)S(1)}, f32[16,256]{1,0:T(8,128)S(1)}, u32[]{:S(2)}, u32[]{:S(2)}) %collective-permute-start.14) | collective-permute-done | bytes 16416 | tf_op jit(solution)/shard_map/ppermute | solution.py:30
  33.8 1.9 %collective-permute-start.15 = (f32[16,256]{1,0:T(8,128)S(1)}, f32[16,256]{1,0:T(8,128)S(1)}, u32[]{:S(2)}, u32[]{:S(2)}) collective-permute-start(f32[16,256]{1,0:T(8,128)S(1)} %add.26), channel_id=1, source_target_pairs={{0,8},{1,9},{2,10},{3,11},{4,12},{5,13},{6,14},{7,15},{8,0},{9,1},... | collective-permute-start | bytes 49160 | tf_op jit(solution)/shard_map/ppermute | solution.py:30
  35.7 0.3 basis.1
  36.0 2.4 %collective-permute-done.15 = f32[16,256]{1,0:T(8,128)S(1)} collective-permute-done((f32[16,256]{1,0:T(8,128)S(1)}, f32[16,256]{1,0:T(8,128)S(1)}, u32[]{:S(2)}, u32[]{:S(2)}) %collective-permute-start.15) | collective-permute-done | bytes 16416 | tf_op jit(solution)/shard_map/ppermute | solution.py:30
  38.5 0.0 collective-permute-start.16
  38.5 1.2 %collective-permute-done.16.other_ref = f32[16,256]{1,0:T(8,128)S(1)} collective-permute-done((f32[16,256]{1,0:T(8,128)S(1)}, f32[16,256]{1,0:T(8,128)S(1)}, u32[]{:S(2)}, u32[]{:S(2)}) %collective-permute-start.16) | collective-permute-done | bytes 16416 | tf_op jit(solution)/shard_map/ppermute | solution.py:34
  39.6 1.5 %error_next.1 = (bf16[1,2048,256]{2,1,0:T(8,128)(2,1)}, f32[32,2048]{1,0:T(8,128)}, f32[32,256]{1,0:T(8,128)}) custom-call(f32[32,2048]{1,0:T(8,128)S(1)} %get-tuple-element.62.basis_ref, f32[32,32]{1,0:T(8,128)S(1)} %get-tuple-element.63.inverse_ref, f32[16,256]{1,0:T(8,128)S(1)} %add.27.mine_ref, f32[16,256]{1,0:T(8,128)S(1)} %collective-permute-done.16.other_ref, ...), custom_call_target="tpu_custom_call" | custom-call | flops 33554432 | bytes 3145728 | tf_op jit(solution)/shard_map/error_next/pallas_call | solution.py:345
  (7 shorter events, 0.1 us)
Async XLA Ops:
  3.0 1.5 %collective-permute-start = (f32[16,2048]{1,0:T(8,128)S(1)}, f32[16,2048]{1,0:T(8,128)S(1)}, u32[]{:S(2)}, u32[]{:S(2)}) collective-permute-start(f32[16,2048]{1,0:T(8,128)S(1)} %get-tuple-element.35), channel_id=1, source_target_pairs={{0,1},{1,0},{2,3},{3,2},{4,5},{5,4},{6,7},{7,6},{8,9},{9,8},{10,11... | collective-permute-start | bytes 393224 | tf_op jit(solution)/shard_map/ppermute | solution.py:34
  4.5 6.7 %collective-permute-start.1 = (f32[16,2048]{1,0:T(8,128)S(1)}, f32[16,2048]{1,0:T(8,128)S(1)}, u32[]{:S(2)}, u32[]{:S(2)}) collective-permute-start(f32[16,2048]{1,0:T(8,128)S(1)} %add.21.after_ref), channel_id=1, source_target_pairs={{0,2},{1,3},{2,0},{3,1},{4,6},{5,7},{6,4},{7,5},{8,10},{9,11},{10,... | collective-permute-start | bytes 393224 | tf_op jit(solution)/shard_map/ppermute | solution.py:30
  8.2 11.0 %collective-permute-start.4 = (f32[256,256]{1,0:T(8,128)S(1)}, f32[256,256]{1,0:T(8,128)S(1)}, u32[]{:S(2)}, u32[]{:S(2)}) collective-permute-start(f32[256,256]{1,0:T(8,128)S(1)} %get-tuple-element.39.refs_0_), channel_id=1, source_target_pairs={{0,1},{1,0},{2,3},{3,2},{4,5},{5,4},{6,7},{7,6},{8,9},{9,8},{10,11... | collective-permute-start | bytes 786440 | tf_op jit(solution)/shard_map/ppermute | solution.py:34
  8.3 11.4 %collective-permute-start.5 = (f32[256,256]{1,0:T(8,128)S(1)}, f32[256,256]{1,0:T(8,128)S(1)}, u32[]{:S(2)}, u32[]{:S(2)}) collective-permute-start(f32[256,256]{1,0:T(8,128)S(1)} %get-tuple-element.40.refs_1_), channel_id=1, source_target_pairs={{0,1},{1,0},{2,3},{3,2},{4,5},{5,4},{6,7},{7,6},{8,9},{9,8},{10,11... | collective-permute-start | bytes 786440 | tf_op jit(solution)/shard_map/ppermute | solution.py:34
  8.8 11.0 %collective-permute-start.6 = (f32[256,256]{1,0:T(8,128)S(1)}, f32[256,256]{1,0:T(8,128)S(1)}, u32[]{:S(2)}, u32[]{:S(2)}) collective-permute-start(f32[256,256]{1,0:T(8,128)S(1)} %get-tuple-element.41.refs_2_), channel_id=1, source_target_pairs={{0,1},{1,0},{2,3},{3,2},{4,5},{5,4},{6,7},{7,6},{8,9},{9,8},{10,11... | collective-permute-start | bytes 786440 | tf_op jit(solution)/shard_map/ppermute | solution.py:34
  11.2 5.1 %collective-permute-start.2 = (f32[16,2048]{1,0:T(8,128)S(1)}, f32[16,2048]{1,0:T(8,128)S(1)}, u32[]{:S(2)}, u32[]{:S(2)}) collective-permute-start(f32[16,2048]{1,0:T(8,128)S(1)} %add.22), channel_id=1, source_target_pairs={{0,4},{1,5},{2,6},{3,7},{4,0},{5,1},{6,2},{7,3},{8,12},{9,13},{10,... | collective-permute-start | bytes 393224 | tf_op jit(solution)/shard_map/ppermute | solution.py:30
  16.4 7.9 %collective-permute-start.3 = (f32[16,2048]{1,0:T(8,128)S(1)}, f32[16,2048]{1,0:T(8,128)S(1)}, u32[]{:S(2)}, u32[]{:S(2)}) collective-permute-start(f32[16,2048]{1,0:T(8,128)S(1)} %add.23), channel_id=1, source_target_pairs={{0,8},{1,9},{2,10},{3,11},{4,12},{5,13},{6,14},{7,15},{8,0},{9,1},... | collective-permute-start | bytes 393224 | tf_op jit(solution)/shard_map/ppermute | solution.py:30
  19.2 5.1 %collective-permute-start.7 = (f32[256,256]{1,0:T(8,128)S(1)}, f32[256,256]{1,0:T(8,128)S(1)}, u32[]{:S(2)}, u32[]{:S(2)}) collective-permute-start(f32[256,256]{1,0:T(8,128)S(1)} %get-tuple-element.42.refs_3_), channel_id=1, source_target_pairs={{0,1},{1,0},{2,3},{3,2},{4,5},{5,4},{6,7},{7,6},{8,9},{9,8},{10,11... | collective-permute-start | bytes 786440 | tf_op jit(solution)/shard_map/ppermute | solution.py:34
  19.2 5.7 %collective-permute-start.8 = (f32[256,256]{1,0:T(8,128)S(1)}, f32[256,256]{1,0:T(8,128)S(1)}, u32[]{:S(2)}, u32[]{:S(2)}) collective-permute-start(f32[256,256]{1,0:T(8,128)S(1)} %get-tuple-element.43.refs_4_), channel_id=1, source_target_pairs={{0,1},{1,0},{2,3},{3,2},{4,5},{5,4},{6,7},{7,6},{8,9},{9,8},{10,11... | collective-permute-start | bytes 786440 | tf_op jit(solution)/shard_map/ppermute | solution.py:34
  19.7 5.2 %collective-permute-start.9 = (f32[256,256]{1,0:T(8,128)S(1)}, f32[256,256]{1,0:T(8,128)S(1)}, u32[]{:S(2)}, u32[]{:S(2)}) collective-permute-start(f32[256,256]{1,0:T(8,128)S(1)} %get-tuple-element.44.refs_5_), channel_id=1, source_target_pairs={{0,1},{1,0},{2,3},{3,2},{4,5},{5,4},{6,7},{7,6},{8,9},{9,8},{10,11... | collective-permute-start | bytes 786440 | tf_op jit(solution)/shard_map/ppermute | solution.py:34
  19.8 5.1 %collective-permute-start.10 = (f32[256,256]{1,0:T(8,128)S(1)}, f32[256,256]{1,0:T(8,128)S(1)}, u32[]{:S(2)}, u32[]{:S(2)}) collective-permute-start(f32[256,256]{1,0:T(8,128)S(1)} %get-tuple-element.45.refs_6_), channel_id=1, source_target_pairs={{0,1},{1,0},{2,3},{3,2},{4,5},{5,4},{6,7},{7,6},{8,9},{9,8},{10,11... | collective-permute-start | bytes 786440 | tf_op jit(solution)/shard_map/ppermute | solution.py:34
  24.3 1.5 %collective-permute-start.11 = (f32[256,256]{1,0:T(8,128)S(1)}, f32[256,256]{1,0:T(8,128)S(1)}, u32[]{:S(2)}, u32[]{:S(2)}) collective-permute-start(f32[256,256]{1,0:T(8,128)S(1)} %get-tuple-element.46.refs_7_), channel_id=1, source_target_pairs={{0,1},{1,0},{2,3},{3,2},{4,5},{5,4},{6,7},{7,6},{8,9},{9,8},{10,11... | collective-permute-start | bytes 786440 | tf_op jit(solution)/shard_map/ppermute | solution.py:34
  24.3 2.0 %collective-permute-start.12 = (f32[16,2048]{1,0:T(8,128)S(1)}, f32[16,2048]{1,0:T(8,128)S(1)}, u32[]{:S(2)}, u32[]{:S(2)}) collective-permute-start(f32[16,2048]{1,0:T(8,128)S(1)} %add.24.first_ref.mine_ref), channel_id=1, source_target_pairs={{0,1},{1,0},{2,3},{3,2},{4,5},{5,4},{6,7},{7,6},{8,9},{9,8},{10,11... | collective-permute-start | bytes 393224 | tf_op jit(solution)/shard_map/ppermute | solution.py:34
  26.3 3.7 %collective-permute-start.13 = (f32[16,256]{1,0:T(8,128)S(1)}, f32[16,256]{1,0:T(8,128)S(1)}, u32[]{:S(2)}, u32[]{:S(2)}) collective-permute-start(f32[16,256]{1,0:T(8,128)S(1)} %product.1), channel_id=1, source_target_pairs={{0,2},{1,3},{2,0},{3,1},{4,6},{5,7},{6,4},{7,5},{8,10},{9,11},{10,... | collective-permute-start | bytes 49160 | tf_op jit(solution)/shard_map/ppermute | solution.py:30
  30.1 3.7 %collective-permute-start.14 = (f32[16,256]{1,0:T(8,128)S(1)}, f32[16,256]{1,0:T(8,128)S(1)}, u32[]{:S(2)}, u32[]{:S(2)}) collective-permute-start(f32[16,256]{1,0:T(8,128)S(1)} %add.25), channel_id=1, source_target_pairs={{0,4},{1,5},{2,6},{3,7},{4,0},{5,1},{6,2},{7,3},{8,12},{9,13},{10,... | collective-permute-start | bytes 49160 | tf_op jit(solution)/shard_map/ppermute | solution.py:30
  33.8 4.6 %collective-permute-start.15 = (f32[16,256]{1,0:T(8,128)S(1)}, f32[16,256]{1,0:T(8,128)S(1)}, u32[]{:S(2)}, u32[]{:S(2)}) collective-permute-start(f32[16,256]{1,0:T(8,128)S(1)} %add.26), channel_id=1, source_target_pairs={{0,8},{1,9},{2,10},{3,11},{4,12},{5,13},{6,14},{7,15},{8,0},{9,1},... | collective-permute-start | bytes 49160 | tf_op jit(solution)/shard_map/ppermute | solution.py:30
  38.5 1.2 %collective-permute-start.16 = (f32[16,256]{1,0:T(8,128)S(1)}, f32[16,256]{1,0:T(8,128)S(1)}, u32[]{:S(2)}, u32[]{:S(2)}) collective-permute-start(f32[16,256]{1,0:T(8,128)S(1)} %add.27.mine_ref), channel_id=1, source_target_pairs={{0,1},{1,0},{2,3},{3,2},{4,5},{5,4},{6,7},{7,6},{8,9},{9,8},{10,11... | collective-permute-start | bytes 49160 | tf_op jit(solution)/shard_map/ppermute | solution.py:34
